TPU v7x, 128 devices: a whole 4x4x4 slice. The times are simulated.
128 devices in a mesh: tm: 16 (over z_lo, y, core), gz: 8 (over z_hi, x).
Axes of the slice: x: 4, y: 4, z: 4 (z_hi: 2, z_lo: 2; z = z_hi * 2 + z_lo), core: 2. Of those that a mesh axis runs over, the one named last changes fastest.
Arguments:
- prev_term: float32 [16, 512, 32, 512], P('tm', None, 'gz'), may hold values from -6 to 6
- last_term: float32 [16, 512, 32, 512], P('tm', None, 'gz'), may hold values from -6 to 6
- cos_sum: float32 [16, 512, 32, 512], P('tm', None, 'gz'), may hold values from -2 to 2
- sin_sum: float32 [16, 512, 32, 512], P('tm', None, 'gz'), may hold values from -2 to 2
- speed_sq: float32 [512, 32, 512], P(None, 'gz'), may hold values from 0.5 to 2
- series_coeffs: float32 [16, 4], P('tm'), may hold values from -1 to 1
Outputs:
- displacement: float32 [512, 32, 512], P('tm', 'gz')
- velocity: float32 [512, 32, 512], P('tm', 'gz')
All inputs are finite; a program needn't handle non-finite values.
Results may differ from a plain program's by a relative error of at most 0.00002.
Values sent between devices are 32-bit elements; how exact they have to be, the bound alone decides.
No kernel may reach another device: no remote copies, remote signals or barrier semaphores. Data moves between devices by JAX's collectives and lax.ppermute only.
A program may use at most 256 MiB of HBM per device.

v0:
```python
import jax
import jax.numpy as jnp
from jax import lax
from jax.sharding import PartitionSpec as P

inverse_bound = 1.0 / 12.0


def with_halo(cells, sides, width):
    for axis, dim in sides:
        count = lax.axis_size(axis)
        ends = count - 1
        head = lax.slice_in_dim(cells, 0, width, axis=dim)
        tail = lax.slice_in_dim(cells, cells.shape[dim] - width, cells.shape[dim], axis=dim)
        cells = jnp.concatenate(
            [
                lax.ppermute(tail, axis, [(i, (i + 1) % count) for i in range(ends)]),
                cells,
                lax.ppermute(head, axis, [((i + 1) % count, i) for i in range(ends)]),
            ],
            axis=dim,
        )
    return cells


def operate(field, speed):
    fpad = jnp.pad(field, ((0, 0), (0, 0), (1, 1)))
    kpad = jnp.pad(speed, ((0, 0), (0, 0), (1, 1)))
    center = fpad[1:-1, 1:-1, 1:-1]
    kcenter = kpad[1:-1, 1:-1, 1:-1]
    total = jnp.zeros(center.shape, jnp.float32)
    for slicer in (
        (slice(2, None), slice(1, -1), slice(1, -1)),
        (slice(0, -2), slice(1, -1), slice(1, -1)),
        (slice(1, -1), slice(2, None), slice(1, -1)),
        (slice(1, -1), slice(0, -2), slice(1, -1)),
        (slice(1, -1), slice(1, -1), slice(2, None)),
        (slice(1, -1), slice(1, -1), slice(0, -2)),
    ):
        total = total + 0.5 * (kcenter + kpad[slicer]) * (center - fpad[slicer])
    return total * inverse_bound - center


def xpadded(field):
    return jnp.pad(field, ((1, 1), (0, 0), (0, 0)))


def local(prev_term, last_term, cos_sum, sin_sum, speed_sq, series_coeffs):
    current = last_term[0]
    previous = prev_term[0]
    coeffs = series_coeffs[0]
    planes = current.shape[1]
    cur_ext, speed_ext = (with_halo(current, (("gz", 1),), 1), with_halo(speed_sq, (("gz", 1),), 1))
    nextterm = 2.0 * operate(xpadded(cur_ext), xpadded(speed_ext)) - previous
    next_ext = with_halo(nextterm, (("gz", 1),), 1)
    next_pad = xpadded(next_ext)
    speed_pad = xpadded(speed_ext)
    part_cos = cos_sum[0]
    part_sin = sin_sum[0]
    finalterm = 2.0 * operate(next_pad, speed_pad) - current
    disp = part_cos + coeffs[0] * nextterm + coeffs[1] * finalterm
    veloc = part_sin + coeffs[2] * nextterm + coeffs[3] * finalterm
    summed = lax.psum_scatter(
        jnp.concatenate([disp, veloc], axis=1), "tm", scatter_dimension=0, tiled=True
    )
    return (summed[:, :planes], summed[:, planes:])


def solution(mesh):
    return jax.shard_map(
        local,
        mesh=mesh,
        in_specs=(
            P("tm", None, "gz", None),
            P("tm", None, "gz", None),
            P("tm", None, "gz", None),
            P("tm", None, "gz", None),
            P(None, "gz", None),
            P("tm", None),
        ),
        out_specs=(P("tm", "gz", None), P("tm", "gz", None)),
        check_vma=False,
    )
```

profile of v0, /device:TPU:6, one launch (start us, length us, event | category | flops | bytes accessed | tf_op | source)
XLA Modules:
  0.0 248.9 jit_solution(12424921133343232789)
XLA Ops:
  7.2 0.0 reduce-scatter.2.cloned.1.call-start
  7.2 3.5 %copy.12 = f32[512,4,512]{2,0,1:T(8,128)S(1)} copy(f32[512,4,512]{2,1,0:T(4,128)} %param.10) | data formatting | bytes 8388608 | tf_op args[4]
  10.7 0.0 copy-start.2
  10.8 0.2 fusion.53
  10.9 6.0 %collective-permute-start = (f32[512,1,512]{2,0,1:T(8,128)S(1)}, f32[512,1,512]{2,0,1:T(8,128)S(1)}, u32[]{:S(2)}, u32[]{:S(2)}) collective-permute-start(f32[512,1,512]{2,0,1:T(8,128)S(1)} %get-tuple-element.6), channel_id=1, source_target_pairs={{0,1},{1,2},{2,3},{3,4},{4,5},{5,6},{6,7},{8,9},{9,10},{10,11},{11... | collective-permute-start | bytes 3145736 | tf_op jit(solution)/shard_map/ppermute | solution.py:17
  16.9 1.9 collective-permute-start.1
  18.8 0.0 copy-done.2
  18.9 1.4 copy.31
  20.2 0.0 copy-start.1
  20.2 0.2 fusion.54
  20.4 7.5 %collective-permute-start.2 = (f32[512,1,512]{2,0,1:T(8,128)S(1)}, f32[512,1,512]{2,0,1:T(8,128)S(1)}, u32[]{:S(2)}, u32[]{:S(2)}) collective-permute-start(f32[512,1,512]{2,0,1:T(8,128)S(1)} %get-tuple-element.8), channel_id=1, source_target_pairs={{0,1},{1,2},{2,3},{3,4},{4,5},{5,6},{6,7},{8,9},{9,10},{10,11},{11... | collective-permute-start | bytes 3145736 | tf_op jit(solution)/shard_map/ppermute | solution.py:17
  27.9 1.9 collective-permute-start.3
  29.9 10.6 %collective-permute-done = f32[512,1,512]{2,0,1:T(8,128)S(1)} collective-permute-done((f32[512,1,512]{2,0,1:T(8,128)S(1)}, f32[512,1,512]{2,0,1:T(8,128)S(1)}, u32[]{:S(2)}, u32[]{:S(2)}) %collective-permute-start) | collective-permute-done | bytes 1048608 | tf_op jit(solution)/shard_map/ppermute | solution.py:17
  40.5 8.0 %collective-permute-done.1 = f32[512,1,512]{2,0,1:T(8,128)S(1)} collective-permute-done((f32[512,1,512]{2,0,1:T(8,128)S(1)}, f32[512,1,512]{2,0,1:T(8,128)S(1)}, u32[]{:S(2)}, u32[]{:S(2)}) %collective-permute-start.1) | collective-permute-done | bytes 1048608 | tf_op jit(solution)/shard_map/ppermute | solution.py:19
  48.5 1.2 select_maximum_fusion.4
  49.7 12.1 %collective-permute-done.2 = f32[512,1,512]{2,0,1:T(8,128)S(1)} collective-permute-done((f32[512,1,512]{2,0,1:T(8,128)S(1)}, f32[512,1,512]{2,0,1:T(8,128)S(1)}, u32[]{:S(2)}, u32[]{:S(2)}) %collective-permute-start.2) | collective-permute-done | bytes 1048608 | tf_op jit(solution)/shard_map/ppermute | solution.py:17
  61.8 7.7 %collective-permute-done.3 = f32[512,1,512]{2,0,1:T(8,128)S(1)} collective-permute-done((f32[512,1,512]{2,0,1:T(8,128)S(1)}, f32[512,1,512]{2,0,1:T(8,128)S(1)}, u32[]{:S(2)}, u32[]{:S(2)}) %collective-permute-start.3) | collective-permute-done | bytes 1048608 | tf_op jit(solution)/shard_map/ppermute | solution.py:19
  69.5 0.0 copy-done.1
  69.5 0.0 copy-start.5
  69.5 1.0 copy-done.5
  70.5 3.2 %select_maximum_fusion.2 = f32[514,6,512]{2,0,1:T(8,128)} fusion(f32[512,1,512]{2,0,1:T(8,128)S(1)} %collective-permute-done.3, f32[512,4,512]{2,0,1:T(8,128)S(1)} %bitcast.21, f32[512,1,512]{2,0,1:T(8,128)S(1)} %collective-permute-done.2), kind=kLoop, calls=%fused_computation.11 | loop fusion | flops 12632064 | bytes 12607488 | tf_op jit(solution)/shard_map/concatenate | solution.py:15
  73.7 15.6 %fusion.12 = f32[512,4,512]{2,0,1:T(8,128)S(1)} fusion(f32[512,4,512]{2,0,1:T(8,128)} %bitcast.22, f32[514,6,512]{2,0,1:T(8,128)} %select_maximum_fusion.2, f32[512,1,512]{2,0,1:T(8,128)S(1)} %collective-permute-done.2, f32[512,1,512]{2,0,1:T(8,128)} %copy-done.5, f32[1,512,4,512]{3,2,1,0:T(4,128)} %param.6, f32[512,4,512]{2,0,1:T(8,128)S(1)} %copy.12, ...), kind=kLoop, calls=%fused_computation.27 | loop fusion | flops 38797312 | bytes 50528256 | tf_op jit(solution)/shard_map/sub | solution.py:54
  89.3 0.0 copy-start
  89.3 0.0 copy-start.6
  89.3 0.2 fusion.52
  89.5 1.9 collective-permute-start.4
  91.4 4.1 %collective-permute-start.5 = (f32[512,1,512]{2,0,1:T(8,128)S(1)}, f32[512,1,512]{2,0,1:T(8,128)S(1)}, u32[]{:S(2)}, u32[]{:S(2)}) collective-permute-start(f32[512,1,512]{2,0,1:T(8,128)S(1)} %get-tuple-element.5), channel_id=1, source_target_pairs={{1,0},{2,1},{3,2},{4,3},{5,4},{6,5},{7,6},{9,8},{10,9},{11,10},{12... | collective-permute-start | bytes 3145736 | tf_op jit(solution)/shard_map/ppermute | solution.py:19
  95.5 0.0 copy-done.6
  95.5 0.6 fusion.56
  96.1 19.0 %collective-permute-done.4 = f32[512,1,512]{2,0,1:T(8,128)S(1)} collective-permute-done((f32[512,1,512]{2,0,1:T(8,128)S(1)}, f32[512,1,512]{2,0,1:T(8,128)S(1)}, u32[]{:S(2)}, u32[]{:S(2)}) %collective-permute-start.4) | collective-permute-done | bytes 1048608 | tf_op jit(solution)/shard_map/ppermute | solution.py:17
  115.1 5.5 %collective-permute-done.5 = f32[512,1,512]{2,0,1:T(8,128)S(1)} collective-permute-done((f32[512,1,512]{2,0,1:T(8,128)S(1)}, f32[512,1,512]{2,0,1:T(8,128)S(1)}, u32[]{:S(2)}, u32[]{:S(2)}) %collective-permute-start.5) | collective-permute-done | bytes 1048608 | tf_op jit(solution)/shard_map/ppermute | solution.py:19
  120.6 0.0 copy-done
  120.6 0.0 copy-start.4
  120.6 3.1 %select_maximum_fusion = f32[514,6,512]{2,0,1:T(8,128)} fusion(f32[512,1,512]{2,0,1:T(8,128)S(1)} %collective-permute-done.5, f32[512,4,512]{2,0,1:T(8,128)S(1)} %fusion.12, f32[512,1,512]{2,0,1:T(8,128)S(1)} %collective-permute-done.4), kind=kLoop, calls=%fused_computation.9 | loop fusion | flops 12632064 | bytes 12607488 | tf_op jit(solution)/shard_map/concatenate | solution.py:15
  123.8 0.0 copy-done.4
  123.8 20.1 %fusion.50 = (f32[512,4,512]{2,0,1:T(8,128)}, f32[512,4,512]{2,0,1:T(8,128)}) fusion(f32[1,512,4,512]{3,2,1,0:T(4,128)} %param.8, f32[512,4,512]{2,0,1:T(8,128)} %copy-done, f32[]{:T(128)} %bitcast.4, f32[]{:T(128)} %bitcast.1, f32[1,512,4,512]{3,2,1,0:T(4,128)} %param.7, f32[512,4,512]{2,0,1:T(8,128)S(1)} %copy.12, f32[514,6,512]{2,0,1:T(8,128)} %select_maximum_fusion, ...), kind=kLoop, calls=%fused_computation.79 | loop fusion | flops 42991616 | bytes 58917888 | tf_op jit(solution)/shard_map/add | solution.py:61
  143.9 0.0 copy-start.3
  143.9 10.1 %fusion.49 = f32[512,4,512]{2,0,1:T(8,128)} fusion(f32[1,512,4,512]{3,2,1,0:T(4,128)} %param.9, f32[512,4,512]{2,0,1:T(8,128)} %get-tuple-element.3, f32[512,4,512]{2,0,1:T(8,128)} %copy-done, f32[]{:T(128)} %bitcast.7, f32[]{:T(128)} %bitcast.6), kind=kLoop, calls=%fused_computation.77 | loop fusion | flops 4194304 | bytes 16777224 | tf_op jit(solution)/shard_map/add | solution.py:62
  153.9 0.0 copy-done.3
  153.9 3.8 %pad_maximum_fusion = f32[512,8,512]{2,0,1:T(8,128)S(1)} fusion(f32[512,4,512]{2,0,1:T(8,128)} %fusion.49, f32[512,4,512]{2,0,1:T(8,128)S(1)} %copy-done.3), kind=kLoop, calls=%fused_computation.2 | loop fusion | flops 2097152 | bytes 16777216 | tf_op jit(solution)/shard_map/concatenate | solution.py:64
  157.8 8.1 %copy.23 = f32[512,8,512]{2,1,0:T(8,128)} copy(f32[512,8,512]{2,0,1:T(8,128)S(1)} %pad_maximum_fusion) | data formatting | bytes 16777216 | tf_op jit(solution)/shard_map/concatenate | solution.py:64
  165.9 0.0 reduce-scatter.2.cloned.1.call-update
  165.9 74.0 %reduce-scatter.2.cloned.1.call-done = f32[32,8,512]{2,1,0:T(8,128)} async-done(((f32[512,8,512]{2,1,0:T(8,128)}), f32[32,8,512]{2,1,0:T(8,128)}) %reduce-scatter.2.cloned.1.call-update) | async-done | bytes 524304 | tf_op jit(solution)/shard_map/reduce_scatter | solution.py:63
  239.9 2.1 fusion.55
Async XLA Ops:
  7.2 232.8 %reduce-scatter.2.cloned.1.call-start = ((), (), s32[]{:S(2)}) async-start(), calls=%async_computation.1 | async-start | bytes 8912896 | tf_op jit(solution)/shard_map/reduce_scatter | solution.py:63
  10.7 8.1 %copy-start.2 = (f32[1,512,4,512]{3,2,1,0:T(4,128)S(1)}, f32[1,512,4,512]{3,2,1,0:T(4,128)}, u32[]{:S(2)}) copy-start(f32[1,512,4,512]{3,2,1,0:T(4,128)} %param.7) | copy-start | bytes 12582916
  10.9 29.5 %collective-permute-start = (f32[512,1,512]{2,0,1:T(8,128)S(1)}, f32[512,1,512]{2,0,1:T(8,128)S(1)}, u32[]{:S(2)}, u32[]{:S(2)}) collective-permute-start(f32[512,1,512]{2,0,1:T(8,128)S(1)} %get-tuple-element.6), channel_id=1, source_target_pairs={{0,1},{1,2},{2,3},{3,4},{4,5},{5,6},{6,7},{8,9},{9,10},{10,11},{11... | collective-permute-start | bytes 3145736 | tf_op jit(solution)/shard_map/ppermute | solution.py:17
  16.9 31.6 %collective-permute-start.1 = (f32[512,1,512]{2,0,1:T(8,128)S(1)}, f32[512,1,512]{2,0,1:T(8,128)S(1)}, u32[]{:S(2)}, u32[]{:S(2)}) collective-permute-start(f32[512,1,512]{2,0,1:T(8,128)S(1)} %get-tuple-element.7), channel_id=1, source_target_pairs={{1,0},{2,1},{3,2},{4,3},{5,4},{6,5},{7,6},{9,8},{10,9},{11,10},{12... | collective-permute-start | bytes 3145736 | tf_op jit(solution)/shard_map/ppermute | solution.py:19
  20.2 49.3 %copy-start.1 = (f32[1,512,4,512]{3,1,2,0:T(8,128)}, f32[1,512,4,512]{3,1,2,0:T(8,128)S(1)}, u32[]{:S(2)}) copy-start(f32[1,512,4,512]{3,1,2,0:T(8,128)S(1)} %copy.31) | copy-start | bytes 12582916
  20.4 41.4 %collective-permute-start.2 = (f32[512,1,512]{2,0,1:T(8,128)S(1)}, f32[512,1,512]{2,0,1:T(8,128)S(1)}, u32[]{:S(2)}, u32[]{:S(2)}) collective-permute-start(f32[512,1,512]{2,0,1:T(8,128)S(1)} %get-tuple-element.8), channel_id=1, source_target_pairs={{0,1},{1,2},{2,3},{3,4},{4,5},{5,6},{6,7},{8,9},{9,10},{10,11},{11... | collective-permute-start | bytes 3145736 | tf_op jit(solution)/shard_map/ppermute | solution.py:17
  27.9 41.6 %collective-permute-start.3 = (f32[512,1,512]{2,0,1:T(8,128)S(1)}, f32[512,1,512]{2,0,1:T(8,128)S(1)}, u32[]{:S(2)}, u32[]{:S(2)}) collective-permute-start(f32[512,1,512]{2,0,1:T(8,128)S(1)} %get-tuple-element.9), channel_id=1, source_target_pairs={{1,0},{2,1},{3,2},{4,3},{5,4},{6,5},{7,6},{9,8},{10,9},{11,10},{12... | collective-permute-start | bytes 3145736 | tf_op jit(solution)/shard_map/ppermute | solution.py:19
  69.5 1.0 copy-start.5
  89.3 31.4 %copy-start = (f32[512,4,512]{2,0,1:T(8,128)}, f32[512,4,512]{2,0,1:T(8,128)S(1)}, u32[]{:S(2)}) copy-start(f32[512,4,512]{2,0,1:T(8,128)S(1)} %fusion.12) | copy-start | bytes 12582916
  89.3 6.2 %copy-start.6 = (f32[1,4]{1,0:T(1,128)S(1)}, f32[1,4]{1,0:T(1,128)}, u32[]{:S(2)}) copy-start(f32[1,4]{1,0:T(1,128)} %param.11) | copy-start | bytes 52
  89.5 25.6 %collective-permute-start.4 = (f32[512,1,512]{2,0,1:T(8,128)S(1)}, f32[512,1,512]{2,0,1:T(8,128)S(1)}, u32[]{:S(2)}, u32[]{:S(2)}) collective-permute-start(f32[512,1,512]{2,0,1:T(8,128)S(1)} %get-tuple-element.4), channel_id=1, source_target_pairs={{0,1},{1,2},{2,3},{3,4},{4,5},{5,6},{6,7},{8,9},{9,10},{10,11},{11... | collective-permute-start | bytes 3145736 | tf_op jit(solution)/shard_map/ppermute | solution.py:17
  91.4 29.2 %collective-permute-start.5 = (f32[512,1,512]{2,0,1:T(8,128)S(1)}, f32[512,1,512]{2,0,1:T(8,128)S(1)}, u32[]{:S(2)}, u32[]{:S(2)}) collective-permute-start(f32[512,1,512]{2,0,1:T(8,128)S(1)} %get-tuple-element.5), channel_id=1, source_target_pairs={{1,0},{2,1},{3,2},{4,3},{5,4},{6,5},{7,6},{9,8},{10,9},{11,10},{12... | collective-permute-start | bytes 3145736 | tf_op jit(solution)/shard_map/ppermute | solution.py:19
  120.6 3.2 %copy-start.4 = (f32[512,1,512]{2,0,1:T(8,128)}, f32[512,1,512]{2,0,1:T(8,128)S(1)}, u32[]{:S(2)}) copy-start(f32[512,1,512]{2,0,1:T(8,128)S(1)} %collective-permute-done.5) | copy-start | bytes 3145732
  143.9 10.1 %copy-start.3 = (f32[512,4,512]{2,0,1:T(8,128)S(1)}, f32[512,4,512]{2,0,1:T(8,128)}, u32[]{:S(2)}) copy-start(f32[512,4,512]{2,0,1:T(8,128)} %get-tuple-element.2) | copy-start | bytes 12582916
Sparse Core Ops, SparseCore 0:
  166.0 73.8 reduce-scatter.1
where the time goes:
time: 249 us
  waiting for transfers between devices  137 us (55%)
  other arithmetic  57.1 us (23%)
  starting transfers between devices  23.4 us (9%)
  local copies, waits for them, and re-layouts  17.2 us (7%)
  between operations  14.2 us (6%)
    reduce_scatter x1, waiting for transfers between devices, local(): lax.psum_scatter(jnp.concatenate([disp, veloc], axis=1), 'tm', scatter_di...  74 us
    ppermute x3, waiting for transfers between devices, with_halo(): lax.ppermute(tail, axis, [(i, (i + 1) % count) for i in range(ends)])  41.6 us
    ppermute x3, waiting for transfers between devices, with_halo(): lax.ppermute(head, axis, [((i + 1) % count, i) for i in range(ends)])  21.3 us
    add x1, other arithmetic, local(): disp = part_cos + coeffs[0] * nextterm + coeffs[1] * finalterm  20.1 us
    sub x1, other arithmetic, local(): nextterm = 2.0 * operate(xpadded(cur_ext), xpadded(speed_ext)) - previous  15.6 us
    ppermute x3, starting transfers between devices, with_halo(): lax.ppermute(tail, axis, [(i, (i + 1) % count) for i in range(ends)])  15.4 us
    add x1, other arithmetic, local(): veloc = part_sin + coeffs[2] * nextterm + coeffs[3] * finalterm  10.1 us
    concatenate x1, local copies, waits for them, and re-layouts, local(): jnp.concatenate([disp, veloc], axis=1)  8.09 us
  transfers between devices with their start and end apart: 7, of which 7 were waited for; matrix products, arithmetic and copies ran while one was open for 1% of the time, Pallas kernels for 0%

commit v1 on v0

v1 whole, which is shorter than its diff:
```python
import functools

import jax
import jax.numpy as jnp
from jax import lax
from jax.experimental import pallas as pl
from jax.experimental.pallas import tpu as pltpu
from jax.sharding import PartitionSpec as P

ROWS = 4
VMEM = 16 * 1024 * 1024
F32 = jnp.float32


def packed(cells):
    x = cells.shape[0]
    return cells.reshape(x, 4, 4, 128).transpose(0, 2, 1, 3).reshape(x, 2, 8, 128)


def unpacked(cells):
    x = cells.shape[0]
    return cells.reshape(x, 4, 4, 128).transpose(0, 2, 1, 3).reshape(x, 4, 512)


def roll(cells, shift):
    return pltpu.roll(cells, shift % 8, 1)


def places(n):
    sub = lax.broadcasted_iota(jnp.int32, (n, 8, 128), 1)
    return sub, lax.rem(sub, 4), lax.broadcasted_iota(jnp.int32, (n, 8, 128), 2)


def spread(field, speed, row, n, lower, upper):
    sub, z, lane = places(n)
    first, at_start, at_end = sub < 4, lane == 0, lane == 127
    v = [field[pl.ds(row + 1, n), h] for h in (0, 1)]
    k = [speed[pl.ds(row + 1, n), h] for h in (0, 1)]

    def ahead(a, b):
        ra, rb = pltpu.roll(a, 127, 2), pltpu.roll(b, 127, 2)
        qa, qb = roll(ra, 4), roll(rb, 4)
        return (
            jnp.where(at_end, jnp.where(first, qa, qb), ra),
            jnp.where(at_end, jnp.where(first, qb, 0.0), rb),
        )

    def behind(a, b, edge):
        ra, rb = pltpu.roll(a, 1, 2), pltpu.roll(b, 1, 2)
        qa, qb = roll(ra, 4), roll(rb, 4)
        return (
            jnp.where(at_start, jnp.where(first, edge, qa), ra),
            jnp.where(at_start, jnp.where(first, qa, qb), rb),
        )

    v_y, k_y = ahead(*v), ahead(*k)
    f_y = [(k[h] + k_y[h]) * (v_y[h] - v[h]) for h in (0, 1)]
    b_y = behind(*f_y, k[0] * v[0])
    out = []
    for h in (0, 1):
        kv = k[h] * v[h]
        f_z = jnp.where(z == 3, -upper * kv, (k[h] + roll(k[h], -1)) * (roll(v[h], -1) - v[h]))
        b_z = jnp.where(z == 0, lower * kv, roll(f_z, 1))
        f_x = (k[h] + speed[pl.ds(row + 2, n), h]) * (field[pl.ds(row + 2, n), h] - v[h])
        b_x = (k[h] + speed[pl.ds(row, n), h]) * (v[h] - field[pl.ds(row, n), h])
        out.append((f_x - b_x) + (f_y[h] - b_y[h]) + (f_z - b_z))
    return v, out


def widen(scratch, main, before, after, block, blocks):
    rows = main.shape[0]
    scratch[pl.ds(1, rows)] = main[...]
    scratch[pl.ds(0, 1)] = jnp.where(block > 0, before[...], 0.0)
    scratch[pl.ds(rows + 1, 1)] = jnp.where(block < blocks - 1, after[...], 0.0)


def next_kernel(real, u, u_b, u_a, k, k_b, k_a, p, n_out, up_out, down_out, own_out, us, ks):
    block, blocks = pl.program_id(0), pl.num_programs(0)
    rows = u.shape[0]
    widen(us, u, u_b, u_a, block, blocks)
    widen(ks, k, k_b, k_a, block, blocks)
    lower, upper = real[0], real[1]
    z = places(ROWS // 2)[1]
    z_all = places(ROWS)[1]

    def pair(cells):
        both = cells.reshape(ROWS // 2, 2, 8, 128)
        return both[:, 0], both[:, 1]

    def top(uu, nn):
        even, odd = pair(jnp.where(z_all == 3, nn, roll(uu, -1)))
        return jnp.where(z < 2, roll(even, -2), odd)

    def bottom(uu, nn):
        even, odd = pair(jnp.where(z_all == 0, uu, roll(nn, 1)))
        return jnp.where(z < 2, even, roll(odd, 2))

    def step(i, carry):
        row = i * ROWS
        v, out = spread(us, ks, row, ROWS, lower, upper)
        n = []
        for h in (0, 1):
            n.append(out[h] * (-1.0 / 12.0) - 2.0 * v[h] - p[pl.ds(row, ROWS), h])
            n_out[pl.ds(row, ROWS), h] = n[h]
        half = pl.ds(i * (ROWS // 2), ROWS // 2)
        up_out[half] = top(v[0], n[0])
        down_out[half] = bottom(v[1], n[1])
        own_out[0, half] = bottom(v[0], n[0])
        own_out[1, half] = top(v[1], n[1])
        return carry

    lax.fori_loop(0, rows // ROWS, step, 0)


def series_kernel(place, real, n, n_b, n_a, k, k_b, k_a, u, cos, sin, d_out, v_out, ns, ks, *, blocks, block_of):
    block = block_of(pl.program_id(0), place)
    rows = u.shape[0]
    widen(ns, n, n_b, n_a, block, blocks)
    widen(ks, k, k_b, k_a, block, blocks)
    lower, upper = real[0], real[1]
    c0, c1, c2, c3 = real[2], real[3], real[4], real[5]

    def step(i, carry):
        row = i * ROWS
        here = pl.ds(row, ROWS)
        v, out = spread(ns, ks, row, ROWS, lower, upper)
        for h in (0, 1):
            final = out[h] * (-1.0 / 12.0) - 2.0 * v[h] - u[here, h]
            d_out[0, here, h] = cos[here, h] + c0 * v[h] + c1 * final
            v_out[0, here, h] = sin[here, h] + c2 * v[h] + c3 * final
        return carry

    lax.fori_loop(0, rows // ROWS, step, 0)


def jump_kernel(place, real, *refs, blocks, block_of):
    own, own_b, own_a, low, low_b, low_a, high, high_b, high_a, other_out, same_out = refs
    turn = pl.program_id(0)
    block = block_of(turn, pl.program_id(1), place)
    pairs = low.shape[0]
    c0, c1, c2, c3 = real[2], real[3], real[4], real[5]

    def moments(jump):
        n = jump.shape[0]
        z = places(n)[1]
        even_slot = lax.rem(z, 2) == 0
        du = jnp.where(even_slot, jump, roll(jump, 1))
        dn = jnp.where(even_slot, roll(jump, -1), jump)
        ca = jnp.where(z == 0, c1, jnp.where(z == 1, c0, jnp.where(z == 2, c3, c2)))
        cb = jnp.where(z == 1, c1, jnp.where(z == 3, c3, 0.0))
        even = ca * jnp.where(z < 2, du, roll(du, 2)) + cb * jnp.where(z < 2, dn, roll(dn, 2))
        odd = ca * jnp.where(z >= 2, du, roll(du, -2)) + cb * jnp.where(z >= 2, dn, roll(dn, -2))
        return even, odd

    def fill(out):
        for h, jumps in (
            (0, [own_b[0] - low_b[...], own[0] - low[...], own_a[0] - low_a[...]]),
            (1, [high_b[...] - own_b[1], high[...] - own[1], high_a[...] - own_a[1]]),
        ):
            _, odd = moments(jumps[0])
            out[0, h, pl.ds(0, 1)] = jnp.where(block > 0, odd, 0.0)
            even, odd = moments(jumps[1])
            out[0, h, pl.ds(1, 2 * pairs)] = jnp.stack([even, odd], axis=1).reshape(2 * pairs, 8, 128)
            even, _ = moments(jumps[2])
            out[0, h, pl.ds(2 * pairs + 1, 1)] = jnp.where(block < blocks - 1, even, 0.0)

    @pl.when(turn == 0)
    def _():
        fill(other_out)

    @pl.when(turn == 1)
    def _():
        fill(same_out)


def mend_kernel(real, d, v, e, e_low, e_high, k, k_low, k_high, d_out, v_out, ds, vs):
    rows = d.shape[0]
    lower, upper = real[0], real[1]
    wide = rows + 2
    z = places(wide)[1]
    factor = []
    for h in (0, 1):
        below = (1.0 - lower) * (k[:, h] + roll(k_low[:, h], -3))
        above = (1.0 - upper) * (k[:, h] + roll(k_high[:, h], 3))
        factor.append(jnp.where(z == 0, below, jnp.where(z == 3, -above, 0.0)) * (1.0 / 12.0))
    from_low = [e[0], e_low[...]]
    from_high = [e_high[...], e[1]]
    direct = []
    for field, slot in ((ds, 0), (vs, 2)):
        for h in (0, 1):
            a = jnp.where(z == 0, roll(from_low[h], -slot), roll(from_high[h], 3 - slot))
            b = jnp.where(z == 0, roll(from_low[h], -slot - 1), roll(from_high[h], 2 - slot))
            w = factor[h] * a
            field[:, h] = w
            direct.append((factor[h] * b + 2.0 * jnp.abs(factor[h]) * w)[1 : rows + 1])
    for field, given, out, direct_of in ((ds, d, d_out, direct[:2]), (vs, v, v_out, direct[2:])):
        w, outflow = spread(field, k, 0, rows, lower, upper)
        for h in (0, 1):
            out[:, h] = given[:, h] + direct_of[h] - outflow[h] * (1.0 / 12.0) - 2.0 * w[h]


def row_specs(rows, total, block_of, tail):
    zeros = (0,) * len(tail)
    return [
        pl.BlockSpec((rows, *tail), lambda *i: (block_of(*i), *zeros)),
        pl.BlockSpec((1, *tail), lambda *i: (jnp.maximum(block_of(*i) * rows - 1, 0), *zeros)),
        pl.BlockSpec((1, *tail), lambda *i: (jnp.minimum(block_of(*i) * rows + rows, total - 1), *zeros)),
    ]


SMEM = pl.BlockSpec(memory_space=pltpu.SMEM)
CELL = (2, 8, 128)


def params():
    return pltpu.CompilerParams(vmem_limit_bytes=VMEM)


def cost(reads, flops=0):
    return pl.CostEstimate(flops=flops, bytes_accessed=reads, transcendentals=0)


def next_terms(real, u, k, p, blocks):
    x = u.shape[0]
    rows = x // blocks
    plain = lambda i: i
    main = pl.BlockSpec((rows, *CELL), lambda i: (i, 0, 0, 0))
    half = pl.BlockSpec((rows // 2, 8, 128), lambda i: (i, 0, 0))
    shape = functools.partial(jax.ShapeDtypeStruct, dtype=F32)
    return pl.pallas_call(
        next_kernel,
        grid=(blocks,),
        out_shape=(shape((x, *CELL)), shape((x // 2, 8, 128)), shape((x // 2, 8, 128)), shape((2, x // 2, 8, 128))),
        in_specs=[SMEM, *row_specs(rows, x, plain, CELL), *row_specs(rows, x, plain, CELL), main],
        out_specs=(main, half, half, pl.BlockSpec((2, rows // 2, 8, 128), lambda i: (0, i, 0, 0))),
        scratch_shapes=[pltpu.VMEM((rows + 2, *CELL), F32)] * 2,
        compiler_params=params(),
        cost_estimate=cost(24 * 1024 * 1024),
    )(real, u, u, u, k, k, k, p)


def target(side, turn, place, core):
    way = 1 - 2 * core
    return ((lax.rem(place[0] + side, 2)) * 4 + lax.rem(place[1] + way * turn + 4, 4)) * 2 + core


def series(place, real, n, k, u, cos, sin, blocks, flip):
    x = u.shape[0]
    rows = x // blocks

    def block_of(j, place):
        core = lax.rem(place[2] + flip, 2)
        return target(j // 4, lax.rem(j, 4), place, core)

    main = pl.BlockSpec((rows, *CELL), lambda j, place: (block_of(j, place), 0, 0, 0))
    shape = jax.ShapeDtypeStruct((blocks // 2, rows, *CELL), F32)
    return pl.pallas_call(
        functools.partial(series_kernel, blocks=blocks, block_of=block_of),
        grid_spec=pltpu.PrefetchScalarGridSpec(
            num_scalar_prefetch=1,
            grid=(blocks // 2,),
            in_specs=[SMEM, *row_specs(rows, x, block_of, CELL), *row_specs(rows, x, block_of, CELL), main, main, main],
            out_specs=(
                pl.BlockSpec((1, rows, *CELL), lambda j, place: (j, 0, 0, 0, 0)),
                pl.BlockSpec((1, rows, *CELL), lambda j, place: (lax.rem(j, 4) * 2 + j // 4, 0, 0, 0, 0)),
            ),
            scratch_shapes=[pltpu.VMEM((rows + 2, *CELL), F32)] * 2,
        ),
        out_shape=(shape, shape),
        compiler_params=params(),
        cost_estimate=cost(14 * 1024 * 1024),
    )(place, real, n, n, n, k, k, k, u, cos, sin)


def jumps(place, real, own, low, high, blocks):
    x = own.shape[1] * 2
    rows = x // blocks
    pairs = rows // 2

    def block_of(turn, j, place):
        core = lax.rem(place[2] + 1 - turn, 2)
        return target(lax.rem(j, 2), j // 2, place, core)

    plane = row_specs(pairs, x // 2, block_of, (8, 128))
    own_specs = [
        pl.BlockSpec((2, n, 8, 128), lambda *i, spec=spec: (0, *spec.index_map(*i)))
        for n, spec in zip((pairs, 1, 1), plane)
    ]
    shape = jax.ShapeDtypeStruct((blocks // 2, 2, rows + 2, 8, 128), F32)
    last = blocks // 2 - 1
    return pl.pallas_call(
        functools.partial(jump_kernel, blocks=blocks, block_of=block_of),
        grid_spec=pltpu.PrefetchScalarGridSpec(
            num_scalar_prefetch=1,
            grid=(2, blocks // 2),
            in_specs=[SMEM, *own_specs, *plane, *plane],
            out_specs=(
                pl.BlockSpec((1, 2, rows + 2, 8, 128), lambda i, j, place: (jnp.where(i == 0, j, last), 0, 0, 0, 0)),
                pl.BlockSpec((1, 2, rows + 2, 8, 128), lambda i, j, place: (jnp.where(i == 0, 0, j), 0, 0, 0, 0)),
            ),
        ),
        out_shape=(shape, shape),
        compiler_params=params(),
        cost_estimate=cost(8 * 1024 * 1024),
    )(place, real, own, own, own, low, low, low, high, high, high)


def mend(real, d, v, e, e_low, e_high, k, k_low, k_high):
    shape = jax.ShapeDtypeStruct(d.shape, F32)
    whole = pl.BlockSpec(memory_space=pltpu.VMEM)
    return pl.pallas_call(
        mend_kernel,
        out_shape=(shape, shape),
        in_specs=[SMEM] + [whole] * 8,
        out_specs=(whole, whole),
        scratch_shapes=[pltpu.VMEM(k.shape, F32)] * 2,
        compiler_params=params(),
        cost_estimate=cost(4 * 1024 * 1024),
    )(real, d, v, e, e_low, e_high, k, k_low, k_high)


COUNT = 16
SLABS = 8


def along_y(sign):
    def goal(i):
        z, y, core = i // 8, (i // 2) % 4, i % 2
        return z * 8 + ((y + sign * (1 - 2 * core)) % 4) * 2 + core

    return [(i, goal(i)) for i in range(COUNT)]


FORTH, BACK = along_y(1), along_y(-1)
ACROSS = [(i, i ^ 8) for i in range(COUNT)]
SIBLING = [(i, i ^ 1) for i in range(COUNT)]
UP = [(i, i + 1) for i in range(SLABS - 1)]
DOWN = [(i + 1, i) for i in range(SLABS - 1)]


def ring(two, one, back, own):
    relayed = lax.ppermute(two, "tm", FORTH)
    direct = lax.ppermute(back, "tm", BACK)
    rest = lax.ppermute(one + relayed, "tm", FORTH)
    return own + direct + rest


def y_then_z(cells):
    cells = cells.reshape(4, 2, *cells.shape[1:])
    mine = ring(cells[2], cells[1], cells[3], cells[0])
    return mine[0] + lax.ppermute(mine[1], "tm", ACROSS)


def z_then_y(cells):
    half = cells.shape[0] // 2
    mine = cells[:half] + lax.ppermute(cells[half:], "tm", ACROSS)
    return ring(mine[2], mine[1], mine[3], mine[0])


def local(prev_term, last_term, cos_sum, sin_sum, speed_sq, series_coeffs):
    u, p, k = packed(last_term[0]), packed(prev_term[0]), packed(speed_sq)
    cos, sin = packed(cos_sum[0]), packed(sin_sum[0])
    blocks = lax.axis_size("tm")
    rows = u.shape[0] // blocks
    me, slab = lax.axis_index("tm"), lax.axis_index("gz")
    place = jnp.stack([me // 8, (me // 2) % 4, me % 2]).astype(jnp.int32)
    ends = jnp.stack([slab == 0, slab == lax.axis_size("gz") - 1]).astype(F32)
    real = jnp.concatenate([ends, series_coeffs[0]])

    start = me * rows
    k_before = lax.dynamic_slice_in_dim(k, jnp.maximum(start - 1, 0), 1)
    k_after = lax.dynamic_slice_in_dim(k, jnp.minimum(start + rows, u.shape[0] - 1), 1)
    k_here = jnp.concatenate(
        [
            jnp.where(me > 0, k_before, 0.0),
            lax.dynamic_slice_in_dim(k, start, rows),
            jnp.where(me < blocks - 1, k_after, 0.0),
        ]
    )
    k_low, k_high = lax.ppermute(k_here, "gz", UP), lax.ppermute(k_here, "gz", DOWN)

    n, up, down, own = next_terms(real, u, k, p, blocks)
    low, high = lax.ppermute(up, "gz", UP), lax.ppermute(down, "gz", DOWN)

    d_other, v_other = series(place, real, n, k, u, cos, sin, blocks, 1)
    d_came, v_came = lax.ppermute(d_other, "tm", SIBLING), lax.ppermute(v_other, "tm", SIBLING)
    d_same, v_same = series(place, real, n, k, u, cos, sin, blocks, 0)
    d = z_then_y(d_same + d_came)
    v = y_then_z(v_same + v_came)

    e_other, e_same = jumps(place, real, own, low, high, blocks)
    e = y_then_z(e_same + lax.ppermute(e_other, "tm", SIBLING))
    e_low, e_high = lax.ppermute(e[1], "gz", UP), lax.ppermute(e[0], "gz", DOWN)

    d, v = mend(real, d, v, e, e_low, e_high, k_here, k_low, k_high)
    return unpacked(d), unpacked(v)


def solution(mesh):
    return jax.shard_map(
        local,
        mesh=mesh,
        in_specs=(
            P("tm", None, "gz", None),
            P("tm", None, "gz", None),
            P("tm", None, "gz", None),
            P("tm", None, "gz", None),
            P(None, "gz", None),
            P("tm", None),
        ),
        out_specs=(P("tm", "gz", None), P("tm", "gz", None)),
        check_vma=False,
    )
```

time: 249 us -> 180 us (0.72)
  waiting for transfers between devices: 137 us -> 38.8 us
  Pallas kernels: 0 us -> 66.6 us
  other arithmetic: 57.1 us -> 10.3 us
  between operations: 14.2 us -> 0.95 us
  starting transfers between devices: 23.4 us -> 35.6 us
  local copies, waits for them, and re-layouts: 17.2 us -> 26 us
    reduce_scatter x1 -> x0, waiting for transfers between devices: 74 us -> none  [local(): lax.psum_scatter(jnp.concatenate([disp, veloc], axis=1), 'tm', scatter_di...]
    pallas_call x0 -> x5, Pallas kernels: none -> 66.6 us  [the longest x2 27.2 us: series(): pl.pallas_call(functools.partial(series_kernel, blocks=blocks, block_of=b...]
    ppermute x6 -> x21, waiting for transfers between devices: 63 us -> 38.8 us  [the longest x3 8.01 us: ring(): rest = lax.ppermute(one + relayed, 'tm', FORTH)]
    add x2 -> x12, other arithmetic: 30.2 us -> 8.68 us  [the longest x1 2.56 us: local(): d = z_then_y(d_same + d_came)]
    unnamed x16 -> x38, local copies, waits for them, and re-layouts: 5.91 us -> 22.8 us
    sub x1 -> x0, other arithmetic: 15.6 us -> none  [local(): nextterm = 2.0 * operate(xpadded(cur_ext), xpadded(speed_ext)) - previous]
    ppermute x6 -> x21, starting transfers between devices: 23.4 us -> 35.6 us  [the longest x3 8.5 us: ring(): direct = lax.ppermute(back, 'tm', BACK)]
    concatenate x4 -> x2, other arithmetic: 11.3 us -> 0.75 us  [the longest x1 0.73 us: local(): real = jnp.concatenate([ends, series_coeffs[0]])]
  transfers between devices with their start and end apart: 7 -> 21, of which waited for: 7 -> 10; matrix products, arithmetic and copies ran while one was open for 1% -> 7% of each run, Pallas kernels for 0% -> 22%
where the time goes in v1:
time: 180 us; the launch traced here: 178 us
  Pallas kernels  66.6 us (37%)
  waiting for transfers between devices  38.8 us (22%)
  starting transfers between devices  35.6 us (20%)
  local copies, waits for them, and re-layouts  26 us (14%)
  other arithmetic  10.3 us (6%)
    pallas_call x2, Pallas kernels, series(): pl.pallas_call(functools.partial(series_kernel, blocks=blocks, block_of=b...  27.2 us
    pallas_call x1, Pallas kernels, next_terms(): pl.pallas_call(next_kernel, grid=(blocks,), out_shape=(shape((x, *CELL)),...  24.2 us
    unnamed x38, local copies, waits for them, and re-layouts  22.8 us
    pallas_call x1, Pallas kernels, jumps(): pl.pallas_call(functools.partial(jump_kernel, blocks=blocks, block_of=blo...  12.7 us
    ppermute x3, starting transfers between devices, ring(): direct = lax.ppermute(back, 'tm', BACK)  8.5 us
    ppermute x3, waiting for transfers between devices, ring(): rest = lax.ppermute(one + relayed, 'tm', FORTH)  8.01 us
    ppermute x2, starting transfers between devices, local(): low, high = (lax.ppermute(up, 'gz', UP), lax.ppermute(down, 'gz', DOWN))  7.61 us
    ppermute x2, waiting for transfers between devices, y_then_z(): return mine[0] + lax.ppermute(mine[1], 'tm', ACROSS)  6.56 us
  transfers between devices with their start and end apart: 21, of which 10 were waited for; matrix products, arithmetic and copies ran while one was open for 7% of the time, Pallas kernels for 22%

profile of v1, /device:TPU:6, one launch (start us, length us, event | category | flops | bytes accessed | tf_op | source)
XLA Modules:
  0.0 178.2 jit_solution(14820385713017128698)
XLA Ops:
  0.7 0.7 pad_maximum_fusion.1.real
  1.4 2.2 %copy-done = f32[512,4,512]{2,1,0:T(4,128)S(1)} copy-done((f32[512,4,512]{2,1,0:T(4,128)S(1)}, f32[512,4,512]{2,1,0:T(4,128)}, u32[]{:S(2)}) %copy-start) | copy-done | bytes 4194328
  3.6 2.2 %copy-done.5 = f32[1,512,4,512]{3,2,1,0:T(4,128)S(1)} copy-done((f32[1,512,4,512]{3,2,1,0:T(4,128)S(1)}, f32[1,512,4,512]{3,2,1,0:T(4,128)}, u32[]{:S(2)}) %copy-start.5) | copy-done | bytes 4194328
  5.8 2.2 %copy-done.11 = f32[1,512,4,512]{3,2,1,0:T(4,128)S(1)} copy-done((f32[1,512,4,512]{3,2,1,0:T(4,128)S(1)}, f32[1,512,4,512]{3,2,1,0:T(4,128)}, u32[]{:S(2)}) %copy-start.11) | copy-done | bytes 4194328
  8.0 24.2 %shard_map.77 = (f32[512,2,8,128]{3,2,1,0:T(8,128)S(1)}, f32[256,8,128]{2,1,0:T(8,128)}, f32[256,8,128]{2,1,0:T(8,128)}, f32[2,256,8,128]{3,2,1,0:T(8,128)S(1)}) custom-call(f32[6]{0:T(128)S(1)} %pad_maximum_fusion.1.real, f32[512,2,8,128]{3,2,1,0:T(8,128)S(1)} %bitcast.82, f32[512,2,8,128]{3,2,1,0:T(8,128)S(1)} %bitcast.83, ...), custom_call_target="tpu_custom_call" | custom-call | bytes 25165824 | tf_op jit(solution)/shard_map/pallas_call | solution.py:230
  32.2 2.0 %copy-done.2 = f32[512,2,8,128]{3,2,1,0:T(8,128)} copy-done((f32[512,2,8,128]{3,2,1,0:T(8,128)}, f32[512,2,8,128]{3,2,1,0:T(8,128)S(1)}, u32[]{:S(2)}) %copy-start.2) | copy-done | bytes 4194328
  34.2 5.7 %collective-permute-start.10 = (f32[256,8,128]{2,1,0:T(8,128)}, f32[256,8,128]{2,1,0:T(8,128)S(1)}, u32[]{:S(2)}, u32[]{:S(2)}) collective-permute-start(f32[256,8,128]{2,1,0:T(8,128)} %get-tuple-element.20), channel_id=1, source_target_pairs={{0,1},{1,2},{2,3},{3,4},{4,5},{5,6},{6,7},{8,9},{9,10},{10,11},{11... | collective-permute-start | bytes 3145736 | tf_op jit(solution)/shard_map/ppermute | solution.py:383
  39.9 1.9 %collective-permute-start.11 = (f32[256,8,128]{2,1,0:T(8,128)}, f32[256,8,128]{2,1,0:T(8,128)}, u32[]{:S(2)}, u32[]{:S(2)}) collective-permute-start(f32[256,8,128]{2,1,0:T(8,128)} %get-tuple-element.21), channel_id=1, source_target_pairs={{1,0},{2,1},{3,2},{4,3},{5,4},{6,5},{7,6},{9,8},{10,9},{11,10},{12... | collective-permute-start | bytes 3145736 | tf_op jit(solution)/shard_map/ppermute | solution.py:383
  41.9 2.2 %copy-done.1 = f32[512,4,512]{2,1,0:T(4,128)S(1)} copy-done((f32[512,4,512]{2,1,0:T(4,128)S(1)}, f32[512,4,512]{2,1,0:T(4,128)}, u32[]{:S(2)}) %copy-start.1) | copy-done | bytes 4194328
  44.1 2.2 %copy-done.3 = f32[512,2,8,128]{3,2,1,0:T(8,128)S(1)} copy-done((f32[512,2,8,128]{3,2,1,0:T(8,128)S(1)}, f32[512,2,8,128]{3,2,1,0:T(8,128)}, u32[]{:S(2)}) %copy-start.3) | copy-done | bytes 4194328
  46.3 2.2 %copy-done.6 = f32[1,512,4,512]{3,2,1,0:T(4,128)S(1)} copy-done((f32[1,512,4,512]{3,2,1,0:T(4,128)S(1)}, f32[1,512,4,512]{3,2,1,0:T(4,128)}, u32[]{:S(2)}) %copy-start.6) | copy-done | bytes 4194328
  48.5 2.2 %copy-done.8 = f32[1,512,4,512]{3,2,1,0:T(4,128)S(1)} copy-done((f32[1,512,4,512]{3,2,1,0:T(4,128)S(1)}, f32[1,512,4,512]{3,2,1,0:T(4,128)}, u32[]{:S(2)}) %copy-start.8) | copy-done | bytes 4194328
  50.7 2.2 %copy-done.10 = f32[1,512,4,512]{3,2,1,0:T(4,128)S(1)} copy-done((f32[1,512,4,512]{3,2,1,0:T(4,128)S(1)}, f32[1,512,4,512]{3,2,1,0:T(4,128)}, u32[]{:S(2)}) %copy-start.10) | copy-done | bytes 4194328
  52.9 14.2 %shard_map.79 = (f32[8,32,2,8,128]{4,3,2,1,0:T(8,128)}, f32[8,32,2,8,128]{4,3,2,1,0:T(8,128)}) custom-call(s32[3]{0:T(128)S(1)} %pad_add_fusion.place, f32[6]{0:T(128)S(1)} %pad_maximum_fusion.1.real, f32[512,2,8,128]{3,2,1,0:T(8,128)S(1)} %copy-done.3, f32[512,2,8,128]{3,2,1,0:T(8,128)S(1)} %copy-done.3, f32[512,2,8,128]{3,2,1,0:T(8,128)S(1)} %copy-done.3, ...), custom_call_target="tpu_custom_call" | custom-call | bytes 14680064 | tf_op jit(solution)/shard_map/pallas_call | solution.py:257
  67.5 2.8 %collective-permute-done.11.refs_6_.refs_7_.refs_8_ = f32[256,8,128]{2,1,0:T(8,128)} collective-permute-done((f32[256,8,128]{2,1,0:T(8,128)}, f32[256,8,128]{2,1,0:T(8,128)}, u32[]{:S(2)}, u32[]{:S(2)}) %collective-permute-start.11) | collective-permute-done | bytes 1048608 | tf_op jit(solution)/shard_map/ppermute | solution.py:383
  70.3 12.7 %shard_map.80 = (f32[8,2,34,8,128]{4,3,2,1,0:T(8,128)}, f32[8,2,34,8,128]{4,3,2,1,0:T(8,128)S(1)}) custom-call(s32[3]{0:T(128)S(1)} %pad_add_fusion.place, f32[6]{0:T(128)S(1)} %pad_maximum_fusion.1.real, f32[2,256,8,128]{3,2,1,0:T(8,128)S(1)} %get-tuple-element.19.refs_0_.refs_1_.refs_2_, f32[2,256,8,128]{3,2,1,0:T(8,128)S(1)} %get-tuple-element.19.refs_0_.refs_1_.refs_2_, ...), custom_call_target="tpu_custom_call" | custom-call | bytes 8388608 | tf_op jit(solution)/shard_map/pallas_call | solution.py:291
  83.1 1.4 copy-done.12
  84.5 13.0 %shard_map.78 = (f32[8,32,2,8,128]{4,3,2,1,0:T(8,128)S(1)}, f32[8,32,2,8,128]{4,3,2,1,0:T(8,128)S(1)}) custom-call(s32[3]{0:T(128)S(1)} %pad_add_fusion.place, f32[6]{0:T(128)S(1)} %pad_maximum_fusion.1.real, f32[512,2,8,128]{3,2,1,0:T(8,128)S(1)} %copy-done.4, f32[512,2,8,128]{3,2,1,0:T(8,128)S(1)} %copy-done.4, f32[512,2,8,128]{3,2,1,0:T(8,128)S(1)} %copy-done.4, ...), custom_call_target="tpu_custom_call" | custom-call | bytes 14680064 | tf_op jit(solution)/shard_map/pallas_call | solution.py:257
  97.6 1.3 copy-done.14
  98.9 2.6 %add.67 = f32[8,32,2,8,128]{4,3,2,1,0:T(8,128)S(1)} add(f32[8,32,2,8,128]{4,3,2,1,0:T(8,128)} %copy-done.14, f32[8,32,2,8,128]{4,3,2,1,0:T(8,128)} %collective-permute-done) | non-fusion elementwise | flops 524288 | bytes 6291456 | tf_op jit(solution)/shard_map/add | solution.py:388
  101.5 1.1 slice.89
  102.6 1.0 collective-permute-start.1
  103.6 2.0 %add.72 = f32[8,32,2,8,128]{4,3,2,1,0:T(8,128)S(1)} add(f32[8,32,2,8,128]{4,3,2,1,0:T(8,128)S(1)} %get-tuple-element.17, f32[8,32,2,8,128]{4,3,2,1,0:T(8,128)} %collective-permute-done.5) | non-fusion elementwise | flops 524288 | bytes 6291456 | tf_op jit(solution)/shard_map/add | solution.py:389
  105.6 0.9 fusion.8
  107.1 1.6 collective-permute-start.7
  108.7 0.7 dynamic-slice_select_fusion.1
  109.4 1.0 constant_dynamic-slice_fusion
  110.4 5.4 %collective-permute-start.19 = (f32[34,2,8,128]{3,2,1,0:T(8,128)S(1)}, f32[34,2,8,128]{3,2,1,0:T(8,128)S(1)}, u32[]{:S(2)}, u32[]{:S(2)}) collective-permute-start(f32[34,2,8,128]{3,2,1,0:T(8,128)S(1)} %pad_maximum_fusion.k), channel_id=1, source_target_pairs={{0,1},{1,2},{2,3},{3,4},{4,5},{5,6},{6,7},{8,9},{9,10},{10,11},{11... | collective-permute-start | bytes 835592 | tf_op jit(solution)/shard_map/ppermute | solution.py:380
  115.8 1.7 collective-permute-start.6
  117.6 2.2 %add.77 = f32[8,2,34,8,128]{4,3,2,1,0:T(8,128)S(1)} add(f32[8,2,34,8,128]{4,3,2,1,0:T(8,128)S(1)} %copy-done.13, f32[8,2,34,8,128]{4,3,2,1,0:T(8,128)} %collective-permute-done.12) | non-fusion elementwise | flops 557056 | bytes 6684672 | tf_op jit(solution)/shard_map/add | solution.py:392
  120.4 1.6 collective-permute-start.8
  122.0 6.4 %collective-permute-done.1 = f32[4,32,2,8,128]{4,3,2,1,0:T(8,128)} collective-permute-done((f32[4,32,2,8,128]{4,3,2,1,0:T(8,128)}, f32[4,32,2,8,128]{4,3,2,1,0:T(8,128)}, u32[]{:S(2)}, u32[]{:S(2)}) %collective-permute-start.1) | collective-permute-done | bytes 1048608 | tf_op jit(solution)/shard_map/ppermute | solution.py:356
  128.5 1.4 slice_add_fusion
  129.9 3.1 %collective-permute-start.13 = (f32[2,2,34,8,128]{4,3,2,1,0:T(8,128)S(1)}, f32[2,2,34,8,128]{4,3,2,1,0:T(8,128)S(1)}, u32[]{:S(2)}, u32[]{:S(2)}) collective-permute-start(f32[2,2,34,8,128]{4,3,2,1,0:T(8,128)S(1)} %get-tuple-element.28), channel_id=1, source_target_pairs={{0,48},{8,24},{16,0},{24,40},{32,16},{40,56},{48,32},{56,8},{64,11... | collective-permute-start | bytes 1671176 | tf_op jit(solution)/shard_map/ppermute | solution.py:343
  133.2 1.9 %collective-permute-start.20 = (f32[34,2,8,128]{3,2,1,0:T(8,128)S(1)}, f32[34,2,8,128]{3,2,1,0:T(8,128)S(1)}, u32[]{:S(2)}, u32[]{:S(2)}) collective-permute-start(f32[34,2,8,128]{3,2,1,0:T(8,128)S(1)} %pad_maximum_fusion.k), channel_id=1, source_target_pairs={{1,0},{2,1},{3,2},{4,3},{5,4},{6,5},{7,6},{9,8},{10,9},{11,10},{12... | collective-permute-start | bytes 835592 | tf_op jit(solution)/shard_map/ppermute | solution.py:380
  135.1 7.3 %collective-permute-done.8 = f32[2,32,2,8,128]{4,3,2,1,0:T(8,128)S(1)} collective-permute-done((f32[2,32,2,8,128]{4,3,2,1,0:T(8,128)S(1)}, f32[2,32,2,8,128]{4,3,2,1,0:T(8,128)S(1)}, u32[]{:S(2)}, u32[]{:S(2)}) %collective-permute-start.8) | collective-permute-done | bytes 524320 | tf_op jit(solution)/shard_map/ppermute | solution.py:344
  142.6 3.5 %collective-permute-done.13 = f32[2,2,34,8,128]{4,3,2,1,0:T(8,128)S(1)} collective-permute-done((f32[2,2,34,8,128]{4,3,2,1,0:T(8,128)S(1)}, f32[2,2,34,8,128]{4,3,2,1,0:T(8,128)S(1)}, u32[]{:S(2)}, u32[]{:S(2)}) %collective-permute-start.13) | collective-permute-done | bytes 557088 | tf_op jit(solution)/shard_map/ppermute | solution.py:343
  146.0 3.7 %collective-permute-start.2 = (f32[32,2,8,128]{3,2,1,0:T(8,128)S(1)}, f32[32,2,8,128]{3,2,1,0:T(8,128)S(1)}, u32[]{:S(2)}, u32[]{:S(2)}) collective-permute-start(f32[32,2,8,128]{3,2,1,0:T(8,128)S(1)} %get-tuple-element.32), channel_id=1, source_target_pairs={{0,48},{8,24},{16,0},{24,40},{32,16},{40,56},{48,32},{56,8},{64,11... | collective-permute-start | bytes 786440 | tf_op jit(solution)/shard_map/ppermute | solution.py:343
  149.7 0.7 collective-permute-done.15
  150.9 4.7 %collective-permute-done.3 = f32[32,2,8,128]{3,2,1,0:T(8,128)S(1)} collective-permute-done((f32[32,2,8,128]{3,2,1,0:T(8,128)S(1)}, f32[32,2,8,128]{3,2,1,0:T(8,128)S(1)}, u32[]{:S(2)}, u32[]{:S(2)}) %collective-permute-start.3) | collective-permute-done | bytes 262176 | tf_op jit(solution)/shard_map/ppermute | solution.py:342
  155.6 2.3 %collective-permute-done.9 = f32[32,2,8,128]{3,2,1,0:T(8,128)S(1)} collective-permute-done((f32[32,2,8,128]{3,2,1,0:T(8,128)S(1)}, f32[32,2,8,128]{3,2,1,0:T(8,128)S(1)}, u32[]{:S(2)}, u32[]{:S(2)}) %collective-permute-start.9) | collective-permute-done | bytes 262176 | tf_op jit(solution)/shard_map/ppermute | solution.py:351
  157.9 0.7 collective-permute-start.4
  158.7 4.2 %collective-permute-done.16 = f32[2,34,8,128]{3,2,1,0:T(8,128)S(1)} collective-permute-done((f32[2,34,8,128]{3,2,1,0:T(8,128)S(1)}, f32[2,34,8,128]{3,2,1,0:T(8,128)S(1)}, u32[]{:S(2)}, u32[]{:S(2)}) %collective-permute-start.16) | collective-permute-done | bytes 278560 | tf_op jit(solution)/shard_map/ppermute | solution.py:351
  163.0 2.2 %collective-permute-start.17 = (f32[34,8,128]{2,1,0:T(8,128)S(1)}, f32[34,8,128]{2,1,0:T(8,128)S(1)}, u32[]{:S(2)}, u32[]{:S(2)}) collective-permute-start(f32[34,8,128]{2,1,0:T(8,128)S(1)} %get-tuple-element.35), channel_id=1, source_target_pairs={{0,1},{1,2},{2,3},{3,4},{4,5},{5,6},{6,7},{8,9},{9,10},{10,11},{11... | collective-permute-start | bytes 417800 | tf_op jit(solution)/shard_map/ppermute | solution.py:393
  165.2 3.6 %collective-permute-start.18 = (f32[34,8,128]{2,1,0:T(8,128)S(1)}, f32[34,8,128]{2,1,0:T(8,128)S(1)}, u32[]{:S(2)}, u32[]{:S(2)}) collective-permute-start(f32[34,8,128]{2,1,0:T(8,128)S(1)} %get-tuple-element.34), channel_id=1, source_target_pairs={{1,0},{2,1},{3,2},{4,3},{5,4},{6,5},{7,6},{9,8},{10,9},{11,10},{12... | collective-permute-start | bytes 417800 | tf_op jit(solution)/shard_map/ppermute | solution.py:393
  168.9 1.0 collective-permute-done.17.e_low
  169.9 5.9 %collective-permute-done.18.e_high = f32[34,8,128]{2,1,0:T(8,128)S(1)} collective-permute-done((f32[34,8,128]{2,1,0:T(8,128)S(1)}, f32[34,8,128]{2,1,0:T(8,128)S(1)}, u32[]{:S(2)}, u32[]{:S(2)}) %collective-permute-start.18) | collective-permute-done | bytes 139296 | tf_op jit(solution)/shard_map/ppermute | solution.py:393
  175.8 2.4 %shard_map.81 = (f32[32,2,8,128]{3,2,1,0:T(8,128)}, f32[32,2,8,128]{3,2,1,0:T(8,128)}) custom-call(f32[6]{0:T(128)S(1)} %pad_maximum_fusion.1.real, f32[32,2,8,128]{3,2,1,0:T(8,128)S(1)} %fusion.6.d, f32[32,2,8,128]{3,2,1,0:T(8,128)S(1)} %fusion.3.v, f32[2,34,8,128]{3,2,1,0:T(8,128)S(1)} %fusion.2.e, f32[34,8,128]{2,1,0:T(8,128)S(1)} %collective-permute-done.17.e_low, ...), custom_call_target="tpu_custom_call" | custom-call | bytes 4194304 | tf_op jit(solution)/shard_map/pallas_call | solution.py:311
  (62 shorter events, 2.9 us)
Async XLA Ops:
  1.4 2.2 %copy-start = (f32[512,4,512]{2,1,0:T(4,128)S(1)}, f32[512,4,512]{2,1,0:T(4,128)}, u32[]{:S(2)}) copy-start(f32[512,4,512]{2,1,0:T(4,128)} %param.10) | copy-start | bytes 12582916
  3.6 2.2 %copy-start.5 = (f32[1,512,4,512]{3,2,1,0:T(4,128)S(1)}, f32[1,512,4,512]{3,2,1,0:T(4,128)}, u32[]{:S(2)}) copy-start(f32[1,512,4,512]{3,2,1,0:T(4,128)} %param.7) | copy-start | bytes 12582916
  5.8 2.2 %copy-start.11 = (f32[1,512,4,512]{3,2,1,0:T(4,128)S(1)}, f32[1,512,4,512]{3,2,1,0:T(4,128)}, u32[]{:S(2)}) copy-start(f32[1,512,4,512]{3,2,1,0:T(4,128)} %param.6) | copy-start | bytes 12582916
  32.2 2.0 %copy-start.2 = (f32[512,2,8,128]{3,2,1,0:T(8,128)}, f32[512,2,8,128]{3,2,1,0:T(8,128)S(1)}, u32[]{:S(2)}) copy-start(f32[512,2,8,128]{3,2,1,0:T(8,128)S(1)} %get-tuple-element.14.n.n_b.n_a) | copy-start | bytes 12582916
  34.2 33.4 %collective-permute-start.10 = (f32[256,8,128]{2,1,0:T(8,128)}, f32[256,8,128]{2,1,0:T(8,128)S(1)}, u32[]{:S(2)}, u32[]{:S(2)}) collective-permute-start(f32[256,8,128]{2,1,0:T(8,128)} %get-tuple-element.20), channel_id=1, source_target_pairs={{0,1},{1,2},{2,3},{3,4},{4,5},{5,6},{6,7},{8,9},{9,10},{10,11},{11... | collective-permute-start | bytes 3145736 | tf_op jit(solution)/shard_map/ppermute | solution.py:383
  39.9 30.4 %collective-permute-start.11 = (f32[256,8,128]{2,1,0:T(8,128)}, f32[256,8,128]{2,1,0:T(8,128)}, u32[]{:S(2)}, u32[]{:S(2)}) collective-permute-start(f32[256,8,128]{2,1,0:T(8,128)} %get-tuple-element.21), channel_id=1, source_target_pairs={{1,0},{2,1},{3,2},{4,3},{5,4},{6,5},{7,6},{9,8},{10,9},{11,10},{12... | collective-permute-start | bytes 3145736 | tf_op jit(solution)/shard_map/ppermute | solution.py:383
  41.9 2.2 %copy-start.1 = (f32[512,4,512]{2,1,0:T(4,128)S(1)}, f32[512,4,512]{2,1,0:T(4,128)}, u32[]{:S(2)}) copy-start(f32[512,4,512]{2,1,0:T(4,128)} %param.10) | copy-start | bytes 12582916
  44.1 2.2 %copy-start.3 = (f32[512,2,8,128]{3,2,1,0:T(8,128)S(1)}, f32[512,2,8,128]{3,2,1,0:T(8,128)}, u32[]{:S(2)}) copy-start(f32[512,2,8,128]{3,2,1,0:T(8,128)} %copy-done.2) | copy-start | bytes 12582916
  46.3 2.2 %copy-start.6 = (f32[1,512,4,512]{3,2,1,0:T(4,128)S(1)}, f32[1,512,4,512]{3,2,1,0:T(4,128)}, u32[]{:S(2)}) copy-start(f32[1,512,4,512]{3,2,1,0:T(4,128)} %param.7) | copy-start | bytes 12582916
  48.5 2.2 %copy-start.8 = (f32[1,512,4,512]{3,2,1,0:T(4,128)S(1)}, f32[1,512,4,512]{3,2,1,0:T(4,128)}, u32[]{:S(2)}) copy-start(f32[1,512,4,512]{3,2,1,0:T(4,128)} %param.8) | copy-start | bytes 12582916
  50.7 2.2 %copy-start.10 = (f32[1,512,4,512]{3,2,1,0:T(4,128)S(1)}, f32[1,512,4,512]{3,2,1,0:T(4,128)}, u32[]{:S(2)}) copy-start(f32[1,512,4,512]{3,2,1,0:T(4,128)} %param.9) | copy-start | bytes 12582916
  67.0 31.8 %collective-permute-start = (f32[8,32,2,8,128]{4,3,2,1,0:T(8,128)}, f32[8,32,2,8,128]{4,3,2,1,0:T(8,128)}, u32[]{:S(2)}, u32[]{:S(2)}) collective-permute-start(f32[8,32,2,8,128]{4,3,2,1,0:T(8,128)} %get-tuple-element.16), channel_id=1, source_target_pairs={{0,8},{8,0},{16,24},{24,16},{32,40},{40,32},{48,56},{56,48},{64,72... | collective-permute-start | bytes 6291464 | tf_op jit(solution)/shard_map/ppermute | solution.py:386
  67.0 36.6 %collective-permute-start.5 = (f32[8,32,2,8,128]{4,3,2,1,0:T(8,128)}, f32[8,32,2,8,128]{4,3,2,1,0:T(8,128)}, u32[]{:S(2)}, u32[]{:S(2)}) collective-permute-start(f32[8,32,2,8,128]{4,3,2,1,0:T(8,128)} %get-tuple-element.18), channel_id=1, source_target_pairs={{0,8},{8,0},{16,24},{24,16},{32,40},{40,32},{48,56},{56,48},{64,72... | collective-permute-start | bytes 6291464 | tf_op jit(solution)/shard_map/ppermute | solution.py:386
  70.3 14.2 %copy-start.4 = (f32[512,2,8,128]{3,2,1,0:T(8,128)S(1)}, f32[512,2,8,128]{3,2,1,0:T(8,128)}, u32[]{:S(2)}) copy-start(f32[512,2,8,128]{3,2,1,0:T(8,128)} %copy-done.2) | copy-start | bytes 12582916
  70.3 14.2 %copy-start.7 = (f32[1,512,4,512]{3,2,1,0:T(4,128)S(1)}, f32[1,512,4,512]{3,2,1,0:T(4,128)}, u32[]{:S(2)}) copy-start(f32[1,512,4,512]{3,2,1,0:T(4,128)} %param.7) | copy-start | bytes 12582916
  70.3 14.2 %copy-start.9 = (f32[1,512,4,512]{3,2,1,0:T(4,128)S(1)}, f32[1,512,4,512]{3,2,1,0:T(4,128)}, u32[]{:S(2)}) copy-start(f32[1,512,4,512]{3,2,1,0:T(4,128)} %param.8) | copy-start | bytes 12582916
  83.1 1.4 copy-start.12
  84.5 33.1 %collective-permute-start.12 = (f32[8,2,34,8,128]{4,3,2,1,0:T(8,128)}, f32[8,2,34,8,128]{4,3,2,1,0:T(8,128)}, u32[]{:S(2)}, u32[]{:S(2)}) collective-permute-start(f32[8,2,34,8,128]{4,3,2,1,0:T(8,128)} %get-tuple-element.23), channel_id=1, source_target_pairs={{0,8},{8,0},{16,24},{24,16},{32,40},{40,32},{48,56},{56,48},{64,72... | collective-permute-start | bytes 6684680 | tf_op jit(solution)/shard_map/ppermute | solution.py:392
  97.5 1.3 copy-start.14
  101.4 4.2 %copy-start.15 = (f32[8,32,2,8,128]{4,3,2,1,0:T(8,128)}, f32[8,32,2,8,128]{4,3,2,1,0:T(8,128)S(1)}, u32[]{:S(2)}) copy-start(f32[8,32,2,8,128]{4,3,2,1,0:T(8,128)S(1)} %add.67) | copy-start | bytes 6291460
  102.6 25.9 %collective-permute-start.1 = (f32[4,32,2,8,128]{4,3,2,1,0:T(8,128)}, f32[4,32,2,8,128]{4,3,2,1,0:T(8,128)}, u32[]{:S(2)}, u32[]{:S(2)}) collective-permute-start(f32[4,32,2,8,128]{4,3,2,1,0:T(8,128)} %slice.89), channel_id=1, source_target_pairs={{0,64},{8,72},{16,80},{24,88},{32,96},{40,104},{48,112},{56,120},{... | collective-permute-start | bytes 3145736 | tf_op jit(solution)/shard_map/ppermute | solution.py:356
  105.6 1.5 copy-start.17
  105.6 12.0 %copy-start.13 = (f32[8,2,34,8,128]{4,3,2,1,0:T(8,128)S(1)}, f32[8,2,34,8,128]{4,3,2,1,0:T(8,128)}, u32[]{:S(2)}) copy-start(f32[8,2,34,8,128]{4,3,2,1,0:T(8,128)} %copy-done.12) | copy-start | bytes 6684676
  107.1 13.2 %collective-permute-start.7 = (f32[2,32,2,8,128]{4,3,2,1,0:T(8,128)}, f32[2,32,2,8,128]{4,3,2,1,0:T(8,128)S(1)}, u32[]{:S(2)}, u32[]{:S(2)}) collective-permute-start(f32[2,32,2,8,128]{4,3,2,1,0:T(8,128)} %get-tuple-element.31), channel_id=1, source_target_pairs={{0,16},{8,56},{16,32},{24,8},{32,48},{40,24},{48,0},{56,40},{64,80... | collective-permute-start | bytes 1572872 | tf_op jit(solution)/shard_map/ppermute | solution.py:342
  110.4 58.5 %collective-permute-start.19 = (f32[34,2,8,128]{3,2,1,0:T(8,128)S(1)}, f32[34,2,8,128]{3,2,1,0:T(8,128)S(1)}, u32[]{:S(2)}, u32[]{:S(2)}) collective-permute-start(f32[34,2,8,128]{3,2,1,0:T(8,128)S(1)} %pad_maximum_fusion.k), channel_id=1, source_target_pairs={{0,1},{1,2},{2,3},{3,4},{4,5},{5,6},{6,7},{8,9},{9,10},{10,11},{11... | collective-permute-start | bytes 835592 | tf_op jit(solution)/shard_map/ppermute | solution.py:380
  115.8 17.3 %collective-permute-start.6 = (f32[2,32,2,8,128]{4,3,2,1,0:T(8,128)S(1)}, f32[2,32,2,8,128]{4,3,2,1,0:T(8,128)S(1)}, u32[]{:S(2)}, u32[]{:S(2)}) collective-permute-start(f32[2,32,2,8,128]{4,3,2,1,0:T(8,128)S(1)} %get-tuple-element.30), channel_id=1, source_target_pairs={{0,48},{8,24},{16,0},{24,40},{32,16},{40,56},{48,32},{56,8},{64,11... | collective-permute-start | bytes 1572872 | tf_op jit(solution)/shard_map/ppermute | solution.py:343
  117.6 2.7 %copy-start.18 = (f32[8,32,2,8,128]{4,3,2,1,0:T(8,128)S(1)}, f32[8,32,2,8,128]{4,3,2,1,0:T(8,128)}, u32[]{:S(2)}) copy-start(f32[8,32,2,8,128]{4,3,2,1,0:T(8,128)} %copy-done.17) | copy-start | bytes 6291460
  119.8 8.7 %copy-start.16 = (f32[8,32,2,8,128]{4,3,2,1,0:T(8,128)S(1)}, f32[8,32,2,8,128]{4,3,2,1,0:T(8,128)}, u32[]{:S(2)}) copy-start(f32[8,32,2,8,128]{4,3,2,1,0:T(8,128)} %copy-done.15) | copy-start | bytes 6291460
  119.9 13.1 %collective-permute-start.14 = (f32[2,2,34,8,128]{4,3,2,1,0:T(8,128)S(1)}, f32[2,2,34,8,128]{4,3,2,1,0:T(8,128)S(1)}, u32[]{:S(2)}, u32[]{:S(2)}) collective-permute-start(f32[2,2,34,8,128]{4,3,2,1,0:T(8,128)S(1)} %get-tuple-element.29), channel_id=1, source_target_pairs={{0,16},{8,56},{16,32},{24,8},{32,48},{40,24},{48,0},{56,40},{64,80... | collective-permute-start | bytes 1671176 | tf_op jit(solution)/shard_map/ppermute | solution.py:342
  120.4 22.0 %collective-permute-start.8 = (f32[2,32,2,8,128]{4,3,2,1,0:T(8,128)S(1)}, f32[2,32,2,8,128]{4,3,2,1,0:T(8,128)S(1)}, u32[]{:S(2)}, u32[]{:S(2)}) collective-permute-start(f32[2,32,2,8,128]{4,3,2,1,0:T(8,128)S(1)} %slice_add_fusion.3), channel_id=1, source_target_pairs={{0,16},{8,56},{16,32},{24,8},{32,48},{40,24},{48,0},{56,40},{64,80... | collective-permute-start | bytes 1572872 | tf_op jit(solution)/shard_map/ppermute | solution.py:344
  129.9 16.2 %collective-permute-start.13 = (f32[2,2,34,8,128]{4,3,2,1,0:T(8,128)S(1)}, f32[2,2,34,8,128]{4,3,2,1,0:T(8,128)S(1)}, u32[]{:S(2)}, u32[]{:S(2)}) collective-permute-start(f32[2,2,34,8,128]{4,3,2,1,0:T(8,128)S(1)} %get-tuple-element.28), channel_id=1, source_target_pairs={{0,48},{8,24},{16,0},{24,40},{32,16},{40,56},{48,32},{56,8},{64,11... | collective-permute-start | bytes 1671176 | tf_op jit(solution)/shard_map/ppermute | solution.py:343
  133.0 17.4 %collective-permute-start.15 = (f32[2,2,34,8,128]{4,3,2,1,0:T(8,128)S(1)}, f32[2,2,34,8,128]{4,3,2,1,0:T(8,128)S(1)}, u32[]{:S(2)}, u32[]{:S(2)}) collective-permute-start(f32[2,2,34,8,128]{4,3,2,1,0:T(8,128)S(1)} %slice_add_fusion.1), channel_id=1, source_target_pairs={{0,16},{8,56},{16,32},{24,8},{32,48},{40,24},{48,0},{56,40},{64,80... | collective-permute-start | bytes 1671176 | tf_op jit(solution)/shard_map/ppermute | solution.py:344
  133.2 35.8 %collective-permute-start.20 = (f32[34,2,8,128]{3,2,1,0:T(8,128)S(1)}, f32[34,2,8,128]{3,2,1,0:T(8,128)S(1)}, u32[]{:S(2)}, u32[]{:S(2)}) collective-permute-start(f32[34,2,8,128]{3,2,1,0:T(8,128)S(1)} %pad_maximum_fusion.k), channel_id=1, source_target_pairs={{1,0},{2,1},{3,2},{4,3},{5,4},{6,5},{7,6},{9,8},{10,9},{11,10},{12... | collective-permute-start | bytes 835592 | tf_op jit(solution)/shard_map/ppermute | solution.py:380
  142.4 13.1 %collective-permute-start.3 = (f32[32,2,8,128]{3,2,1,0:T(8,128)S(1)}, f32[32,2,8,128]{3,2,1,0:T(8,128)S(1)}, u32[]{:S(2)}, u32[]{:S(2)}) collective-permute-start(f32[32,2,8,128]{3,2,1,0:T(8,128)S(1)} %get-tuple-element.33), channel_id=1, source_target_pairs={{0,16},{8,56},{16,32},{24,8},{32,48},{40,24},{48,0},{56,40},{64,80... | collective-permute-start | bytes 786440 | tf_op jit(solution)/shard_map/ppermute | solution.py:342
  146.0 19.2 %collective-permute-start.2 = (f32[32,2,8,128]{3,2,1,0:T(8,128)S(1)}, f32[32,2,8,128]{3,2,1,0:T(8,128)S(1)}, u32[]{:S(2)}, u32[]{:S(2)}) collective-permute-start(f32[32,2,8,128]{3,2,1,0:T(8,128)S(1)} %get-tuple-element.32), channel_id=1, source_target_pairs={{0,48},{8,24},{16,0},{24,40},{32,16},{40,56},{48,32},{56,8},{64,11... | collective-permute-start | bytes 786440 | tf_op jit(solution)/shard_map/ppermute | solution.py:343
  150.4 7.5 %collective-permute-start.9 = (f32[32,2,8,128]{3,2,1,0:T(8,128)S(1)}, f32[32,2,8,128]{3,2,1,0:T(8,128)S(1)}, u32[]{:S(2)}, u32[]{:S(2)}) collective-permute-start(f32[32,2,8,128]{3,2,1,0:T(8,128)S(1)} %slice_bitcast_fusion.2), channel_id=1, source_target_pairs={{0,64},{8,72},{16,80},{24,88},{32,96},{40,104},{48,112},{56,120},{... | collective-permute-start | bytes 786440 | tf_op jit(solution)/shard_map/ppermute | solution.py:351
  155.6 7.3 %collective-permute-start.16 = (f32[2,34,8,128]{3,2,1,0:T(8,128)S(1)}, f32[2,34,8,128]{3,2,1,0:T(8,128)S(1)}, u32[]{:S(2)}, u32[]{:S(2)}) collective-permute-start(f32[2,34,8,128]{3,2,1,0:T(8,128)S(1)} %slice_bitcast_fusion), channel_id=1, source_target_pairs={{0,64},{8,72},{16,80},{24,88},{32,96},{40,104},{48,112},{56,120},{... | collective-permute-start | bytes 835592 | tf_op jit(solution)/shard_map/ppermute | solution.py:351
  157.9 10.9 %collective-permute-start.4 = (f32[32,2,8,128]{3,2,1,0:T(8,128)S(1)}, f32[32,2,8,128]{3,2,1,0:T(8,128)S(1)}, u32[]{:S(2)}, u32[]{:S(2)}) collective-permute-start(f32[32,2,8,128]{3,2,1,0:T(8,128)S(1)} %fusion.4), channel_id=1, source_target_pairs={{0,16},{8,56},{16,32},{24,8},{32,48},{40,24},{48,0},{56,40},{64,80... | collective-permute-start | bytes 786440 | tf_op jit(solution)/shard_map/ppermute | solution.py:344
  163.0 6.9 %collective-permute-start.17 = (f32[34,8,128]{2,1,0:T(8,128)S(1)}, f32[34,8,128]{2,1,0:T(8,128)S(1)}, u32[]{:S(2)}, u32[]{:S(2)}) collective-permute-start(f32[34,8,128]{2,1,0:T(8,128)S(1)} %get-tuple-element.35), channel_id=1, source_target_pairs={{0,1},{1,2},{2,3},{3,4},{4,5},{5,6},{6,7},{8,9},{9,10},{10,11},{11... | collective-permute-start | bytes 417800 | tf_op jit(solution)/shard_map/ppermute | solution.py:393
  165.2 10.6 %collective-permute-start.18 = (f32[34,8,128]{2,1,0:T(8,128)S(1)}, f32[34,8,128]{2,1,0:T(8,128)S(1)}, u32[]{:S(2)}, u32[]{:S(2)}) collective-permute-start(f32[34,8,128]{2,1,0:T(8,128)S(1)} %get-tuple-element.34), channel_id=1, source_target_pairs={{1,0},{2,1},{3,2},{4,3},{5,4},{6,5},{7,6},{9,8},{10,9},{11,10},{12... | collective-permute-start | bytes 417800 | tf_op jit(solution)/shard_map/ppermute | solution.py:393

commit v2 on v1

v2 whole, which is shorter than its diff:
```python
import jax
import jax.numpy as jnp
from jax import lax
from jax.experimental import pallas as pl
from jax.experimental.pallas import tpu as pltpu
from jax.sharding import PartitionSpec as P

CHIPS = 8
GROUP = 16
PLANES = ((3, 0), (0, 1), (0, 0), (3, 1))
MIB = 1024 * 1024
F32 = jnp.float32


def packed(cells):
    x = cells.shape[0]
    return cells.reshape(x, 4, 4, 128).transpose(0, 2, 1, 3).reshape(x, 2, 8, 128)


def unpacked(cells):
    x = cells.shape[0]
    return cells.reshape(x, 4, 4, 128).transpose(0, 2, 1, 3).reshape(x, 4, 512)


def roll(cells, shift):
    return pltpu.roll(cells, shift % 8, 1)


def places(n):
    sub = lax.broadcasted_iota(jnp.int32, (n, 8, 128), 1)
    return sub, lax.rem(sub, 4), lax.broadcasted_iota(jnp.int32, (n, 8, 128), 2)


def spread(field, speed, row, n, lower, upper):
    sub, z, lane = places(n)
    first, at_start, at_end = sub < 4, lane == 0, lane == 127
    v = [field[pl.ds(row + 1, n), h] for h in (0, 1)]
    k = [speed[pl.ds(row + 1, n), h] for h in (0, 1)]

    def ahead(a, b):
        ra, rb = pltpu.roll(a, 127, 2), pltpu.roll(b, 127, 2)
        qa, qb = roll(ra, 4), roll(rb, 4)
        return (
            jnp.where(at_end, jnp.where(first, qa, qb), ra),
            jnp.where(at_end, jnp.where(first, qb, 0.0), rb),
        )

    def behind(a, b, edge):
        ra, rb = pltpu.roll(a, 1, 2), pltpu.roll(b, 1, 2)
        qa, qb = roll(ra, 4), roll(rb, 4)
        return (
            jnp.where(at_start, jnp.where(first, edge, qa), ra),
            jnp.where(at_start, jnp.where(first, qa, qb), rb),
        )

    v_y, k_y = ahead(*v), ahead(*k)
    f_y = [(k[h] + k_y[h]) * (v_y[h] - v[h]) for h in (0, 1)]
    b_y = behind(*f_y, k[0] * v[0])
    out = []
    for h in (0, 1):
        kv = k[h] * v[h]
        f_z = jnp.where(z == 3, -upper * kv, (k[h] + roll(k[h], -1)) * (roll(v[h], -1) - v[h]))
        b_z = jnp.where(z == 0, lower * kv, roll(f_z, 1))
        f_x = (k[h] + speed[pl.ds(row + 2, n), h]) * (field[pl.ds(row + 2, n), h] - v[h])
        b_x = (k[h] + speed[pl.ds(row, n), h]) * (v[h] - field[pl.ds(row, n), h])
        out.append((f_x - b_x) + (f_y[h] - b_y[h]) + (f_z - b_z))
    return v, out


def widen(scratch, main, before, after, block, blocks):
    rows = main.shape[0]
    scratch[pl.ds(1, rows)] = main[...]
    scratch[pl.ds(0, 1)] = jnp.where(block > 0, before[...], 0.0)
    scratch[pl.ds(rows + 1, 1)] = jnp.where(block < blocks - 1, after[...], 0.0)


def series_kernel(place, real, u, k, p, cos, sin, d_other, d_same, v_other, v_same, n_up, n_down, n_low, n_high,
                  us, ks, ns, ds, vs, fx, fy, fw, fz, fm, planes, in_sem, out_sem, plane_sem):
    cells = u.shape[0] // 16
    rows = cells // CHIPS
    half_rows = rows // 2
    lower, upper, c0, c1, c2, c3 = (real[i] for i in range(6))
    sub = lax.broadcasted_iota(jnp.int32, (8, 128), 0)
    lane = lax.broadcasted_iota(jnp.int32, (8, 128), 1)
    z = lax.rem(sub, 4)
    first, at_start, at_end = sub < 4, lane == 0, lane == 127
    open_up, open_down = jnp.where(z == 3, 0.0, 1.0), jnp.where(z == 0, 0.0, 1.0)
    y_first, y_last = jnp.logical_and(first, at_start), jnp.logical_and(jnp.logical_not(first), at_end)
    outer = jnp.where(z == 0, lower, 0.0) + jnp.where(z == 3, upper, 0.0)

    def arrays():
        return ((u, us, 16), (k, ks, 16), (p, ns, 16), (cos, ds, 0), (sin, vs, 0))

    def loads(c, which):
        return [
            pltpu.make_async_copy(a.at[pl.ds(c * rows * 16, rows * 16)], b.at[pl.ds(c * rows * 16 + off, rows * 16)], in_sem.at[i, c])
            for i, (a, b, off) in enumerate(arrays()) if i in which
        ]

    for c in range(CHIPS):
        for copy in loads(c, (0, 1, 2)):
            copy.start()
        if c:
            for copy in loads(c - 1, (3, 4)):
                copy.start()
    for copy in loads(CHIPS - 1, (3, 4)):
        copy.start()
    nothing = jnp.zeros((16, 128), F32)
    fx[0:16] = nothing
    fz[0:16] = nothing
    for ref in (us, ks, ns):
        ref[0:16] = nothing
        ref[(cells + 1) * 16 : (cells + 2) * 16] = nothing

    def at(ref, row, by=0):
        return ref[pl.ds(row + by, 8), :]

    def ahead(ref, row, here):
        return pltpu.roll(jnp.where(at_start, at(ref, row, 4), here), 127, 1)

    def behind(ref, row, here):
        return pltpu.roll(jnp.where(at_end, at(ref, row, -4), here), 1, 1)

    def up(here):
        return pltpu.roll(here, 7, 0)

    def down(here):
        return pltpu.roll(here, 1, 0)

    def first_pass(c):
        def step(i, carry):
            start = (c * rows + i * GROUP + 1) * 16
            kk, uu, kx = {}, {}, {}

            def center(seen, ref, g, h):
                if (g, h) not in seen:
                    seen[g, h] = at(ref, start + g * 16 + h * 8)
                return seen[g, h]

            for h in (0, 1):
                kx[-1, h] = center(kk, ks, -1, h) + center(kk, ks, 0, h)
            for g in range(GROUP):
                for h in (0, 1):
                    row = start + g * 16 + h * 8
                    k0 = center(kk, ks, g, h)
                    kx[g, h] = k0 + center(kk, ks, g + 1, h)
                    ky, kw = k0 + ahead(ks, row, k0), k0 + behind(ks, row, k0)
                    if h == 0:
                        face_w = jnp.where(y_first, k0, kw)
                        face_y, kw = ky, jnp.where(y_first, 0.0, kw)
                    else:
                        face_y = jnp.where(y_last, k0, ky)
                        face_w, ky = kw, jnp.where(y_last, 0.0, ky)
                    kz, kv = (k0 + up(k0)) * open_up, (k0 + down(k0)) * open_down
                    mid = 24.0 - (((kx[g, h] + kx[g - 1, h]) + (face_y + face_w)) + ((kz + kv) + outer * k0))
                    for ref, value in ((fx, kx[g, h]), (fy, ky), (fw, kw), (fz, kz), (fm, mid)):
                        ref[pl.ds(row, 8), :] = value
                    v = center(uu, us, g, h)
                    out = (kx[g, h] * center(uu, us, g + 1, h) + kx[g - 1, h] * center(uu, us, g - 1, h)) + (kz * up(v) + kv * down(v))
                    out = out + (ky * ahead(us, row, v) + kw * behind(us, row, v)) + mid * v
                    ns[pl.ds(row, 8), :] = out * (-1.0 / 12.0) - at(ns, row)
            return carry

        lax.fori_loop(0, rows // GROUP, step, 0)

        def gather(i, carry):
            for b in range(2):
                x = c * rows + i * 16 + b * 8
                for j, (zz, h) in enumerate(PLANES):
                    for q in (0, 1):
                        planes[j, pl.ds(x, 8), q * 128 : (q + 1) * 128] = ns[pl.ds((x + 1) * 16 + h * 8 + q * 4 + zz, 8, stride=16), :]
            return carry

        lax.fori_loop(0, rows // 16, gather, 0)

    def second_pass(c):
        def step(i, carry):
            start = (c * rows + i * GROUP + 1) * 16
            nn, kx = {}, {}

            def center(seen, ref, g, h):
                if (g, h) not in seen:
                    seen[g, h] = at(ref, start + g * 16 + h * 8)
                return seen[g, h]

            for g in range(GROUP):
                for h in (0, 1):
                    row = start + g * 16 + h * 8
                    v = center(nn, ns, g, h)
                    kz = at(fz, row)
                    out = center(kx, fx, g, h) * center(nn, ns, g + 1, h) + center(kx, fx, g - 1, h) * center(nn, ns, g - 1, h)
                    out = out + (kz * up(v) + down(kz) * down(v))
                    out = out + (at(fy, row) * ahead(ns, row, v) + at(fw, row) * behind(ns, row, v)) + at(fm, row) * v
                    final = out * (-1.0 / 12.0) - at(us, row)
                    ds[pl.ds(row - 16, 8), :] = at(ds, row, -16) + c0 * v + c1 * final
                    vs[pl.ds(row - 16, 8), :] = at(vs, row, -16) + c2 * v + c3 * final
            return carry

        lax.fori_loop(0, rows // GROUP, step, 0)

    def plane_stores(c):
        here = pl.ds(c * rows, rows)
        return [
            pltpu.make_async_copy(planes.at[j, here], out.at[here], plane_sem.at[j, c])
            for j, out in enumerate((n_up, n_down, n_low, n_high))
        ]

    def stores(c, core, same):
        way = 1 - 2 * core
        turn = lax.rem(way * (lax.rem(c, 4) - place[1]) + 8, 4)
        side = lax.rem(c // 4 + place[0], 2)
        here = pl.ds((c * rows + core * half_rows) * 16, half_rows * 16)
        d_to, v_to = (d_same, v_same) if same else (d_other, v_other)
        return [
            pltpu.make_async_copy(ds.at[here], d_to.at[side * 4 + turn], out_sem.at[0, core, c]),
            pltpu.make_async_copy(vs.at[here], v_to.at[turn * 2 + side], out_sem.at[1, core, c]),
        ]

    def chunk(c, carry):
        @pl.when(c < CHIPS)
        def _():
            @pl.when(c == 0)
            def _():
                for copy in loads(c, (0, 1, 2)):
                    copy.wait()

            @pl.when(c + 1 < CHIPS)
            def _():
                for copy in loads(c + 1, (0, 1, 2)):
                    copy.wait()

            first_pass(c)
            for copy in plane_stores(c):
                copy.start()

        @pl.when(c > 0)
        def _():
            for copy in loads(c - 1, (3, 4)):
                copy.wait()
            second_pass(c - 1)
            for core in (0, 1):
                for same in (True, False):
                    @pl.when((place[2] == core) == same)
                    def _():
                        for copy in stores(c - 1, core, same):
                            copy.start()

        return carry

    lax.fori_loop(0, CHIPS + 1, chunk, 0)

    def end(c, carry):
        for copy in plane_stores(c):
            copy.wait()
        for core in (0, 1):
            for copy in stores(c, core, True):
                copy.wait()
        return carry

    lax.fori_loop(0, CHIPS, end, 0)

def mend_kernel(real, d, v, e, e_low, e_high, k, k_low, k_high, d_out, v_out, ds, vs):
    rows = d.shape[0]
    lower, upper = real[0], real[1]
    wide = rows + 2
    z = places(wide)[1]
    factor = []
    for h in (0, 1):
        below = (1.0 - lower) * (k[:, h] + roll(k_low[:, h], -3))
        above = (1.0 - upper) * (k[:, h] + roll(k_high[:, h], 3))
        factor.append(jnp.where(z == 0, below, jnp.where(z == 3, -above, 0.0)) * (1.0 / 12.0))
    from_low = [e[0], e_low[...]]
    from_high = [e_high[...], e[1]]
    direct = []
    for field, slot in ((ds, 0), (vs, 2)):
        for h in (0, 1):
            a = jnp.where(z == 0, roll(from_low[h], -slot), roll(from_high[h], 3 - slot))
            b = jnp.where(z == 0, roll(from_low[h], -slot - 1), roll(from_high[h], 2 - slot))
            w = factor[h] * a
            field[:, h] = w
            direct.append((factor[h] * b + 2.0 * jnp.abs(factor[h]) * w)[1 : rows + 1])
    for field, given, out, direct_of in ((ds, d, d_out, direct[:2]), (vs, v, v_out, direct[2:])):
        w, outflow = spread(field, k, 0, rows, lower, upper)
        for h in (0, 1):
            out[:, h] = given[:, h] + direct_of[h] - outflow[h] * (1.0 / 12.0) - 2.0 * w[h]


def planes_kernel(u, *refs):
    outs, (us, planes, in_sem, out_sem) = refs[:4], refs[4:]
    cells = u.shape[0] // 16
    rows = cells // CHIPS

    def load(c):
        here = pl.ds(c * rows * 16, rows * 16)
        return pltpu.make_async_copy(u.at[here], us.at[here], in_sem.at[c])

    def stores(c):
        here = pl.ds(c * rows, rows)
        return [pltpu.make_async_copy(planes.at[j, here], out.at[here], out_sem.at[j, c]) for j, out in enumerate(outs)]

    for c in range(CHIPS):
        load(c).start()

    def chunk(c, carry):
        load(c).wait()
        for i in range(rows // 8):
            x = c * rows + i * 8
            for j, (z, h) in enumerate(PLANES):
                for q in (0, 1):
                    planes[j, pl.ds(x, 8), q * 128 : (q + 1) * 128] = us[pl.ds(x * 16 + h * 8 + q * 4 + z, 8, stride=16), :]
        for copy in stores(c):
            copy.start()
        return carry

    lax.fori_loop(0, CHIPS, chunk, 0)

    def end(c, carry):
        for copy in stores(c):
            copy.wait()
        return carry

    lax.fori_loop(0, CHIPS, end, 0)


def jumps_kernel(place, real, *refs):
    ins, other, same, es, buffers, in_sem, out_sem = refs[:8], *refs[8:]
    cells = ins[0].shape[0]
    parts = 2 * CHIPS
    rows = cells // parts
    chunks = 4
    size = cells // chunks
    c0, c1, c2, c3 = (real[2 + i] for i in range(4))

    def loads(c):
        here = pl.ds(c * size, size)
        return [pltpu.make_async_copy(a.at[here], buffers.at[j, here], in_sem.at[j, c]) for j, a in enumerate(ins)]

    def stores(d, is_same):
        chip, core = d // 2, d % 2
        way = 1 - 2 * core
        slot = lax.rem(way * (chip % 4 - place[1]) + 8, 4) * 2 + lax.rem(chip // 4 + place[0], 2)
        here = pl.ds(d * rows * 8, (rows + 2) * 8)
        to = same if is_same else other
        return [pltpu.make_async_copy(es.at[h, here], to.at[slot, h], out_sem.at[h, d]) for h in (0, 1)]

    def send(d):
        for is_same in (True, False):
            @pl.when((place[2] == d % 2) == is_same)
            def _():
                for copy in stores(d, is_same):
                    copy.start()

    for c in range(chunks):
        for copy in loads(c):
            copy.start()
    nothing = jnp.zeros((8, 128), F32)
    for h in (0, 1):
        es[h, 0:8] = nothing
        es[h, (cells + 1) * 8 : (cells + 2) * 8] = nothing
    sent = 0
    for c in range(chunks):
        for copy in loads(c):
            copy.wait()

        def step(i, carry):
            x = c * size + i * 8
            for h in (0, 1):
                for q in (0, 1):
                    u_own, n_own, u_near, n_near = (buffers[4 * h + j, pl.ds(x, 8), q * 128 : (q + 1) * 128] for j in range(4))
                    du, dn = (u_own - u_near, n_own - n_near) if h == 0 else (u_near - u_own, n_near - n_own)
                    for m, value in enumerate((c1 * du, c0 * du + c1 * dn, c3 * du, c2 * du + c3 * dn)):
                        es[h, pl.ds((x + 1) * 8 + q * 4 + m, 8, stride=8), :] = value
            return carry

        lax.fori_loop(0, size // 8, step, 0, unroll=2)
        ready = parts if c == chunks - 1 else (c + 1) * size // rows - 1
        for d in range(sent, ready):
            send(d)
        sent = ready
    for d in range(parts):
        for copy in stores(d, True):
            copy.wait()


ANYWHERE = pl.BlockSpec(memory_space=pl.ANY)
SMEM = pl.BlockSpec(memory_space=pltpu.SMEM)


def params(mib):
    return pltpu.CompilerParams(vmem_limit_bytes=mib * MIB)


def cost(mib):
    return pl.CostEstimate(flops=0, bytes_accessed=mib * MIB, transcendentals=0)


def flat(cells):
    return cells.reshape(-1, 128)


def planes_of(u):
    cells = u.shape[0] // 16
    return pl.pallas_call(
        planes_kernel,
        out_shape=(jax.ShapeDtypeStruct((cells, 256), F32),) * 4,
        in_specs=[ANYWHERE],
        out_specs=(ANYWHERE,) * 4,
        scratch_shapes=[
            pltpu.VMEM((cells * 16, 128), F32),
            pltpu.VMEM((4, cells, 256), F32),
            pltpu.SemaphoreType.DMA((CHIPS,)),
            pltpu.SemaphoreType.DMA((4, CHIPS)),
        ],
        compiler_params=params(48),
        cost_estimate=cost(6),
    )(u)


def series(place, real, u, k, p, cos, sin):
    cells = u.shape[0] // 16
    share = jax.ShapeDtypeStruct((CHIPS, cells, 128), F32)
    plane = jax.ShapeDtypeStruct((cells, 256), F32)
    wide = pltpu.VMEM(((cells + 2) * 16, 128), F32)
    exact = pltpu.VMEM((cells * 16, 128), F32)
    return pl.pallas_call(
        series_kernel,
        out_shape=(share,) * 4 + (plane,) * 4,
        in_specs=[SMEM, SMEM] + [ANYWHERE] * 5,
        out_specs=(ANYWHERE,) * 8,
        scratch_shapes=[wide, wide, wide, exact, exact, wide, wide, wide, wide, wide]
        + [
            pltpu.VMEM((4, cells, 256), F32),
            pltpu.SemaphoreType.DMA((5, CHIPS)),
            pltpu.SemaphoreType.DMA((2, 2, CHIPS)),
            pltpu.SemaphoreType.DMA((4, CHIPS)),
        ],
        compiler_params=params(56),
        cost_estimate=cost(45),
    )(place, real, u, k, p, cos, sin)


def jumps(place, real, below, above):
    cells = below[0].shape[0]
    rows = cells // (2 * CHIPS)
    shape = jax.ShapeDtypeStruct((CHIPS, 2, (rows + 2) * 8, 128), F32)
    return pl.pallas_call(
        jumps_kernel,
        out_shape=(shape, shape),
        in_specs=[SMEM, SMEM] + [ANYWHERE] * 8,
        out_specs=(ANYWHERE,) * 2,
        scratch_shapes=[
            pltpu.VMEM((2, (cells + 2) * 8, 128), F32),
            pltpu.VMEM((8, cells, 256), F32),
            pltpu.SemaphoreType.DMA((8, 4)),
            pltpu.SemaphoreType.DMA((2, 2 * CHIPS)),
        ],
        compiler_params=params(24),
        cost_estimate=cost(9),
    )(place, real, *below, *above)


def mend(real, d, v, e, e_low, e_high, k, k_low, k_high):
    shape = jax.ShapeDtypeStruct(d.shape, F32)
    whole = pl.BlockSpec(memory_space=pltpu.VMEM)
    return pl.pallas_call(
        mend_kernel,
        out_shape=(shape, shape),
        in_specs=[SMEM] + [whole] * 8,
        out_specs=(whole, whole),
        scratch_shapes=[pltpu.VMEM(k.shape, F32)] * 2,
        compiler_params=params(16),
        cost_estimate=cost(4),
    )(real, d, v, e, e_low, e_high, k, k_low, k_high)


CELL = (2, 8, 128)
COUNT = 16
SLABS = 8


def along_y(sign):
    def goal(i):
        z, y, core = i // 8, (i // 2) % 4, i % 2
        return z * 8 + ((y + sign * (1 - 2 * core)) % 4) * 2 + core

    return [(i, goal(i)) for i in range(COUNT)]


FORTH, BACK = along_y(1), along_y(-1)
ACROSS = [(i, i ^ 8) for i in range(COUNT)]
SIBLING = [(i, i ^ 1) for i in range(COUNT)]
UP = [(i, i + 1) for i in range(SLABS - 1)]
DOWN = [(i + 1, i) for i in range(SLABS - 1)]


def ring(two, one, back, own):
    relayed = lax.ppermute(two, "tm", FORTH)
    direct = lax.ppermute(back, "tm", BACK)
    rest = lax.ppermute(one + relayed, "tm", FORTH)
    return own + direct + rest


def y_then_z(cells):
    cells = cells.reshape(4, 2, *cells.shape[1:])
    mine = ring(cells[2], cells[1], cells[3], cells[0])
    return mine[0] + lax.ppermute(mine[1], "tm", ACROSS)


def z_then_y(cells):
    half = cells.shape[0] // 2
    mine = cells[:half] + lax.ppermute(cells[half:], "tm", ACROSS)
    return ring(mine[2], mine[1], mine[3], mine[0])


def local(prev_term, last_term, cos_sum, sin_sum, speed_sq, series_coeffs):
    u, p, k = packed(last_term[0]), packed(prev_term[0]), packed(speed_sq)
    cos, sin = packed(cos_sum[0]), packed(sin_sum[0])
    blocks = lax.axis_size("tm")
    rows = u.shape[0] // blocks
    me, slab = lax.axis_index("tm"), lax.axis_index("gz")
    place = jnp.stack([me // 8, (me // 2) % 4, me % 2]).astype(jnp.int32)
    ends = jnp.stack([slab == 0, slab == lax.axis_size("gz") - 1]).astype(F32)
    real = jnp.concatenate([ends, series_coeffs[0]])

    start = me * rows
    k_before = lax.dynamic_slice_in_dim(k, jnp.maximum(start - 1, 0), 1)
    k_after = lax.dynamic_slice_in_dim(k, jnp.minimum(start + rows, u.shape[0] - 1), 1)
    k_here = jnp.concatenate(
        [
            jnp.where(me > 0, k_before, 0.0),
            lax.dynamic_slice_in_dim(k, start, rows),
            jnp.where(me < blocks - 1, k_after, 0.0),
        ]
    )
    k_low, k_high = lax.ppermute(k_here, "gz", UP), lax.ppermute(k_here, "gz", DOWN)

    u_flat = flat(u)
    u_up, u_down, u_low, u_high = planes_of(u_flat)
    u_below, u_above = lax.ppermute(u_up, "gz", UP), lax.ppermute(u_down, "gz", DOWN)

    d_other, d_same, v_other, v_same, n_up, n_down, n_low, n_high = series(place, real, u_flat, flat(k), flat(p), flat(cos), flat(sin))
    n_below, n_above = lax.ppermute(n_up, "gz", UP), lax.ppermute(n_down, "gz", DOWN)
    d = z_then_y(d_same + lax.ppermute(d_other, "tm", SIBLING)).reshape(rows, *CELL)
    v = y_then_z(v_same + lax.ppermute(v_other, "tm", SIBLING)).reshape(rows, *CELL)

    e_other, e_same = jumps(place, real, (u_low, n_low, u_below, n_below), (u_high, n_high, u_above, n_above))
    e = y_then_z(e_same + lax.ppermute(e_other, "tm", SIBLING)).reshape(2, rows + 2, 8, 128)
    e_low, e_high = lax.ppermute(e[1], "gz", UP), lax.ppermute(e[0], "gz", DOWN)

    d, v = mend(real, d, v, e, e_low, e_high, k_here, k_low, k_high)
    return unpacked(d), unpacked(v)


def solution(mesh):
    return jax.shard_map(
        local,
        mesh=mesh,
        in_specs=(
            P("tm", None, "gz", None),
            P("tm", None, "gz", None),
            P("tm", None, "gz", None),
            P("tm", None, "gz", None),
            P(None, "gz", None),
            P("tm", None),
        ),
        out_specs=(P("tm", "gz", None), P("tm", "gz", None)),
        check_vma=False,
    )
```

time: 180 us -> 155 us (0.86)
  Pallas kernels: 66.6 us -> 35.7 us
  local copies, waits for them, and re-layouts: 26 us -> 8.44 us
  waiting for transfers between devices: 38.8 us -> 55.2 us
  starting transfers between devices: 35.6 us -> 43.6 us
    pallas_call x4 -> x3, Pallas kernels: 64.1 us -> 33.3 us  [the longest x1 17 us: series(): pl.pallas_call(series_kernel, out_shape=(share,) * 4 + (plane,) * 4, in_s...]
    ppermute x3 -> x5, waiting for transfers between devices: 2.78 us -> 24.1 us  [the longest x1 9.47 us: local(): lax.ppermute(n_down, 'gz', DOWN)]
    unnamed x38 -> x24, local copies, waits for them, and re-layouts: 22.8 us -> 5.16 us
    ppermute x3 -> x5, starting transfers between devices: 7.61 us -> 13.5 us  [the longest x1 5.7 us: local(): lax.ppermute(u_up, 'gz', UP)]
    ppermute x3, waiting for transfers between devices: 8.01 us -> 2.57 us  [ring(): rest = lax.ppermute(one + relayed, 'tm', FORTH)]
    ppermute x1, starting transfers between devices: 1.92 us -> 5.56 us  [local(): lax.ppermute(k_here, 'gz', DOWN)]
    ppermute x1, starting transfers between devices: 5.42 us -> 1.92 us  [local(): lax.ppermute(k_here, 'gz', UP)]
  transfers between devices with their start and end apart: 21 -> 23, of which waited for: 10 -> 12; matrix products, arithmetic and copies ran while one was open for 7% -> 9% of each run, Pallas kernels for 22% -> 18%
where the time goes in v2:
time: 155 us; the launch traced here: 154 us
  waiting for transfers between devices  55.2 us (36%)
  starting transfers between devices  43.6 us (28%)
  Pallas kernels  35.7 us (23%)
  other arithmetic  10 us (6%)
  local copies, waits for them, and re-layouts  8.44 us (5%)
    pallas_call x1, Pallas kernels, series(): pl.pallas_call(series_kernel, out_shape=(share,) * 4 + (plane,) * 4, in_s...  17 us
    pallas_call x1, Pallas kernels, jumps(): pl.pallas_call(jumps_kernel, out_shape=(shape, shape), in_specs=[SMEM, SM...  11.3 us
    ppermute x1, waiting for transfers between devices, local(): lax.ppermute(n_down, 'gz', DOWN)  9.47 us
    ppermute x3, starting transfers between devices, ring(): direct = lax.ppermute(back, 'tm', BACK)  8.33 us
    ppermute x1, waiting for transfers between devices, local(): lax.ppermute(u_down, 'gz', DOWN)  8.29 us
    ppermute x1, waiting for transfers between devices, z_then_y(): mine = cells[:half] + lax.ppermute(cells[half:], 'tm', ACROSS)  7.09 us
    ppermute x1, waiting for transfers between devices, local(): lax.ppermute(n_up, 'gz', UP)  6.3 us
    ppermute x1, starting transfers between devices, local(): lax.ppermute(u_up, 'gz', UP)  5.7 us
  transfers between devices with their start and end apart: 23, of which 12 were waited for; matrix products, arithmetic and copies ran while one was open for 9% of the time, Pallas kernels for 18%

profile of v2, /device:TPU:6, one launch (start us, length us, event | category | flops | bytes accessed | tf_op | source)
XLA Modules:
  0.0 153.9 jit_solution(8653709679293750541)
XLA Ops:
  0.6 4.9 %shard_map.78 = (f32[512,256]{1,0:T(8,128)S(1)}, f32[512,256]{1,0:T(8,128)S(1)}, f32[512,256]{1,0:T(8,128)S(1)}, f32[512,256]{1,0:T(8,128)S(1)}) custom-call(f32[8192,128]{1,0:T(8,128)} %bitcast.79), custom_call_target="tpu_custom_call" | custom-call | bytes 6291456 | tf_op jit(solution)/shard_map/pallas_call | solution.py:403
  5.6 5.7 %collective-permute-start.10 = (f32[512,256]{1,0:T(8,128)S(1)}, f32[512,256]{1,0:T(8,128)S(1)}, u32[]{:S(2)}, u32[]{:S(2)}) collective-permute-start(f32[512,256]{1,0:T(8,128)S(1)} %get-tuple-element.24), channel_id=1, source_target_pairs={{0,1},{1,2},{2,3},{3,4},{4,5},{5,6},{6,7},{8,9},{9,10},{10,11},{11... | collective-permute-start | bytes 1572872 | tf_op jit(solution)/shard_map/ppermute | solution.py:539
  11.4 0.6 pad_maximum_fusion.1.real
  12.0 0.6 pad_add_fusion.place
  12.6 17.0 %shard_map.77 = (f32[8,512,128]{2,1,0:T(8,128)}, f32[8,512,128]{2,1,0:T(8,128)}, f32[8,512,128]{2,1,0:T(8,128)}, f32[8,512,128]{2,1,0:T(8,128)}, f32[512,256]{1,...) custom-call(s32[3]{0:T(128)} %pad_add_fusion.place, f32[6]{0:T(128)} %pad_maximum_fusion.1.real, ...), custom_call_target="tpu_custom_call" | custom-call | bytes 47185920 | tf_op jit(solution)/shard_map/pallas_call | solution.py:425
  29.6 3.4 %collective-permute-start.11 = (f32[512,256]{1,0:T(8,128)}, f32[512,256]{1,0:T(8,128)S(1)}, u32[]{:S(2)}, u32[]{:S(2)}) collective-permute-start(f32[512,256]{1,0:T(8,128)} %get-tuple-element.25), channel_id=1, source_target_pairs={{0,1},{1,2},{2,3},{3,4},{4,5},{5,6},{6,7},{8,9},{9,10},{10,11},{11... | collective-permute-start | bytes 1572872 | tf_op jit(solution)/shard_map/ppermute | solution.py:542
  33.0 2.4 %collective-permute-start.12 = (f32[512,256]{1,0:T(8,128)S(1)}, f32[512,256]{1,0:T(8,128)S(1)}, u32[]{:S(2)}, u32[]{:S(2)}) collective-permute-start(f32[512,256]{1,0:T(8,128)S(1)} %get-tuple-element.28), channel_id=1, source_target_pairs={{1,0},{2,1},{3,2},{4,3},{5,4},{6,5},{7,6},{9,8},{10,9},{11,10},{12... | collective-permute-start | bytes 1572872 | tf_op jit(solution)/shard_map/ppermute | solution.py:539
  35.5 1.9 %collective-permute-start.13 = (f32[512,256]{1,0:T(8,128)}, f32[512,256]{1,0:T(8,128)S(1)}, u32[]{:S(2)}, u32[]{:S(2)}) collective-permute-start(f32[512,256]{1,0:T(8,128)} %get-tuple-element.29), channel_id=1, source_target_pairs={{1,0},{2,1},{3,2},{4,3},{5,4},{6,5},{7,6},{9,8},{10,9},{11,10},{12... | collective-permute-start | bytes 1572872 | tf_op jit(solution)/shard_map/ppermute | solution.py:542
  37.5 0.8 copy-done
  38.8 6.3 %collective-permute-done.11.refs_3_ = f32[512,256]{1,0:T(8,128)S(1)} collective-permute-done((f32[512,256]{1,0:T(8,128)}, f32[512,256]{1,0:T(8,128)S(1)}, u32[]{:S(2)}, u32[]{:S(2)}) %collective-permute-start.11) | collective-permute-done | bytes 524320 | tf_op jit(solution)/shard_map/ppermute | solution.py:542
  45.1 8.3 %collective-permute-done.12.refs_6_ = f32[512,256]{1,0:T(8,128)S(1)} collective-permute-done((f32[512,256]{1,0:T(8,128)S(1)}, f32[512,256]{1,0:T(8,128)S(1)}, u32[]{:S(2)}, u32[]{:S(2)}) %collective-permute-start.12) | collective-permute-done | bytes 524320 | tf_op jit(solution)/shard_map/ppermute | solution.py:539
  53.4 9.5 %collective-permute-done.13.refs_7_ = f32[512,256]{1,0:T(8,128)S(1)} collective-permute-done((f32[512,256]{1,0:T(8,128)}, f32[512,256]{1,0:T(8,128)S(1)}, u32[]{:S(2)}, u32[]{:S(2)}) %collective-permute-start.13) | collective-permute-done | bytes 524320 | tf_op jit(solution)/shard_map/ppermute | solution.py:542
  62.9 1.0 copy-done.1
  63.9 1.0 copy-done.2
  65.0 1.0 copy-done.3
  66.0 11.3 %shard_map.79 = (f32[8,2,272,128]{3,2,1,0:T(8,128)}, f32[8,2,272,128]{3,2,1,0:T(8,128)S(1)}) custom-call(s32[3]{0:T(128)S(1)} %copy-done.5, f32[6]{0:T(128)S(1)} %copy-done.4, f32[512,256]{1,0:T(8,128)S(1)} %get-tuple-element.22.refs_0_, f32[512,256]{1,0:T(8,128)S(1)} %copy-done.2, f32[512,256]{1,0:T(8,128)S(1)} %copy-done.1, ...), custom_call_target="tpu_custom_call" | custom-call | bytes 9437184 | tf_op jit(solution)/shard_map/pallas_call | solution.py:446
  77.4 2.4 %add.67 = f32[8,512,128]{2,1,0:T(8,128)S(1)} add(f32[8,512,128]{2,1,0:T(8,128)} %get-tuple-element.18, f32[8,512,128]{2,1,0:T(8,128)} %collective-permute-done) | non-fusion elementwise | flops 524288 | bytes 6291456 | tf_op jit(solution)/shard_map/add | solution.py:543
  79.9 1.0 slice.91
  81.0 1.0 collective-permute-start.1
  82.0 0.7 copy-done.10
  82.6 1.9 %add.72 = f32[8,512,128]{2,1,0:T(8,128)S(1)} add(f32[8,512,128]{2,1,0:T(8,128)S(1)} %copy-done.10, f32[8,512,128]{2,1,0:T(8,128)} %collective-permute-done.5) | non-fusion elementwise | flops 524288 | bytes 6291456 | tf_op jit(solution)/shard_map/add | solution.py:544
  84.5 1.1 fusion.8
  85.6 0.5 copy-done.8
  86.1 1.6 %collective-permute-start.7 = (f32[2,512,128]{2,1,0:T(8,128)}, f32[2,512,128]{2,1,0:T(8,128)}, u32[]{:S(2)}, u32[]{:S(2)}) collective-permute-start(f32[2,512,128]{2,1,0:T(8,128)} %get-tuple-element.39), channel_id=1, source_target_pairs={{0,16},{8,56},{16,32},{24,8},{32,48},{40,24},{48,0},{56,40},{64,80... | collective-permute-start | bytes 1572872 | tf_op jit(solution)/shard_map/ppermute | solution.py:497
  87.8 0.7 dynamic-slice_select_fusion.1
  88.5 1.0 constant_dynamic-slice_fusion
  89.5 1.9 %collective-permute-start.21 = (f32[34,2,8,128]{3,2,1,0:T(8,128)S(1)}, f32[34,2,8,128]{3,2,1,0:T(8,128)S(1)}, u32[]{:S(2)}, u32[]{:S(2)}) collective-permute-start(f32[34,2,8,128]{3,2,1,0:T(8,128)S(1)} %pad_maximum_fusion.k), channel_id=1, source_target_pairs={{0,1},{1,2},{2,3},{3,4},{4,5},{5,6},{6,7},{8,9},{9,10},{10,11},{11... | collective-permute-start | bytes 835592 | tf_op jit(solution)/shard_map/ppermute | solution.py:535
  91.4 1.7 %collective-permute-start.6 = (f32[2,512,128]{2,1,0:T(8,128)}, f32[2,512,128]{2,1,0:T(8,128)S(1)}, u32[]{:S(2)}, u32[]{:S(2)}) collective-permute-start(f32[2,512,128]{2,1,0:T(8,128)} %get-tuple-element.38), channel_id=1, source_target_pairs={{0,48},{8,24},{16,0},{24,40},{32,16},{40,56},{48,32},{56,8},{64,11... | collective-permute-start | bytes 1572872 | tf_op jit(solution)/shard_map/ppermute | solution.py:498
  93.1 2.1 %add.77 = f32[8,2,272,128]{3,2,1,0:T(8,128)S(1)} add(f32[8,2,272,128]{3,2,1,0:T(8,128)S(1)} %get-tuple-element.30, f32[8,2,272,128]{3,2,1,0:T(8,128)} %collective-permute-done.14) | non-fusion elementwise | flops 557056 | bytes 6684672 | tf_op jit(solution)/shard_map/add | solution.py:547
  95.8 1.1 collective-permute-done.7
  96.9 1.1 slice_add_fusion.3
  98.0 1.6 %collective-permute-start.8 = (f32[2,512,128]{2,1,0:T(8,128)S(1)}, f32[2,512,128]{2,1,0:T(8,128)S(1)}, u32[]{:S(2)}, u32[]{:S(2)}) collective-permute-start(f32[2,512,128]{2,1,0:T(8,128)S(1)} %slice_add_fusion.3), channel_id=1, source_target_pairs={{0,16},{8,56},{16,32},{24,8},{32,48},{40,24},{48,0},{56,40},{64,80... | collective-permute-start | bytes 1572872 | tf_op jit(solution)/shard_map/ppermute | solution.py:499
  99.6 7.1 %collective-permute-done.1 = f32[4,512,128]{2,1,0:T(8,128)S(1)} collective-permute-done((f32[4,512,128]{2,1,0:T(8,128)}, f32[4,512,128]{2,1,0:T(8,128)S(1)}, u32[]{:S(2)}, u32[]{:S(2)}) %collective-permute-start.1) | collective-permute-done | bytes 1048608 | tf_op jit(solution)/shard_map/ppermute | solution.py:511
  106.7 3.0 %collective-permute-start.15 = (f32[2,2,272,128]{3,2,1,0:T(8,128)S(1)}, f32[2,2,272,128]{3,2,1,0:T(8,128)S(1)}, u32[]{:S(2)}, u32[]{:S(2)}) collective-permute-start(f32[2,2,272,128]{3,2,1,0:T(8,128)S(1)} %get-tuple-element.36), channel_id=1, source_target_pairs={{0,48},{8,24},{16,0},{24,40},{32,16},{40,56},{48,32},{56,8},{64,11... | collective-permute-start | bytes 1671176 | tf_op jit(solution)/shard_map/ppermute | solution.py:498
  110.1 5.6 %collective-permute-start.22 = (f32[34,2,8,128]{3,2,1,0:T(8,128)S(1)}, f32[34,2,8,128]{3,2,1,0:T(8,128)S(1)}, u32[]{:S(2)}, u32[]{:S(2)}) collective-permute-start(f32[34,2,8,128]{3,2,1,0:T(8,128)S(1)} %pad_maximum_fusion.k), channel_id=1, source_target_pairs={{1,0},{2,1},{3,2},{4,3},{5,4},{6,5},{7,6},{9,8},{10,9},{11,10},{12... | collective-permute-start | bytes 835592 | tf_op jit(solution)/shard_map/ppermute | solution.py:535
  115.6 2.6 %collective-permute-done.8 = f32[2,512,128]{2,1,0:T(8,128)S(1)} collective-permute-done((f32[2,512,128]{2,1,0:T(8,128)S(1)}, f32[2,512,128]{2,1,0:T(8,128)S(1)}, u32[]{:S(2)}, u32[]{:S(2)}) %collective-permute-start.8) | collective-permute-done | bytes 524320 | tf_op jit(solution)/shard_map/ppermute | solution.py:499
  118.3 4.4 %collective-permute-done.15 = f32[2,2,272,128]{3,2,1,0:T(8,128)S(1)} collective-permute-done((f32[2,2,272,128]{3,2,1,0:T(8,128)S(1)}, f32[2,2,272,128]{3,2,1,0:T(8,128)S(1)}, u32[]{:S(2)}, u32[]{:S(2)}) %collective-permute-start.15) | collective-permute-done | bytes 557088 | tf_op jit(solution)/shard_map/ppermute | solution.py:498
  122.8 3.7 %collective-permute-start.2 = (f32[512,128]{1,0:T(8,128)S(1)}, f32[512,128]{1,0:T(8,128)S(1)}, u32[]{:S(2)}, u32[]{:S(2)}) collective-permute-start(f32[512,128]{1,0:T(8,128)S(1)} %get-tuple-element.40), channel_id=1, source_target_pairs={{0,48},{8,24},{16,0},{24,40},{32,16},{40,56},{48,32},{56,8},{64,11... | collective-permute-start | bytes 786440 | tf_op jit(solution)/shard_map/ppermute | solution.py:498
  126.4 1.0 collective-permute-start.9
  127.6 4.2 %collective-permute-done.3 = f32[512,128]{1,0:T(8,128)S(1)} collective-permute-done((f32[512,128]{1,0:T(8,128)S(1)}, f32[512,128]{1,0:T(8,128)S(1)}, u32[]{:S(2)}, u32[]{:S(2)}) %collective-permute-start.3) | collective-permute-done | bytes 262176 | tf_op jit(solution)/shard_map/ppermute | solution.py:497
  131.8 1.0 collective-permute-start.18
  132.9 2.4 %collective-permute-done.9 = f32[512,128]{1,0:T(8,128)S(1)} collective-permute-done((f32[512,128]{1,0:T(8,128)S(1)}, f32[512,128]{1,0:T(8,128)S(1)}, u32[]{:S(2)}, u32[]{:S(2)}) %collective-permute-start.9) | collective-permute-done | bytes 262176 | tf_op jit(solution)/shard_map/ppermute | solution.py:506
  135.8 3.1 %collective-permute-done.18 = f32[2,272,128]{2,1,0:T(8,128)S(1)} collective-permute-done((f32[2,272,128]{2,1,0:T(8,128)S(1)}, f32[2,272,128]{2,1,0:T(8,128)S(1)}, u32[]{:S(2)}, u32[]{:S(2)}) %collective-permute-start.18) | collective-permute-done | bytes 278560 | tf_op jit(solution)/shard_map/ppermute | solution.py:506
  139.0 1.9 %collective-permute-start.19 = (f32[34,8,128]{2,1,0:T(8,128)S(1)}, f32[34,8,128]{2,1,0:T(8,128)S(1)}, u32[]{:S(2)}, u32[]{:S(2)}) collective-permute-start(f32[34,8,128]{2,1,0:T(8,128)S(1)} %get-tuple-element.43), channel_id=1, source_target_pairs={{0,1},{1,2},{2,3},{3,4},{4,5},{5,6},{6,7},{8,9},{9,10},{10,11},{11... | collective-permute-start | bytes 417800 | tf_op jit(solution)/shard_map/ppermute | solution.py:548
  141.0 4.3 %collective-permute-start.20 = (f32[34,8,128]{2,1,0:T(8,128)S(1)}, f32[34,8,128]{2,1,0:T(8,128)S(1)}, u32[]{:S(2)}, u32[]{:S(2)}) collective-permute-start(f32[34,8,128]{2,1,0:T(8,128)S(1)} %get-tuple-element.42), channel_id=1, source_target_pairs={{1,0},{2,1},{3,2},{4,3},{5,4},{6,5},{7,6},{9,8},{10,9},{11,10},{12... | collective-permute-start | bytes 417800 | tf_op jit(solution)/shard_map/ppermute | solution.py:548
  145.4 1.0 collective-permute-done.19.e_low
  146.4 5.2 %collective-permute-done.20.e_high = f32[34,8,128]{2,1,0:T(8,128)S(1)} collective-permute-done((f32[34,8,128]{2,1,0:T(8,128)S(1)}, f32[34,8,128]{2,1,0:T(8,128)S(1)}, u32[]{:S(2)}, u32[]{:S(2)}) %collective-permute-start.20) | collective-permute-done | bytes 139296 | tf_op jit(solution)/shard_map/ppermute | solution.py:548
  151.5 2.4 %shard_map.80 = (f32[32,2,8,128]{3,2,1,0:T(8,128)}, f32[32,2,8,128]{3,2,1,0:T(8,128)}) custom-call(f32[6]{0:T(128)S(1)} %copy-done.4, f32[32,2,8,128]{3,2,1,0:T(8,128)S(1)} %bitcast.78, f32[32,2,8,128]{3,2,1,0:T(8,128)S(1)} %bitcast.77, f32[2,34,8,128]{3,2,1,0:T(8,128)S(1)} %bitcast.76, f32[34,8,128]{2,1,0:T(8,128)S(1)} %collective-permute-done.19.e_low, ...), custom_call_target="tpu_custom_call" | custom-call | bytes 4194304 | tf_op jit(solution)/shard_map/pallas_call | solution.py:465
  (51 shorter events, 2.7 us)
Async XLA Ops:
  0.6 10.8 %copy-start.11 = (f32[1,4]{1,0:T(1,128)S(1)}, f32[1,4]{1,0:T(1,128)}, u32[]{:S(2)}) copy-start(f32[1,4]{1,0:T(1,128)} %param.11) | copy-start | bytes 52
  5.6 31.9 %collective-permute-start.10 = (f32[512,256]{1,0:T(8,128)S(1)}, f32[512,256]{1,0:T(8,128)S(1)}, u32[]{:S(2)}, u32[]{:S(2)}) collective-permute-start(f32[512,256]{1,0:T(8,128)S(1)} %get-tuple-element.24), channel_id=1, source_target_pairs={{0,1},{1,2},{2,3},{3,4},{4,5},{5,6},{6,7},{8,9},{9,10},{10,11},{11... | collective-permute-start | bytes 1572872 | tf_op jit(solution)/shard_map/ppermute | solution.py:539
  12.6 50.3 %copy-start.4 = (f32[6]{0:T(128)S(1)}, f32[6]{0:T(128)}, u32[]{:S(2)}) copy-start(f32[6]{0:T(128)} %pad_maximum_fusion.1.real) | copy-start | bytes 76
  12.6 50.3 %copy-start.5 = (s32[3]{0:T(128)S(1)}, s32[3]{0:T(128)}, u32[]{:S(2)}) copy-start(s32[3]{0:T(128)} %pad_add_fusion.place) | copy-start | bytes 40
  29.6 15.5 %collective-permute-start.11 = (f32[512,256]{1,0:T(8,128)}, f32[512,256]{1,0:T(8,128)S(1)}, u32[]{:S(2)}, u32[]{:S(2)}) collective-permute-start(f32[512,256]{1,0:T(8,128)} %get-tuple-element.25), channel_id=1, source_target_pairs={{0,1},{1,2},{2,3},{3,4},{4,5},{5,6},{6,7},{8,9},{9,10},{10,11},{11... | collective-permute-start | bytes 1572872 | tf_op jit(solution)/shard_map/ppermute | solution.py:542
  33.0 20.4 %collective-permute-start.12 = (f32[512,256]{1,0:T(8,128)S(1)}, f32[512,256]{1,0:T(8,128)S(1)}, u32[]{:S(2)}, u32[]{:S(2)}) collective-permute-start(f32[512,256]{1,0:T(8,128)S(1)} %get-tuple-element.28), channel_id=1, source_target_pairs={{1,0},{2,1},{3,2},{4,3},{5,4},{6,5},{7,6},{9,8},{10,9},{11,10},{12... | collective-permute-start | bytes 1572872 | tf_op jit(solution)/shard_map/ppermute | solution.py:539
  35.5 27.4 %collective-permute-start.13 = (f32[512,256]{1,0:T(8,128)}, f32[512,256]{1,0:T(8,128)S(1)}, u32[]{:S(2)}, u32[]{:S(2)}) collective-permute-start(f32[512,256]{1,0:T(8,128)} %get-tuple-element.29), channel_id=1, source_target_pairs={{1,0},{2,1},{3,2},{4,3},{5,4},{6,5},{7,6},{9,8},{10,9},{11,10},{12... | collective-permute-start | bytes 1572872 | tf_op jit(solution)/shard_map/ppermute | solution.py:542
  37.4 40.0 %collective-permute-start = (f32[8,512,128]{2,1,0:T(8,128)}, f32[8,512,128]{2,1,0:T(8,128)}, u32[]{:S(2)}, u32[]{:S(2)}) collective-permute-start(f32[8,512,128]{2,1,0:T(8,128)} %get-tuple-element.19), channel_id=1, source_target_pairs={{0,8},{8,0},{16,24},{24,16},{32,40},{40,32},{48,56},{56,48},{64,72... | collective-permute-start | bytes 6291464 | tf_op jit(solution)/shard_map/ppermute | solution.py:543
  37.5 0.8 copy-start
  38.3 43.6 %collective-permute-start.5 = (f32[8,512,128]{2,1,0:T(8,128)}, f32[8,512,128]{2,1,0:T(8,128)}, u32[]{:S(2)}, u32[]{:S(2)}) collective-permute-start(f32[8,512,128]{2,1,0:T(8,128)} %get-tuple-element.21), channel_id=1, source_target_pairs={{0,8},{8,0},{16,24},{24,16},{32,40},{40,32},{48,56},{56,48},{64,72... | collective-permute-start | bytes 6291464 | tf_op jit(solution)/shard_map/ppermute | solution.py:544
  62.9 1.0 copy-start.1
  63.9 1.0 copy-start.2
  65.0 1.0 copy-start.3
  77.3 15.8 %collective-permute-start.14 = (f32[8,2,272,128]{3,2,1,0:T(8,128)}, f32[8,2,272,128]{3,2,1,0:T(8,128)}, u32[]{:S(2)}, u32[]{:S(2)}) collective-permute-start(f32[8,2,272,128]{3,2,1,0:T(8,128)} %get-tuple-element.31), channel_id=1, source_target_pairs={{0,8},{8,0},{16,24},{24,16},{32,40},{40,32},{48,56},{56,48},{64,72... | collective-permute-start | bytes 6684680 | tf_op jit(solution)/shard_map/ppermute | solution.py:547
  79.9 4.6 %copy-start.6 = (f32[8,512,128]{2,1,0:T(8,128)}, f32[8,512,128]{2,1,0:T(8,128)S(1)}, u32[]{:S(2)}) copy-start(f32[8,512,128]{2,1,0:T(8,128)S(1)} %add.67) | copy-start | bytes 6291460
  79.9 2.7 %copy-start.10 = (f32[8,512,128]{2,1,0:T(8,128)S(1)}, f32[8,512,128]{2,1,0:T(8,128)}, u32[]{:S(2)}) copy-start(f32[8,512,128]{2,1,0:T(8,128)} %get-tuple-element.20) | copy-start | bytes 6291460
  81.0 25.7 %collective-permute-start.1 = (f32[4,512,128]{2,1,0:T(8,128)}, f32[4,512,128]{2,1,0:T(8,128)S(1)}, u32[]{:S(2)}, u32[]{:S(2)}) collective-permute-start(f32[4,512,128]{2,1,0:T(8,128)} %slice.91), channel_id=1, source_target_pairs={{0,64},{8,72},{16,80},{24,88},{32,96},{40,104},{48,112},{56,120},{... | collective-permute-start | bytes 3145736 | tf_op jit(solution)/shard_map/ppermute | solution.py:511
  84.5 1.7 %copy-start.8 = (f32[8,512,128]{2,1,0:T(8,128)}, f32[8,512,128]{2,1,0:T(8,128)S(1)}, u32[]{:S(2)}) copy-start(f32[8,512,128]{2,1,0:T(8,128)S(1)} %add.72) | copy-start | bytes 6291460
  86.1 10.7 %collective-permute-start.7 = (f32[2,512,128]{2,1,0:T(8,128)}, f32[2,512,128]{2,1,0:T(8,128)}, u32[]{:S(2)}, u32[]{:S(2)}) collective-permute-start(f32[2,512,128]{2,1,0:T(8,128)} %get-tuple-element.39), channel_id=1, source_target_pairs={{0,16},{8,56},{16,32},{24,8},{32,48},{40,24},{48,0},{56,40},{64,80... | collective-permute-start | bytes 1572872 | tf_op jit(solution)/shard_map/ppermute | solution.py:497
  89.5 55.8 %collective-permute-start.21 = (f32[34,2,8,128]{3,2,1,0:T(8,128)S(1)}, f32[34,2,8,128]{3,2,1,0:T(8,128)S(1)}, u32[]{:S(2)}, u32[]{:S(2)}) collective-permute-start(f32[34,2,8,128]{3,2,1,0:T(8,128)S(1)} %pad_maximum_fusion.k), channel_id=1, source_target_pairs={{0,1},{1,2},{2,3},{3,4},{4,5},{5,6},{6,7},{8,9},{9,10},{10,11},{11... | collective-permute-start | bytes 835592 | tf_op jit(solution)/shard_map/ppermute | solution.py:535
  91.4 18.6 %collective-permute-start.6 = (f32[2,512,128]{2,1,0:T(8,128)}, f32[2,512,128]{2,1,0:T(8,128)S(1)}, u32[]{:S(2)}, u32[]{:S(2)}) collective-permute-start(f32[2,512,128]{2,1,0:T(8,128)} %get-tuple-element.38), channel_id=1, source_target_pairs={{0,48},{8,24},{16,0},{24,40},{32,16},{40,56},{48,32},{56,8},{64,11... | collective-permute-start | bytes 1572872 | tf_op jit(solution)/shard_map/ppermute | solution.py:498
  93.1 3.8 %copy-start.9 = (f32[8,512,128]{2,1,0:T(8,128)S(1)}, f32[8,512,128]{2,1,0:T(8,128)}, u32[]{:S(2)}) copy-start(f32[8,512,128]{2,1,0:T(8,128)} %copy-done.8) | copy-start | bytes 6291460
  95.2 14.5 %copy-start.7 = (f32[8,512,128]{2,1,0:T(8,128)S(1)}, f32[8,512,128]{2,1,0:T(8,128)}, u32[]{:S(2)}) copy-start(f32[8,512,128]{2,1,0:T(8,128)} %copy-done.6) | copy-start | bytes 6291460
  95.3 14.6 %collective-permute-start.16 = (f32[2,2,272,128]{3,2,1,0:T(8,128)S(1)}, f32[2,2,272,128]{3,2,1,0:T(8,128)S(1)}, u32[]{:S(2)}, u32[]{:S(2)}) collective-permute-start(f32[2,2,272,128]{3,2,1,0:T(8,128)S(1)} %get-tuple-element.37), channel_id=1, source_target_pairs={{0,16},{8,56},{16,32},{24,8},{32,48},{40,24},{48,0},{56,40},{64,80... | collective-permute-start | bytes 1671176 | tf_op jit(solution)/shard_map/ppermute | solution.py:497
  98.0 20.2 %collective-permute-start.8 = (f32[2,512,128]{2,1,0:T(8,128)S(1)}, f32[2,512,128]{2,1,0:T(8,128)S(1)}, u32[]{:S(2)}, u32[]{:S(2)}) collective-permute-start(f32[2,512,128]{2,1,0:T(8,128)S(1)} %slice_add_fusion.3), channel_id=1, source_target_pairs={{0,16},{8,56},{16,32},{24,8},{32,48},{40,24},{48,0},{56,40},{64,80... | collective-permute-start | bytes 1572872 | tf_op jit(solution)/shard_map/ppermute | solution.py:499
  106.7 16.1 %collective-permute-start.15 = (f32[2,2,272,128]{3,2,1,0:T(8,128)S(1)}, f32[2,2,272,128]{3,2,1,0:T(8,128)S(1)}, u32[]{:S(2)}, u32[]{:S(2)}) collective-permute-start(f32[2,2,272,128]{3,2,1,0:T(8,128)S(1)} %get-tuple-element.36), channel_id=1, source_target_pairs={{0,48},{8,24},{16,0},{24,40},{32,16},{40,56},{48,32},{56,8},{64,11... | collective-permute-start | bytes 1671176 | tf_op jit(solution)/shard_map/ppermute | solution.py:498
  109.9 16.5 %collective-permute-start.17 = (f32[2,2,272,128]{3,2,1,0:T(8,128)S(1)}, f32[2,2,272,128]{3,2,1,0:T(8,128)S(1)}, u32[]{:S(2)}, u32[]{:S(2)}) collective-permute-start(f32[2,2,272,128]{3,2,1,0:T(8,128)S(1)} %slice_add_fusion.1), channel_id=1, source_target_pairs={{0,16},{8,56},{16,32},{24,8},{32,48},{40,24},{48,0},{56,40},{64,80... | collective-permute-start | bytes 1671176 | tf_op jit(solution)/shard_map/ppermute | solution.py:499
  110.1 35.3 %collective-permute-start.22 = (f32[34,2,8,128]{3,2,1,0:T(8,128)S(1)}, f32[34,2,8,128]{3,2,1,0:T(8,128)S(1)}, u32[]{:S(2)}, u32[]{:S(2)}) collective-permute-start(f32[34,2,8,128]{3,2,1,0:T(8,128)S(1)} %pad_maximum_fusion.k), channel_id=1, source_target_pairs={{1,0},{2,1},{3,2},{4,3},{5,4},{6,5},{7,6},{9,8},{10,9},{11,10},{12... | collective-permute-start | bytes 835592 | tf_op jit(solution)/shard_map/ppermute | solution.py:535
  118.2 13.6 %collective-permute-start.3 = (f32[512,128]{1,0:T(8,128)S(1)}, f32[512,128]{1,0:T(8,128)S(1)}, u32[]{:S(2)}, u32[]{:S(2)}) collective-permute-start(f32[512,128]{1,0:T(8,128)S(1)} %get-tuple-element.41), channel_id=1, source_target_pairs={{0,16},{8,56},{16,32},{24,8},{32,48},{40,24},{48,0},{56,40},{64,80... | collective-permute-start | bytes 786440 | tf_op jit(solution)/shard_map/ppermute | solution.py:497
  122.8 18.2 %collective-permute-start.2 = (f32[512,128]{1,0:T(8,128)S(1)}, f32[512,128]{1,0:T(8,128)S(1)}, u32[]{:S(2)}, u32[]{:S(2)}) collective-permute-start(f32[512,128]{1,0:T(8,128)S(1)} %get-tuple-element.40), channel_id=1, source_target_pairs={{0,48},{8,24},{16,0},{24,40},{32,16},{40,56},{48,32},{56,8},{64,11... | collective-permute-start | bytes 786440 | tf_op jit(solution)/shard_map/ppermute | solution.py:498
  126.4 8.8 %collective-permute-start.9 = (f32[512,128]{1,0:T(8,128)S(1)}, f32[512,128]{1,0:T(8,128)S(1)}, u32[]{:S(2)}, u32[]{:S(2)}) collective-permute-start(f32[512,128]{1,0:T(8,128)S(1)} %slice_bitcast_fusion.2), channel_id=1, source_target_pairs={{0,64},{8,72},{16,80},{24,88},{32,96},{40,104},{48,112},{56,120},{... | collective-permute-start | bytes 786440 | tf_op jit(solution)/shard_map/ppermute | solution.py:506
  131.8 7.2 %collective-permute-start.18 = (f32[2,272,128]{2,1,0:T(8,128)S(1)}, f32[2,272,128]{2,1,0:T(8,128)S(1)}, u32[]{:S(2)}, u32[]{:S(2)}) collective-permute-start(f32[2,272,128]{2,1,0:T(8,128)S(1)} %slice_bitcast_fusion), channel_id=1, source_target_pairs={{0,64},{8,72},{16,80},{24,88},{32,96},{40,104},{48,112},{56,120},{... | collective-permute-start | bytes 835592 | tf_op jit(solution)/shard_map/ppermute | solution.py:506
  135.3 10.0 %collective-permute-start.4 = (f32[512,128]{1,0:T(8,128)S(1)}, f32[512,128]{1,0:T(8,128)S(1)}, u32[]{:S(2)}, u32[]{:S(2)}) collective-permute-start(f32[512,128]{1,0:T(8,128)S(1)} %fusion.4), channel_id=1, source_target_pairs={{0,16},{8,56},{16,32},{24,8},{32,48},{40,24},{48,0},{56,40},{64,80... | collective-permute-start | bytes 786440 | tf_op jit(solution)/shard_map/ppermute | solution.py:499
  139.0 7.3 %collective-permute-start.19 = (f32[34,8,128]{2,1,0:T(8,128)S(1)}, f32[34,8,128]{2,1,0:T(8,128)S(1)}, u32[]{:S(2)}, u32[]{:S(2)}) collective-permute-start(f32[34,8,128]{2,1,0:T(8,128)S(1)} %get-tuple-element.43), channel_id=1, source_target_pairs={{0,1},{1,2},{2,3},{3,4},{4,5},{5,6},{6,7},{8,9},{9,10},{10,11},{11... | collective-permute-start | bytes 417800 | tf_op jit(solution)/shard_map/ppermute | solution.py:548
  141.0 10.6 %collective-permute-start.20 = (f32[34,8,128]{2,1,0:T(8,128)S(1)}, f32[34,8,128]{2,1,0:T(8,128)S(1)}, u32[]{:S(2)}, u32[]{:S(2)}) collective-permute-start(f32[34,8,128]{2,1,0:T(8,128)S(1)} %get-tuple-element.42), channel_id=1, source_target_pairs={{1,0},{2,1},{3,2},{4,3},{5,4},{6,5},{7,6},{9,8},{10,9},{11,10},{12... | collective-permute-start | bytes 417800 | tf_op jit(solution)/shard_map/ppermute | solution.py:548

commit v3 on v2

--- a/solution.py
+++ b/solution.py
@@ -6,8 +6,10 @@
 from jax.sharding import PartitionSpec as P
 
 CHIPS = 8
+COUNT = 16
+SLABS = 8
 GROUP = 16
-PLANES = ((3, 0), (0, 1), (0, 0), (3, 1))
+KEPT = ((0, 0), (3, 1))
 MIB = 1024 * 1024
 F32 = jnp.float32
 
@@ -74,12 +76,15 @@
     scratch[pl.ds(rows + 1, 1)] = jnp.where(block < blocks - 1, after[...], 0.0)
 
 
-def series_kernel(place, real, u, k, p, cos, sin, d_other, d_same, v_other, v_same, n_up, n_down, n_low, n_high,
+def series_kernel(coeffs, u, k, p, cos, sin, d_other, d_same, v_other, v_same, below, above,
                   us, ks, ns, ds, vs, fx, fy, fw, fz, fm, planes, in_sem, out_sem, plane_sem):
     cells = u.shape[0] // 16
     rows = cells // CHIPS
     half_rows = rows // 2
-    lower, upper, c0, c1, c2, c3 = (real[i] for i in range(6))
+    my_z, my_y, my_core = where_am_i()
+    slab = lax.axis_index("gz")
+    lower, upper = jnp.where(slab == 0, 1.0, 0.0), jnp.where(slab == SLABS - 1, 1.0, 0.0)
+    c0, c1, c2, c3 = (coeffs[0, i] for i in range(4))
     sub = lax.broadcasted_iota(jnp.int32, (8, 128), 0)
     lane = lax.broadcasted_iota(jnp.int32, (8, 128), 1)
     z = lax.rem(sub, 4)
@@ -166,9 +171,11 @@
         def gather(i, carry):
             for b in range(2):
                 x = c * rows + i * 16 + b * 8
-                for j, (zz, h) in enumerate(PLANES):
-                    for q in (0, 1):
-                        planes[j, pl.ds(x, 8), q * 128 : (q + 1) * 128] = ns[pl.ds((x + 1) * 16 + h * 8 + q * 4 + zz, 8, stride=16), :]
+                for j, (z, h) in enumerate(KEPT):
+                    for f, ref in enumerate((us, ns)):
+                        for q in (0, 1):
+                            lanes = pl.ds(f * 256 + q * 128, 128)
+                            planes[j, pl.ds(x, 8), lanes] = ref[pl.ds((x + 1) * 16 + h * 8 + q * 4 + z, 8, stride=16), :]
             return carry
 
         lax.fori_loop(0, rows // 16, gather, 0)
@@ -202,13 +209,13 @@
         here = pl.ds(c * rows, rows)
         return [
             pltpu.make_async_copy(planes.at[j, here], out.at[here], plane_sem.at[j, c])
-            for j, out in enumerate((n_up, n_down, n_low, n_high))
+            for j, out in enumerate((below, above))
         ]
 
     def stores(c, core, same):
         way = 1 - 2 * core
-        turn = lax.rem(way * (lax.rem(c, 4) - place[1]) + 8, 4)
-        side = lax.rem(c // 4 + place[0], 2)
+        turn = lax.rem(way * (lax.rem(c, 4) - my_y) + 8, 4)
+        side = lax.rem(c // 4 + my_z, 2)
         here = pl.ds((c * rows + core * half_rows) * 16, half_rows * 16)
         d_to, v_to = (d_same, v_same) if same else (d_other, v_other)
         return [
@@ -240,7 +247,7 @@
             second_pass(c - 1)
             for core in (0, 1):
                 for same in (True, False):
-                    @pl.when((place[2] == core) == same)
+                    @pl.when((my_core == core) == same)
                     def _():
                         for copy in stores(c - 1, core, same):
                             copy.start()
@@ -259,9 +266,10 @@
 
     lax.fori_loop(0, CHIPS, end, 0)
 
-def mend_kernel(real, d, v, e, e_low, e_high, k, k_low, k_high, d_out, v_out, ds, vs):
+def mend_kernel(d, v, e, e_low, e_high, k, k_low, k_high, d_out, v_out, ds, vs):
     rows = d.shape[0]
-    lower, upper = real[0], real[1]
+    slab = lax.axis_index("gz")
+    lower, upper = jnp.where(slab == 0, 1.0, 0.0), jnp.where(slab == SLABS - 1, 1.0, 0.0)
     wide = rows + 2
     z = places(wide)[1]
     factor = []
@@ -285,29 +293,105 @@
             out[:, h] = given[:, h] + direct_of[h] - outflow[h] * (1.0 / 12.0) - 2.0 * w[h]
 
 
-def planes_kernel(u, *refs):
-    outs, (us, planes, in_sem, out_sem) = refs[:4], refs[4:]
+def where_am_i():
+    me = lax.axis_index("tm")
+    return me // 8, lax.rem(me // 2, 4), lax.rem(me, 2)
+
+
+def edge_kernel(u, k, p, up, down, k_here, us, ks, ps, edges, kb, in_sem, out_sem, k_sem):
     cells = u.shape[0] // 16
     rows = cells // CHIPS
-
-    def load(c):
-        here = pl.ds(c * rows * 16, rows * 16)
-        return pltpu.make_async_copy(u.at[here], us.at[here], in_sem.at[c])
+    mine = cells // (2 * CHIPS)
+    me = lax.axis_index("tm")
+
+    def loads(c):
+        here, there = pl.ds(c * rows * 16, rows * 16), pl.ds((c * rows + 1) * 16, rows * 16)
+        return [
+            pltpu.make_async_copy(u.at[here], us.at[there], in_sem.at[0, c]),
+            pltpu.make_async_copy(k.at[here], ks.at[there], in_sem.at[1, c]),
+            pltpu.make_async_copy(p.at[here], ps.at[here], in_sem.at[2, c]),
+        ]
 
     def stores(c):
         here = pl.ds(c * rows, rows)
-        return [pltpu.make_async_copy(planes.at[j, here], out.at[here], out_sem.at[j, c]) for j, out in enumerate(outs)]
-
+        return [pltpu.make_async_copy(edges.at[j, here], out.at[here], out_sem.at[j, c]) for j, out in enumerate((up, down))]
+
+    own = pltpu.make_async_copy(k.at[pl.ds(me * mine * 16, mine * 16)], kb.at[pl.ds(16, mine * 16)], k_sem.at[0])
+    before = pltpu.make_async_copy(k.at[pl.ds(jnp.maximum(me * mine - 1, 0) * 16, 16)], kb.at[pl.ds(0, 16)], k_sem.at[1])
+    after = pltpu.make_async_copy(
+        k.at[pl.ds(jnp.minimum((me + 1) * mine, cells - 1) * 16, 16)], kb.at[pl.ds((mine + 1) * 16, 16)], k_sem.at[2]
+    )
+    own.start()
+    before.start()
+    after.start()
     for c in range(CHIPS):
-        load(c).start()
+        for copy in loads(c):
+            copy.start()
+    nothing = jnp.zeros((16, 128), F32)
+    for ref in (us, ks):
+        ref[0:16] = nothing
+        ref[(cells + 1) * 16 : (cells + 2) * 16] = nothing
+    own.wait()
+    before.wait()
+    after.wait()
+
+    @pl.when(me == 0)
+    def _():
+        kb[0:16] = nothing
+
+    @pl.when(me == 2 * CHIPS - 1)
+    def _():
+        kb[(mine + 1) * 16 : (mine + 2) * 16] = nothing
+
+    speeds = pltpu.make_async_copy(kb, k_here, k_sem.at[3])
+    speeds.start()
+    lane = lax.broadcasted_iota(jnp.int32, (8, 128), 1)
+    at_start, at_end = lane == 0, lane == 127
+
+    def shifted(cells_of, yt):
+        after = pltpu.roll(cells_of[yt + 1], 127, 1) if yt < 3 else 0.0
+        before = pltpu.roll(cells_of[yt - 1], 1, 1) if yt > 0 else 0.0
+        here = cells_of[yt]
+        return (
+            jnp.where(at_end, after, pltpu.roll(here, 127, 1)),
+            jnp.where(at_start, before, pltpu.roll(here, 1, 1)),
+        )
 
     def chunk(c, carry):
-        load(c).wait()
-        for i in range(rows // 8):
-            x = c * rows + i * 8
-            for j, (z, h) in enumerate(PLANES):
-                for q in (0, 1):
-                    planes[j, pl.ds(x, 8), q * 128 : (q + 1) * 128] = us[pl.ds(x * 16 + h * 8 + q * 4 + z, 8, stride=16), :]
+        @pl.when(c == 0)
+        def _():
+            for copy in loads(c):
+                copy.wait()
+
+        @pl.when(c + 1 < CHIPS)
+        def _():
+            for copy in loads(c + 1):
+                copy.wait()
+
+        def step(i, carry):
+            for g in range(4):
+                x = c * rows + i * 32 + g * 8
+                for j, (z, inner, turns) in enumerate(((3, 2, (0, 1)), (0, 1, (2, 3)))):
+
+                    def at(ref, yt, by=0, zz=z):
+                        return ref[pl.ds((x + 1 + by) * 16 + yt * 4 + zz, 8, stride=16), :]
+
+                    near = [yt for yt in range(4) if turns[0] - 1 <= yt <= turns[1] + 1]
+                    vs, qs = {yt: at(us, yt) for yt in near}, {yt: at(ks, yt) for yt in near}
+                    for yt in turns:
+                        v, q = vs[yt], qs[yt]
+                        pairs = [*zip(shifted(vs, yt), shifted(qs, yt))]
+                        pairs += [(at(us, yt, by), at(ks, yt, by)) for by in (1, -1)]
+                        pairs.append((at(us, yt, 0, inner), at(ks, yt, 0, inner)))
+                        flows = [(q + q_n) * (v_n - v) for v_n, q_n in pairs]
+                        flow = (flows[0] + flows[1]) + (flows[2] + flows[3]) + flows[4]
+                        n = flow * (-1.0 / 12.0) - 2.0 * v - ps[pl.ds(x * 16 + yt * 4 + z, 8, stride=16), :]
+                        here = (yt - turns[0]) * 128
+                        edges[j, pl.ds(x, 8), here : here + 128] = v
+                        edges[j, pl.ds(x, 8), here + 256 : here + 384] = n
+            return carry
+
+        lax.fori_loop(0, rows // 32, step, 0)
         for copy in stores(c):
             copy.start()
         return carry
@@ -320,16 +404,18 @@
         return carry
 
     lax.fori_loop(0, CHIPS, end, 0)
-
-
-def jumps_kernel(place, real, *refs):
-    ins, other, same, es, buffers, in_sem, out_sem = refs[:8], *refs[8:]
+    speeds.wait()
+
+
+def jumps_kernel(coeffs, *refs):
+    ins, other, same, es, buffers, in_sem, out_sem = refs[:4], *refs[4:]
     cells = ins[0].shape[0]
     parts = 2 * CHIPS
     rows = cells // parts
     chunks = 4
     size = cells // chunks
-    c0, c1, c2, c3 = (real[2 + i] for i in range(4))
+    c0, c1, c2, c3 = (coeffs[0, i] for i in range(4))
+    my_z, my_y, my_core = where_am_i()
 
     def loads(c):
         here = pl.ds(c * size, size)
@@ -338,14 +424,14 @@
     def stores(d, is_same):
         chip, core = d // 2, d % 2
         way = 1 - 2 * core
-        slot = lax.rem(way * (chip % 4 - place[1]) + 8, 4) * 2 + lax.rem(chip // 4 + place[0], 2)
+        slot = lax.rem(way * (chip % 4 - my_y) + 8, 4) * 2 + lax.rem(chip // 4 + my_z, 2)
         here = pl.ds(d * rows * 8, (rows + 2) * 8)
         to = same if is_same else other
         return [pltpu.make_async_copy(es.at[h, here], to.at[slot, h], out_sem.at[h, d]) for h in (0, 1)]
 
     def send(d):
         for is_same in (True, False):
-            @pl.when((place[2] == d % 2) == is_same)
+            @pl.when((my_core == d % 2) == is_same)
             def _():
                 for copy in stores(d, is_same):
                     copy.start()
@@ -366,13 +452,15 @@
             x = c * size + i * 8
             for h in (0, 1):
                 for q in (0, 1):
-                    u_own, n_own, u_near, n_near = (buffers[4 * h + j, pl.ds(x, 8), q * 128 : (q + 1) * 128] for j in range(4))
-                    du, dn = (u_own - u_near, n_own - n_near) if h == 0 else (u_near - u_own, n_near - n_own)
+                    du, dn = (
+                        (1 - 2 * h) * (buffers[2 * h, pl.ds(x, 8), at : at + 128] - buffers[2 * h + 1, pl.ds(x, 8), at : at + 128])
+                        for at in (q * 128, 256 + q * 128)
+                    )
                     for m, value in enumerate((c1 * du, c0 * du + c1 * dn, c3 * du, c2 * du + c3 * dn)):
                         es[h, pl.ds((x + 1) * 8 + q * 4 + m, 8, stride=8), :] = value
             return carry
 
-        lax.fori_loop(0, size // 8, step, 0, unroll=2)
+        lax.fori_loop(0, size // 8, step, 0, unroll=8)
         ready = parts if c == chunks - 1 else (c + 1) * size // rows - 1
         for d in range(sent, ready):
             send(d)
@@ -398,84 +486,89 @@
     return cells.reshape(-1, 128)
 
 
-def planes_of(u):
+def edges_of(u, k, p):
     cells = u.shape[0] // 16
+    mine = cells // (2 * CHIPS)
+    wide = pltpu.VMEM(((cells + 2) * 16, 128), F32)
+    edge = jax.ShapeDtypeStruct((cells, 512), F32)
     return pl.pallas_call(
-        planes_kernel,
-        out_shape=(jax.ShapeDtypeStruct((cells, 256), F32),) * 4,
-        in_specs=[ANYWHERE],
-        out_specs=(ANYWHERE,) * 4,
+        edge_kernel,
+        out_shape=(edge, edge, jax.ShapeDtypeStruct(((mine + 2) * 16, 128), F32)),
+        in_specs=[ANYWHERE] * 3,
+        out_specs=(ANYWHERE,) * 3,
         scratch_shapes=[
+            wide,
+            wide,
             pltpu.VMEM((cells * 16, 128), F32),
-            pltpu.VMEM((4, cells, 256), F32),
-            pltpu.SemaphoreType.DMA((CHIPS,)),
-            pltpu.SemaphoreType.DMA((4, CHIPS)),
+            pltpu.VMEM((2, cells, 512), F32),
+            pltpu.VMEM(((mine + 2) * 16, 128), F32),
+            pltpu.SemaphoreType.DMA((3, CHIPS)),
+            pltpu.SemaphoreType.DMA((2, CHIPS)),
+            pltpu.SemaphoreType.DMA((4,)),
         ],
-        compiler_params=params(48),
-        cost_estimate=cost(6),
-    )(u)
-
-
-def series(place, real, u, k, p, cos, sin):
+        compiler_params=params(56),
+        cost_estimate=cost(16),
+    )(u, k, p)
+
+
+def series(coeffs, u, k, p, cos, sin):
     cells = u.shape[0] // 16
     share = jax.ShapeDtypeStruct((CHIPS, cells, 128), F32)
-    plane = jax.ShapeDtypeStruct((cells, 256), F32)
+    plane = jax.ShapeDtypeStruct((cells, 512), F32)
     wide = pltpu.VMEM(((cells + 2) * 16, 128), F32)
     exact = pltpu.VMEM((cells * 16, 128), F32)
     return pl.pallas_call(
         series_kernel,
-        out_shape=(share,) * 4 + (plane,) * 4,
-        in_specs=[SMEM, SMEM] + [ANYWHERE] * 5,
-        out_specs=(ANYWHERE,) * 8,
+        out_shape=(share,) * 4 + (plane,) * 2,
+        in_specs=[SMEM] + [ANYWHERE] * 5,
+        out_specs=(ANYWHERE,) * 6,
         scratch_shapes=[wide, wide, wide, exact, exact, wide, wide, wide, wide, wide]
         + [
-            pltpu.VMEM((4, cells, 256), F32),
+            pltpu.VMEM((2, cells, 512), F32),
             pltpu.SemaphoreType.DMA((5, CHIPS)),
             pltpu.SemaphoreType.DMA((2, 2, CHIPS)),
-            pltpu.SemaphoreType.DMA((4, CHIPS)),
+            pltpu.SemaphoreType.DMA((2, CHIPS)),
         ],
         compiler_params=params(56),
         cost_estimate=cost(45),
-    )(place, real, u, k, p, cos, sin)
-
-
-def jumps(place, real, below, above):
+    )(coeffs, u, k, p, cos, sin)
+
+
+def jumps(coeffs, below, above):
     cells = below[0].shape[0]
     rows = cells // (2 * CHIPS)
     shape = jax.ShapeDtypeStruct((CHIPS, 2, (rows + 2) * 8, 128), F32)
     return pl.pallas_call(
         jumps_kernel,
         out_shape=(shape, shape),
-        in_specs=[SMEM, SMEM] + [ANYWHERE] * 8,
+        in_specs=[SMEM] + [ANYWHERE] * 4,
         out_specs=(ANYWHERE,) * 2,
         scratch_shapes=[
             pltpu.VMEM((2, (cells + 2) * 8, 128), F32),
-            pltpu.VMEM((8, cells, 256), F32),
-            pltpu.SemaphoreType.DMA((8, 4)),
+            pltpu.VMEM((4, cells, 512), F32),
+            pltpu.SemaphoreType.DMA((4, 4)),
             pltpu.SemaphoreType.DMA((2, 2 * CHIPS)),
         ],
         compiler_params=params(24),
         cost_estimate=cost(9),
-    )(place, real, *below, *above)
-
-
-def mend(real, d, v, e, e_low, e_high, k, k_low, k_high):
+    )(coeffs, *below, *above)
+
+
+def mend(d, v, e, e_low, e_high, k, k_low, k_high):
     shape = jax.ShapeDtypeStruct(d.shape, F32)
     whole = pl.BlockSpec(memory_space=pltpu.VMEM)
     return pl.pallas_call(
         mend_kernel,
         out_shape=(shape, shape),
-        in_specs=[SMEM] + [whole] * 8,
+        in_specs=[whole] * 8,
         out_specs=(whole, whole),
         scratch_shapes=[pltpu.VMEM(k.shape, F32)] * 2,
         compiler_params=params(16),
         cost_estimate=cost(4),
-    )(real, d, v, e, e_low, e_high, k, k_low, k_high)
+    )(d, v, e, e_low, e_high, k, k_low, k_high)
 
 
 CELL = (2, 8, 128)
-COUNT = 16
-SLABS = 8
 
 
 def along_y(sign):
@@ -513,41 +606,29 @@
 
 
 def local(prev_term, last_term, cos_sum, sin_sum, speed_sq, series_coeffs):
-    u, p, k = packed(last_term[0]), packed(prev_term[0]), packed(speed_sq)
-    cos, sin = packed(cos_sum[0]), packed(sin_sum[0])
-    blocks = lax.axis_size("tm")
-    rows = u.shape[0] // blocks
-    me, slab = lax.axis_index("tm"), lax.axis_index("gz")
-    place = jnp.stack([me // 8, (me // 2) % 4, me % 2]).astype(jnp.int32)
-    ends = jnp.stack([slab == 0, slab == lax.axis_size("gz") - 1]).astype(F32)
-    real = jnp.concatenate([ends, series_coeffs[0]])
-
-    start = me * rows
-    k_before = lax.dynamic_slice_in_dim(k, jnp.maximum(start - 1, 0), 1)
-    k_after = lax.dynamic_slice_in_dim(k, jnp.minimum(start + rows, u.shape[0] - 1), 1)
-    k_here = jnp.concatenate(
-        [
-            jnp.where(me > 0, k_before, 0.0),
-            lax.dynamic_slice_in_dim(k, start, rows),
-            jnp.where(me < blocks - 1, k_after, 0.0),
-        ]
+    u, p, k = flat(packed(last_term[0])), flat(packed(prev_term[0])), flat(packed(speed_sq))
+    cos, sin = flat(packed(cos_sum[0])), flat(packed(sin_sum[0]))
+    rows = last_term.shape[1] // COUNT
+
+    up, down, k_here = edges_of(u, k, p)
+    from_below, from_above = lax.ppermute(up, "gz", UP), lax.ppermute(down, "gz", DOWN)
+    k_low, k_high = lax.ppermute(k_here, "gz", UP), lax.ppermute(k_here, "gz", DOWN)
+
+    d_other, d_same, v_other, v_same, below, above = series(series_coeffs, u, k, p, cos, sin)
+    d_sum = d_same + lax.ppermute(d_other, "tm", SIBLING)
+    v_sum = v_same + lax.ppermute(v_other, "tm", SIBLING)
+    _, _, from_below, from_above, k_low, k_high = lax.optimization_barrier(
+        (d_sum, v_sum, from_below, from_above, k_low, k_high)
     )
-    k_low, k_high = lax.ppermute(k_here, "gz", UP), lax.ppermute(k_here, "gz", DOWN)
-
-    u_flat = flat(u)
-    u_up, u_down, u_low, u_high = planes_of(u_flat)
-    u_below, u_above = lax.ppermute(u_up, "gz", UP), lax.ppermute(u_down, "gz", DOWN)
-
-    d_other, d_same, v_other, v_same, n_up, n_down, n_low, n_high = series(place, real, u_flat, flat(k), flat(p), flat(cos), flat(sin))
-    n_below, n_above = lax.ppermute(n_up, "gz", UP), lax.ppermute(n_down, "gz", DOWN)
-    d = z_then_y(d_same + lax.ppermute(d_other, "tm", SIBLING)).reshape(rows, *CELL)
-    v = y_then_z(v_same + lax.ppermute(v_other, "tm", SIBLING)).reshape(rows, *CELL)
-
-    e_other, e_same = jumps(place, real, (u_low, n_low, u_below, n_below), (u_high, n_high, u_above, n_above))
+    d = z_then_y(d_sum).reshape(rows, *CELL)
+    v = y_then_z(v_sum).reshape(rows, *CELL)
+
+    e_other, e_same = jumps(series_coeffs, (below, from_below), (above, from_above))
     e = y_then_z(e_same + lax.ppermute(e_other, "tm", SIBLING)).reshape(2, rows + 2, 8, 128)
     e_low, e_high = lax.ppermute(e[1], "gz", UP), lax.ppermute(e[0], "gz", DOWN)
 
-    d, v = mend(real, d, v, e, e_low, e_high, k_here, k_low, k_high)
+    k_here, k_low, k_high = (a.reshape(rows + 2, *CELL) for a in (k_here, k_low, k_high))
+    d, v = mend(d, v, e, e_low, e_high, k_here, k_low, k_high)
     return unpacked(d), unpacked(v)
 
 

time: 155 us -> 143 us (0.923)
  other arithmetic: 10 us -> 1.25 us
  waiting for transfers between devices: 55.2 us -> 63.1 us
  local copies, waits for them, and re-layouts: 8.44 us -> 1.68 us
  starting transfers between devices: 43.6 us -> 40.2 us
    ppermute x6 -> x4, waiting for transfers between devices: 24.1 us -> 0.01 us  [the longest x1 0.01 us: local(): d_sum = d_same + lax.ppermute(d_other, 'tm', SIBLING)]
    ppermute x1, waiting for transfers between devices: 0.01 us -> 15.7 us  [local(): lax.ppermute(k_here, 'gz', UP)]
    ppermute x1, waiting for transfers between devices: 0.01 us -> 7.62 us  [local(): lax.ppermute(k_here, 'gz', DOWN)]
    ppermute x6 -> x4, starting transfers between devices: 14 us -> 8.19 us  [the longest x1 5.7 us: local(): lax.ppermute(up, 'gz', UP)]
    ppermute x1, starting transfers between devices: 1.92 us -> 7.54 us  [local(): lax.ppermute(k_here, 'gz', UP)]
    ppermute x3, waiting for transfers between devices: 5.26 us -> 10.6 us  [ring(): relayed = lax.ppermute(two, 'tm', FORTH)]
    ppermute x3, waiting for transfers between devices: 4.42 us -> 8.28 us  [ring(): direct = lax.ppermute(back, 'tm', BACK)]
    add x2, other arithmetic: 4.29 us -> 0.48 us  [the longest x1 0.27 us: local(): v_sum = v_same + lax.ppermute(v_other, 'tm', SIBLING)]
  transfers between devices with their start and end apart: 23 -> 21, of which waited for: 12 -> 10; matrix products, arithmetic and copies ran while one was open for 9% -> 1% of each run, Pallas kernels for 18% -> 6%
where the time goes in v3:
time: 143 us
  waiting for transfers between devices  63.1 us (44%)
  starting transfers between devices  40.2 us (28%)
  Pallas kernels  35.6 us (25%)
  local copies, waits for them, and re-layouts  1.68 us (1%)
    pallas_call x1, Pallas kernels, series(): pl.pallas_call(series_kernel, out_shape=(share,) * 4 + (plane,) * 2, in_s...  16.8 us
    ppermute x1, waiting for transfers between devices, local(): lax.ppermute(k_here, 'gz', UP)  15.7 us
    ppermute x3, waiting for transfers between devices, ring(): relayed = lax.ppermute(two, 'tm', FORTH)  10.6 us
    pallas_call x1, Pallas kernels, edges_of(): pl.pallas_call(edge_kernel, out_shape=(edge, edge, jax.ShapeDtypeStruct((...  8.98 us
    ppermute x1, waiting for transfers between devices, z_then_y(): mine = cells[:half] + lax.ppermute(cells[half:], 'tm', ACROSS)  8.5 us
    ppermute x3, waiting for transfers between devices, ring(): direct = lax.ppermute(back, 'tm', BACK)  8.28 us
    pallas_call x1, Pallas kernels, jumps(): pl.pallas_call(jumps_kernel, out_shape=(shape, shape), in_specs=[SMEM] +...  7.98 us
    ppermute x1, waiting for transfers between devices, local(): lax.ppermute(k_here, 'gz', DOWN)  7.62 us
  transfers between devices with their start and end apart: 21, of which 10 were waited for; matrix products, arithmetic and copies ran while one was open for 1% of the time, Pallas kernels for 6%

profile of v3, /device:TPU:6, one launch (start us, length us, event | category | flops | bytes accessed | tf_op | source)
XLA Modules:
  0.0 142.7 jit_solution(7399007736098979623)
XLA Ops:
  0.6 16.8 %shard_map.77 = (f32[8,512,128]{2,1,0:T(8,128)}, f32[8,512,128]{2,1,0:T(8,128)}, f32[8,512,128]{2,1,0:T(8,128)}, f32[8,512,128]{2,1,0:T(8,128)}, f32[512,512]{1,0:T(8,128)}, /*index=5*/f32[512,512]{1,0:T(8,128)}) custom-call(f32[1,4]{1,0:T(1,128)} %coeffs.3, f32[8192,128]{1,0:T(8,128)} %bitcast.77, f32[8192,128]{1,0:T(8,128)} %bitcast.79, ...), custom_call_target="tpu_custom_call" | custom-call | bytes 47185920 | tf_op jit(solution)/shard_map/pallas_call | solution.py:520
  17.4 0.1 collective-permute-start
  17.5 0.5 collective-permute-start.5
  18.0 9.0 %shard_map.78 = (f32[512,512]{1,0:T(8,128)}, f32[512,512]{1,0:T(8,128)}, f32[544,128]{1,0:T(8,128)}) custom-call(f32[8192,128]{1,0:T(8,128)} %bitcast.78, f32[8192,128]{1,0:T(8,128)} %bitcast.80, f32[8192,128]{1,0:T(8,128)} %bitcast.82), custom_call_target="tpu_custom_call" | custom-call | bytes 16777216 | tf_op jit(solution)/shard_map/pallas_call | solution.py:494
  27.0 5.7 %collective-permute-start.10 = (f32[512,512]{1,0:T(8,128)}, f32[512,512]{1,0:T(8,128)S(1)}, u32[]{:S(2)}, u32[]{:S(2)}) collective-permute-start(f32[512,512]{1,0:T(8,128)} %get-tuple-element.24), channel_id=1, source_target_pairs={{0,1},{1,2},{2,3},{3,4},{4,5},{5,6},{6,7},{8,9},{9,10},{10,11},{11... | collective-permute-start | bytes 3145736 | tf_op jit(solution)/shard_map/ppermute | solution.py:614
  32.7 1.9 %collective-permute-start.11 = (f32[512,512]{1,0:T(8,128)}, f32[512,512]{1,0:T(8,128)S(1)}, u32[]{:S(2)}, u32[]{:S(2)}) collective-permute-start(f32[512,512]{1,0:T(8,128)} %get-tuple-element.25), channel_id=1, source_target_pairs={{1,0},{2,1},{3,2},{4,3},{5,4},{6,5},{7,6},{9,8},{10,9},{11,10},{12... | collective-permute-start | bytes 3145736 | tf_op jit(solution)/shard_map/ppermute | solution.py:614
  34.6 7.5 %collective-permute-start.12 = (f32[544,128]{1,0:T(8,128)}, f32[544,128]{1,0:T(8,128)S(1)}, u32[]{:S(2)}, u32[]{:S(2)}) collective-permute-start(f32[544,128]{1,0:T(8,128)} %get-tuple-element.26), channel_id=1, source_target_pairs={{0,1},{1,2},{2,3},{3,4},{4,5},{5,6},{6,7},{8,9},{9,10},{10,11},{11... | collective-permute-start | bytes 835592 | tf_op jit(solution)/shard_map/ppermute | solution.py:615
  42.2 0.0 collective-permute-done
  42.2 1.9 %collective-permute-start.13 = (f32[544,128]{1,0:T(8,128)}, f32[544,128]{1,0:T(8,128)S(1)}, u32[]{:S(2)}, u32[]{:S(2)}) collective-permute-start(f32[544,128]{1,0:T(8,128)} %get-tuple-element.26), channel_id=1, source_target_pairs={{1,0},{2,1},{3,2},{4,3},{5,4},{6,5},{7,6},{9,8},{10,9},{11,10},{12... | collective-permute-start | bytes 835592 | tf_op jit(solution)/shard_map/ppermute | solution.py:615
  44.1 0.2 add.45
  44.4 1.4 copy-done.4
  45.7 0.3 add.50
  46.0 15.7 %collective-permute-done.12 = f32[544,128]{1,0:T(8,128)S(1)} collective-permute-done((f32[544,128]{1,0:T(8,128)}, f32[544,128]{1,0:T(8,128)S(1)}, u32[]{:S(2)}, u32[]{:S(2)}) %collective-permute-start.12) | collective-permute-done | bytes 278560 | tf_op jit(solution)/shard_map/ppermute | solution.py:615
  61.6 7.6 %collective-permute-done.13 = f32[544,128]{1,0:T(8,128)S(1)} collective-permute-done((f32[544,128]{1,0:T(8,128)}, f32[544,128]{1,0:T(8,128)S(1)}, u32[]{:S(2)}, u32[]{:S(2)}) %collective-permute-start.13) | collective-permute-done | bytes 278560 | tf_op jit(solution)/shard_map/ppermute | solution.py:615
  69.3 8.0 %shard_map.79 = (f32[8,2,272,128]{3,2,1,0:T(8,128)S(1)}, f32[8,2,272,128]{3,2,1,0:T(8,128)S(1)}) custom-call(f32[1,4]{1,0:T(1,128)S(1)} %copy-done.3, f32[512,512]{1,0:T(8,128)S(1)} %copy-done, f32[512,512]{1,0:T(8,128)S(1)} %collective-permute-done.10.refs_1_, f32[512,512]{1,0:T(8,128)S(1)} %copy-done.1, f32[512,512]{1,0:T(8,128)S(1)} %collective-permute-done.11.refs_3_), custom_call_target="tpu_custom_call" | custom-call | bytes 9437184 | tf_op jit(solution)/shard_map/pallas_call | solution.py:541
  77.3 0.1 collective-permute-start.14
  77.4 0.1 slice.91
  77.5 1.1 collective-permute-start.1
  78.5 0.1 fusion.8
  78.6 1.7 %collective-permute-start.7 = (f32[2,512,128]{2,1,0:T(8,128)S(1)}, f32[2,512,128]{2,1,0:T(8,128)S(1)}, u32[]{:S(2)}, u32[]{:S(2)}) collective-permute-start(f32[2,512,128]{2,1,0:T(8,128)S(1)} %get-tuple-element.39), channel_id=1, source_target_pairs={{0,16},{8,56},{16,32},{24,8},{32,48},{40,24},{48,0},{56,40},{64,80... | collective-permute-start | bytes 1572872 | tf_op jit(solution)/shard_map/ppermute | solution.py:590
  80.3 1.6 %collective-permute-start.6 = (f32[2,512,128]{2,1,0:T(8,128)S(1)}, f32[2,512,128]{2,1,0:T(8,128)S(1)}, u32[]{:S(2)}, u32[]{:S(2)}) collective-permute-start(f32[2,512,128]{2,1,0:T(8,128)S(1)} %get-tuple-element.38), channel_id=1, source_target_pairs={{0,48},{8,24},{16,0},{24,40},{32,16},{40,56},{48,32},{56,8},{64,11... | collective-permute-start | bytes 1572872 | tf_op jit(solution)/shard_map/ppermute | solution.py:591
  81.9 0.2 add.55
  82.1 0.1 fusion.7
  82.2 1.4 %collective-permute-start.16 = (f32[2,2,272,128]{3,2,1,0:T(8,128)S(1)}, f32[2,2,272,128]{3,2,1,0:T(8,128)S(1)}, u32[]{:S(2)}, u32[]{:S(2)}) collective-permute-start(f32[2,2,272,128]{3,2,1,0:T(8,128)S(1)} %get-tuple-element.37), channel_id=1, source_target_pairs={{0,16},{8,56},{16,32},{24,8},{32,48},{40,24},{48,0},{56,40},{64,80... | collective-permute-start | bytes 1671176 | tf_op jit(solution)/shard_map/ppermute | solution.py:590
  83.6 9.0 %collective-permute-done.7 = f32[2,512,128]{2,1,0:T(8,128)S(1)} collective-permute-done((f32[2,512,128]{2,1,0:T(8,128)S(1)}, f32[2,512,128]{2,1,0:T(8,128)S(1)}, u32[]{:S(2)}, u32[]{:S(2)}) %collective-permute-start.7) | collective-permute-done | bytes 524320 | tf_op jit(solution)/shard_map/ppermute | solution.py:590
  92.6 0.1 slice_add_fusion.3
  92.7 1.9 %collective-permute-start.8 = (f32[2,512,128]{2,1,0:T(8,128)S(1)}, f32[2,512,128]{2,1,0:T(8,128)S(1)}, u32[]{:S(2)}, u32[]{:S(2)}) collective-permute-start(f32[2,512,128]{2,1,0:T(8,128)S(1)} %slice_add_fusion.3), channel_id=1, source_target_pairs={{0,16},{8,56},{16,32},{24,8},{32,48},{40,24},{48,0},{56,40},{64,80... | collective-permute-start | bytes 1572872 | tf_op jit(solution)/shard_map/ppermute | solution.py:592
  94.6 8.5 %collective-permute-done.1 = f32[4,512,128]{2,1,0:T(8,128)S(1)} collective-permute-done((f32[4,512,128]{2,1,0:T(8,128)S(1)}, f32[4,512,128]{2,1,0:T(8,128)S(1)}, u32[]{:S(2)}, u32[]{:S(2)}) %collective-permute-start.1) | collective-permute-done | bytes 1048608 | tf_op jit(solution)/shard_map/ppermute | solution.py:604
  103.1 0.1 slice_add_fusion
  103.2 3.1 %collective-permute-start.15 = (f32[2,2,272,128]{3,2,1,0:T(8,128)S(1)}, f32[2,2,272,128]{3,2,1,0:T(8,128)S(1)}, u32[]{:S(2)}, u32[]{:S(2)}) collective-permute-start(f32[2,2,272,128]{3,2,1,0:T(8,128)S(1)} %get-tuple-element.36), channel_id=1, source_target_pairs={{0,48},{8,24},{16,0},{24,40},{32,16},{40,56},{48,32},{56,8},{64,11... | collective-permute-start | bytes 1671176 | tf_op jit(solution)/shard_map/ppermute | solution.py:591
  106.3 0.1 slice_add_fusion.1
  106.3 0.1 collective-permute-start.17
  106.5 0.6 collective-permute-start.3
  107.1 2.8 %collective-permute-start.2 = (f32[512,128]{1,0:T(8,128)S(1)}, f32[512,128]{1,0:T(8,128)S(1)}, u32[]{:S(2)}, u32[]{:S(2)}) collective-permute-start(f32[512,128]{1,0:T(8,128)S(1)} %get-tuple-element.40), channel_id=1, source_target_pairs={{0,48},{8,24},{16,0},{24,40},{32,16},{40,56},{48,32},{56,8},{64,11... | collective-permute-start | bytes 786440 | tf_op jit(solution)/shard_map/ppermute | solution.py:591
  109.8 0.1 fusion.1
  110.0 1.0 collective-permute-start.9
  111.0 8.3 %collective-permute-done.15 = f32[2,2,272,128]{3,2,1,0:T(8,128)S(1)} collective-permute-done((f32[2,2,272,128]{3,2,1,0:T(8,128)S(1)}, f32[2,2,272,128]{3,2,1,0:T(8,128)S(1)}, u32[]{:S(2)}, u32[]{:S(2)}) %collective-permute-start.15) | collective-permute-done | bytes 557088 | tf_op jit(solution)/shard_map/ppermute | solution.py:591
  119.3 2.3 %collective-permute-done.17 = f32[2,2,272,128]{3,2,1,0:T(8,128)S(1)} collective-permute-done((f32[2,2,272,128]{3,2,1,0:T(8,128)S(1)}, f32[2,2,272,128]{3,2,1,0:T(8,128)S(1)}, u32[]{:S(2)}, u32[]{:S(2)}) %collective-permute-start.17) | collective-permute-done | bytes 557088 | tf_op jit(solution)/shard_map/ppermute | solution.py:592
  121.6 0.1 fusion
  121.7 1.0 collective-permute-start.18
  122.7 1.6 %collective-permute-done.3 = f32[512,128]{1,0:T(8,128)S(1)} collective-permute-done((f32[512,128]{1,0:T(8,128)S(1)}, f32[512,128]{1,0:T(8,128)S(1)}, u32[]{:S(2)}, u32[]{:S(2)}) %collective-permute-start.3) | collective-permute-done | bytes 262176 | tf_op jit(solution)/shard_map/ppermute | solution.py:590
  124.4 0.4 collective-permute-start.4
  124.8 3.5 %collective-permute-done.18 = f32[2,272,128]{2,1,0:T(8,128)S(1)} collective-permute-done((f32[2,272,128]{2,1,0:T(8,128)S(1)}, f32[2,272,128]{2,1,0:T(8,128)S(1)}, u32[]{:S(2)}, u32[]{:S(2)}) %collective-permute-start.18) | collective-permute-done | bytes 278560 | tf_op jit(solution)/shard_map/ppermute | solution.py:599
  128.4 1.9 %collective-permute-start.19 = (f32[34,8,128]{2,1,0:T(8,128)S(1)}, f32[34,8,128]{2,1,0:T(8,128)S(1)}, u32[]{:S(2)}, u32[]{:S(2)}) collective-permute-start(f32[34,8,128]{2,1,0:T(8,128)S(1)} %get-tuple-element.43), channel_id=1, source_target_pairs={{0,1},{1,2},{2,3},{3,4},{4,5},{5,6},{6,7},{8,9},{9,10},{10,11},{11... | collective-permute-start | bytes 417800 | tf_op jit(solution)/shard_map/ppermute | solution.py:628
  130.3 3.9 %collective-permute-start.20 = (f32[34,8,128]{2,1,0:T(8,128)S(1)}, f32[34,8,128]{2,1,0:T(8,128)S(1)}, u32[]{:S(2)}, u32[]{:S(2)}) collective-permute-start(f32[34,8,128]{2,1,0:T(8,128)S(1)} %get-tuple-element.42), channel_id=1, source_target_pairs={{1,0},{2,1},{3,2},{4,3},{5,4},{6,5},{7,6},{9,8},{10,9},{11,10},{12... | collective-permute-start | bytes 417800 | tf_op jit(solution)/shard_map/ppermute | solution.py:628
  134.3 1.0 collective-permute-done.19.e_low
  135.3 5.5 %collective-permute-done.20.e_high = f32[34,8,128]{2,1,0:T(8,128)S(1)} collective-permute-done((f32[34,8,128]{2,1,0:T(8,128)S(1)}, f32[34,8,128]{2,1,0:T(8,128)S(1)}, u32[]{:S(2)}, u32[]{:S(2)}) %collective-permute-start.20) | collective-permute-done | bytes 139296 | tf_op jit(solution)/shard_map/ppermute | solution.py:628
  140.9 1.8 %shard_map.80 = (f32[32,2,8,128]{3,2,1,0:T(8,128)}, f32[32,2,8,128]{3,2,1,0:T(8,128)}) custom-call(f32[32,2,8,128]{3,2,1,0:T(8,128)S(1)} %bitcast.73, f32[32,2,8,128]{3,2,1,0:T(8,128)S(1)} %bitcast.72, f32[2,34,8,128]{3,2,1,0:T(8,128)S(1)} %bitcast.71, f32[34,8,128]{2,1,0:T(8,128)S(1)} %collective-permute-done.19.e_low, ...), custom_call_target="tpu_custom_call" | custom-call | bytes 4194304 | tf_op jit(solution)/shard_map/pallas_call | solution.py:560
  (29 shorter events, 0.3 us)
Async XLA Ops:
  17.4 24.8 %collective-permute-start = (f32[8,512,128]{2,1,0:T(8,128)}, f32[8,512,128]{2,1,0:T(8,128)S(1)}, u32[]{:S(2)}, u32[]{:S(2)}) collective-permute-start(f32[8,512,128]{2,1,0:T(8,128)} %get-tuple-element.20), channel_id=1, source_target_pairs={{0,8},{8,0},{16,24},{24,16},{32,40},{40,32},{48,56},{56,48},{64,72... | collective-permute-start | bytes 6291464 | tf_op jit(solution)/shard_map/ppermute | solution.py:618
  17.5 26.6 %copy-start.5 = (f32[8,512,128]{2,1,0:T(8,128)S(1)}, f32[8,512,128]{2,1,0:T(8,128)}, u32[]{:S(2)}) copy-start(f32[8,512,128]{2,1,0:T(8,128)} %get-tuple-element.19) | copy-start | bytes 6291460
  17.5 26.8 %collective-permute-start.5 = (f32[8,512,128]{2,1,0:T(8,128)}, f32[8,512,128]{2,1,0:T(8,128)S(1)}, u32[]{:S(2)}, u32[]{:S(2)}) collective-permute-start(f32[8,512,128]{2,1,0:T(8,128)} %get-tuple-element.22), channel_id=1, source_target_pairs={{0,8},{8,0},{16,24},{24,16},{32,40},{40,32},{48,56},{56,48},{64,72... | collective-permute-start | bytes 6291464 | tf_op jit(solution)/shard_map/ppermute | solution.py:619
  27.0 42.3 %collective-permute-start.10 = (f32[512,512]{1,0:T(8,128)}, f32[512,512]{1,0:T(8,128)S(1)}, u32[]{:S(2)}, u32[]{:S(2)}) collective-permute-start(f32[512,512]{1,0:T(8,128)} %get-tuple-element.24), channel_id=1, source_target_pairs={{0,1},{1,2},{2,3},{3,4},{4,5},{5,6},{6,7},{8,9},{9,10},{10,11},{11... | collective-permute-start | bytes 3145736 | tf_op jit(solution)/shard_map/ppermute | solution.py:614
  32.7 36.6 %collective-permute-start.11 = (f32[512,512]{1,0:T(8,128)}, f32[512,512]{1,0:T(8,128)S(1)}, u32[]{:S(2)}, u32[]{:S(2)}) collective-permute-start(f32[512,512]{1,0:T(8,128)} %get-tuple-element.25), channel_id=1, source_target_pairs={{1,0},{2,1},{3,2},{4,3},{5,4},{6,5},{7,6},{9,8},{10,9},{11,10},{12... | collective-permute-start | bytes 3145736 | tf_op jit(solution)/shard_map/ppermute | solution.py:614
  34.6 27.0 %collective-permute-start.12 = (f32[544,128]{1,0:T(8,128)}, f32[544,128]{1,0:T(8,128)S(1)}, u32[]{:S(2)}, u32[]{:S(2)}) collective-permute-start(f32[544,128]{1,0:T(8,128)} %get-tuple-element.26), channel_id=1, source_target_pairs={{0,1},{1,2},{2,3},{3,4},{4,5},{5,6},{6,7},{8,9},{9,10},{10,11},{11... | collective-permute-start | bytes 835592 | tf_op jit(solution)/shard_map/ppermute | solution.py:615
  42.2 27.1 %collective-permute-start.13 = (f32[544,128]{1,0:T(8,128)}, f32[544,128]{1,0:T(8,128)S(1)}, u32[]{:S(2)}, u32[]{:S(2)}) collective-permute-start(f32[544,128]{1,0:T(8,128)} %get-tuple-element.26), channel_id=1, source_target_pairs={{1,0},{2,1},{3,2},{4,3},{5,4},{6,5},{7,6},{9,8},{10,9},{11,10},{12... | collective-permute-start | bytes 835592 | tf_op jit(solution)/shard_map/ppermute | solution.py:615
  44.1 1.6 %copy-start.4 = (f32[8,512,128]{2,1,0:T(8,128)S(1)}, f32[8,512,128]{2,1,0:T(8,128)}, u32[]{:S(2)}) copy-start(f32[8,512,128]{2,1,0:T(8,128)} %get-tuple-element.21) | copy-start | bytes 6291460
  45.7 23.6 %copy-start = (f32[512,512]{1,0:T(8,128)S(1)}, f32[512,512]{1,0:T(8,128)}, u32[]{:S(2)}) copy-start(f32[512,512]{1,0:T(8,128)} %get-tuple-element.23.refs_0_) | copy-start | bytes 3145732
  45.7 23.6 %copy-start.1 = (f32[512,512]{1,0:T(8,128)S(1)}, f32[512,512]{1,0:T(8,128)}, u32[]{:S(2)}) copy-start(f32[512,512]{1,0:T(8,128)} %get-tuple-element.28.refs_2_) | copy-start | bytes 3145732
  45.7 23.6 %copy-start.3 = (f32[1,4]{1,0:T(1,128)S(1)}, f32[1,4]{1,0:T(1,128)}, u32[]{:S(2)}) copy-start(f32[1,4]{1,0:T(1,128)} %coeffs.3) | copy-start | bytes 52
  77.3 4.6 %collective-permute-start.14 = (f32[8,2,272,128]{3,2,1,0:T(8,128)S(1)}, f32[8,2,272,128]{3,2,1,0:T(8,128)S(1)}, u32[]{:S(2)}, u32[]{:S(2)}) collective-permute-start(f32[8,2,272,128]{3,2,1,0:T(8,128)S(1)} %get-tuple-element.31), channel_id=1, source_target_pairs={{0,8},{8,0},{16,24},{24,16},{32,40},{40,32},{48,56},{56,48},{64,72... | collective-permute-start | bytes 6684680 | tf_op jit(solution)/shard_map/ppermute | solution.py:627
  77.5 25.6 %collective-permute-start.1 = (f32[4,512,128]{2,1,0:T(8,128)S(1)}, f32[4,512,128]{2,1,0:T(8,128)S(1)}, u32[]{:S(2)}, u32[]{:S(2)}) collective-permute-start(f32[4,512,128]{2,1,0:T(8,128)S(1)} %slice.91), channel_id=1, source_target_pairs={{0,64},{8,72},{16,80},{24,88},{32,96},{40,104},{48,112},{56,120},{... | collective-permute-start | bytes 3145736 | tf_op jit(solution)/shard_map/ppermute | solution.py:604
  78.6 14.1 %collective-permute-start.7 = (f32[2,512,128]{2,1,0:T(8,128)S(1)}, f32[2,512,128]{2,1,0:T(8,128)S(1)}, u32[]{:S(2)}, u32[]{:S(2)}) collective-permute-start(f32[2,512,128]{2,1,0:T(8,128)S(1)} %get-tuple-element.39), channel_id=1, source_target_pairs={{0,16},{8,56},{16,32},{24,8},{32,48},{40,24},{48,0},{56,40},{64,80... | collective-permute-start | bytes 1572872 | tf_op jit(solution)/shard_map/ppermute | solution.py:590
  80.3 26.8 %collective-permute-start.6 = (f32[2,512,128]{2,1,0:T(8,128)S(1)}, f32[2,512,128]{2,1,0:T(8,128)S(1)}, u32[]{:S(2)}, u32[]{:S(2)}) collective-permute-start(f32[2,512,128]{2,1,0:T(8,128)S(1)} %get-tuple-element.38), channel_id=1, source_target_pairs={{0,48},{8,24},{16,0},{24,40},{32,16},{40,56},{48,32},{56,8},{64,11... | collective-permute-start | bytes 1572872 | tf_op jit(solution)/shard_map/ppermute | solution.py:591
  82.2 24.1 %collective-permute-start.16 = (f32[2,2,272,128]{3,2,1,0:T(8,128)S(1)}, f32[2,2,272,128]{3,2,1,0:T(8,128)S(1)}, u32[]{:S(2)}, u32[]{:S(2)}) collective-permute-start(f32[2,2,272,128]{3,2,1,0:T(8,128)S(1)} %get-tuple-element.37), channel_id=1, source_target_pairs={{0,16},{8,56},{16,32},{24,8},{32,48},{40,24},{48,0},{56,40},{64,80... | collective-permute-start | bytes 1671176 | tf_op jit(solution)/shard_map/ppermute | solution.py:590
  92.7 17.2 %collective-permute-start.8 = (f32[2,512,128]{2,1,0:T(8,128)S(1)}, f32[2,512,128]{2,1,0:T(8,128)S(1)}, u32[]{:S(2)}, u32[]{:S(2)}) collective-permute-start(f32[2,512,128]{2,1,0:T(8,128)S(1)} %slice_add_fusion.3), channel_id=1, source_target_pairs={{0,16},{8,56},{16,32},{24,8},{32,48},{40,24},{48,0},{56,40},{64,80... | collective-permute-start | bytes 1572872 | tf_op jit(solution)/shard_map/ppermute | solution.py:592
  103.2 16.1 %collective-permute-start.15 = (f32[2,2,272,128]{3,2,1,0:T(8,128)S(1)}, f32[2,2,272,128]{3,2,1,0:T(8,128)S(1)}, u32[]{:S(2)}, u32[]{:S(2)}) collective-permute-start(f32[2,2,272,128]{3,2,1,0:T(8,128)S(1)} %get-tuple-element.36), channel_id=1, source_target_pairs={{0,48},{8,24},{16,0},{24,40},{32,16},{40,56},{48,32},{56,8},{64,11... | collective-permute-start | bytes 1671176 | tf_op jit(solution)/shard_map/ppermute | solution.py:591
  106.3 15.2 %collective-permute-start.17 = (f32[2,2,272,128]{3,2,1,0:T(8,128)S(1)}, f32[2,2,272,128]{3,2,1,0:T(8,128)S(1)}, u32[]{:S(2)}, u32[]{:S(2)}) collective-permute-start(f32[2,2,272,128]{3,2,1,0:T(8,128)S(1)} %slice_add_fusion.1), channel_id=1, source_target_pairs={{0,16},{8,56},{16,32},{24,8},{32,48},{40,24},{48,0},{56,40},{64,80... | collective-permute-start | bytes 1671176 | tf_op jit(solution)/shard_map/ppermute | solution.py:592
  106.5 17.9 %collective-permute-start.3 = (f32[512,128]{1,0:T(8,128)S(1)}, f32[512,128]{1,0:T(8,128)S(1)}, u32[]{:S(2)}, u32[]{:S(2)}) collective-permute-start(f32[512,128]{1,0:T(8,128)S(1)} %get-tuple-element.41), channel_id=1, source_target_pairs={{0,16},{8,56},{16,32},{24,8},{32,48},{40,24},{48,0},{56,40},{64,80... | collective-permute-start | bytes 786440 | tf_op jit(solution)/shard_map/ppermute | solution.py:590
  107.1 27.2 %collective-permute-start.2 = (f32[512,128]{1,0:T(8,128)S(1)}, f32[512,128]{1,0:T(8,128)S(1)}, u32[]{:S(2)}, u32[]{:S(2)}) collective-permute-start(f32[512,128]{1,0:T(8,128)S(1)} %get-tuple-element.40), channel_id=1, source_target_pairs={{0,48},{8,24},{16,0},{24,40},{32,16},{40,56},{48,32},{56,8},{64,11... | collective-permute-start | bytes 786440 | tf_op jit(solution)/shard_map/ppermute | solution.py:591
  110.0 14.8 %collective-permute-start.9 = (f32[512,128]{1,0:T(8,128)S(1)}, f32[512,128]{1,0:T(8,128)S(1)}, u32[]{:S(2)}, u32[]{:S(2)}) collective-permute-start(f32[512,128]{1,0:T(8,128)S(1)} %slice_bitcast_fusion.2), channel_id=1, source_target_pairs={{0,64},{8,72},{16,80},{24,88},{32,96},{40,104},{48,112},{56,120},{... | collective-permute-start | bytes 786440 | tf_op jit(solution)/shard_map/ppermute | solution.py:599
  121.7 19.2 %copy-start.2 = (f32[544,128]{1,0:T(8,128)S(1)}, f32[544,128]{1,0:T(8,128)}, u32[]{:S(2)}) copy-start(f32[544,128]{1,0:T(8,128)} %get-tuple-element.26) | copy-start | bytes 835588
  121.7 6.6 %collective-permute-start.18 = (f32[2,272,128]{2,1,0:T(8,128)S(1)}, f32[2,272,128]{2,1,0:T(8,128)S(1)}, u32[]{:S(2)}, u32[]{:S(2)}) collective-permute-start(f32[2,272,128]{2,1,0:T(8,128)S(1)} %slice_bitcast_fusion), channel_id=1, source_target_pairs={{0,64},{8,72},{16,80},{24,88},{32,96},{40,104},{48,112},{56,120},{... | collective-permute-start | bytes 835592 | tf_op jit(solution)/shard_map/ppermute | solution.py:599
  124.4 9.8 %collective-permute-start.4 = (f32[512,128]{1,0:T(8,128)S(1)}, f32[512,128]{1,0:T(8,128)S(1)}, u32[]{:S(2)}, u32[]{:S(2)}) collective-permute-start(f32[512,128]{1,0:T(8,128)S(1)} %fusion.4), channel_id=1, source_target_pairs={{0,16},{8,56},{16,32},{24,8},{32,48},{40,24},{48,0},{56,40},{64,80... | collective-permute-start | bytes 786440 | tf_op jit(solution)/shard_map/ppermute | solution.py:592
  128.4 6.9 %collective-permute-start.19 = (f32[34,8,128]{2,1,0:T(8,128)S(1)}, f32[34,8,128]{2,1,0:T(8,128)S(1)}, u32[]{:S(2)}, u32[]{:S(2)}) collective-permute-start(f32[34,8,128]{2,1,0:T(8,128)S(1)} %get-tuple-element.43), channel_id=1, source_target_pairs={{0,1},{1,2},{2,3},{3,4},{4,5},{5,6},{6,7},{8,9},{9,10},{10,11},{11... | collective-permute-start | bytes 417800 | tf_op jit(solution)/shard_map/ppermute | solution.py:628
  130.3 10.6 %collective-permute-start.20 = (f32[34,8,128]{2,1,0:T(8,128)S(1)}, f32[34,8,128]{2,1,0:T(8,128)S(1)}, u32[]{:S(2)}, u32[]{:S(2)}) collective-permute-start(f32[34,8,128]{2,1,0:T(8,128)S(1)} %get-tuple-element.42), channel_id=1, source_target_pairs={{1,0},{2,1},{3,2},{4,3},{5,4},{6,5},{7,6},{9,8},{10,9},{11,10},{12... | collective-permute-start | bytes 417800 | tf_op jit(solution)/shard_map/ppermute | solution.py:628

commit v4 on v2

v4 whole, which is shorter than its diff:
```python
import jax
import jax.numpy as jnp
from jax import lax
from jax.experimental import pallas as pl
from jax.experimental.pallas import tpu as pltpu
from jax.sharding import PartitionSpec as P

CHIPS = 8
COUNT = 16
SLABS = 8
GROUP = 16
MIB = 1024 * 1024
F32 = jnp.float32


def packed(cells):
    x = cells.shape[0]
    return cells.reshape(x, 4, 4, 128).transpose(0, 2, 1, 3).reshape(x, 2, 8, 128)


def unpacked(cells):
    x = cells.shape[0]
    return cells.reshape(x, 4, 4, 128).transpose(0, 2, 1, 3).reshape(x, 4, 512)


def roll(cells, shift):
    return pltpu.roll(cells, shift % 8, 1)


def places(n):
    sub = lax.broadcasted_iota(jnp.int32, (n, 8, 128), 1)
    return sub, lax.rem(sub, 4), lax.broadcasted_iota(jnp.int32, (n, 8, 128), 2)


def spread(field, speed, row, n, lower, upper):
    sub, z, lane = places(n)
    first, at_start, at_end = sub < 4, lane == 0, lane == 127
    v = [field[pl.ds(row + 1, n), h] for h in (0, 1)]
    k = [speed[pl.ds(row + 1, n), h] for h in (0, 1)]

    def ahead(a, b):
        ra, rb = pltpu.roll(a, 127, 2), pltpu.roll(b, 127, 2)
        qa, qb = roll(ra, 4), roll(rb, 4)
        return (
            jnp.where(at_end, jnp.where(first, qa, qb), ra),
            jnp.where(at_end, jnp.where(first, qb, 0.0), rb),
        )

    def behind(a, b, edge):
        ra, rb = pltpu.roll(a, 1, 2), pltpu.roll(b, 1, 2)
        qa, qb = roll(ra, 4), roll(rb, 4)
        return (
            jnp.where(at_start, jnp.where(first, edge, qa), ra),
            jnp.where(at_start, jnp.where(first, qa, qb), rb),
        )

    v_y, k_y = ahead(*v), ahead(*k)
    f_y = [(k[h] + k_y[h]) * (v_y[h] - v[h]) for h in (0, 1)]
    b_y = behind(*f_y, k[0] * v[0])
    out = []
    for h in (0, 1):
        kv = k[h] * v[h]
        f_z = jnp.where(z == 3, -upper * kv, (k[h] + roll(k[h], -1)) * (roll(v[h], -1) - v[h]))
        b_z = jnp.where(z == 0, lower * kv, roll(f_z, 1))
        f_x = (k[h] + speed[pl.ds(row + 2, n), h]) * (field[pl.ds(row + 2, n), h] - v[h])
        b_x = (k[h] + speed[pl.ds(row, n), h]) * (v[h] - field[pl.ds(row, n), h])
        out.append((f_x - b_x) + (f_y[h] - b_y[h]) + (f_z - b_z))
    return v, out


def widen(scratch, main, before, after, block, blocks):
    rows = main.shape[0]
    scratch[pl.ds(1, rows)] = main[...]
    scratch[pl.ds(0, 1)] = jnp.where(block > 0, before[...], 0.0)
    scratch[pl.ds(rows + 1, 1)] = jnp.where(block < blocks - 1, after[...], 0.0)


def where_am_i():
    me = lax.axis_index("tm")
    return me // 8, lax.rem(me // 2, 4), lax.rem(me, 2)


def series_kernel(coeffs, u, k, p, cos, sin, d_other, d_same, v_other, v_same, low_other, low_same, high_other, high_same,
                  us, ks, ns, ds, vs, fx, fy, fw, fz, fm, es, in_sem, out_sem, edge_sem):
    cells = u.shape[0] // 16
    rows = cells // CHIPS
    half_rows = rows // 2
    my_z, my_y, my_core = where_am_i()
    slab = lax.axis_index("gz")
    lower, upper = jnp.where(slab == 0, 1.0, 0.0), jnp.where(slab == SLABS - 1, 1.0, 0.0)
    c0, c1, c2, c3 = (coeffs[0, i] for i in range(4))
    sub = lax.broadcasted_iota(jnp.int32, (8, 128), 0)
    lane = lax.broadcasted_iota(jnp.int32, (8, 128), 1)
    z = lax.rem(sub, 4)
    first, at_start, at_end = sub < 4, lane == 0, lane == 127
    open_up, open_down = jnp.where(z == 3, 0.0, 1.0), jnp.where(z == 0, 0.0, 1.0)
    of_u = jnp.where(z == 0, c1, jnp.where(z == 1, c0, jnp.where(z == 2, c3, c2)))
    of_n = jnp.where(z == 1, c1, jnp.where(z == 3, c3, 0.0))
    y_first, y_last = jnp.logical_and(first, at_start), jnp.logical_and(jnp.logical_not(first), at_end)
    outer = jnp.where(z == 0, lower, 0.0) + jnp.where(z == 3, upper, 0.0)

    def arrays():
        return ((u, us, 16), (k, ks, 16), (p, ns, 16), (cos, ds, 0), (sin, vs, 0))

    def loads(c, which):
        return [
            pltpu.make_async_copy(a.at[pl.ds(c * rows * 16, rows * 16)], b.at[pl.ds(c * rows * 16 + off, rows * 16)], in_sem.at[i, c])
            for i, (a, b, off) in enumerate(arrays()) if i in which
        ]

    for c in range(CHIPS):
        for copy in loads(c, (0, 1, 2)):
            copy.start()
        if c:
            for copy in loads(c - 1, (3, 4)):
                copy.start()
    for copy in loads(CHIPS - 1, (3, 4)):
        copy.start()
    nothing = jnp.zeros((16, 128), F32)
    fx[0:16] = nothing
    fz[0:16] = nothing
    for side in (0, 1):
        es[side, 0:16] = nothing
        es[side, (cells + 1) * 16 : (cells + 2) * 16] = nothing
    for ref in (us, ks, ns):
        ref[0:16] = nothing
        ref[(cells + 1) * 16 : (cells + 2) * 16] = nothing

    def at(ref, row, by=0):
        return ref[pl.ds(row + by, 8), :]

    def ahead(ref, row, here):
        return pltpu.roll(jnp.where(at_start, at(ref, row, 4), here), 127, 1)

    def behind(ref, row, here):
        return pltpu.roll(jnp.where(at_end, at(ref, row, -4), here), 1, 1)

    def up(here):
        return pltpu.roll(here, 7, 0)

    def down(here):
        return pltpu.roll(here, 1, 0)

    def first_pass(c):
        def step(i, carry):
            start = (c * rows + i * GROUP + 1) * 16
            kk, uu, kx = {}, {}, {}

            def center(seen, ref, g, h):
                if (g, h) not in seen:
                    seen[g, h] = at(ref, start + g * 16 + h * 8)
                return seen[g, h]

            for h in (0, 1):
                kx[-1, h] = center(kk, ks, -1, h) + center(kk, ks, 0, h)
            for g in range(GROUP):
                for h in (0, 1):
                    row = start + g * 16 + h * 8
                    k0 = center(kk, ks, g, h)
                    kx[g, h] = k0 + center(kk, ks, g + 1, h)
                    ky, kw = k0 + ahead(ks, row, k0), k0 + behind(ks, row, k0)
                    if h == 0:
                        face_w = jnp.where(y_first, k0, kw)
                        face_y, kw = ky, jnp.where(y_first, 0.0, kw)
                    else:
                        face_y = jnp.where(y_last, k0, ky)
                        face_w, ky = kw, jnp.where(y_last, 0.0, ky)
                    kz, kv = (k0 + up(k0)) * open_up, (k0 + down(k0)) * open_down
                    mid = 24.0 - (((kx[g, h] + kx[g - 1, h]) + (face_y + face_w)) + ((kz + kv) + outer * k0))
                    for ref, value in ((fx, kx[g, h]), (fy, ky), (fw, kw), (fz, kz), (fm, mid)):
                        ref[pl.ds(row, 8), :] = value
                    v = center(uu, us, g, h)
                    out = (kx[g, h] * center(uu, us, g + 1, h) + kx[g - 1, h] * center(uu, us, g - 1, h)) + (kz * up(v) + kv * down(v))
                    out = out + (ky * ahead(us, row, v) + kw * behind(us, row, v)) + mid * v
                    ns[pl.ds(row, 8), :] = out * (-1.0 / 12.0) - at(ns, row)
            return carry

        lax.fori_loop(0, rows // GROUP, step, 0)

    def moments(c):
        def spread(ref, row, plane):
            return jnp.where(first, ref[pl.ds(row + plane, 1), :], ref[pl.ds(row + 4 + plane, 1), :])

        def step(i, carry):
            for g in range(2 * GROUP):
                row = (c * rows + 1) * 16 + (i * 2 * GROUP + g) * 8
                for side, plane in ((0, 0), (1, 3)):
                    es[side, pl.ds(row, 8), :] = of_u * spread(us, row, plane) + of_n * spread(ns, row, plane)
            return carry

        lax.fori_loop(0, rows // GROUP, step, 0)

    def second_pass(c):
        def step(i, carry):
            start = (c * rows + i * GROUP + 1) * 16
            nn, kx = {}, {}

            def center(seen, ref, g, h):
                if (g, h) not in seen:
                    seen[g, h] = at(ref, start + g * 16 + h * 8)
                return seen[g, h]

            for g in range(GROUP):
                for h in (0, 1):
                    row = start + g * 16 + h * 8
                    v = center(nn, ns, g, h)
                    kz = at(fz, row)
                    out = center(kx, fx, g, h) * center(nn, ns, g + 1, h) + center(kx, fx, g - 1, h) * center(nn, ns, g - 1, h)
                    out = out + (kz * up(v) + down(kz) * down(v))
                    out = out + (at(fy, row) * ahead(ns, row, v) + at(fw, row) * behind(ns, row, v)) + at(fm, row) * v
                    final = out * (-1.0 / 12.0) - at(us, row)
                    ds[pl.ds(row - 16, 8), :] = at(ds, row, -16) + c0 * v + c1 * final
                    vs[pl.ds(row - 16, 8), :] = at(vs, row, -16) + c2 * v + c3 * final
            return carry

        lax.fori_loop(0, rows // GROUP, step, 0)

    def slots(c, core):
        turn = lax.rem((1 - 2 * core) * (lax.rem(c, 4) - my_y) + 8, 4)
        side = lax.rem(c // 4 + my_z, 2)
        return turn * 2 + side, side * 4 + turn

    def stores(c, core, same):
        here = pl.ds((c * rows + core * half_rows) * 16, half_rows * 16)
        y_slot, z_slot = slots(c, core)
        return [
            pltpu.make_async_copy(ds.at[here], (d_same if same else d_other).at[y_slot], out_sem.at[0, core, c]),
            pltpu.make_async_copy(vs.at[here], (v_same if same else v_other).at[z_slot], out_sem.at[1, core, c]),
        ]

    def edge_stores(c, core, same):
        here = pl.ds((c * rows + core * half_rows) * 16, (half_rows + 2) * 16)
        y_slot, z_slot = slots(c, core)
        return [
            pltpu.make_async_copy(es.at[0, here], (low_same if same else low_other).at[y_slot], edge_sem.at[0, core, c]),
            pltpu.make_async_copy(es.at[1, here], (high_same if same else high_other).at[z_slot], edge_sem.at[1, core, c]),
        ]

    def send(copies, c, core):
        for same in (True, False):
            @pl.when((my_core == core) == same)
            def _():
                for copy in copies(c, core, same):
                    copy.start()

    def chunk(c, carry):
        @pl.when(c < CHIPS)
        def _():
            @pl.when(c == 0)
            def _():
                for copy in loads(c, (0, 1, 2)):
                    copy.wait()

            @pl.when(c + 1 < CHIPS)
            def _():
                for copy in loads(c + 1, (0, 1, 2)):
                    copy.wait()

            first_pass(c)
            moments(c)
            send(edge_stores, c, 0)

        @pl.when(c > 0)
        def _():
            send(edge_stores, c - 1, 1)
            for copy in loads(c - 1, (3, 4)):
                copy.wait()
            second_pass(c - 1)
            for core in (0, 1):
                send(stores, c - 1, core)

        return carry

    lax.fori_loop(0, CHIPS + 1, chunk, 0)

    def end(c, carry):
        for core in (0, 1):
            for copy in stores(c, core, True) + edge_stores(c, core, True):
                copy.wait()
        return carry

    lax.fori_loop(0, CHIPS, end, 0)


def mend_kernel(d, v, low, high, below, above, k, k_low, k_high, d_out, v_out, ds, vs):
    rows = d.shape[0]
    slab = lax.axis_index("gz")
    lower, upper = jnp.where(slab == 0, 1.0, 0.0), jnp.where(slab == SLABS - 1, 1.0, 0.0)
    wide = rows + 2
    z = places(wide)[1]
    factor = []
    for h in (0, 1):
        under = (1.0 - lower) * (k[:, h] + roll(k_low[:, h], -3))
        over = (1.0 - upper) * (k[:, h] + roll(k_high[:, h], 3))
        factor.append(jnp.where(z == 0, under, jnp.where(z == 3, -over, 0.0)) * (1.0 / 12.0))
    from_low = [low[:, h] - below[:, h] for h in (0, 1)]
    from_high = [above[:, h] - high[:, h] for h in (0, 1)]
    direct = []
    for field, slot in ((ds, 0), (vs, 2)):
        for h in (0, 1):
            a = jnp.where(z == 0, roll(from_low[h], -slot), roll(from_high[h], 3 - slot))
            b = jnp.where(z == 0, roll(from_low[h], -slot - 1), roll(from_high[h], 2 - slot))
            w = factor[h] * a
            field[:, h] = w
            direct.append((factor[h] * b + 2.0 * jnp.abs(factor[h]) * w)[1 : rows + 1])
    for field, given, out, direct_of in ((ds, d, d_out, direct[:2]), (vs, v, v_out, direct[2:])):
        w, outflow = spread(field, k, 0, rows, lower, upper)
        for h in (0, 1):
            out[:, h] = given[:, h] + direct_of[h] - outflow[h] * (1.0 / 12.0) - 2.0 * w[h]


ANYWHERE = pl.BlockSpec(memory_space=pl.ANY)
SMEM = pl.BlockSpec(memory_space=pltpu.SMEM)


def params(mib):
    return pltpu.CompilerParams(vmem_limit_bytes=mib * MIB)


def cost(mib):
    return pl.CostEstimate(flops=0, bytes_accessed=mib * MIB, transcendentals=0)


def flat(cells):
    return cells.reshape(-1, 128)


def series(coeffs, u, k, p, cos, sin):
    cells = u.shape[0] // 16
    share = jax.ShapeDtypeStruct((CHIPS, cells, 128), F32)
    edge = jax.ShapeDtypeStruct((CHIPS, (cells // COUNT + 2) * 16, 128), F32)
    wide = pltpu.VMEM(((cells + 2) * 16, 128), F32)
    exact = pltpu.VMEM((cells * 16, 128), F32)
    return pl.pallas_call(
        series_kernel,
        out_shape=(share,) * 4 + (edge,) * 4,
        in_specs=[SMEM] + [ANYWHERE] * 5,
        out_specs=(ANYWHERE,) * 8,
        scratch_shapes=[wide, wide, wide, exact, exact, wide, wide, wide, wide, wide]
        + [
            pltpu.VMEM((2, (cells + 2) * 16, 128), F32),
            pltpu.SemaphoreType.DMA((5, CHIPS)),
            pltpu.SemaphoreType.DMA((2, 2, CHIPS)),
            pltpu.SemaphoreType.DMA((2, 2, CHIPS)),
        ],
        compiler_params=params(56),
        cost_estimate=cost(45),
    )(coeffs, u, k, p, cos, sin)


def mend(d, v, low, high, below, above, k, k_low, k_high):
    shape = jax.ShapeDtypeStruct(d.shape, F32)
    whole = pl.BlockSpec(memory_space=pltpu.VMEM)
    return pl.pallas_call(
        mend_kernel,
        out_shape=(shape, shape),
        in_specs=[whole] * 9,
        out_specs=(whole, whole),
        scratch_shapes=[pltpu.VMEM(k.shape, F32)] * 2,
        compiler_params=params(16),
        cost_estimate=cost(4),
    )(d, v, low, high, below, above, k, k_low, k_high)


CELL = (2, 8, 128)


def along_y(sign):
    def goal(i):
        z, y, core = i // 8, (i // 2) % 4, i % 2
        return z * 8 + ((y + sign * (1 - 2 * core)) % 4) * 2 + core

    return [(i, goal(i)) for i in range(COUNT)]


FORTH, BACK = along_y(1), along_y(-1)
ACROSS = [(i, i ^ 8) for i in range(COUNT)]
SIBLING = [(i, i ^ 1) for i in range(COUNT)]
UP = [(i, i + 1) for i in range(SLABS - 1)]
DOWN = [(i + 1, i) for i in range(SLABS - 1)]


def swap(same, other):
    return same + lax.ppermute(other, "tm", SIBLING)


def ring_ends(two, back):
    return lax.ppermute(two, "tm", FORTH), lax.ppermute(back, "tm", BACK)


def ring_close(one, own, relayed, direct):
    return own + direct + lax.ppermute(one + relayed, "tm", FORTH)


def local(prev_term, last_term, cos_sum, sin_sum, speed_sq, series_coeffs):
    u, p, k = flat(packed(last_term[0])), flat(packed(prev_term[0])), flat(packed(speed_sq))
    cos, sin = flat(packed(cos_sum[0])), flat(packed(sin_sum[0]))
    rows = last_term.shape[1] // COUNT
    me = lax.axis_index("tm")

    d_other, d_same, v_other, v_same, low_other, low_same, high_other, high_same = series(series_coeffs, u, k, p, cos, sin)
    low, high = swap(low_same, low_other), swap(high_same, high_other)
    d_other, v_other, low, high = lax.optimization_barrier((d_other, v_other, low, high))
    d, v = swap(d_same, d_other), swap(v_same, v_other)

    start = me * rows * 16
    k_here = jnp.concatenate(
        [
            jnp.where(me > 0, lax.dynamic_slice_in_dim(k, jnp.maximum(start - 16, 0), 16), 0.0),
            lax.dynamic_slice_in_dim(k, start, rows * 16),
            jnp.where(me < COUNT - 1, lax.dynamic_slice_in_dim(k, jnp.minimum(start + rows * 16, k.shape[0] - 16), 16), 0.0),
        ]
    )
    k_low, k_high = lax.ppermute(k_here, "gz", UP), lax.ppermute(k_here, "gz", DOWN)

    low, d = (a.reshape(4, 2, *a.shape[1:]) for a in (low, d))
    low_ends, d_ends = ring_ends(low[2], low[3]), ring_ends(d[2], d[3])
    high = high[:4] + lax.ppermute(high[4:], "tm", ACROSS)
    v = v[:4] + lax.ppermute(v[4:], "tm", ACROSS)
    low = ring_close(low[1], low[0], *low_ends)
    high = ring_close(high[1], high[0], *ring_ends(high[2], high[3]))
    low = low[0] + lax.ppermute(low[1], "tm", ACROSS)
    below, above = lax.ppermute(high, "gz", UP), lax.ppermute(low, "gz", DOWN)
    d = ring_close(d[1], d[0], *d_ends)
    v = ring_close(v[1], v[0], *ring_ends(v[2], v[3]))
    d = d[0] + lax.ppermute(d[1], "tm", ACROSS)

    wide = (a.reshape(rows + 2, *CELL) for a in (low, high, below, above, k_here, k_low, k_high))
    d, v = mend(d.reshape(rows, *CELL), v.reshape(rows, *CELL), *wide)
    return unpacked(d), unpacked(v)


def solution(mesh):
    return jax.shard_map(
        local,
        mesh=mesh,
        in_specs=(
            P("tm", None, "gz", None),
            P("tm", None, "gz", None),
            P("tm", None, "gz", None),
            P("tm", None, "gz", None),
            P(None, "gz", None),
            P("tm", None),
        ),
        out_specs=(P("tm", "gz", None), P("tm", "gz", None)),
        check_vma=False,
    )
```

time: 155 us -> 129 us (0.83)
  the two profiles are of different devices: /device:TPU:6 before, /device:TPU:102 now
where the time goes in v4:
time: 129 us
  waiting for transfers between devices  70.6 us (55%)
  starting transfers between devices  24.3 us (19%)
  Pallas kernels  20 us (16%)
  other arithmetic  8.71 us (7%)
  local copies, waits for them, and re-layouts  4.43 us (3%)
    ppermute x8, waiting for transfers between devices, ring_ends(): return (lax.ppermute(two, 'tm', FORTH), lax.ppermute(back, 'tm', BACK))  21 us
    pallas_call x1, Pallas kernels, series(): pl.pallas_call(series_kernel, out_shape=(share,) * 4 + (edge,) * 4, in_sp...  18.1 us
    ppermute x1, waiting for transfers between devices, local(): d = d[0] + lax.ppermute(d[1], 'tm', ACROSS)  10.7 us
    ppermute x1, waiting for transfers between devices, local(): v = v[:4] + lax.ppermute(v[4:], 'tm', ACROSS)  10.1 us
    ppermute x4, waiting for transfers between devices, ring_close(): return own + direct + lax.ppermute(one + relayed, 'tm', FORTH)  9.89 us
    ppermute x8, starting transfers between devices, ring_ends(): return (lax.ppermute(two, 'tm', FORTH), lax.ppermute(back, 'tm', BACK))  9.01 us
    ppermute x2, waiting for transfers between devices, local(): below, above = (lax.ppermute(high, 'gz', UP), lax.ppermute(low, 'gz', DOWN))  7.02 us
    ppermute x1, waiting for transfers between devices, local(): high = high[:4] + lax.ppermute(high[4:], 'tm', ACROSS)  6.79 us
  transfers between devices with their start and end apart: 24, of which 12 were waited for; matrix products, arithmetic and copies ran while one was open for 9% of the time, Pallas kernels for 0%

profile of v4, /device:TPU:102, one launch (start us, length us, event | category | flops | bytes accessed | tf_op | source)
XLA Modules:
  0.0 128.9 jit_solution(9087434739610677670)
XLA Ops:
  0.6 18.1 %shard_map.77 = (f32[8,512,128]{2,1,0:T(8,128)}, f32[8,512,128]{2,1,0:T(8,128)}, f32[8,512,128]{2,1,0:T(8,128)}, f32[8,512,128]{2,1,0:T(8,128)}, f32[8,544,128]{...) custom-call(f32[1,4]{1,0:T(1,128)} %coeffs.1, f32[8192,128]{1,0:T(8,128)} %bitcast.96, ...), custom_call_target="tpu_custom_call" | custom-call | bytes 47185920 | tf_op jit(solution)/shard_map/pallas_call | solution.py:334
  18.8 0.1 collective-permute-start.1
  18.9 0.5 collective-permute-start
  19.3 4.0 %collective-permute-done.1 = f32[8,544,128]{2,1,0:T(8,128)S(1)} collective-permute-done((f32[8,544,128]{2,1,0:T(8,128)}, f32[8,544,128]{2,1,0:T(8,128)S(1)}, u32[]{:S(2)}, u32[]{:S(2)}) %collective-permute-start.1) | collective-permute-done | bytes 2228256 | tf_op jit(solution)/shard_map/ppermute | solution.py:384
  23.4 2.1 %add.72 = f32[8,544,128]{2,1,0:T(8,128)S(1)} add(f32[8,544,128]{2,1,0:T(8,128)} %get-tuple-element.21, f32[8,544,128]{2,1,0:T(8,128)S(1)} %collective-permute-done.1) | non-fusion elementwise | flops 557056 | bytes 6684672 | tf_op jit(solution)/shard_map/add | solution.py:384
  25.5 1.0 collective-permute-done
  26.6 0.2 add.71
  26.8 0.1 copy-done
  26.9 1.1 slice.99
  28.0 0.4 collective-permute-start.16
  28.4 0.5 collective-permute-start.2
  28.9 1.1 fusion.9
  30.0 1.6 %collective-permute-start.13 = (f32[2,544,128]{2,1,0:T(8,128)}, f32[2,544,128]{2,1,0:T(8,128)}, u32[]{:S(2)}, u32[]{:S(2)}) collective-permute-start(f32[2,544,128]{2,1,0:T(8,128)} %get-tuple-element.33), channel_id=1, source_target_pairs={{0,16},{8,56},{16,32},{24,8},{32,48},{40,24},{48,0},{56,40},{64,80... | collective-permute-start | bytes 1671176 | tf_op jit(solution)/shard_map/ppermute | solution.py:388
  31.6 1.1 constant_dynamic-slice_fusion
  32.7 1.7 %collective-permute-start.12 = (f32[2,544,128]{2,1,0:T(8,128)}, f32[2,544,128]{2,1,0:T(8,128)S(1)}, u32[]{:S(2)}, u32[]{:S(2)}) collective-permute-start(f32[2,544,128]{2,1,0:T(8,128)} %get-tuple-element.32), channel_id=1, source_target_pairs={{0,48},{8,24},{16,0},{24,40},{32,16},{40,56},{48,32},{56,8},{64,11... | collective-permute-start | bytes 1671176 | tf_op jit(solution)/shard_map/ppermute | solution.py:388
  34.4 9.5 %collective-permute-done.13 = f32[2,544,128]{2,1,0:T(8,128)} collective-permute-done((f32[2,544,128]{2,1,0:T(8,128)}, f32[2,544,128]{2,1,0:T(8,128)}, u32[]{:S(2)}, u32[]{:S(2)}) %collective-permute-start.13) | collective-permute-done | bytes 557088 | tf_op jit(solution)/shard_map/ppermute | solution.py:388
  43.9 1.1 slice_add_fusion.2
  45.1 2.2 %collective-permute-start.14 = (f32[2,544,128]{2,1,0:T(8,128)S(1)}, f32[2,544,128]{2,1,0:T(8,128)S(1)}, u32[]{:S(2)}, u32[]{:S(2)}) collective-permute-start(f32[2,544,128]{2,1,0:T(8,128)S(1)} %slice_add_fusion.2), channel_id=1, source_target_pairs={{0,16},{8,56},{16,32},{24,8},{32,48},{40,24},{48,0},{56,40},{64,80... | collective-permute-start | bytes 1671176 | tf_op jit(solution)/shard_map/ppermute | solution.py:392
  47.3 0.7 dynamic-slice_select_fusion.1
  48.0 6.8 %collective-permute-done.16 = f32[4,544,128]{2,1,0:T(8,128)S(1)} collective-permute-done((f32[4,544,128]{2,1,0:T(8,128)}, f32[4,544,128]{2,1,0:T(8,128)S(1)}, u32[]{:S(2)}, u32[]{:S(2)}) %collective-permute-start.16) | collective-permute-done | bytes 1114144 | tf_op jit(solution)/shard_map/ppermute | solution.py:418
  54.8 0.2 slice_add_fusion
  55.1 1.6 %collective-permute-start.18 = (f32[544,128]{1,0:T(8,128)S(1)}, f32[544,128]{1,0:T(8,128)S(1)}, u32[]{:S(2)}, u32[]{:S(2)}) collective-permute-start(f32[544,128]{1,0:T(8,128)S(1)} %get-tuple-element.37), channel_id=1, source_target_pairs={{0,16},{8,56},{16,32},{24,8},{32,48},{40,24},{48,0},{56,40},{64,80... | collective-permute-start | bytes 835592 | tf_op jit(solution)/shard_map/ppermute | solution.py:388
  56.7 0.3 collective-permute-done.14
  57.1 0.1 add_add_fusion
  57.2 1.4 %collective-permute-start.15 = (f32[544,128]{1,0:T(8,128)S(1)}, f32[544,128]{1,0:T(8,128)S(1)}, u32[]{:S(2)}, u32[]{:S(2)}) collective-permute-start(f32[544,128]{1,0:T(8,128)S(1)} %slice_bitcast_fusion.4), channel_id=1, source_target_pairs={{0,64},{8,72},{16,80},{24,88},{32,96},{40,104},{48,112},{56,120},{... | collective-permute-start | bytes 835592 | tf_op jit(solution)/shard_map/ppermute | solution.py:422
  58.6 1.9 %add.78 = f32[8,512,128]{2,1,0:T(8,128)S(1)} add(f32[8,512,128]{2,1,0:T(8,128)S(1)} %copy-done.4, f32[8,512,128]{2,1,0:T(8,128)} %collective-permute-done.7) | non-fusion elementwise | flops 524288 | bytes 6291456 | tf_op jit(solution)/shard_map/add | solution.py:384
  60.6 0.8 collective-permute-start.8
  61.3 0.7 copy-done.3
  62.1 1.9 %add.73 = f32[8,512,128]{2,1,0:T(8,128)S(1)} add(f32[8,512,128]{2,1,0:T(8,128)S(1)} %copy-done.3, f32[8,512,128]{2,1,0:T(8,128)} %collective-permute-done.2) | non-fusion elementwise | flops 524288 | bytes 6291456 | tf_op jit(solution)/shard_map/add | solution.py:384
  64.0 0.6 collective-permute-start.4
  64.6 1.3 %collective-permute-start.22 = (f32[544,128]{1,0:T(8,128)S(1)}, f32[544,128]{1,0:T(8,128)S(1)}, u32[]{:S(2)}, u32[]{:S(2)}) collective-permute-start(f32[544,128]{1,0:T(8,128)S(1)} %pad_maximum_fusion), channel_id=1, source_target_pairs={{0,1},{1,2},{2,3},{3,4},{4,5},{5,6},{6,7},{8,9},{9,10},{10,11},{11... | collective-permute-start | bytes 835592 | tf_op jit(solution)/shard_map/ppermute | solution.py:414
  66.0 2.8 %collective-permute-start.17 = (f32[544,128]{1,0:T(8,128)S(1)}, f32[544,128]{1,0:T(8,128)S(1)}, u32[]{:S(2)}, u32[]{:S(2)}) collective-permute-start(f32[544,128]{1,0:T(8,128)S(1)} %get-tuple-element.36), channel_id=1, source_target_pairs={{0,48},{8,24},{16,0},{24,40},{32,16},{40,56},{48,32},{56,8},{64,11... | collective-permute-start | bytes 835592 | tf_op jit(solution)/shard_map/ppermute | solution.py:388
  68.9 9.4 %collective-permute-done.4 = f32[2,512,128]{2,1,0:T(8,128)S(1)} collective-permute-done((f32[2,512,128]{2,1,0:T(8,128)S(1)}, f32[2,512,128]{2,1,0:T(8,128)S(1)}, u32[]{:S(2)}, u32[]{:S(2)}) %collective-permute-start.4) | collective-permute-done | bytes 524320 | tf_op jit(solution)/shard_map/ppermute | solution.py:388
  78.3 10.1 %collective-permute-done.8 = f32[4,512,128]{2,1,0:T(8,128)S(1)} collective-permute-done((f32[4,512,128]{2,1,0:T(8,128)S(1)}, f32[4,512,128]{2,1,0:T(8,128)S(1)}, u32[]{:S(2)}, u32[]{:S(2)}) %collective-permute-start.8) | collective-permute-done | bytes 1048608 | tf_op jit(solution)/shard_map/ppermute | solution.py:419
  88.4 0.1 slice_add_fusion.1
  88.6 0.7 collective-permute-start.10
  89.2 9.5 %collective-permute-done.5 = f32[2,512,128]{2,1,0:T(8,128)S(1)} collective-permute-done((f32[2,512,128]{2,1,0:T(8,128)S(1)}, f32[2,512,128]{2,1,0:T(8,128)S(1)}, u32[]{:S(2)}, u32[]{:S(2)}) %collective-permute-start.5) | collective-permute-done | bytes 524320 | tf_op jit(solution)/shard_map/ppermute | solution.py:392
  98.8 0.1 fusion
  98.9 0.6 collective-permute-start.6
  99.5 2.1 %collective-permute-done.10 = f32[512,128]{1,0:T(8,128)S(1)} collective-permute-done((f32[512,128]{1,0:T(8,128)S(1)}, f32[512,128]{1,0:T(8,128)S(1)}, u32[]{:S(2)}, u32[]{:S(2)}) %collective-permute-start.10) | collective-permute-done | bytes 262176 | tf_op jit(solution)/shard_map/ppermute | solution.py:388
  101.6 2.7 %collective-permute-start.23 = (f32[544,128]{1,0:T(8,128)S(1)}, f32[544,128]{1,0:T(8,128)S(1)}, u32[]{:S(2)}, u32[]{:S(2)}) collective-permute-start(f32[544,128]{1,0:T(8,128)S(1)} %pad_maximum_fusion), channel_id=1, source_target_pairs={{1,0},{2,1},{3,2},{4,3},{5,4},{6,5},{7,6},{9,8},{10,9},{11,10},{12... | collective-permute-start | bytes 835592 | tf_op jit(solution)/shard_map/ppermute | solution.py:414
  104.4 2.1 %collective-permute-start.11 = (f32[512,128]{1,0:T(8,128)S(1)}, f32[512,128]{1,0:T(8,128)S(1)}, u32[]{:S(2)}, u32[]{:S(2)}) collective-permute-start(f32[512,128]{1,0:T(8,128)S(1)} %fusion.5), channel_id=1, source_target_pairs={{0,16},{8,56},{16,32},{24,8},{32,48},{40,24},{48,0},{56,40},{64,80... | collective-permute-start | bytes 786440 | tf_op jit(solution)/shard_map/ppermute | solution.py:392
  106.6 10.7 %collective-permute-done.6 = f32[512,128]{1,0:T(8,128)S(1)} collective-permute-done((f32[512,128]{1,0:T(8,128)S(1)}, f32[512,128]{1,0:T(8,128)S(1)}, u32[]{:S(2)}, u32[]{:S(2)}) %collective-permute-start.6) | collective-permute-done | bytes 262176 | tf_op jit(solution)/shard_map/ppermute | solution.py:426
  117.3 1.3 %collective-permute-start.21 = (f32[544,128]{1,0:T(8,128)S(1)}, f32[544,128]{1,0:T(8,128)S(1)}, u32[]{:S(2)}, u32[]{:S(2)}) collective-permute-start(f32[544,128]{1,0:T(8,128)S(1)} %fusion.4), channel_id=1, source_target_pairs={{1,0},{2,1},{3,2},{4,3},{5,4},{6,5},{7,6},{9,8},{10,9},{11,10},{12... | collective-permute-start | bytes 835592 | tf_op jit(solution)/shard_map/ppermute | solution.py:423
  118.6 1.3 %collective-permute-start.20 = (f32[544,128]{1,0:T(8,128)S(1)}, f32[544,128]{1,0:T(8,128)S(1)}, u32[]{:S(2)}, u32[]{:S(2)}) collective-permute-start(f32[544,128]{1,0:T(8,128)S(1)} %fusion.3), channel_id=1, source_target_pairs={{0,1},{1,2},{2,3},{3,4},{4,5},{5,6},{6,7},{8,9},{9,10},{10,11},{11... | collective-permute-start | bytes 835592 | tf_op jit(solution)/shard_map/ppermute | solution.py:423
  120.0 2.6 %collective-permute-done.21 = f32[544,128]{1,0:T(8,128)S(1)} collective-permute-done((f32[544,128]{1,0:T(8,128)S(1)}, f32[544,128]{1,0:T(8,128)S(1)}, u32[]{:S(2)}, u32[]{:S(2)}) %collective-permute-start.21) | collective-permute-done | bytes 278560 | tf_op jit(solution)/shard_map/ppermute | solution.py:423
  122.6 4.4 %collective-permute-done.20 = f32[544,128]{1,0:T(8,128)S(1)} collective-permute-done((f32[544,128]{1,0:T(8,128)S(1)}, f32[544,128]{1,0:T(8,128)S(1)}, u32[]{:S(2)}, u32[]{:S(2)}) %collective-permute-start.20) | collective-permute-done | bytes 278560 | tf_op jit(solution)/shard_map/ppermute | solution.py:423
  127.1 1.8 %shard_map.78 = (f32[32,2,8,128]{3,2,1,0:T(8,128)}, f32[32,2,8,128]{3,2,1,0:T(8,128)}) custom-call(f32[32,2,8,128]{3,2,1,0:T(8,128)S(1)} %bitcast.87, f32[32,2,8,128]{3,2,1,0:T(8,128)S(1)} %bitcast.88, f32[34,2,8,128]{3,2,1,0:T(8,128)S(1)} %bitcast.85, f32[34,2,8,128]{3,2,1,0:T(8,128)S(1)} %bitcast.86, f32[34,2,8,128]{3,2,1,0:T(8,128)S(1)} %bitcast.92, ...), custom_call_target="tpu_custom_call" | custom-call | bytes 4194304 | tf_op jit(solution)/shard_map/pallas_call | solution.py:354
  (39 shorter events, 0.7 us)
Async XLA Ops:
  18.8 4.6 %collective-permute-start.1 = (f32[8,544,128]{2,1,0:T(8,128)}, f32[8,544,128]{2,1,0:T(8,128)S(1)}, u32[]{:S(2)}, u32[]{:S(2)}) collective-permute-start(f32[8,544,128]{2,1,0:T(8,128)} %get-tuple-element.22), channel_id=1, source_target_pairs={{0,8},{8,0},{16,24},{24,16},{32,40},{40,32},{48,56},{56,48},{64,72... | collective-permute-start | bytes 6684680 | tf_op jit(solution)/shard_map/ppermute | solution.py:384
  18.9 7.7 %collective-permute-start = (f32[8,544,128]{2,1,0:T(8,128)}, f32[8,544,128]{2,1,0:T(8,128)S(1)}, u32[]{:S(2)}, u32[]{:S(2)}) collective-permute-start(f32[8,544,128]{2,1,0:T(8,128)} %get-tuple-element.20), channel_id=1, source_target_pairs={{0,8},{8,0},{16,24},{24,16},{32,40},{40,32},{48,56},{56,48},{64,72... | collective-permute-start | bytes 6684680 | tf_op jit(solution)/shard_map/ppermute | solution.py:384
  23.4 3.2 %copy-start.2 = (f32[8,544,128]{2,1,0:T(8,128)S(1)}, f32[8,544,128]{2,1,0:T(8,128)}, u32[]{:S(2)}) copy-start(f32[8,544,128]{2,1,0:T(8,128)} %get-tuple-element.19) | copy-start | bytes 6684676
  25.5 1.4 %copy-start = (f32[8,544,128]{2,1,0:T(8,128)}, f32[8,544,128]{2,1,0:T(8,128)S(1)}, u32[]{:S(2)}) copy-start(f32[8,544,128]{2,1,0:T(8,128)S(1)} %add.72) | copy-start | bytes 6684676
  28.0 26.8 %collective-permute-start.16 = (f32[4,544,128]{2,1,0:T(8,128)}, f32[4,544,128]{2,1,0:T(8,128)S(1)}, u32[]{:S(2)}, u32[]{:S(2)}) collective-permute-start(f32[4,544,128]{2,1,0:T(8,128)} %slice.99), channel_id=1, source_target_pairs={{0,64},{8,72},{16,80},{24,88},{32,96},{40,104},{48,112},{56,120},{... | collective-permute-start | bytes 3342344 | tf_op jit(solution)/shard_map/ppermute | solution.py:418
  28.4 30.2 %collective-permute-start.7 = (f32[8,512,128]{2,1,0:T(8,128)}, f32[8,512,128]{2,1,0:T(8,128)}, u32[]{:S(2)}, u32[]{:S(2)}) collective-permute-start(f32[8,512,128]{2,1,0:T(8,128)} %get-tuple-element.25), channel_id=1, source_target_pairs={{0,8},{8,0},{16,24},{24,16},{32,40},{40,32},{48,56},{56,48},{64,72... | collective-permute-start | bytes 6291464 | tf_op jit(solution)/shard_map/ppermute | solution.py:384
  28.4 32.9 %collective-permute-start.2 = (f32[8,512,128]{2,1,0:T(8,128)}, f32[8,512,128]{2,1,0:T(8,128)}, u32[]{:S(2)}, u32[]{:S(2)}) collective-permute-start(f32[8,512,128]{2,1,0:T(8,128)} %get-tuple-element.23), channel_id=1, source_target_pairs={{0,8},{8,0},{16,24},{24,16},{32,40},{40,32},{48,56},{56,48},{64,72... | collective-permute-start | bytes 6291464 | tf_op jit(solution)/shard_map/ppermute | solution.py:384
  30.0 13.9 %collective-permute-start.13 = (f32[2,544,128]{2,1,0:T(8,128)}, f32[2,544,128]{2,1,0:T(8,128)}, u32[]{:S(2)}, u32[]{:S(2)}) collective-permute-start(f32[2,544,128]{2,1,0:T(8,128)} %get-tuple-element.33), channel_id=1, source_target_pairs={{0,16},{8,56},{16,32},{24,8},{32,48},{40,24},{48,0},{56,40},{64,80... | collective-permute-start | bytes 1671176 | tf_op jit(solution)/shard_map/ppermute | solution.py:388
  31.6 23.2 %copy-start.1 = (f32[8,544,128]{2,1,0:T(8,128)S(1)}, f32[8,544,128]{2,1,0:T(8,128)}, u32[]{:S(2)}) copy-start(f32[8,544,128]{2,1,0:T(8,128)} %copy-done) | copy-start | bytes 6684676
  32.7 24.0 %collective-permute-start.12 = (f32[2,544,128]{2,1,0:T(8,128)}, f32[2,544,128]{2,1,0:T(8,128)S(1)}, u32[]{:S(2)}, u32[]{:S(2)}) collective-permute-start(f32[2,544,128]{2,1,0:T(8,128)} %get-tuple-element.32), channel_id=1, source_target_pairs={{0,48},{8,24},{16,0},{24,40},{32,16},{40,56},{48,32},{56,8},{64,11... | collective-permute-start | bytes 1671176 | tf_op jit(solution)/shard_map/ppermute | solution.py:388
  45.1 12.0 %collective-permute-start.14 = (f32[2,544,128]{2,1,0:T(8,128)S(1)}, f32[2,544,128]{2,1,0:T(8,128)S(1)}, u32[]{:S(2)}, u32[]{:S(2)}) collective-permute-start(f32[2,544,128]{2,1,0:T(8,128)S(1)} %slice_add_fusion.2), channel_id=1, source_target_pairs={{0,16},{8,56},{16,32},{24,8},{32,48},{40,24},{48,0},{56,40},{64,80... | collective-permute-start | bytes 1671176 | tf_op jit(solution)/shard_map/ppermute | solution.py:392
  55.0 3.6 %copy-start.4 = (f32[8,512,128]{2,1,0:T(8,128)S(1)}, f32[8,512,128]{2,1,0:T(8,128)}, u32[]{:S(2)}) copy-start(f32[8,512,128]{2,1,0:T(8,128)} %get-tuple-element.24) | copy-start | bytes 6291460
  55.1 10.9 %collective-permute-start.18 = (f32[544,128]{1,0:T(8,128)S(1)}, f32[544,128]{1,0:T(8,128)S(1)}, u32[]{:S(2)}, u32[]{:S(2)}) collective-permute-start(f32[544,128]{1,0:T(8,128)S(1)} %get-tuple-element.37), channel_id=1, source_target_pairs={{0,16},{8,56},{16,32},{24,8},{32,48},{40,24},{48,0},{56,40},{64,80... | collective-permute-start | bytes 835592 | tf_op jit(solution)/shard_map/ppermute | solution.py:388
  57.2 11.6 %collective-permute-start.15 = (f32[544,128]{1,0:T(8,128)S(1)}, f32[544,128]{1,0:T(8,128)S(1)}, u32[]{:S(2)}, u32[]{:S(2)}) collective-permute-start(f32[544,128]{1,0:T(8,128)S(1)} %slice_bitcast_fusion.4), channel_id=1, source_target_pairs={{0,64},{8,72},{16,80},{24,88},{32,96},{40,104},{48,112},{56,120},{... | collective-permute-start | bytes 835592 | tf_op jit(solution)/shard_map/ppermute | solution.py:422
  60.5 1.6 %copy-start.3 = (f32[8,512,128]{2,1,0:T(8,128)S(1)}, f32[8,512,128]{2,1,0:T(8,128)}, u32[]{:S(2)}) copy-start(f32[8,512,128]{2,1,0:T(8,128)} %get-tuple-element.16) | copy-start | bytes 6291460
  60.6 27.8 %collective-permute-start.8 = (f32[4,512,128]{2,1,0:T(8,128)S(1)}, f32[4,512,128]{2,1,0:T(8,128)S(1)}, u32[]{:S(2)}, u32[]{:S(2)}) collective-permute-start(f32[4,512,128]{2,1,0:T(8,128)S(1)} %slice.111), channel_id=1, source_target_pairs={{0,64},{8,72},{16,80},{24,88},{32,96},{40,104},{48,112},{56,120},{... | collective-permute-start | bytes 3145736 | tf_op jit(solution)/shard_map/ppermute | solution.py:419
  64.0 14.2 %collective-permute-start.4 = (f32[2,512,128]{2,1,0:T(8,128)S(1)}, f32[2,512,128]{2,1,0:T(8,128)S(1)}, u32[]{:S(2)}, u32[]{:S(2)}) collective-permute-start(f32[2,512,128]{2,1,0:T(8,128)S(1)} %get-tuple-element.35), channel_id=1, source_target_pairs={{0,16},{8,56},{16,32},{24,8},{32,48},{40,24},{48,0},{56,40},{64,80... | collective-permute-start | bytes 1572872 | tf_op jit(solution)/shard_map/ppermute | solution.py:388
  64.6 55.4 %collective-permute-start.22 = (f32[544,128]{1,0:T(8,128)S(1)}, f32[544,128]{1,0:T(8,128)S(1)}, u32[]{:S(2)}, u32[]{:S(2)}) collective-permute-start(f32[544,128]{1,0:T(8,128)S(1)} %pad_maximum_fusion), channel_id=1, source_target_pairs={{0,1},{1,2},{2,3},{3,4},{4,5},{5,6},{6,7},{8,9},{9,10},{10,11},{11... | collective-permute-start | bytes 835592 | tf_op jit(solution)/shard_map/ppermute | solution.py:414
  66.0 35.7 %collective-permute-start.17 = (f32[544,128]{1,0:T(8,128)S(1)}, f32[544,128]{1,0:T(8,128)S(1)}, u32[]{:S(2)}, u32[]{:S(2)}) collective-permute-start(f32[544,128]{1,0:T(8,128)S(1)} %get-tuple-element.36), channel_id=1, source_target_pairs={{0,48},{8,24},{16,0},{24,40},{32,16},{40,56},{48,32},{56,8},{64,11... | collective-permute-start | bytes 835592 | tf_op jit(solution)/shard_map/ppermute | solution.py:388
  68.8 35.6 %collective-permute-start.19 = (f32[544,128]{1,0:T(8,128)S(1)}, f32[544,128]{1,0:T(8,128)S(1)}, u32[]{:S(2)}, u32[]{:S(2)}) collective-permute-start(f32[544,128]{1,0:T(8,128)S(1)} %fusion.1), channel_id=1, source_target_pairs={{0,16},{8,56},{16,32},{24,8},{32,48},{40,24},{48,0},{56,40},{64,80... | collective-permute-start | bytes 835592 | tf_op jit(solution)/shard_map/ppermute | solution.py:392
  78.3 10.3 %collective-permute-start.3 = (f32[2,512,128]{2,1,0:T(8,128)S(1)}, f32[2,512,128]{2,1,0:T(8,128)S(1)}, u32[]{:S(2)}, u32[]{:S(2)}) collective-permute-start(f32[2,512,128]{2,1,0:T(8,128)S(1)} %get-tuple-element.34), channel_id=1, source_target_pairs={{0,48},{8,24},{16,0},{24,40},{32,16},{40,56},{48,32},{56,8},{64,11... | collective-permute-start | bytes 1572872 | tf_op jit(solution)/shard_map/ppermute | solution.py:388
  88.4 10.4 %collective-permute-start.5 = (f32[2,512,128]{2,1,0:T(8,128)S(1)}, f32[2,512,128]{2,1,0:T(8,128)S(1)}, u32[]{:S(2)}, u32[]{:S(2)}) collective-permute-start(f32[2,512,128]{2,1,0:T(8,128)S(1)} %slice_add_fusion.3), channel_id=1, source_target_pairs={{0,16},{8,56},{16,32},{24,8},{32,48},{40,24},{48,0},{56,40},{64,80... | collective-permute-start | bytes 1572872 | tf_op jit(solution)/shard_map/ppermute | solution.py:392
  88.6 13.0 %collective-permute-start.10 = (f32[512,128]{1,0:T(8,128)S(1)}, f32[512,128]{1,0:T(8,128)S(1)}, u32[]{:S(2)}, u32[]{:S(2)}) collective-permute-start(f32[512,128]{1,0:T(8,128)S(1)} %get-tuple-element.39), channel_id=1, source_target_pairs={{0,16},{8,56},{16,32},{24,8},{32,48},{40,24},{48,0},{56,40},{64,80... | collective-permute-start | bytes 786440 | tf_op jit(solution)/shard_map/ppermute | solution.py:388
  98.9 18.4 %collective-permute-start.6 = (f32[512,128]{1,0:T(8,128)S(1)}, f32[512,128]{1,0:T(8,128)S(1)}, u32[]{:S(2)}, u32[]{:S(2)}) collective-permute-start(f32[512,128]{1,0:T(8,128)S(1)} %slice_bitcast_fusion.10), channel_id=1, source_target_pairs={{0,64},{8,72},{16,80},{24,88},{32,96},{40,104},{48,112},{56,120},{... | collective-permute-start | bytes 786440 | tf_op jit(solution)/shard_map/ppermute | solution.py:426
  101.6 17.0 %collective-permute-start.9 = (f32[512,128]{1,0:T(8,128)S(1)}, f32[512,128]{1,0:T(8,128)S(1)}, u32[]{:S(2)}, u32[]{:S(2)}) collective-permute-start(f32[512,128]{1,0:T(8,128)S(1)} %get-tuple-element.38), channel_id=1, source_target_pairs={{0,48},{8,24},{16,0},{24,40},{32,16},{40,56},{48,32},{56,8},{64,11... | collective-permute-start | bytes 786440 | tf_op jit(solution)/shard_map/ppermute | solution.py:388
  101.6 18.4 %collective-permute-start.23 = (f32[544,128]{1,0:T(8,128)S(1)}, f32[544,128]{1,0:T(8,128)S(1)}, u32[]{:S(2)}, u32[]{:S(2)}) collective-permute-start(f32[544,128]{1,0:T(8,128)S(1)} %pad_maximum_fusion), channel_id=1, source_target_pairs={{1,0},{2,1},{3,2},{4,3},{5,4},{6,5},{7,6},{9,8},{10,9},{11,10},{12... | collective-permute-start | bytes 835592 | tf_op jit(solution)/shard_map/ppermute | solution.py:414
  104.4 15.5 %collective-permute-start.11 = (f32[512,128]{1,0:T(8,128)S(1)}, f32[512,128]{1,0:T(8,128)S(1)}, u32[]{:S(2)}, u32[]{:S(2)}) collective-permute-start(f32[512,128]{1,0:T(8,128)S(1)} %fusion.5), channel_id=1, source_target_pairs={{0,16},{8,56},{16,32},{24,8},{32,48},{40,24},{48,0},{56,40},{64,80... | collective-permute-start | bytes 786440 | tf_op jit(solution)/shard_map/ppermute | solution.py:392
  117.3 5.3 %collective-permute-start.21 = (f32[544,128]{1,0:T(8,128)S(1)}, f32[544,128]{1,0:T(8,128)S(1)}, u32[]{:S(2)}, u32[]{:S(2)}) collective-permute-start(f32[544,128]{1,0:T(8,128)S(1)} %fusion.4), channel_id=1, source_target_pairs={{1,0},{2,1},{3,2},{4,3},{5,4},{6,5},{7,6},{9,8},{10,9},{11,10},{12... | collective-permute-start | bytes 835592 | tf_op jit(solution)/shard_map/ppermute | solution.py:423
  118.6 8.4 %collective-permute-start.20 = (f32[544,128]{1,0:T(8,128)S(1)}, f32[544,128]{1,0:T(8,128)S(1)}, u32[]{:S(2)}, u32[]{:S(2)}) collective-permute-start(f32[544,128]{1,0:T(8,128)S(1)} %fusion.3), channel_id=1, source_target_pairs={{0,1},{1,2},{2,3},{3,4},{4,5},{5,6},{6,7},{8,9},{9,10},{10,11},{11... | collective-permute-start | bytes 835592 | tf_op jit(solution)/shard_map/ppermute | solution.py:423

commit v5 on v4

--- a/solution.py
+++ b/solution.py
@@ -380,16 +380,24 @@
 DOWN = [(i + 1, i) for i in range(SLABS - 1)]
 
 
-def swap(same, other):
-    return same + lax.ppermute(other, "tm", SIBLING)
-
-
-def ring_ends(two, back):
-    return lax.ppermute(two, "tm", FORTH), lax.ppermute(back, "tm", BACK)
-
-
-def ring_close(one, own, relayed, direct):
-    return own + direct + lax.ppermute(one + relayed, "tm", FORTH)
+def to_sibling(other):
+    return lax.ppermute(other, "tm", SIBLING)
+
+
+def forth(cells):
+    return lax.ppermute(cells, "tm", FORTH)
+
+
+def back(cells):
+    return lax.ppermute(cells, "tm", BACK)
+
+
+def across(cells):
+    return lax.ppermute(cells, "tm", ACROSS)
+
+
+def after(first, then):
+    return lax.optimization_barrier((first, then))
 
 
 def local(prev_term, last_term, cos_sum, sin_sum, speed_sq, series_coeffs):
@@ -399,9 +407,19 @@
     me = lax.axis_index("tm")
 
     d_other, d_same, v_other, v_same, low_other, low_same, high_other, high_same = series(series_coeffs, u, k, p, cos, sin)
-    low, high = swap(low_same, low_other), swap(high_same, high_other)
-    d_other, v_other, low, high = lax.optimization_barrier((d_other, v_other, low, high))
-    d, v = swap(d_same, d_other), swap(v_same, v_other)
+
+    def blocks(same, came, *at):
+        return lax.slice_in_dim(same, *at) + lax.slice_in_dim(came, *at)
+
+    high_came, low_came = to_sibling(high_other), to_sibling(low_other)
+    (high_came, low_came), (d_other, v_other) = after((high_came, low_came), (d_other, v_other))
+    d_came, v_came = to_sibling(d_other), to_sibling(v_other)
+
+    high_far = across(blocks(high_same, high_came, 4, 8))
+    low_two = forth(blocks(low_same, low_came, 4, 6))
+    low_back = back(blocks(low_same, low_came, 6, 8))
+    d_two = forth(blocks(d_same, d_came, 4, 6))
+    d_back = back(blocks(d_same, d_came, 6, 8))
 
     start = me * rows * 16
     k_here = jnp.concatenate(
@@ -413,17 +431,27 @@
     )
     k_low, k_high = lax.ppermute(k_here, "gz", UP), lax.ppermute(k_here, "gz", DOWN)
 
-    low, d = (a.reshape(4, 2, *a.shape[1:]) for a in (low, d))
-    low_ends, d_ends = ring_ends(low[2], low[3]), ring_ends(d[2], d[3])
-    high = high[:4] + lax.ppermute(high[4:], "tm", ACROSS)
-    v = v[:4] + lax.ppermute(v[4:], "tm", ACROSS)
-    low = ring_close(low[1], low[0], *low_ends)
-    high = ring_close(high[1], high[0], *ring_ends(high[2], high[3]))
-    low = low[0] + lax.ppermute(low[1], "tm", ACROSS)
-    below, above = lax.ppermute(high, "gz", UP), lax.ppermute(low, "gz", DOWN)
-    d = ring_close(d[1], d[0], *d_ends)
-    v = ring_close(v[1], v[0], *ring_ends(v[2], v[3]))
-    d = d[0] + lax.ppermute(d[1], "tm", ACROSS)
+    low_rest = forth(blocks(low_same, low_came, 2, 4) + low_two)
+    v_sent = blocks(v_same, v_came, 4, 8)
+    (d_two, v_sent, k_low, k_high), high_far = after((d_two, v_sent, k_low, k_high), high_far)
+    v_far = across(v_sent)
+    d_rest = forth(blocks(d_same, d_came, 2, 4) + d_two)
+
+    high = blocks(high_same, high_came, 0, 4) + high_far
+    high_two, high_back = forth(high[2]), back(high[3])
+    low = blocks(low_same, low_came, 0, 2) + low_back + low_rest
+    low_far = across(low[1])
+    high_rest = forth(high[1] + high_two)
+    low = low[0] + low_far
+    high = high[0] + high_back + high_rest
+    above, below = lax.ppermute(low, "gz", DOWN), lax.ppermute(high, "gz", UP)
+
+    d = blocks(d_same, d_came, 0, 2) + d_back + d_rest
+    d = d[0] + across(d[1])
+    v = blocks(v_same, v_came, 0, 4) + v_far
+    v_two, v_back = forth(v[2]), back(v[3])
+    (above, below), v_two = after((above, below), v_two)
+    v = v[0] + v_back + forth(v[1] + v_two)
 
     wide = (a.reshape(rows + 2, *CELL) for a in (low, high, below, above, k_here, k_low, k_high))
     d, v = mend(d.reshape(rows, *CELL), v.reshape(rows, *CELL), *wide)

time: 129 us -> 128 us (level)
  waiting for transfers between devices: 70.6 us -> 62.7 us
  other arithmetic: 8.71 us -> 15.8 us
  local copies, waits for them, and re-layouts: 4.43 us -> 1.26 us
  starting transfers between devices: 24.3 us -> 27.2 us
    ppermute x22, waiting for transfers between devices: 70.6 us -> 61.2 us  [the longest x4 34.2 us: across(): return lax.ppermute(cells, 'tm', ACROSS)]
    add x16, other arithmetic: 7.96 us -> 15.1 us  [the longest x4 8.08 us: blocks(): return lax.slice_in_dim(same, *at) + lax.slice_in_dim(came, *at)]
    ppermute x22, starting transfers between devices: 20.2 us -> 23.2 us  [the longest x4 10.4 us: back(): return lax.ppermute(cells, 'tm', BACK)]
    slice x4 -> x0, local copies, waits for them, and re-layouts: 2.33 us -> none  [the longest x2 1.19 us: local(): low_ends, d_ends = (ring_ends(low[2], low[3]), ring_ends(d[2], d[3]))]
    ppermute x1, waiting for transfers between devices: 0.01 us -> 1.48 us  [local(): lax.ppermute(k_here, 'gz', UP)]
  transfers between devices with their start and end apart: 24 -> 24, of which waited for: 12 -> 11; matrix products, arithmetic and copies ran while one was open for 9% -> 13% of each run, Pallas kernels for 0% -> 0%
where the time goes in v5:
time: 128 us
  waiting for transfers between devices  62.7 us (49%)
  starting transfers between devices  27.2 us (21%)
  Pallas kernels  20 us (16%)
  other arithmetic  15.8 us (12%)
    ppermute x4, waiting for transfers between devices, across(): return lax.ppermute(cells, 'tm', ACROSS)  34.2 us
    ppermute x8, waiting for transfers between devices, forth(): return lax.ppermute(cells, 'tm', FORTH)  19.2 us
    pallas_call x1, Pallas kernels, series(): pl.pallas_call(series_kernel, out_shape=(share,) * 4 + (edge,) * 4, in_sp...  18.2 us
    ppermute x4, starting transfers between devices, back(): return lax.ppermute(cells, 'tm', BACK)  10.4 us
    add x4, other arithmetic, blocks(): return lax.slice_in_dim(same, *at) + lax.slice_in_dim(came, *at)  8.08 us
    ppermute x4, waiting for transfers between devices, to_sibling(): return lax.ppermute(other, 'tm', SIBLING)  7.24 us
    ppermute x8, starting transfers between devices, forth(): return lax.ppermute(cells, 'tm', FORTH)  6.1 us
    ppermute x4, starting transfers between devices, across(): return lax.ppermute(cells, 'tm', ACROSS)  3.01 us
  transfers between devices with their start and end apart: 24, of which 11 were waited for; matrix products, arithmetic and copies ran while one was open for 13% of the time, Pallas kernels for 0%

profile of v5, /device:TPU:102, one launch (start us, length us, event | category | flops | bytes accessed | tf_op | source)
XLA Modules:
  0.0 127.9 jit_solution(6056852724482726932)
XLA Ops:
  0.6 18.2 %shard_map.77 = (f32[8,512,128]{2,1,0:T(8,128)}, f32[8,512,128]{2,1,0:T(8,128)}, f32[8,512,128]{2,1,0:T(8,128)}, f32[8,512,128]{2,1,0:T(8,128)}, f32[8,544,128]{...) custom-call(f32[1,4]{1,0:T(1,128)} %coeffs.1, f32[8192,128]{1,0:T(8,128)} %bitcast.96, ...), custom_call_target="tpu_custom_call" | custom-call | bytes 47185920 | tf_op jit(solution)/shard_map/pallas_call | solution.py:334
  18.8 0.1 collective-permute-start
  18.9 0.5 collective-permute-start.1
  19.4 4.0 %collective-permute-done = f32[8,544,128]{2,1,0:T(8,128)S(1)} collective-permute-done((f32[8,544,128]{2,1,0:T(8,128)}, f32[8,544,128]{2,1,0:T(8,128)S(1)}, u32[]{:S(2)}, u32[]{:S(2)}) %collective-permute-start) | collective-permute-done | bytes 2228256 | tf_op jit(solution)/shard_map/ppermute | solution.py:384
  23.4 3.2 %collective-permute-done.1 = f32[8,544,128]{2,1,0:T(8,128)S(1)} collective-permute-done((f32[8,544,128]{2,1,0:T(8,128)}, f32[8,544,128]{2,1,0:T(8,128)S(1)}, u32[]{:S(2)}, u32[]{:S(2)}) %collective-permute-start.1) | collective-permute-done | bytes 2228256 | tf_op jit(solution)/shard_map/ppermute | solution.py:384
  26.6 0.1 collective-permute-start.2
  26.8 0.4 collective-permute-start.5
  27.1 2.5 %slice_add_fusion.4 = (f32[2,544,128]{2,1,0:T(8,128)}, f32[2,544,128]{2,1,0:T(8,128)}) fusion(f32[8,544,128]{2,1,0:T(8,128)S(1)} %collective-permute-done.1, f32[8,544,128]{2,1,0:T(8,128)} %get-tuple-element.36), kind=kLoop, calls=%fused_computation.8 | loop fusion | flops 278528 | bytes 3342336 | tf_op jit(solution)/shard_map/add | solution.py:412
  29.6 1.6 %collective-permute-start.14 = (f32[2,544,128]{2,1,0:T(8,128)}, f32[2,544,128]{2,1,0:T(8,128)}, u32[]{:S(2)}, u32[]{:S(2)}) collective-permute-start(f32[2,544,128]{2,1,0:T(8,128)} %get-tuple-element.47), channel_id=1, source_target_pairs={{0,16},{8,56},{16,32},{24,8},{32,48},{40,24},{48,0},{56,40},{64,80... | collective-permute-start | bytes 1671176 | tf_op jit(solution)/shard_map/ppermute | solution.py:388
  31.2 2.4 %slice_add_fusion = f32[4,544,128]{2,1,0:T(8,128)} fusion(f32[8,544,128]{2,1,0:T(8,128)} %copy-done.3, f32[8,544,128]{2,1,0:T(8,128)S(1)} %copy-done.1), kind=kLoop, calls=%fused_computation.1 | loop fusion | flops 278528 | bytes 3342336 | tf_op jit(solution)/shard_map/add | solution.py:412
  33.6 0.4 collective-permute-start.8
  34.0 0.7 dynamic-slice_select_fusion.1
  34.8 1.1 constant_dynamic-slice_fusion
  35.9 2.7 %collective-permute-start.7 = (f32[544,128]{1,0:T(8,128)S(1)}, f32[544,128]{1,0:T(8,128)S(1)}, u32[]{:S(2)}, u32[]{:S(2)}) collective-permute-start(f32[544,128]{1,0:T(8,128)S(1)} %pad_maximum_fusion), channel_id=1, source_target_pairs={{1,0},{2,1},{3,2},{4,3},{5,4},{6,5},{7,6},{9,8},{10,9},{11,10},{12... | collective-permute-start | bytes 835592 | tf_op jit(solution)/shard_map/ppermute | solution.py:432
  38.7 1.3 %collective-permute-start.6 = (f32[544,128]{1,0:T(8,128)S(1)}, f32[544,128]{1,0:T(8,128)S(1)}, u32[]{:S(2)}, u32[]{:S(2)}) collective-permute-start(f32[544,128]{1,0:T(8,128)S(1)} %pad_maximum_fusion), channel_id=1, source_target_pairs={{0,1},{1,2},{2,3},{3,4},{4,5},{5,6},{6,7},{8,9},{9,10},{10,11},{11... | collective-permute-start | bytes 835592 | tf_op jit(solution)/shard_map/ppermute | solution.py:432
  40.0 1.8 %slice_add_fusion.7 = (f32[2,512,128]{2,1,0:T(8,128)S(1)}, f32[2,512,128]{2,1,0:T(8,128)S(1)}) fusion(f32[8,512,128]{2,1,0:T(8,128)} %collective-permute-done.2, f32[8,512,128]{2,1,0:T(8,128)} %get-tuple-element.24), kind=kLoop, calls=%fused_computation.12 | loop fusion | flops 262144 | bytes 3145728 | tf_op jit(solution)/shard_map/add | solution.py:412
  41.8 1.6 %collective-permute-start.4 = (f32[2,512,128]{2,1,0:T(8,128)S(1)}, f32[2,512,128]{2,1,0:T(8,128)S(1)}, u32[]{:S(2)}, u32[]{:S(2)}) collective-permute-start(f32[2,512,128]{2,1,0:T(8,128)S(1)} %get-tuple-element.49), channel_id=1, source_target_pairs={{0,16},{8,56},{16,32},{24,8},{32,48},{40,24},{48,0},{56,40},{64,80... | collective-permute-start | bytes 1572872 | tf_op jit(solution)/shard_map/ppermute | solution.py:388
  43.4 1.3 %add_add_fusion.1 = f32[2,544,128]{2,1,0:T(8,128)S(1)} fusion(f32[2,544,128]{2,1,0:T(8,128)} %collective-permute-done.14, f32[8,544,128]{2,1,0:T(8,128)S(1)} %collective-permute-done.1, f32[8,544,128]{2,1,0:T(8,128)S(1)} %copy-done), kind=kLoop, calls=%fused_computation.6 | loop fusion | flops 278528 | bytes 2228224 | tf_op jit(solution)/shard_map/add | solution.py:434
  44.8 1.8 %collective-permute-start.13 = (f32[2,544,128]{2,1,0:T(8,128)S(1)}, f32[2,544,128]{2,1,0:T(8,128)S(1)}, u32[]{:S(2)}, u32[]{:S(2)}) collective-permute-start(f32[2,544,128]{2,1,0:T(8,128)S(1)} %copy-done.7), channel_id=1, source_target_pairs={{0,48},{8,24},{16,0},{24,40},{32,16},{40,56},{48,32},{56,8},{64,11... | collective-permute-start | bytes 1671176 | tf_op jit(solution)/shard_map/ppermute | solution.py:392
  46.5 1.4 %slice_add_fusion.2 = f32[4,512,128]{2,1,0:T(8,128)S(1)} fusion(f32[8,512,128]{2,1,0:T(8,128)} %collective-permute-done.5, f32[8,512,128]{2,1,0:T(8,128)S(1)} %copy-done.6), kind=kLoop, calls=%fused_computation.4 | loop fusion | flops 262144 | bytes 3145728 | tf_op jit(solution)/shard_map/add | solution.py:412
  47.9 0.4 collective-permute-start.15
  48.3 1.5 %collective-permute-done.6 = f32[544,128]{1,0:T(8,128)S(1)} collective-permute-done((f32[544,128]{1,0:T(8,128)S(1)}, f32[544,128]{1,0:T(8,128)S(1)}, u32[]{:S(2)}, u32[]{:S(2)}) %collective-permute-start.6) | collective-permute-done | bytes 278560 | tf_op jit(solution)/shard_map/ppermute | solution.py:432
  49.8 17.2 %collective-permute-done.8 = f32[4,544,128]{2,1,0:T(8,128)} collective-permute-done((f32[4,544,128]{2,1,0:T(8,128)}, f32[4,544,128]{2,1,0:T(8,128)}, u32[]{:S(2)}, u32[]{:S(2)}) %collective-permute-start.8) | collective-permute-done | bytes 1114144 | tf_op jit(solution)/shard_map/ppermute | solution.py:396
  67.1 1.5 %add_add_fusion = f32[4,544,128]{2,1,0:T(8,128)S(1)} fusion(f32[4,544,128]{2,1,0:T(8,128)} %collective-permute-done.8, f32[8,544,128]{2,1,0:T(8,128)S(1)} %copy-done.4, f32[8,544,128]{2,1,0:T(8,128)S(1)} %copy-done.2), kind=kLoop, calls=%fused_computation | loop fusion | flops 557056 | bytes 4456448 | tf_op jit(solution)/shard_map/add | solution.py:440
  68.6 0.1 collective-permute-start.19
  68.7 0.1 add_add_fusion.2
  68.9 0.5 collective-permute-start.16
  69.4 1.6 %collective-permute-start.11 = (f32[4,512,128]{2,1,0:T(8,128)S(1)}, f32[4,512,128]{2,1,0:T(8,128)S(1)}, u32[]{:S(2)}, u32[]{:S(2)}) collective-permute-start(f32[4,512,128]{2,1,0:T(8,128)S(1)} %slice_add_fusion.2), channel_id=1, source_target_pairs={{0,64},{8,72},{16,80},{24,88},{32,96},{40,104},{48,112},{56,120},{... | collective-permute-start | bytes 3145736 | tf_op jit(solution)/shard_map/ppermute | solution.py:396
  71.0 3.2 %collective-permute-start.18 = (f32[544,128]{1,0:T(8,128)S(1)}, f32[544,128]{1,0:T(8,128)S(1)}, u32[]{:S(2)}, u32[]{:S(2)}) collective-permute-start(f32[544,128]{1,0:T(8,128)S(1)} %get-tuple-element.52), channel_id=1, source_target_pairs={{0,48},{8,24},{16,0},{24,40},{32,16},{40,56},{48,32},{56,8},{64,11... | collective-permute-start | bytes 835592 | tf_op jit(solution)/shard_map/ppermute | solution.py:392
  74.2 3.8 %collective-permute-done.19 = f32[544,128]{1,0:T(8,128)S(1)} collective-permute-done((f32[544,128]{1,0:T(8,128)S(1)}, f32[544,128]{1,0:T(8,128)S(1)}, u32[]{:S(2)}, u32[]{:S(2)}) %collective-permute-start.19) | collective-permute-done | bytes 278560 | tf_op jit(solution)/shard_map/ppermute | solution.py:388
  78.0 0.1 collective-permute-start.20
  78.1 0.3 collective-permute-done.16
  78.4 1.3 %collective-permute-start.17 = (f32[544,128]{1,0:T(8,128)S(1)}, f32[544,128]{1,0:T(8,128)S(1)}, u32[]{:S(2)}, u32[]{:S(2)}) collective-permute-start(f32[544,128]{1,0:T(8,128)S(1)} %fusion.7), channel_id=1, source_target_pairs={{1,0},{2,1},{3,2},{4,3},{5,4},{6,5},{7,6},{9,8},{10,9},{11,10},{12... | collective-permute-start | bytes 835592 | tf_op jit(solution)/shard_map/ppermute | solution.py:447
  79.7 3.5 %collective-permute-start.3 = (f32[2,512,128]{2,1,0:T(8,128)S(1)}, f32[2,512,128]{2,1,0:T(8,128)S(1)}, u32[]{:S(2)}, u32[]{:S(2)}) collective-permute-start(f32[2,512,128]{2,1,0:T(8,128)S(1)} %get-tuple-element.48), channel_id=1, source_target_pairs={{0,48},{8,24},{16,0},{24,40},{32,16},{40,56},{48,32},{56,8},{64,11... | collective-permute-start | bytes 1572872 | tf_op jit(solution)/shard_map/ppermute | solution.py:392
  83.2 1.2 fusion.1
  84.4 1.0 collective-permute-start.9
  85.3 3.2 %collective-permute-done.20 = f32[544,128]{1,0:T(8,128)S(1)} collective-permute-done((f32[544,128]{1,0:T(8,128)S(1)}, f32[544,128]{1,0:T(8,128)S(1)}, u32[]{:S(2)}, u32[]{:S(2)}) %collective-permute-start.20) | collective-permute-done | bytes 278560 | tf_op jit(solution)/shard_map/ppermute | solution.py:388
  88.6 1.3 %collective-permute-start.21 = (f32[544,128]{1,0:T(8,128)S(1)}, f32[544,128]{1,0:T(8,128)S(1)}, u32[]{:S(2)}, u32[]{:S(2)}) collective-permute-start(f32[544,128]{1,0:T(8,128)S(1)} %fusion.6), channel_id=1, source_target_pairs={{0,1},{1,2},{2,3},{3,4},{4,5},{5,6},{6,7},{8,9},{9,10},{10,11},{11... | collective-permute-start | bytes 835592 | tf_op jit(solution)/shard_map/ppermute | solution.py:447
  89.9 16.7 %collective-permute-done.11 = f32[4,512,128]{2,1,0:T(8,128)S(1)} collective-permute-done((f32[4,512,128]{2,1,0:T(8,128)S(1)}, f32[4,512,128]{2,1,0:T(8,128)S(1)}, u32[]{:S(2)}, u32[]{:S(2)}) %collective-permute-start.11) | collective-permute-done | bytes 1048608 | tf_op jit(solution)/shard_map/ppermute | solution.py:396
  106.6 1.5 %fusion = f32[4,512,128]{2,1,0:T(8,128)S(1)} fusion(f32[4,512,128]{2,1,0:T(8,128)S(1)} %collective-permute-done.11, f32[8,512,128]{2,1,0:T(8,128)} %collective-permute-done.5, f32[8,512,128]{2,1,0:T(8,128)S(1)} %copy-done.6), kind=kLoop, calls=%fused_computation.3 | loop fusion | flops 524288 | bytes 4194304 | tf_op jit(solution)/shard_map/add | solution.py:451
  108.1 1.3 %collective-permute-start.22 = (f32[512,128]{1,0:T(8,128)S(1)}, f32[512,128]{1,0:T(8,128)S(1)}, u32[]{:S(2)}, u32[]{:S(2)}) collective-permute-start(f32[512,128]{1,0:T(8,128)S(1)} %get-tuple-element.55), channel_id=1, source_target_pairs={{0,16},{8,56},{16,32},{24,8},{32,48},{40,24},{48,0},{56,40},{64,80... | collective-permute-start | bytes 786440 | tf_op jit(solution)/shard_map/ppermute | solution.py:388
  109.4 1.2 fusion.3
  110.6 0.5 collective-permute-start.10
  111.1 2.0 %collective-permute-start.12 = (f32[512,128]{1,0:T(8,128)S(1)}, f32[512,128]{1,0:T(8,128)S(1)}, u32[]{:S(2)}, u32[]{:S(2)}) collective-permute-start(f32[512,128]{1,0:T(8,128)S(1)} %get-tuple-element.54), channel_id=1, source_target_pairs={{0,48},{8,24},{16,0},{24,40},{32,16},{40,56},{48,32},{56,8},{64,11... | collective-permute-start | bytes 786440 | tf_op jit(solution)/shard_map/ppermute | solution.py:392
  113.1 5.2 %collective-permute-done.22 = f32[512,128]{1,0:T(8,128)S(1)} collective-permute-done((f32[512,128]{1,0:T(8,128)S(1)}, f32[512,128]{1,0:T(8,128)S(1)}, u32[]{:S(2)}, u32[]{:S(2)}) %collective-permute-start.22) | collective-permute-done | bytes 262176 | tf_op jit(solution)/shard_map/ppermute | solution.py:388
  118.4 0.6 collective-permute-done.12
  119.0 6.9 %collective-permute-done.23 = f32[512,128]{1,0:T(8,128)S(1)} collective-permute-done((f32[512,128]{1,0:T(8,128)S(1)}, f32[512,128]{1,0:T(8,128)S(1)}, u32[]{:S(2)}, u32[]{:S(2)}) %collective-permute-start.23) | collective-permute-done | bytes 262176 | tf_op jit(solution)/shard_map/ppermute | solution.py:388
  126.0 1.8 %shard_map.78 = (f32[32,2,8,128]{3,2,1,0:T(8,128)}, f32[32,2,8,128]{3,2,1,0:T(8,128)}) custom-call(f32[32,2,8,128]{3,2,1,0:T(8,128)S(1)} %bitcast.87, f32[32,2,8,128]{3,2,1,0:T(8,128)S(1)} %bitcast.88, f32[34,2,8,128]{3,2,1,0:T(8,128)S(1)} %bitcast.85, f32[34,2,8,128]{3,2,1,0:T(8,128)S(1)} %bitcast.86, f32[34,2,8,128]{3,2,1,0:T(8,128)S(1)} %bitcast.92, ...), custom_call_target="tpu_custom_call" | custom-call | bytes 4194304 | tf_op jit(solution)/shard_map/pallas_call | solution.py:354
  (41 shorter events, 0.5 us)
Async XLA Ops:
  18.8 4.6 %collective-permute-start = (f32[8,544,128]{2,1,0:T(8,128)}, f32[8,544,128]{2,1,0:T(8,128)S(1)}, u32[]{:S(2)}, u32[]{:S(2)}) collective-permute-start(f32[8,544,128]{2,1,0:T(8,128)} %get-tuple-element.25), channel_id=1, source_target_pairs={{0,8},{8,0},{16,24},{24,16},{32,40},{40,32},{48,56},{56,48},{64,72... | collective-permute-start | bytes 6684680 | tf_op jit(solution)/shard_map/ppermute | solution.py:384
  18.9 7.7 %collective-permute-start.1 = (f32[8,544,128]{2,1,0:T(8,128)}, f32[8,544,128]{2,1,0:T(8,128)S(1)}, u32[]{:S(2)}, u32[]{:S(2)}) collective-permute-start(f32[8,544,128]{2,1,0:T(8,128)} %get-tuple-element.26), channel_id=1, source_target_pairs={{0,8},{8,0},{16,24},{24,16},{32,40},{40,32},{48,56},{56,48},{64,72... | collective-permute-start | bytes 6684680 | tf_op jit(solution)/shard_map/ppermute | solution.py:384
  23.4 3.2 %copy-start.3 = (f32[8,544,128]{2,1,0:T(8,128)}, f32[8,544,128]{2,1,0:T(8,128)S(1)}, u32[]{:S(2)}) copy-start(f32[8,544,128]{2,1,0:T(8,128)S(1)} %collective-permute-done) | copy-start | bytes 6684676
  26.6 12.0 %collective-permute-start.2 = (f32[8,512,128]{2,1,0:T(8,128)}, f32[8,512,128]{2,1,0:T(8,128)}, u32[]{:S(2)}, u32[]{:S(2)}) collective-permute-start(f32[8,512,128]{2,1,0:T(8,128)} %get-tuple-element.29), channel_id=1, source_target_pairs={{0,8},{8,0},{16,24},{24,16},{32,40},{40,32},{48,56},{56,48},{64,72... | collective-permute-start | bytes 6291464 | tf_op jit(solution)/shard_map/ppermute | solution.py:384
  26.8 18.0 %collective-permute-start.5 = (f32[8,512,128]{2,1,0:T(8,128)}, f32[8,512,128]{2,1,0:T(8,128)}, u32[]{:S(2)}, u32[]{:S(2)}) collective-permute-start(f32[8,512,128]{2,1,0:T(8,128)} %get-tuple-element.31), channel_id=1, source_target_pairs={{0,8},{8,0},{16,24},{24,16},{32,40},{40,32},{48,56},{56,48},{64,72... | collective-permute-start | bytes 6291464 | tf_op jit(solution)/shard_map/ppermute | solution.py:384
  27.1 4.1 %copy-start.1 = (f32[8,544,128]{2,1,0:T(8,128)S(1)}, f32[8,544,128]{2,1,0:T(8,128)}, u32[]{:S(2)}) copy-start(f32[8,544,128]{2,1,0:T(8,128)} %get-tuple-element.32) | copy-start | bytes 6684676
  29.6 12.1 %collective-permute-start.14 = (f32[2,544,128]{2,1,0:T(8,128)}, f32[2,544,128]{2,1,0:T(8,128)}, u32[]{:S(2)}, u32[]{:S(2)}) collective-permute-start(f32[2,544,128]{2,1,0:T(8,128)} %get-tuple-element.47), channel_id=1, source_target_pairs={{0,16},{8,56},{16,32},{24,8},{32,48},{40,24},{48,0},{56,40},{64,80... | collective-permute-start | bytes 1671176 | tf_op jit(solution)/shard_map/ppermute | solution.py:388
  33.6 33.4 %collective-permute-start.8 = (f32[4,544,128]{2,1,0:T(8,128)}, f32[4,544,128]{2,1,0:T(8,128)}, u32[]{:S(2)}, u32[]{:S(2)}) collective-permute-start(f32[4,544,128]{2,1,0:T(8,128)} %slice_add_fusion), channel_id=1, source_target_pairs={{0,64},{8,72},{16,80},{24,88},{32,96},{40,104},{48,112},{56,120},{... | collective-permute-start | bytes 3342344 | tf_op jit(solution)/shard_map/ppermute | solution.py:396
  34.8 8.7 %copy-start = (f32[8,544,128]{2,1,0:T(8,128)S(1)}, f32[8,544,128]{2,1,0:T(8,128)}, u32[]{:S(2)}) copy-start(f32[8,544,128]{2,1,0:T(8,128)} %get-tuple-element.36) | copy-start | bytes 6684676
  35.9 12.0 %collective-permute-start.7 = (f32[544,128]{1,0:T(8,128)S(1)}, f32[544,128]{1,0:T(8,128)S(1)}, u32[]{:S(2)}, u32[]{:S(2)}) collective-permute-start(f32[544,128]{1,0:T(8,128)S(1)} %pad_maximum_fusion), channel_id=1, source_target_pairs={{1,0},{2,1},{3,2},{4,3},{5,4},{6,5},{7,6},{9,8},{10,9},{11,10},{12... | collective-permute-start | bytes 835592 | tf_op jit(solution)/shard_map/ppermute | solution.py:432
  38.7 11.2 %collective-permute-start.6 = (f32[544,128]{1,0:T(8,128)S(1)}, f32[544,128]{1,0:T(8,128)S(1)}, u32[]{:S(2)}, u32[]{:S(2)}) collective-permute-start(f32[544,128]{1,0:T(8,128)S(1)} %pad_maximum_fusion), channel_id=1, source_target_pairs={{0,1},{1,2},{2,3},{3,4},{4,5},{5,6},{6,7},{8,9},{9,10},{10,11},{11... | collective-permute-start | bytes 835592 | tf_op jit(solution)/shard_map/ppermute | solution.py:432
  40.0 4.8 %copy-start.7 = (f32[2,544,128]{2,1,0:T(8,128)S(1)}, f32[2,544,128]{2,1,0:T(8,128)}, u32[]{:S(2)}) copy-start(f32[2,544,128]{2,1,0:T(8,128)} %get-tuple-element.46) | copy-start | bytes 1671172
  40.0 6.5 %copy-start.6 = (f32[8,512,128]{2,1,0:T(8,128)S(1)}, f32[8,512,128]{2,1,0:T(8,128)}, u32[]{:S(2)}) copy-start(f32[8,512,128]{2,1,0:T(8,128)} %get-tuple-element.30) | copy-start | bytes 6291460
  41.8 25.3 %collective-permute-start.4 = (f32[2,512,128]{2,1,0:T(8,128)S(1)}, f32[2,512,128]{2,1,0:T(8,128)S(1)}, u32[]{:S(2)}, u32[]{:S(2)}) collective-permute-start(f32[2,512,128]{2,1,0:T(8,128)S(1)} %get-tuple-element.49), channel_id=1, source_target_pairs={{0,16},{8,56},{16,32},{24,8},{32,48},{40,24},{48,0},{56,40},{64,80... | collective-permute-start | bytes 1572872 | tf_op jit(solution)/shard_map/ppermute | solution.py:388
  43.4 23.6 %copy-start.4 = (f32[8,544,128]{2,1,0:T(8,128)S(1)}, f32[8,544,128]{2,1,0:T(8,128)}, u32[]{:S(2)}) copy-start(f32[8,544,128]{2,1,0:T(8,128)} %copy-done.3) | copy-start | bytes 6684676
  44.7 22.3 %copy-start.2 = (f32[8,544,128]{2,1,0:T(8,128)S(1)}, f32[8,544,128]{2,1,0:T(8,128)}, u32[]{:S(2)}) copy-start(f32[8,544,128]{2,1,0:T(8,128)} %get-tuple-element.32) | copy-start | bytes 6684676
  44.8 23.9 %collective-permute-start.13 = (f32[2,544,128]{2,1,0:T(8,128)S(1)}, f32[2,544,128]{2,1,0:T(8,128)S(1)}, u32[]{:S(2)}, u32[]{:S(2)}) collective-permute-start(f32[2,544,128]{2,1,0:T(8,128)S(1)} %copy-done.7), channel_id=1, source_target_pairs={{0,48},{8,24},{16,0},{24,40},{32,16},{40,56},{48,32},{56,8},{64,11... | collective-permute-start | bytes 1671176 | tf_op jit(solution)/shard_map/ppermute | solution.py:392
  47.9 20.8 %collective-permute-start.15 = (f32[2,544,128]{2,1,0:T(8,128)S(1)}, f32[2,544,128]{2,1,0:T(8,128)S(1)}, u32[]{:S(2)}, u32[]{:S(2)}) collective-permute-start(f32[2,544,128]{2,1,0:T(8,128)S(1)} %add_add_fusion.1), channel_id=1, source_target_pairs={{0,16},{8,56},{16,32},{24,8},{32,48},{40,24},{48,0},{56,40},{64,80... | collective-permute-start | bytes 1671176 | tf_op jit(solution)/shard_map/ppermute | solution.py:388
  68.6 14.6 %copy-start.5 = (f32[8,512,128]{2,1,0:T(8,128)S(1)}, f32[8,512,128]{2,1,0:T(8,128)}, u32[]{:S(2)}) copy-start(f32[8,512,128]{2,1,0:T(8,128)} %get-tuple-element.24) | copy-start | bytes 6291460
  68.6 9.4 %collective-permute-start.19 = (f32[544,128]{1,0:T(8,128)S(1)}, f32[544,128]{1,0:T(8,128)S(1)}, u32[]{:S(2)}, u32[]{:S(2)}) collective-permute-start(f32[544,128]{1,0:T(8,128)S(1)} %get-tuple-element.53), channel_id=1, source_target_pairs={{0,16},{8,56},{16,32},{24,8},{32,48},{40,24},{48,0},{56,40},{64,80... | collective-permute-start | bytes 835592 | tf_op jit(solution)/shard_map/ppermute | solution.py:388
  68.9 9.5 %collective-permute-start.16 = (f32[544,128]{1,0:T(8,128)S(1)}, f32[544,128]{1,0:T(8,128)S(1)}, u32[]{:S(2)}, u32[]{:S(2)}) collective-permute-start(f32[544,128]{1,0:T(8,128)S(1)} %slice_bitcast_fusion.4), channel_id=1, source_target_pairs={{0,64},{8,72},{16,80},{24,88},{32,96},{40,104},{48,112},{56,120},{... | collective-permute-start | bytes 835592 | tf_op jit(solution)/shard_map/ppermute | solution.py:396
  69.4 37.2 %collective-permute-start.11 = (f32[4,512,128]{2,1,0:T(8,128)S(1)}, f32[4,512,128]{2,1,0:T(8,128)S(1)}, u32[]{:S(2)}, u32[]{:S(2)}) collective-permute-start(f32[4,512,128]{2,1,0:T(8,128)S(1)} %slice_add_fusion.2), channel_id=1, source_target_pairs={{0,64},{8,72},{16,80},{24,88},{32,96},{40,104},{48,112},{56,120},{... | collective-permute-start | bytes 3145736 | tf_op jit(solution)/shard_map/ppermute | solution.py:396
  71.0 13.4 %collective-permute-start.18 = (f32[544,128]{1,0:T(8,128)S(1)}, f32[544,128]{1,0:T(8,128)S(1)}, u32[]{:S(2)}, u32[]{:S(2)}) collective-permute-start(f32[544,128]{1,0:T(8,128)S(1)} %get-tuple-element.52), channel_id=1, source_target_pairs={{0,48},{8,24},{16,0},{24,40},{32,16},{40,56},{48,32},{56,8},{64,11... | collective-permute-start | bytes 835592 | tf_op jit(solution)/shard_map/ppermute | solution.py:392
  78.0 10.5 %collective-permute-start.20 = (f32[544,128]{1,0:T(8,128)S(1)}, f32[544,128]{1,0:T(8,128)S(1)}, u32[]{:S(2)}, u32[]{:S(2)}) collective-permute-start(f32[544,128]{1,0:T(8,128)S(1)} %fusion.4), channel_id=1, source_target_pairs={{0,16},{8,56},{16,32},{24,8},{32,48},{40,24},{48,0},{56,40},{64,80... | collective-permute-start | bytes 835592 | tf_op jit(solution)/shard_map/ppermute | solution.py:388
  78.4 34.6 %collective-permute-start.17 = (f32[544,128]{1,0:T(8,128)S(1)}, f32[544,128]{1,0:T(8,128)S(1)}, u32[]{:S(2)}, u32[]{:S(2)}) collective-permute-start(f32[544,128]{1,0:T(8,128)S(1)} %fusion.7), channel_id=1, source_target_pairs={{1,0},{2,1},{3,2},{4,3},{5,4},{6,5},{7,6},{9,8},{10,9},{11,10},{12... | collective-permute-start | bytes 835592 | tf_op jit(solution)/shard_map/ppermute | solution.py:447
  79.7 29.6 %collective-permute-start.3 = (f32[2,512,128]{2,1,0:T(8,128)S(1)}, f32[2,512,128]{2,1,0:T(8,128)S(1)}, u32[]{:S(2)}, u32[]{:S(2)}) collective-permute-start(f32[2,512,128]{2,1,0:T(8,128)S(1)} %get-tuple-element.48), channel_id=1, source_target_pairs={{0,48},{8,24},{16,0},{24,40},{32,16},{40,56},{48,32},{56,8},{64,11... | collective-permute-start | bytes 1572872 | tf_op jit(solution)/shard_map/ppermute | solution.py:392
  84.4 25.0 %collective-permute-start.9 = (f32[2,512,128]{2,1,0:T(8,128)S(1)}, f32[2,512,128]{2,1,0:T(8,128)S(1)}, u32[]{:S(2)}, u32[]{:S(2)}) collective-permute-start(f32[2,512,128]{2,1,0:T(8,128)S(1)} %fusion.1), channel_id=1, source_target_pairs={{0,16},{8,56},{16,32},{24,8},{32,48},{40,24},{48,0},{56,40},{64,80... | collective-permute-start | bytes 1572872 | tf_op jit(solution)/shard_map/ppermute | solution.py:388
  88.6 24.5 %collective-permute-start.21 = (f32[544,128]{1,0:T(8,128)S(1)}, f32[544,128]{1,0:T(8,128)S(1)}, u32[]{:S(2)}, u32[]{:S(2)}) collective-permute-start(f32[544,128]{1,0:T(8,128)S(1)} %fusion.6), channel_id=1, source_target_pairs={{0,1},{1,2},{2,3},{3,4},{4,5},{5,6},{6,7},{8,9},{9,10},{10,11},{11... | collective-permute-start | bytes 835592 | tf_op jit(solution)/shard_map/ppermute | solution.py:447
  108.1 10.2 %collective-permute-start.22 = (f32[512,128]{1,0:T(8,128)S(1)}, f32[512,128]{1,0:T(8,128)S(1)}, u32[]{:S(2)}, u32[]{:S(2)}) collective-permute-start(f32[512,128]{1,0:T(8,128)S(1)} %get-tuple-element.55), channel_id=1, source_target_pairs={{0,16},{8,56},{16,32},{24,8},{32,48},{40,24},{48,0},{56,40},{64,80... | collective-permute-start | bytes 786440 | tf_op jit(solution)/shard_map/ppermute | solution.py:388
  110.6 7.8 %collective-permute-start.10 = (f32[512,128]{1,0:T(8,128)S(1)}, f32[512,128]{1,0:T(8,128)S(1)}, u32[]{:S(2)}, u32[]{:S(2)}) collective-permute-start(f32[512,128]{1,0:T(8,128)S(1)} %slice_bitcast_fusion.10), channel_id=1, source_target_pairs={{0,64},{8,72},{16,80},{24,88},{32,96},{40,104},{48,112},{56,120},{... | collective-permute-start | bytes 786440 | tf_op jit(solution)/shard_map/ppermute | solution.py:396
  111.1 7.9 %collective-permute-start.12 = (f32[512,128]{1,0:T(8,128)S(1)}, f32[512,128]{1,0:T(8,128)S(1)}, u32[]{:S(2)}, u32[]{:S(2)}) collective-permute-start(f32[512,128]{1,0:T(8,128)S(1)} %get-tuple-element.54), channel_id=1, source_target_pairs={{0,48},{8,24},{16,0},{24,40},{32,16},{40,56},{48,32},{56,8},{64,11... | collective-permute-start | bytes 786440 | tf_op jit(solution)/shard_map/ppermute | solution.py:392
  118.3 7.7 %collective-permute-start.23 = (f32[512,128]{1,0:T(8,128)S(1)}, f32[512,128]{1,0:T(8,128)S(1)}, u32[]{:S(2)}, u32[]{:S(2)}) collective-permute-start(f32[512,128]{1,0:T(8,128)S(1)} %fusion.8), channel_id=1, source_target_pairs={{0,16},{8,56},{16,32},{24,8},{32,48},{40,24},{48,0},{56,40},{64,80... | collective-permute-start | bytes 786440 | tf_op jit(solution)/shard_map/ppermute | solution.py:388

commit v6 on v5

--- a/solution.py
+++ b/solution.py
@@ -117,8 +117,6 @@
     for copy in loads(CHIPS - 1, (3, 4)):
         copy.start()
     nothing = jnp.zeros((16, 128), F32)
-    fx[0:16] = nothing
-    fz[0:16] = nothing
     for side in (0, 1):
         es[side, 0:16] = nothing
         es[side, (cells + 1) * 16 : (cells + 2) * 16] = nothing
@@ -144,6 +142,7 @@
     def first_pass(c):
         def step(i, carry):
             start = (c * rows + i * GROUP + 1) * 16
+            ring = (lax.rem(c, 2) * rows + i * GROUP) * 16
             kk, uu, kx = {}, {}, {}
 
             def center(seen, ref, g, h):
@@ -168,7 +167,7 @@
                     kz, kv = (k0 + up(k0)) * open_up, (k0 + down(k0)) * open_down
                     mid = 24.0 - (((kx[g, h] + kx[g - 1, h]) + (face_y + face_w)) + ((kz + kv) + outer * k0))
                     for ref, value in ((fx, kx[g, h]), (fy, ky), (fw, kw), (fz, kz), (fm, mid)):
-                        ref[pl.ds(row, 8), :] = value
+                        ref[pl.ds(ring + g * 16 + h * 8, 8), :] = value
                     v = center(uu, us, g, h)
                     out = (kx[g, h] * center(uu, us, g + 1, h) + kx[g - 1, h] * center(uu, us, g - 1, h)) + (kz * up(v) + kv * down(v))
                     out = out + (ky * ahead(us, row, v) + kw * behind(us, row, v)) + mid * v
@@ -193,21 +192,24 @@
     def second_pass(c):
         def step(i, carry):
             start = (c * rows + i * GROUP + 1) * 16
+            ring = (lax.rem(c, 2) * rows + i * GROUP) * 16
             nn, kx = {}, {}
 
-            def center(seen, ref, g, h):
-                if (g, h) not in seen:
-                    seen[g, h] = at(ref, start + g * 16 + h * 8)
-                return seen[g, h]
-
+            def center(g, h):
+                if (g, h) not in nn:
+                    nn[g, h] = at(ns, start + g * 16 + h * 8)
+                return nn[g, h]
+
+            for h in (0, 1):
+                kx[-1, h] = at(ks, start + h * 8, -16) + at(ks, start + h * 8)
             for g in range(GROUP):
                 for h in (0, 1):
                     row = start + g * 16 + h * 8
-                    v = center(nn, ns, g, h)
-                    kz = at(fz, row)
-                    out = center(kx, fx, g, h) * center(nn, ns, g + 1, h) + center(kx, fx, g - 1, h) * center(nn, ns, g - 1, h)
+                    v = center(g, h)
+                    kx[g, h], ky, kw, kz, mid = (at(ref, ring + g * 16 + h * 8) for ref in (fx, fy, fw, fz, fm))
+                    out = kx[g, h] * center(g + 1, h) + kx[g - 1, h] * center(g - 1, h)
                     out = out + (kz * up(v) + down(kz) * down(v))
-                    out = out + (at(fy, row) * ahead(ns, row, v) + at(fw, row) * behind(ns, row, v)) + at(fm, row) * v
+                    out = out + (ky * ahead(ns, row, v) + kw * behind(ns, row, v)) + mid * v
                     final = out * (-1.0 / 12.0) - at(us, row)
                     ds[pl.ds(row - 16, 8), :] = at(ds, row, -16) + c0 * v + c1 * final
                     vs[pl.ds(row - 16, 8), :] = at(vs, row, -16) + c2 * v + c3 * final
@@ -327,8 +329,9 @@
 
 def series(coeffs, u, k, p, cos, sin):
     cells = u.shape[0] // 16
-    share = jax.ShapeDtypeStruct((CHIPS, cells, 128), F32)
-    edge = jax.ShapeDtypeStruct((CHIPS, (cells // COUNT + 2) * 16, 128), F32)
+    share = pltpu.VMEM((CHIPS, cells, 128), F32)
+    edge = pltpu.VMEM((CHIPS, (cells // COUNT + 2) * 16, 128), F32)
+    ring = pltpu.VMEM((2 * cells // CHIPS * 16, 128), F32)
     wide = pltpu.VMEM(((cells + 2) * 16, 128), F32)
     exact = pltpu.VMEM((cells * 16, 128), F32)
     return pl.pallas_call(
@@ -336,14 +339,14 @@
         out_shape=(share,) * 4 + (edge,) * 4,
         in_specs=[SMEM] + [ANYWHERE] * 5,
         out_specs=(ANYWHERE,) * 8,
-        scratch_shapes=[wide, wide, wide, exact, exact, wide, wide, wide, wide, wide]
+        scratch_shapes=[wide, wide, wide, exact, exact, ring, ring, ring, ring, ring]
         + [
             pltpu.VMEM((2, (cells + 2) * 16, 128), F32),
             pltpu.SemaphoreType.DMA((5, CHIPS)),
             pltpu.SemaphoreType.DMA((2, 2, CHIPS)),
             pltpu.SemaphoreType.DMA((2, 2, CHIPS)),
         ],
-        compiler_params=params(56),
+        compiler_params=params(36),
         cost_estimate=cost(45),
     )(coeffs, u, k, p, cos, sin)
 
@@ -432,15 +435,17 @@
     k_low, k_high = lax.ppermute(k_here, "gz", UP), lax.ppermute(k_here, "gz", DOWN)
 
     low_rest = forth(blocks(low_same, low_came, 2, 4) + low_two)
-    v_sent = blocks(v_same, v_came, 4, 8)
-    (d_two, v_sent, k_low, k_high), high_far = after((d_two, v_sent, k_low, k_high), high_far)
-    v_far = across(v_sent)
+    v_ends, v_rest = blocks(v_same, v_came, 6, 8), blocks(v_same, v_came, 4, 6)
+    (d_two, v_ends, v_rest, k_low, k_high), high_far = after((d_two, v_ends, v_rest, k_low, k_high), high_far)
+    v_far_ends = across(v_ends)
     d_rest = forth(blocks(d_same, d_came, 2, 4) + d_two)
 
     high = blocks(high_same, high_came, 0, 4) + high_far
     high_two, high_back = forth(high[2]), back(high[3])
     low = blocks(low_same, low_came, 0, 2) + low_back + low_rest
-    low_far = across(low[1])
+    v_far_ends, low_sent = after(v_far_ends, low[1])
+    low_far = across(low_sent)
+    v_far = across(v_rest)
     high_rest = forth(high[1] + high_two)
     low = low[0] + low_far
     high = high[0] + high_back + high_rest
@@ -448,8 +453,9 @@
 
     d = blocks(d_same, d_came, 0, 2) + d_back + d_rest
     d = d[0] + across(d[1])
-    v = blocks(v_same, v_came, 0, 4) + v_far
-    v_two, v_back = forth(v[2]), back(v[3])
+    v_ends = blocks(v_same, v_came, 2, 4) + v_far_ends
+    v_two, v_back = forth(v_ends[0]), back(v_ends[1])
+    v = blocks(v_same, v_came, 0, 2) + v_far
     (above, below), v_two = after((above, below), v_two)
     v = v[0] + v_back + forth(v[1] + v_two)
 

time: 128 us -> 132 us (1.031)
  the two profiles are of different devices: /device:TPU:102 before, /device:TPU:6 now
where the time goes in v6:
time: 132 us; the launch traced here: 131 us
  waiting for transfers between devices  54.5 us (41%)
  starting transfers between devices  34.5 us (26%)
  Pallas kernels  21.5 us (16%)
  other arithmetic  16.7 us (13%)
  local copies, waits for them, and re-layouts  3.06 us (2%)
    ppermute x8, waiting for transfers between devices, forth(): return lax.ppermute(cells, 'tm', FORTH)  20.6 us
    pallas_call x1, Pallas kernels, series(): pl.pallas_call(series_kernel, out_shape=(share,) * 4 + (edge,) * 4, in_sp...  19.7 us
    ppermute x5, waiting for transfers between devices, across(): return lax.ppermute(cells, 'tm', ACROSS)  12.6 us
    ppermute x4, starting transfers between devices, back(): return lax.ppermute(cells, 'tm', BACK)  8.07 us
    ppermute x1, waiting for transfers between devices, local(): lax.ppermute(k_here, 'gz', DOWN)  7.8 us
    ppermute x4, waiting for transfers between devices, to_sibling(): return lax.ppermute(other, 'tm', SIBLING)  7.03 us
    add x4, other arithmetic, blocks(): return lax.slice_in_dim(same, *at) + lax.slice_in_dim(came, *at)  6.58 us
    ppermute x2, waiting for transfers between devices, local(): above, below = (lax.ppermute(low, 'gz', DOWN), lax.ppermute(high, 'gz', UP))  6.45 us
  transfers between devices with their start and end apart: 25, of which 12 were waited for; matrix products, arithmetic and copies ran while one was open for 14% of the time, Pallas kernels for 0%

profile of v6, /device:TPU:6, one launch (start us, length us, event | category | flops | bytes accessed | tf_op | source)
XLA Modules:
  0.0 131.2 jit_solution(11410750157566226882)
XLA Ops:
  0.6 0.6 copy-done.5
  1.3 19.7 %shard_map.77 = (f32[8,512,128]{2,1,0:T(8,128)}, f32[8,512,128]{2,1,0:T(8,128)S(1)}, f32[8,512,128]{2,1,0:T(8,128)}, f32[8,512,128]{2,1,0:T(8,128)S(1)}, f32[8,5...) custom-call(f32[1,4]{1,0:T(1,128)S(1)} %copy-done.5, ...), custom_call_target="tpu_custom_call" | custom-call | bytes 47185920 | tf_op jit(solution)/shard_map/pallas_call | solution.py:337
  21.0 1.3 copy-done.3
  22.3 0.5 collective-permute-start.1
  22.8 3.8 %collective-permute-done = f32[8,544,128]{2,1,0:T(8,128)S(1)} collective-permute-done((f32[8,544,128]{2,1,0:T(8,128)S(1)}, f32[8,544,128]{2,1,0:T(8,128)S(1)}, u32[]{:S(2)}, u32[]{:S(2)}) %collective-permute-start) | collective-permute-done | bytes 2228256 | tf_op jit(solution)/shard_map/ppermute | solution.py:387
  26.7 3.2 %collective-permute-done.1 = f32[8,544,128]{2,1,0:T(8,128)S(1)} collective-permute-done((f32[8,544,128]{2,1,0:T(8,128)S(1)}, f32[8,544,128]{2,1,0:T(8,128)S(1)}, u32[]{:S(2)}, u32[]{:S(2)}) %collective-permute-start.1) | collective-permute-done | bytes 2228256 | tf_op jit(solution)/shard_map/ppermute | solution.py:387
  29.8 0.1 collective-permute-start.2
  30.0 0.4 collective-permute-start.5
  30.4 1.1 slice_add_fusion.2
  31.5 1.6 %collective-permute-start.14 = (f32[2,544,128]{2,1,0:T(8,128)S(1)}, f32[2,544,128]{2,1,0:T(8,128)}, u32[]{:S(2)}, u32[]{:S(2)}) collective-permute-start(f32[2,544,128]{2,1,0:T(8,128)S(1)} %get-tuple-element.53), channel_id=1, source_target_pairs={{0,16},{8,56},{16,32},{24,8},{32,48},{40,24},{48,0},{56,40},{64,80... | collective-permute-start | bytes 1671176 | tf_op jit(solution)/shard_map/ppermute | solution.py:391
  33.0 1.7 %collective-permute-start.13 = (f32[2,544,128]{2,1,0:T(8,128)}, f32[2,544,128]{2,1,0:T(8,128)}, u32[]{:S(2)}, u32[]{:S(2)}) collective-permute-start(f32[2,544,128]{2,1,0:T(8,128)} %get-tuple-element.52), channel_id=1, source_target_pairs={{0,48},{8,24},{16,0},{24,40},{32,16},{40,56},{48,32},{56,8},{64,11... | collective-permute-start | bytes 1671176 | tf_op jit(solution)/shard_map/ppermute | solution.py:395
  34.7 2.3 %slice_add_fusion = f32[4,544,128]{2,1,0:T(8,128)} fusion(f32[8,544,128]{2,1,0:T(8,128)} %copy-done.6, f32[8,544,128]{2,1,0:T(8,128)S(1)} %get-tuple-element.35), kind=kLoop, calls=%fused_computation.1 | loop fusion | flops 278528 | bytes 3342336 | tf_op jit(solution)/shard_map/add | solution.py:415
  37.0 1.9 %collective-permute-start.8 = (f32[4,544,128]{2,1,0:T(8,128)}, f32[4,544,128]{2,1,0:T(8,128)}, u32[]{:S(2)}, u32[]{:S(2)}) collective-permute-start(f32[4,544,128]{2,1,0:T(8,128)} %slice_add_fusion), channel_id=1, source_target_pairs={{0,64},{8,72},{16,80},{24,88},{32,96},{40,104},{48,112},{56,120},{... | collective-permute-start | bytes 3342344 | tf_op jit(solution)/shard_map/ppermute | solution.py:399
  39.0 7.1 %collective-permute-done.14 = f32[2,544,128]{2,1,0:T(8,128)} collective-permute-done((f32[2,544,128]{2,1,0:T(8,128)S(1)}, f32[2,544,128]{2,1,0:T(8,128)}, u32[]{:S(2)}, u32[]{:S(2)}) %collective-permute-start.14) | collective-permute-done | bytes 557088 | tf_op jit(solution)/shard_map/ppermute | solution.py:391
  46.1 2.3 %add_add_fusion.1 = f32[2,544,128]{2,1,0:T(8,128)} fusion(f32[2,544,128]{2,1,0:T(8,128)} %collective-permute-done.14, f32[8,544,128]{2,1,0:T(8,128)} %copy-done.8, f32[8,544,128]{2,1,0:T(8,128)} %copy-done), kind=kLoop, calls=%fused_computation.3 | loop fusion | flops 278528 | bytes 2228224 | tf_op jit(solution)/shard_map/add | solution.py:437
  48.3 1.8 %collective-permute-start.15 = (f32[2,544,128]{2,1,0:T(8,128)}, f32[2,544,128]{2,1,0:T(8,128)}, u32[]{:S(2)}, u32[]{:S(2)}) collective-permute-start(f32[2,544,128]{2,1,0:T(8,128)} %add_add_fusion.1), channel_id=1, source_target_pairs={{0,16},{8,56},{16,32},{24,8},{32,48},{40,24},{48,0},{56,40},{64,80... | collective-permute-start | bytes 1671176 | tf_op jit(solution)/shard_map/ppermute | solution.py:391
  50.1 0.7 dynamic-slice_select_fusion.1
  50.8 1.0 constant_dynamic-slice_fusion
  51.8 5.7 %collective-permute-start.6 = (f32[544,128]{1,0:T(8,128)S(1)}, f32[544,128]{1,0:T(8,128)S(1)}, u32[]{:S(2)}, u32[]{:S(2)}) collective-permute-start(f32[544,128]{1,0:T(8,128)S(1)} %pad_maximum_fusion), channel_id=1, source_target_pairs={{0,1},{1,2},{2,3},{3,4},{4,5},{5,6},{6,7},{8,9},{9,10},{10,11},{11... | collective-permute-start | bytes 835592 | tf_op jit(solution)/shard_map/ppermute | solution.py:435
  57.5 1.6 %slice_add_fusion.9 = (f32[2,512,128]{2,1,0:T(8,128)S(1)}, f32[2,512,128]{2,1,0:T(8,128)S(1)}) fusion(f32[8,512,128]{2,1,0:T(8,128)} %collective-permute-done.2, f32[8,512,128]{2,1,0:T(8,128)} %copy-done.1), kind=kLoop, calls=%fused_computation.15 | loop fusion | flops 262144 | bytes 3145728 | tf_op jit(solution)/shard_map/add | solution.py:415
  59.2 2.1 %collective-permute-start.7 = (f32[544,128]{1,0:T(8,128)S(1)}, f32[544,128]{1,0:T(8,128)S(1)}, u32[]{:S(2)}, u32[]{:S(2)}) collective-permute-start(f32[544,128]{1,0:T(8,128)S(1)} %pad_maximum_fusion), channel_id=1, source_target_pairs={{1,0},{2,1},{3,2},{4,3},{5,4},{6,5},{7,6},{9,8},{10,9},{11,10},{12... | collective-permute-start | bytes 835592 | tf_op jit(solution)/shard_map/ppermute | solution.py:435
  61.3 2.0 %collective-permute-start.4 = (f32[2,512,128]{2,1,0:T(8,128)S(1)}, f32[2,512,128]{2,1,0:T(8,128)S(1)}, u32[]{:S(2)}, u32[]{:S(2)}) collective-permute-start(f32[2,512,128]{2,1,0:T(8,128)S(1)} %get-tuple-element.57), channel_id=1, source_target_pairs={{0,16},{8,56},{16,32},{24,8},{32,48},{40,24},{48,0},{56,40},{64,80... | collective-permute-start | bytes 1572872 | tf_op jit(solution)/shard_map/ppermute | solution.py:391
  63.3 1.7 %add_add_fusion.2 = f32[2,544,128]{2,1,0:T(8,128)S(1)} fusion(f32[2,544,128]{2,1,0:T(8,128)} %collective-permute-done.15, f32[2,544,128]{2,1,0:T(8,128)} %collective-permute-done.13, f32[8,544,128]{2,1,0:T(8,128)} %copy-done.8, f32[8,544,128]{2,1,0:T(8,128)} %copy-done), kind=kLoop, calls=%fused_computation.4 | loop fusion | flops 417792 | bytes 2785280 | tf_op jit(solution)/shard_map/add | solution.py:445
  64.9 1.5 %slice_add_fusion.5 = (f32[2,512,128]{2,1,0:T(8,128)S(1)}, f32[2,512,128]{2,1,0:T(8,128)S(1)}) fusion(f32[8,512,128]{2,1,0:T(8,128)} %collective-permute-done.5, f32[8,512,128]{2,1,0:T(8,128)S(1)} %copy-done.4), kind=kLoop, calls=%fused_computation.10 | loop fusion | flops 262144 | bytes 3145728 | tf_op jit(solution)/shard_map/add | solution.py:415
  66.5 7.8 %collective-permute-done.7 = f32[544,128]{1,0:T(8,128)S(1)} collective-permute-done((f32[544,128]{1,0:T(8,128)S(1)}, f32[544,128]{1,0:T(8,128)S(1)}, u32[]{:S(2)}, u32[]{:S(2)}) %collective-permute-start.7) | collective-permute-done | bytes 278560 | tf_op jit(solution)/shard_map/ppermute | solution.py:435
  74.3 1.2 collective-permute-start.12
  75.4 1.0 collective-permute-start.11
  76.4 1.5 %add_add_fusion = f32[4,544,128]{2,1,0:T(8,128)S(1)} fusion(f32[4,544,128]{2,1,0:T(8,128)} %collective-permute-done.8, f32[8,544,128]{2,1,0:T(8,128)S(1)} %copy-done.7, f32[8,544,128]{2,1,0:T(8,128)S(1)} %get-tuple-element.35), kind=kLoop, calls=%fused_computation | loop fusion | flops 557056 | bytes 4456448 | tf_op jit(solution)/shard_map/add | solution.py:443
  78.1 3.3 %collective-permute-start.3 = (f32[2,512,128]{2,1,0:T(8,128)S(1)}, f32[2,512,128]{2,1,0:T(8,128)S(1)}, u32[]{:S(2)}, u32[]{:S(2)}) collective-permute-start(f32[2,512,128]{2,1,0:T(8,128)S(1)} %get-tuple-element.56), channel_id=1, source_target_pairs={{0,48},{8,24},{16,0},{24,40},{32,16},{40,56},{48,32},{56,8},{64,11... | collective-permute-start | bytes 1572872 | tf_op jit(solution)/shard_map/ppermute | solution.py:395
  81.3 0.1 collective-permute-start.19
  81.4 1.2 fusion.2
  82.6 6.2 %collective-permute-done.20 = f32[544,128]{1,0:T(8,128)S(1)} collective-permute-done((f32[544,128]{1,0:T(8,128)S(1)}, f32[544,128]{1,0:T(8,128)S(1)}, u32[]{:S(2)}, u32[]{:S(2)}) %collective-permute-start.20) | collective-permute-done | bytes 278560 | tf_op jit(solution)/shard_map/ppermute | solution.py:391
  88.8 0.3 collective-permute-done.12
  89.2 10.3 %collective-permute-done.11 = f32[2,512,128]{2,1,0:T(8,128)S(1)} collective-permute-done((f32[2,512,128]{2,1,0:T(8,128)S(1)}, f32[2,512,128]{2,1,0:T(8,128)S(1)}, u32[]{:S(2)}, u32[]{:S(2)}) %collective-permute-start.11) | collective-permute-done | bytes 524320 | tf_op jit(solution)/shard_map/ppermute | solution.py:399
  99.5 0.9 collective-permute-start.17
  100.4 1.4 %fusion.1 = (f32[2,512,128]{2,1,0:T(8,128)S(1)}, f32[2,512,128]{2,1,0:T(8,128)S(1)}) fusion(f32[2,512,128]{2,1,0:T(8,128)S(1)} %collective-permute-done.11, f32[8,512,128]{2,1,0:T(8,128)} %collective-permute-done.5, f32[8,512,128]{2,1,0:T(8,128)S(1)} %copy-done.4, f32[2,512,128]{2,1,0:T(8,128)S(1)} %collective-permute-done.12), kind=kLoop, calls=%fused_computation.9 | loop fusion | flops 524288 | bytes 4194304 | tf_op jit(solution)/shard_map/add | solution.py:458
  102.0 0.2 collective-permute-done.21
  102.2 3.0 %collective-permute-start.16 = (f32[512,128]{1,0:T(8,128)S(1)}, f32[512,128]{1,0:T(8,128)S(1)}, u32[]{:S(2)}, u32[]{:S(2)}) collective-permute-start(f32[512,128]{1,0:T(8,128)S(1)} %get-tuple-element.64), channel_id=1, source_target_pairs={{0,48},{8,24},{16,0},{24,40},{32,16},{40,56},{48,32},{56,8},{64,11... | collective-permute-start | bytes 786440 | tf_op jit(solution)/shard_map/ppermute | solution.py:395
  105.3 2.0 %collective-permute-done.17 = f32[544,128]{1,0:T(8,128)S(1)} collective-permute-done((f32[544,128]{1,0:T(8,128)S(1)}, f32[544,128]{1,0:T(8,128)S(1)}, u32[]{:S(2)}, u32[]{:S(2)}) %collective-permute-start.17) | collective-permute-done | bytes 278560 | tf_op jit(solution)/shard_map/ppermute | solution.py:399
  107.2 2.2 %collective-permute-start.22 = (f32[544,128]{1,0:T(8,128)S(1)}, f32[544,128]{1,0:T(8,128)S(1)}, u32[]{:S(2)}, u32[]{:S(2)}) collective-permute-start(f32[544,128]{1,0:T(8,128)S(1)} %fusion.7), channel_id=1, source_target_pairs={{0,1},{1,2},{2,3},{3,4},{4,5},{5,6},{6,7},{8,9},{9,10},{10,11},{11... | collective-permute-start | bytes 835592 | tf_op jit(solution)/shard_map/ppermute | solution.py:452
  109.5 3.7 %collective-permute-start.18 = (f32[544,128]{1,0:T(8,128)S(1)}, f32[544,128]{1,0:T(8,128)S(1)}, u32[]{:S(2)}, u32[]{:S(2)}) collective-permute-start(f32[544,128]{1,0:T(8,128)S(1)} %fusion.8), channel_id=1, source_target_pairs={{1,0},{2,1},{3,2},{4,3},{5,4},{6,5},{7,6},{9,8},{10,9},{11,10},{12... | collective-permute-start | bytes 835592 | tf_op jit(solution)/shard_map/ppermute | solution.py:452
  113.1 1.2 fusion.4
  114.3 0.9 collective-permute-start.10
  115.2 0.7 collective-permute-done.22
  115.9 5.7 %collective-permute-done.18 = f32[544,128]{1,0:T(8,128)S(1)} collective-permute-done((f32[544,128]{1,0:T(8,128)S(1)}, f32[544,128]{1,0:T(8,128)S(1)}, u32[]{:S(2)}, u32[]{:S(2)}) %collective-permute-start.18) | collective-permute-done | bytes 278560 | tf_op jit(solution)/shard_map/ppermute | solution.py:452
  121.7 0.5 collective-permute-start.24
  122.2 7.1 %collective-permute-done.24 = f32[512,128]{1,0:T(8,128)S(1)} collective-permute-done((f32[512,128]{1,0:T(8,128)S(1)}, f32[512,128]{1,0:T(8,128)S(1)}, u32[]{:S(2)}, u32[]{:S(2)}) %collective-permute-start.24) | collective-permute-done | bytes 262176 | tf_op jit(solution)/shard_map/ppermute | solution.py:391
  129.4 1.8 %shard_map.78 = (f32[32,2,8,128]{3,2,1,0:T(8,128)}, f32[32,2,8,128]{3,2,1,0:T(8,128)}) custom-call(f32[32,2,8,128]{3,2,1,0:T(8,128)S(1)} %bitcast.87, f32[32,2,8,128]{3,2,1,0:T(8,128)S(1)} %bitcast.88, f32[34,2,8,128]{3,2,1,0:T(8,128)S(1)} %bitcast.86, f32[34,2,8,128]{3,2,1,0:T(8,128)S(1)} %bitcast.85, f32[34,2,8,128]{3,2,1,0:T(8,128)S(1)} %bitcast.91, ...), custom_call_target="tpu_custom_call" | custom-call | bytes 4194304 | tf_op jit(solution)/shard_map/pallas_call | solution.py:357
  (45 shorter events, 0.6 us)
Async XLA Ops:
  0.6 0.7 copy-start.5
  21.0 1.3 %copy-start.3 = (f32[8,512,128]{2,1,0:T(8,128)}, f32[8,512,128]{2,1,0:T(8,128)S(1)}, u32[]{:S(2)}) copy-start(f32[8,512,128]{2,1,0:T(8,128)S(1)} %get-tuple-element.33) | copy-start | bytes 6291460
  22.3 8.1 %copy-start = (f32[8,544,128]{2,1,0:T(8,128)}, f32[8,544,128]{2,1,0:T(8,128)S(1)}, u32[]{:S(2)}) copy-start(f32[8,544,128]{2,1,0:T(8,128)S(1)} %get-tuple-element.40) | copy-start | bytes 6684676
  22.3 9.1 %copy-start.1 = (f32[8,512,128]{2,1,0:T(8,128)}, f32[8,512,128]{2,1,0:T(8,128)S(1)}, u32[]{:S(2)}) copy-start(f32[8,512,128]{2,1,0:T(8,128)S(1)} %get-tuple-element.27) | copy-start | bytes 6291460
  22.3 4.3 %collective-permute-start = (f32[8,544,128]{2,1,0:T(8,128)S(1)}, f32[8,544,128]{2,1,0:T(8,128)S(1)}, u32[]{:S(2)}, u32[]{:S(2)}) collective-permute-start(f32[8,544,128]{2,1,0:T(8,128)S(1)} %get-tuple-element.28), channel_id=1, source_target_pairs={{0,8},{8,0},{16,24},{24,16},{32,40},{40,32},{48,56},{56,48},{64,72... | collective-permute-start | bytes 6684680 | tf_op jit(solution)/shard_map/ppermute | solution.py:387
  22.3 7.5 %collective-permute-start.1 = (f32[8,544,128]{2,1,0:T(8,128)S(1)}, f32[8,544,128]{2,1,0:T(8,128)S(1)}, u32[]{:S(2)}, u32[]{:S(2)}) collective-permute-start(f32[8,544,128]{2,1,0:T(8,128)S(1)} %get-tuple-element.29), channel_id=1, source_target_pairs={{0,8},{8,0},{16,24},{24,16},{32,40},{40,32},{48,56},{56,48},{64,72... | collective-permute-start | bytes 6684680 | tf_op jit(solution)/shard_map/ppermute | solution.py:387
  26.7 4.8 %copy-start.6 = (f32[8,544,128]{2,1,0:T(8,128)}, f32[8,544,128]{2,1,0:T(8,128)S(1)}, u32[]{:S(2)}) copy-start(f32[8,544,128]{2,1,0:T(8,128)S(1)} %collective-permute-done) | copy-start | bytes 6684676
  29.8 3.2 %copy-start.8 = (f32[8,544,128]{2,1,0:T(8,128)}, f32[8,544,128]{2,1,0:T(8,128)S(1)}, u32[]{:S(2)}) copy-start(f32[8,544,128]{2,1,0:T(8,128)S(1)} %collective-permute-done.1) | copy-start | bytes 6684676
  29.8 22.0 %collective-permute-start.2 = (f32[8,512,128]{2,1,0:T(8,128)}, f32[8,512,128]{2,1,0:T(8,128)}, u32[]{:S(2)}, u32[]{:S(2)}) collective-permute-start(f32[8,512,128]{2,1,0:T(8,128)} %get-tuple-element.32), channel_id=1, source_target_pairs={{0,8},{8,0},{16,24},{24,16},{32,40},{40,32},{48,56},{56,48},{64,72... | collective-permute-start | bytes 6291464 | tf_op jit(solution)/shard_map/ppermute | solution.py:387
  30.0 35.0 %collective-permute-start.5 = (f32[8,512,128]{2,1,0:T(8,128)}, f32[8,512,128]{2,1,0:T(8,128)}, u32[]{:S(2)}, u32[]{:S(2)}) collective-permute-start(f32[8,512,128]{2,1,0:T(8,128)} %get-tuple-element.34), channel_id=1, source_target_pairs={{0,8},{8,0},{16,24},{24,16},{32,40},{40,32},{48,56},{56,48},{64,72... | collective-permute-start | bytes 6291464 | tf_op jit(solution)/shard_map/ppermute | solution.py:387
  31.5 14.6 %collective-permute-start.14 = (f32[2,544,128]{2,1,0:T(8,128)S(1)}, f32[2,544,128]{2,1,0:T(8,128)}, u32[]{:S(2)}, u32[]{:S(2)}) collective-permute-start(f32[2,544,128]{2,1,0:T(8,128)S(1)} %get-tuple-element.53), channel_id=1, source_target_pairs={{0,16},{8,56},{16,32},{24,8},{32,48},{40,24},{48,0},{56,40},{64,80... | collective-permute-start | bytes 1671176 | tf_op jit(solution)/shard_map/ppermute | solution.py:391
  33.0 26.1 %collective-permute-start.13 = (f32[2,544,128]{2,1,0:T(8,128)}, f32[2,544,128]{2,1,0:T(8,128)}, u32[]{:S(2)}, u32[]{:S(2)}) collective-permute-start(f32[2,544,128]{2,1,0:T(8,128)} %get-tuple-element.52), channel_id=1, source_target_pairs={{0,48},{8,24},{16,0},{24,40},{32,16},{40,56},{48,32},{56,8},{64,11... | collective-permute-start | bytes 1671176 | tf_op jit(solution)/shard_map/ppermute | solution.py:395
  37.0 37.2 %collective-permute-start.8 = (f32[4,544,128]{2,1,0:T(8,128)}, f32[4,544,128]{2,1,0:T(8,128)}, u32[]{:S(2)}, u32[]{:S(2)}) collective-permute-start(f32[4,544,128]{2,1,0:T(8,128)} %slice_add_fusion), channel_id=1, source_target_pairs={{0,64},{8,72},{16,80},{24,88},{32,96},{40,104},{48,112},{56,120},{... | collective-permute-start | bytes 3342344 | tf_op jit(solution)/shard_map/ppermute | solution.py:399
  48.3 12.9 %collective-permute-start.15 = (f32[2,544,128]{2,1,0:T(8,128)}, f32[2,544,128]{2,1,0:T(8,128)}, u32[]{:S(2)}, u32[]{:S(2)}) collective-permute-start(f32[2,544,128]{2,1,0:T(8,128)} %add_add_fusion.1), channel_id=1, source_target_pairs={{0,16},{8,56},{16,32},{24,8},{32,48},{40,24},{48,0},{56,40},{64,80... | collective-permute-start | bytes 1671176 | tf_op jit(solution)/shard_map/ppermute | solution.py:391
  51.8 14.6 %collective-permute-start.6 = (f32[544,128]{1,0:T(8,128)S(1)}, f32[544,128]{1,0:T(8,128)S(1)}, u32[]{:S(2)}, u32[]{:S(2)}) collective-permute-start(f32[544,128]{1,0:T(8,128)S(1)} %pad_maximum_fusion), channel_id=1, source_target_pairs={{0,1},{1,2},{2,3},{3,4},{4,5},{5,6},{6,7},{8,9},{9,10},{10,11},{11... | collective-permute-start | bytes 835592 | tf_op jit(solution)/shard_map/ppermute | solution.py:435
  59.2 5.8 %copy-start.4 = (f32[8,512,128]{2,1,0:T(8,128)S(1)}, f32[8,512,128]{2,1,0:T(8,128)}, u32[]{:S(2)}) copy-start(f32[8,512,128]{2,1,0:T(8,128)} %copy-done.3) | copy-start | bytes 6291460
  59.2 15.1 %collective-permute-start.7 = (f32[544,128]{1,0:T(8,128)S(1)}, f32[544,128]{1,0:T(8,128)S(1)}, u32[]{:S(2)}, u32[]{:S(2)}) collective-permute-start(f32[544,128]{1,0:T(8,128)S(1)} %pad_maximum_fusion), channel_id=1, source_target_pairs={{1,0},{2,1},{3,2},{4,3},{5,4},{6,5},{7,6},{9,8},{10,9},{11,10},{12... | collective-permute-start | bytes 835592 | tf_op jit(solution)/shard_map/ppermute | solution.py:435
  61.3 13.0 %collective-permute-start.4 = (f32[2,512,128]{2,1,0:T(8,128)S(1)}, f32[2,512,128]{2,1,0:T(8,128)S(1)}, u32[]{:S(2)}, u32[]{:S(2)}) collective-permute-start(f32[2,512,128]{2,1,0:T(8,128)S(1)} %get-tuple-element.57), channel_id=1, source_target_pairs={{0,16},{8,56},{16,32},{24,8},{32,48},{40,24},{48,0},{56,40},{64,80... | collective-permute-start | bytes 1572872 | tf_op jit(solution)/shard_map/ppermute | solution.py:391
  64.9 11.5 %copy-start.7 = (f32[8,544,128]{2,1,0:T(8,128)S(1)}, f32[8,544,128]{2,1,0:T(8,128)}, u32[]{:S(2)}) copy-start(f32[8,544,128]{2,1,0:T(8,128)} %copy-done.6) | copy-start | bytes 6684676
  74.3 7.1 %copy-start.2 = (f32[8,512,128]{2,1,0:T(8,128)S(1)}, f32[8,512,128]{2,1,0:T(8,128)}, u32[]{:S(2)}) copy-start(f32[8,512,128]{2,1,0:T(8,128)} %copy-done.1) | copy-start | bytes 6291460
  74.3 14.9 %collective-permute-start.12 = (f32[2,512,128]{2,1,0:T(8,128)S(1)}, f32[2,512,128]{2,1,0:T(8,128)S(1)}, u32[]{:S(2)}, u32[]{:S(2)}) collective-permute-start(f32[2,512,128]{2,1,0:T(8,128)S(1)} %get-tuple-element.39), channel_id=1, source_target_pairs={{0,64},{8,72},{16,80},{24,88},{32,96},{40,104},{48,112},{56,120},{... | collective-permute-start | bytes 1572872 | tf_op jit(solution)/shard_map/ppermute | solution.py:399
  75.4 24.0 %collective-permute-start.11 = (f32[2,512,128]{2,1,0:T(8,128)S(1)}, f32[2,512,128]{2,1,0:T(8,128)S(1)}, u32[]{:S(2)}, u32[]{:S(2)}) collective-permute-start(f32[2,512,128]{2,1,0:T(8,128)S(1)} %get-tuple-element.38), channel_id=1, source_target_pairs={{0,64},{8,72},{16,80},{24,88},{32,96},{40,104},{48,112},{56,120},{... | collective-permute-start | bytes 1572872 | tf_op jit(solution)/shard_map/ppermute | solution.py:399
  77.9 10.9 %collective-permute-start.20 = (f32[544,128]{1,0:T(8,128)S(1)}, f32[544,128]{1,0:T(8,128)S(1)}, u32[]{:S(2)}, u32[]{:S(2)}) collective-permute-start(f32[544,128]{1,0:T(8,128)S(1)} %get-tuple-element.63), channel_id=1, source_target_pairs={{0,16},{8,56},{16,32},{24,8},{32,48},{40,24},{48,0},{56,40},{64,80... | collective-permute-start | bytes 835592 | tf_op jit(solution)/shard_map/ppermute | solution.py:391
  78.1 31.4 %collective-permute-start.3 = (f32[2,512,128]{2,1,0:T(8,128)S(1)}, f32[2,512,128]{2,1,0:T(8,128)S(1)}, u32[]{:S(2)}, u32[]{:S(2)}) collective-permute-start(f32[2,512,128]{2,1,0:T(8,128)S(1)} %get-tuple-element.56), channel_id=1, source_target_pairs={{0,48},{8,24},{16,0},{24,40},{32,16},{40,56},{48,32},{56,8},{64,11... | collective-permute-start | bytes 1572872 | tf_op jit(solution)/shard_map/ppermute | solution.py:395
  81.3 20.6 %collective-permute-start.19 = (f32[544,128]{1,0:T(8,128)S(1)}, f32[544,128]{1,0:T(8,128)S(1)}, u32[]{:S(2)}, u32[]{:S(2)}) collective-permute-start(f32[544,128]{1,0:T(8,128)S(1)} %get-tuple-element.62), channel_id=1, source_target_pairs={{0,48},{8,24},{16,0},{24,40},{32,16},{40,56},{48,32},{56,8},{64,11... | collective-permute-start | bytes 835592 | tf_op jit(solution)/shard_map/ppermute | solution.py:395
  88.8 24.3 %collective-permute-start.9 = (f32[2,512,128]{2,1,0:T(8,128)S(1)}, f32[2,512,128]{2,1,0:T(8,128)S(1)}, u32[]{:S(2)}, u32[]{:S(2)}) collective-permute-start(f32[2,512,128]{2,1,0:T(8,128)S(1)} %fusion.2), channel_id=1, source_target_pairs={{0,16},{8,56},{16,32},{24,8},{32,48},{40,24},{48,0},{56,40},{64,80... | collective-permute-start | bytes 1572872 | tf_op jit(solution)/shard_map/ppermute | solution.py:391
  89.2 13.0 %collective-permute-start.21 = (f32[544,128]{1,0:T(8,128)S(1)}, f32[544,128]{1,0:T(8,128)S(1)}, u32[]{:S(2)}, u32[]{:S(2)}) collective-permute-start(f32[544,128]{1,0:T(8,128)S(1)} %fusion.5), channel_id=1, source_target_pairs={{0,16},{8,56},{16,32},{24,8},{32,48},{40,24},{48,0},{56,40},{64,80... | collective-permute-start | bytes 835592 | tf_op jit(solution)/shard_map/ppermute | solution.py:391
  99.5 7.8 %collective-permute-start.17 = (f32[544,128]{1,0:T(8,128)S(1)}, f32[544,128]{1,0:T(8,128)S(1)}, u32[]{:S(2)}, u32[]{:S(2)}) collective-permute-start(f32[544,128]{1,0:T(8,128)S(1)} %slice_bitcast_fusion.5), channel_id=1, source_target_pairs={{0,64},{8,72},{16,80},{24,88},{32,96},{40,104},{48,112},{56,120},{... | collective-permute-start | bytes 835592 | tf_op jit(solution)/shard_map/ppermute | solution.py:399
  101.9 13.3 %collective-permute-start.23 = (f32[512,128]{1,0:T(8,128)S(1)}, f32[512,128]{1,0:T(8,128)S(1)}, u32[]{:S(2)}, u32[]{:S(2)}) collective-permute-start(f32[512,128]{1,0:T(8,128)S(1)} %get-tuple-element.65), channel_id=1, source_target_pairs={{0,16},{8,56},{16,32},{24,8},{32,48},{40,24},{48,0},{56,40},{64,80... | collective-permute-start | bytes 786440 | tf_op jit(solution)/shard_map/ppermute | solution.py:391
  102.2 20.0 %collective-permute-start.16 = (f32[512,128]{1,0:T(8,128)S(1)}, f32[512,128]{1,0:T(8,128)S(1)}, u32[]{:S(2)}, u32[]{:S(2)}) collective-permute-start(f32[512,128]{1,0:T(8,128)S(1)} %get-tuple-element.64), channel_id=1, source_target_pairs={{0,48},{8,24},{16,0},{24,40},{32,16},{40,56},{48,32},{56,8},{64,11... | collective-permute-start | bytes 786440 | tf_op jit(solution)/shard_map/ppermute | solution.py:395
  107.2 8.7 %collective-permute-start.22 = (f32[544,128]{1,0:T(8,128)S(1)}, f32[544,128]{1,0:T(8,128)S(1)}, u32[]{:S(2)}, u32[]{:S(2)}) collective-permute-start(f32[544,128]{1,0:T(8,128)S(1)} %fusion.7), channel_id=1, source_target_pairs={{0,1},{1,2},{2,3},{3,4},{4,5},{5,6},{6,7},{8,9},{9,10},{10,11},{11... | collective-permute-start | bytes 835592 | tf_op jit(solution)/shard_map/ppermute | solution.py:452
  109.5 12.2 %collective-permute-start.18 = (f32[544,128]{1,0:T(8,128)S(1)}, f32[544,128]{1,0:T(8,128)S(1)}, u32[]{:S(2)}, u32[]{:S(2)}) collective-permute-start(f32[544,128]{1,0:T(8,128)S(1)} %fusion.8), channel_id=1, source_target_pairs={{1,0},{2,1},{3,2},{4,3},{5,4},{6,5},{7,6},{9,8},{10,9},{11,10},{12... | collective-permute-start | bytes 835592 | tf_op jit(solution)/shard_map/ppermute | solution.py:452
  114.3 7.8 %collective-permute-start.10 = (f32[512,128]{1,0:T(8,128)S(1)}, f32[512,128]{1,0:T(8,128)S(1)}, u32[]{:S(2)}, u32[]{:S(2)}) collective-permute-start(f32[512,128]{1,0:T(8,128)S(1)} %slice_bitcast_fusion.10), channel_id=1, source_target_pairs={{0,64},{8,72},{16,80},{24,88},{32,96},{40,104},{48,112},{56,120},{... | collective-permute-start | bytes 786440 | tf_op jit(solution)/shard_map/ppermute | solution.py:399
  121.7 7.7 %collective-permute-start.24 = (f32[512,128]{1,0:T(8,128)S(1)}, f32[512,128]{1,0:T(8,128)S(1)}, u32[]{:S(2)}, u32[]{:S(2)}) collective-permute-start(f32[512,128]{1,0:T(8,128)S(1)} %fusion.9), channel_id=1, source_target_pairs={{0,16},{8,56},{16,32},{24,8},{32,48},{40,24},{48,0},{56,40},{64,80... | collective-permute-start | bytes 786440 | tf_op jit(solution)/shard_map/ppermute | solution.py:391

commit v7 on v5

--- a/solution.py
+++ b/solution.py
@@ -80,7 +80,7 @@
     return me // 8, lax.rem(me // 2, 4), lax.rem(me, 2)
 
 
-def series_kernel(coeffs, u, k, p, cos, sin, d_other, d_same, v_other, v_same, low_other, low_same, high_other, high_same,
+def series_kernel(coeffs, u, k, p, cos, sin, far_other, far_same, near_other, near_same, ends_other, ends_same, rest_other, rest_same,
                   us, ks, ns, ds, vs, fx, fy, fw, fz, fm, es, in_sem, out_sem, edge_sem):
     cells = u.shape[0] // 16
     rows = cells // CHIPS
@@ -215,33 +215,34 @@
 
         lax.fori_loop(0, rows // GROUP, step, 0)
 
-    def slots(c, core):
-        turn = lax.rem((1 - 2 * core) * (lax.rem(c, 4) - my_y) + 8, 4)
-        side = lax.rem(c // 4 + my_z, 2)
-        return turn * 2 + side, side * 4 + turn
-
-    def stores(c, core, same):
+    def place(c, core):
+        return lax.rem((1 - 2 * core) * (lax.rem(c, 4) - my_y) + 8, 4), lax.rem(c // 4 + my_z, 2)
+
+    def stores(c, core, same, far):
+        turn, _ = place(c, core)
         here = pl.ds((c * rows + core * half_rows) * 16, half_rows * 16)
-        y_slot, z_slot = slots(c, core)
-        return [
-            pltpu.make_async_copy(ds.at[here], (d_same if same else d_other).at[y_slot], out_sem.at[0, core, c]),
-            pltpu.make_async_copy(vs.at[here], (v_same if same else v_other).at[z_slot], out_sem.at[1, core, c]),
-        ]
-
-    def edge_stores(c, core, same):
+        to = ((far_other, far_same) if far else (near_other, near_same))[same]
+        return [pltpu.make_async_copy(a.at[here], to.at[turn, i], out_sem.at[i, core, c]) for i, a in enumerate((ds, vs))]
+
+    def edge_stores(c, core, same, is_end):
+        turn, side = place(c, core)
         here = pl.ds((c * rows + core * half_rows) * 16, (half_rows + 2) * 16)
-        y_slot, z_slot = slots(c, core)
-        return [
-            pltpu.make_async_copy(es.at[0, here], (low_same if same else low_other).at[y_slot], edge_sem.at[0, core, c]),
-            pltpu.make_async_copy(es.at[1, here], (high_same if same else high_other).at[z_slot], edge_sem.at[1, core, c]),
-        ]
-
-    def send(copies, c, core):
-        for same in (True, False):
-            @pl.when((my_core == core) == same)
-            def _():
-                for copy in copies(c, core, same):
-                    copy.start()
+        to = ((ends_other, ends_same) if is_end else (rest_other, rest_same))[same]
+        return [pltpu.make_async_copy(es.at[i, here], to.at[lax.rem(turn, 2), side, i], edge_sem.at[i, core, c]) for i in (0, 1)]
+
+    def send(copies, c, core, test):
+        for same in (0, 1):
+            for kind in (0, 1):
+                @pl.when(((my_core == core) == (same == 1)) & (test(*place(c, core)) == (kind == 1)))
+                def _():
+                    for copy in copies(c, core, same, kind):
+                        copy.start()
+
+    def send_edges(c, core):
+        send(edge_stores, c, core, lambda turn, side: turn >= 2)
+
+    def send_series(c, core):
+        send(stores, c, core, lambda turn, side: side == 1)
 
     def chunk(c, carry):
         @pl.when(c < CHIPS)
@@ -258,16 +259,16 @@
 
             first_pass(c)
             moments(c)
-            send(edge_stores, c, 0)
+            send_edges(c, 0)
 
         @pl.when(c > 0)
         def _():
-            send(edge_stores, c - 1, 1)
+            send_edges(c - 1, 1)
             for copy in loads(c - 1, (3, 4)):
                 copy.wait()
             second_pass(c - 1)
             for core in (0, 1):
-                send(stores, c - 1, core)
+                send_series(c - 1, core)
 
         return carry
 
@@ -275,7 +276,7 @@
 
     def end(c, carry):
         for core in (0, 1):
-            for copy in stores(c, core, True) + edge_stores(c, core, True):
+            for copy in stores(c, core, 1, 1) + edge_stores(c, core, 1, 1):
                 copy.wait()
         return carry
 
@@ -327,8 +328,8 @@
 
 def series(coeffs, u, k, p, cos, sin):
     cells = u.shape[0] // 16
-    share = jax.ShapeDtypeStruct((CHIPS, cells, 128), F32)
-    edge = jax.ShapeDtypeStruct((CHIPS, (cells // COUNT + 2) * 16, 128), F32)
+    share = jax.ShapeDtypeStruct((4, 2, cells // COUNT * 16, 128), F32)
+    edge = jax.ShapeDtypeStruct((2, 2, 2, (cells // COUNT + 2) * 16, 128), F32)
     wide = pltpu.VMEM(((cells + 2) * 16, 128), F32)
     exact = pltpu.VMEM((cells * 16, 128), F32)
     return pl.pallas_call(
@@ -406,20 +407,14 @@
     rows = last_term.shape[1] // COUNT
     me = lax.axis_index("tm")
 
-    d_other, d_same, v_other, v_same, low_other, low_same, high_other, high_same = series(series_coeffs, u, k, p, cos, sin)
-
-    def blocks(same, came, *at):
-        return lax.slice_in_dim(same, *at) + lax.slice_in_dim(came, *at)
-
-    high_came, low_came = to_sibling(high_other), to_sibling(low_other)
-    (high_came, low_came), (d_other, v_other) = after((high_came, low_came), (d_other, v_other))
-    d_came, v_came = to_sibling(d_other), to_sibling(v_other)
-
-    high_far = across(blocks(high_same, high_came, 4, 8))
-    low_two = forth(blocks(low_same, low_came, 4, 6))
-    low_back = back(blocks(low_same, low_came, 6, 8))
-    d_two = forth(blocks(d_same, d_came, 4, 6))
-    d_back = back(blocks(d_same, d_came, 6, 8))
+    outs = series(series_coeffs, u, k, p, cos, sin)
+    far_other, far_same, near_other, near_same, ends_other, ends_same, rest_other, rest_same = outs
+
+    far_came, ends_came = to_sibling(far_other), to_sibling(ends_other)
+    rest_came, near_came = to_sibling(rest_other), to_sibling(near_other)
+    far_came = across(far_same + far_came)
+    ends_two = forth(ends_same[0] + ends_came[0])
+    ends_back = back(ends_same[1] + ends_came[1])
 
     start = me * rows * 16
     k_here = jnp.concatenate(
@@ -431,27 +426,19 @@
     )
     k_low, k_high = lax.ppermute(k_here, "gz", UP), lax.ppermute(k_here, "gz", DOWN)
 
-    low_rest = forth(blocks(low_same, low_came, 2, 4) + low_two)
-    v_sent = blocks(v_same, v_came, 4, 8)
-    (d_two, v_sent, k_low, k_high), high_far = after((d_two, v_sent, k_low, k_high), high_far)
-    v_far = across(v_sent)
-    d_rest = forth(blocks(d_same, d_came, 2, 4) + d_two)
-
-    high = blocks(high_same, high_came, 0, 4) + high_far
-    high_two, high_back = forth(high[2]), back(high[3])
-    low = blocks(low_same, low_came, 0, 2) + low_back + low_rest
-    low_far = across(low[1])
-    high_rest = forth(high[1] + high_two)
-    low = low[0] + low_far
-    high = high[0] + high_back + high_rest
+    ring = forth(rest_same[1] + rest_came[1] + ends_two)
+    (k_low, k_high, near_came), far_came = after((k_low, k_high, near_came), far_came)
+    edge_far = across(rest_same[0, 1] + rest_came[0, 1] + ends_back[1] + ring[1])
+    edge = rest_same[0, 0] + rest_came[0, 0] + ends_back[0] + ring[0] + edge_far
+    low, high = edge[0], edge[1]
     above, below = lax.ppermute(low, "gz", DOWN), lax.ppermute(high, "gz", UP)
 
-    d = blocks(d_same, d_came, 0, 2) + d_back + d_rest
-    d = d[0] + across(d[1])
-    v = blocks(v_same, v_came, 0, 4) + v_far
-    v_two, v_back = forth(v[2]), back(v[3])
-    (above, below), v_two = after((above, below), v_two)
-    v = v[0] + v_back + forth(v[1] + v_two)
+    def both(turn):
+        return near_same[turn] + near_came[turn] + far_came[turn]
+
+    two, direct = forth(both(2)), back(both(3))
+    result = both(0) + direct + forth(both(1) + two)
+    d, v = result[0], result[1]
 
     wide = (a.reshape(rows + 2, *CELL) for a in (low, high, below, above, k_here, k_low, k_high))
     d, v = mend(d.reshape(rows, *CELL), v.reshape(rows, *CELL), *wide)

time: 128 us -> 122 us (0.953)
  the two profiles are of different devices: /device:TPU:102 before, /device:TPU:6 now
where the time goes in v7:
time: 122 us
  waiting for transfers between devices  53.8 us (44%)
  starting transfers between devices  30.1 us (25%)
  Pallas kernels  20.1 us (16%)
  other arithmetic  15.9 us (13%)
    ppermute x4, waiting for transfers between devices, forth(): return lax.ppermute(cells, 'tm', FORTH)  20.1 us
    pallas_call x1, Pallas kernels, series(): pl.pallas_call(series_kernel, out_shape=(share,) * 4 + (edge,) * 4, in_sp...  18.2 us
    ppermute x1, waiting for transfers between devices, local(): lax.ppermute(k_here, 'gz', DOWN)  11.7 us
    ppermute x2, waiting for transfers between devices, local(): above, below = (lax.ppermute(low, 'gz', DOWN), lax.ppermute(high, 'gz', UP))  10.1 us
    ppermute x2, starting transfers between devices, local(): above, below = (lax.ppermute(low, 'gz', DOWN), lax.ppermute(high, 'gz', UP))  7.13 us
    ppermute x2, starting transfers between devices, back(): return lax.ppermute(cells, 'tm', BACK)  6.14 us
    ppermute x1, starting transfers between devices, local(): lax.ppermute(k_here, 'gz', UP)  6 us
    ppermute x1, waiting for transfers between devices, local(): lax.ppermute(k_here, 'gz', UP)  5.69 us
  transfers between devices with their start and end apart: 16, of which 9 were waited for; matrix products, arithmetic and copies ran while one was open for 14% of the time, Pallas kernels for 0%

profile of v7, /device:TPU:6, one launch (start us, length us, event | category | flops | bytes accessed | tf_op | source)
XLA Modules:
  0.0 121.8 jit_solution(8511051360499877046)
XLA Ops:
  0.6 18.2 %shard_map.77 = (f32[4,2,512,128]{3,2,1,0:T(8,128)}, f32[4,2,512,128]{3,2,1,0:T(8,128)}, f32[4,2,512,128]{3,2,1,0:T(8,128)}, f32[4,2,512,128]{3,2,1,0:T(8,128)},...) custom-call(f32[1,4]{1,0:T(1,128)} %coeffs.1, ...), custom_call_target="tpu_custom_call" | custom-call | bytes 47185920 | tf_op jit(solution)/shard_map/pallas_call | solution.py:335
  18.9 0.1 collective-permute-start.9
  19.0 0.5 collective-permute-start.3
  19.5 0.1 collective-permute-start.8
  19.6 4.0 %collective-permute-done.9 = f32[2,2,2,544,128]{4,3,2,1,0:T(8,128)S(1)} collective-permute-done((f32[2,2,2,544,128]{4,3,2,1,0:T(8,128)}, f32[2,2,2,544,128]{4,3,2,1,0:T(8,128)S(1)}, u32[]{:S(2)}, u32[]{:S(2)}) %collective-permute-start.9) | collective-permute-done | bytes 2228256 | tf_op jit(solution)/shard_map/ppermute | solution.py:385
  23.5 3.1 %fusion.3 = (f32[2,2,544,128]{3,2,1,0:T(8,128)S(1)}, f32[2,2,544,128]{3,2,1,0:T(8,128)}) fusion(f32[2,2,2,544,128]{4,3,2,1,0:T(8,128)S(1)} %collective-permute-done.9, f32[2,2,2,544,128]{4,3,2,1,0:T(8,128)} %get-tuple-element.24), kind=kLoop, calls=%fused_computation.6 | loop fusion | flops 557056 | bytes 6684672 | tf_op jit(solution)/shard_map/add | solution.py:417
  26.6 1.6 %collective-permute-start.11 = (f32[2,2,544,128]{3,2,1,0:T(8,128)}, f32[2,2,544,128]{3,2,1,0:T(8,128)}, u32[]{:S(2)}, u32[]{:S(2)}) collective-permute-start(f32[2,2,544,128]{3,2,1,0:T(8,128)} %get-tuple-element.33), channel_id=1, source_target_pairs={{0,16},{8,56},{16,32},{24,8},{32,48},{40,24},{48,0},{56,40},{64,80... | collective-permute-start | bytes 3342344 | tf_op jit(solution)/shard_map/ppermute | solution.py:389
  28.2 1.3 %collective-permute-start.2 = (f32[4,2,512,128]{3,2,1,0:T(8,128)}, f32[4,2,512,128]{3,2,1,0:T(8,128)}, u32[]{:S(2)}, u32[]{:S(2)}) collective-permute-start(f32[4,2,512,128]{3,2,1,0:T(8,128)} %get-tuple-element.17), channel_id=1, source_target_pairs={{0,8},{8,0},{16,24},{24,16},{32,40},{40,32},{48,56},{56,48},{64,72... | collective-permute-start | bytes 6291464 | tf_op jit(solution)/shard_map/ppermute | solution.py:385
  29.5 0.1 collective-permute-done.3
  29.5 0.0 copy-done.1
  29.5 1.5 %add.114 = f32[4,2,512,128]{3,2,1,0:T(8,128)} add(f32[4,2,512,128]{3,2,1,0:T(8,128)S(1)} %copy-done.1, f32[4,2,512,128]{3,2,1,0:T(8,128)S(1)} %collective-permute-done.3) | non-fusion elementwise | flops 524288 | bytes 6291456 | tf_op jit(solution)/shard_map/add | solution.py:415
  31.0 1.9 %collective-permute-start.4 = (f32[4,2,512,128]{3,2,1,0:T(8,128)}, f32[4,2,512,128]{3,2,1,0:T(8,128)}, u32[]{:S(2)}, u32[]{:S(2)}) collective-permute-start(f32[4,2,512,128]{3,2,1,0:T(8,128)} %add.114), channel_id=1, source_target_pairs={{0,64},{8,72},{16,80},{24,88},{32,96},{40,104},{48,112},{56,120},{... | collective-permute-start | bytes 6291464 | tf_op jit(solution)/shard_map/ppermute | solution.py:397
  32.9 3.1 %collective-permute-start.10 = (f32[2,2,544,128]{3,2,1,0:T(8,128)S(1)}, f32[2,2,544,128]{3,2,1,0:T(8,128)}, u32[]{:S(2)}, u32[]{:S(2)}) collective-permute-start(f32[2,2,544,128]{3,2,1,0:T(8,128)S(1)} %get-tuple-element.32), channel_id=1, source_target_pairs={{0,48},{8,24},{16,0},{24,40},{32,16},{40,56},{48,32},{56,8},{64,11... | collective-permute-start | bytes 3342344 | tf_op jit(solution)/shard_map/ppermute | solution.py:393
  36.0 0.0 collective-permute-done.8
  36.0 14.3 %collective-permute-done.11 = f32[2,2,544,128]{3,2,1,0:T(8,128)} collective-permute-done((f32[2,2,544,128]{3,2,1,0:T(8,128)}, f32[2,2,544,128]{3,2,1,0:T(8,128)}, u32[]{:S(2)}, u32[]{:S(2)}) %collective-permute-start.11) | collective-permute-done | bytes 1114144 | tf_op jit(solution)/shard_map/ppermute | solution.py:389
  50.4 0.0 copy-done
  50.4 2.8 %fusion.2 = f32[2,2,544,128]{3,2,1,0:T(8,128)} fusion(f32[2,2,544,128]{3,2,1,0:T(8,128)} %collective-permute-done.11, f32[2,2,2,544,128]{4,3,2,1,0:T(8,128)} %collective-permute-done.8, f32[2,2,2,544,128]{4,3,2,1,0:T(8,128)S(1)} %copy-done), kind=kLoop, calls=%fused_computation.4 | loop fusion | flops 557056 | bytes 4456448 | tf_op jit(solution)/shard_map/add | solution.py:429
  53.1 0.5 collective-permute-start.12
  53.7 0.7 dynamic-slice_select_fusion.1
  54.4 1.0 constant_dynamic-slice_fusion
  55.4 6.0 %collective-permute-start = (f32[544,128]{1,0:T(8,128)S(1)}, f32[544,128]{1,0:T(8,128)S(1)}, u32[]{:S(2)}, u32[]{:S(2)}) collective-permute-start(f32[544,128]{1,0:T(8,128)S(1)} %pad_maximum_fusion), channel_id=1, source_target_pairs={{0,1},{1,2},{2,3},{3,4},{4,5},{5,6},{6,7},{8,9},{9,10},{10,11},{11... | collective-permute-start | bytes 835592 | tf_op jit(solution)/shard_map/ppermute | solution.py:427
  61.4 5.7 %collective-permute-done = f32[544,128]{1,0:T(8,128)S(1)} collective-permute-done((f32[544,128]{1,0:T(8,128)S(1)}, f32[544,128]{1,0:T(8,128)S(1)}, u32[]{:S(2)}, u32[]{:S(2)}) %collective-permute-start) | collective-permute-done | bytes 278560 | tf_op jit(solution)/shard_map/ppermute | solution.py:427
  67.1 1.9 %collective-permute-start.1 = (f32[544,128]{1,0:T(8,128)S(1)}, f32[544,128]{1,0:T(8,128)S(1)}, u32[]{:S(2)}, u32[]{:S(2)}) collective-permute-start(f32[544,128]{1,0:T(8,128)S(1)} %pad_maximum_fusion), channel_id=1, source_target_pairs={{1,0},{2,1},{3,2},{4,3},{5,4},{6,5},{7,6},{9,8},{10,9},{11,10},{12... | collective-permute-start | bytes 835592 | tf_op jit(solution)/shard_map/ppermute | solution.py:427
  69.0 11.7 %collective-permute-done.1 = f32[544,128]{1,0:T(8,128)S(1)} collective-permute-done((f32[544,128]{1,0:T(8,128)S(1)}, f32[544,128]{1,0:T(8,128)S(1)}, u32[]{:S(2)}, u32[]{:S(2)}) %collective-permute-start.1) | collective-permute-done | bytes 278560 | tf_op jit(solution)/shard_map/ppermute | solution.py:427
  80.7 0.0 collective-permute-done.2
  80.7 0.0 collective-permute-done.4
  80.7 2.0 %add_bitcast_fusion.1 = (f32[2,512,128]{2,1,0:T(8,128)S(1)}, f32[2,512,128]{2,1,0:T(8,128)S(1)}) fusion(f32[4,2,512,128]{3,2,1,0:T(8,128)} %collective-permute-done.4, f32[4,2,512,128]{3,2,1,0:T(8,128)} %collective-permute-done.2, f32[4,2,512,128]{3,2,1,0:T(8,128)} %get-tuple-element.16), kind=kLoop, calls=%fused_computation.24 | loop fusion | flops 524288 | bytes 4194304 | tf_op jit(solution)/shard_map/add | solution.py:437
  82.7 0.0 copy-start.2
  82.7 0.1 collective-permute-start.6
  82.8 0.0 collective-permute-done.10
  82.8 0.0 collective-permute-done.12
  82.8 1.6 %fusion.4 = f32[2,544,128]{2,1,0:T(8,128)S(1)} fusion(f32[2,2,544,128]{3,2,1,0:T(8,128)} %collective-permute-done.12, f32[2,2,544,128]{3,2,1,0:T(8,128)} %collective-permute-done.10, f32[2,2,2,544,128]{4,3,2,1,0:T(8,128)} %collective-permute-done.8, f32[2,2,2,544,128]{4,3,2,1,0:T(8,128)S(1)} %copy-done), kind=kLoop, calls=%fused_computation.8 | loop fusion | flops 417792 | bytes 2785280 | tf_op jit(solution)/shard_map/add | solution.py:431
  84.4 2.7 %collective-permute-start.13 = (f32[2,544,128]{2,1,0:T(8,128)S(1)}, f32[2,544,128]{2,1,0:T(8,128)S(1)}, u32[]{:S(2)}, u32[]{:S(2)}) collective-permute-start(f32[2,544,128]{2,1,0:T(8,128)S(1)} %fusion.4), channel_id=1, source_target_pairs={{0,64},{8,72},{16,80},{24,88},{32,96},{40,104},{48,112},{56,120},{... | collective-permute-start | bytes 1671176 | tf_op jit(solution)/shard_map/ppermute | solution.py:397
  87.2 3.1 %collective-permute-start.5 = (f32[2,512,128]{2,1,0:T(8,128)S(1)}, f32[2,512,128]{2,1,0:T(8,128)S(1)}, u32[]{:S(2)}, u32[]{:S(2)}) collective-permute-start(f32[2,512,128]{2,1,0:T(8,128)S(1)} %get-tuple-element.30), channel_id=1, source_target_pairs={{0,48},{8,24},{16,0},{24,40},{32,16},{40,56},{48,32},{56,8},{64,11... | collective-permute-start | bytes 1572872 | tf_op jit(solution)/shard_map/ppermute | solution.py:393
  90.3 5.7 %collective-permute-done.6 = f32[2,512,128]{2,1,0:T(8,128)S(1)} collective-permute-done((f32[2,512,128]{2,1,0:T(8,128)S(1)}, f32[2,512,128]{2,1,0:T(8,128)S(1)}, u32[]{:S(2)}, u32[]{:S(2)}) %collective-permute-start.6) | collective-permute-done | bytes 524320 | tf_op jit(solution)/shard_map/ppermute | solution.py:389
  96.0 1.3 %bitcast_add_fusion = f32[2,512,128]{2,1,0:T(8,128)S(1)} fusion(f32[2,512,128]{2,1,0:T(8,128)S(1)} %collective-permute-done.6, f32[4,2,512,128]{3,2,1,0:T(8,128)} %collective-permute-done.4, f32[4,2,512,128]{3,2,1,0:T(8,128)} %collective-permute-done.2, f32[4,2,512,128]{3,2,1,0:T(8,128)S(1)} %copy-done.2), kind=kLoop, calls=%fused_computation.20 | loop fusion | flops 393216 | bytes 2621440 | tf_op jit(solution)/shard_map/add | solution.py:440
  97.3 0.1 collective-permute-start.7
  97.4 2.3 %collective-permute-done.13 = f32[2,544,128]{2,1,0:T(8,128)S(1)} collective-permute-done((f32[2,544,128]{2,1,0:T(8,128)S(1)}, f32[2,544,128]{2,1,0:T(8,128)S(1)}, u32[]{:S(2)}, u32[]{:S(2)}) %collective-permute-start.13) | collective-permute-done | bytes 557088 | tf_op jit(solution)/shard_map/ppermute | solution.py:397
  99.7 1.5 %fusion.8 = f32[2,544,128]{2,1,0:T(8,128)S(1)} fusion(f32[2,544,128]{2,1,0:T(8,128)S(1)} %collective-permute-done.13, f32[2,2,544,128]{3,2,1,0:T(8,128)} %collective-permute-done.12, f32[2,2,544,128]{3,2,1,0:T(8,128)} %collective-permute-done.10, f32[2,2,2,544,128]{4,3,2,1,0:T(8,128)} %collective-permute-done.8, f32[2,2,2,544,128]{4,3,2,1,0:T(8,128)S(1)} %copy-done), kind=kLoop, calls=%fused_computation.15 | loop fusion | flops 557056 | bytes 3342336 | tf_op jit(solution)/shard_map/add | solution.py:432
  101.2 0.1 slice_bitcast_fusion.5
  101.3 5.2 %collective-permute-start.14 = (f32[544,128]{1,0:T(8,128)S(1)}, f32[544,128]{1,0:T(8,128)S(1)}, u32[]{:S(2)}, u32[]{:S(2)}) collective-permute-start(f32[544,128]{1,0:T(8,128)S(1)} %get-tuple-element.37), channel_id=1, source_target_pairs={{0,1},{1,2},{2,3},{3,4},{4,5},{5,6},{6,7},{8,9},{9,10},{10,11},{11... | collective-permute-start | bytes 835592 | tf_op jit(solution)/shard_map/ppermute | solution.py:434
  106.5 1.9 %collective-permute-start.15 = (f32[544,128]{1,0:T(8,128)S(1)}, f32[544,128]{1,0:T(8,128)S(1)}, u32[]{:S(2)}, u32[]{:S(2)}) collective-permute-start(f32[544,128]{1,0:T(8,128)S(1)} %get-tuple-element.36), channel_id=1, source_target_pairs={{1,0},{2,1},{3,2},{4,3},{5,4},{6,5},{7,6},{9,8},{10,9},{11,10},{12... | collective-permute-start | bytes 835592 | tf_op jit(solution)/shard_map/ppermute | solution.py:434
  108.5 0.0 collective-permute-done.5
  108.5 0.0 collective-permute-done.7
  108.5 1.4 %fusion.11 = f32[2,512,128]{2,1,0:T(8,128)S(1)} fusion(f32[2,512,128]{2,1,0:T(8,128)S(1)} %collective-permute-done.7, f32[2,512,128]{2,1,0:T(8,128)S(1)} %collective-permute-done.5, f32[4,2,512,128]{3,2,1,0:T(8,128)} %collective-permute-done.4, f32[4,2,512,128]{3,2,1,0:T(8,128)} %collective-permute-done.2, f32[4,2,512,128]{3,2,1,0:T(8,128)S(1)} %copy-done.2), kind=kLoop, calls=%fused_computation.22 | loop fusion | flops 524288 | bytes 3145728 | tf_op jit(solution)/shard_map/add | solution.py:440
  109.9 2.3 %collective-permute-done.14 = f32[544,128]{1,0:T(8,128)S(1)} collective-permute-done((f32[544,128]{1,0:T(8,128)S(1)}, f32[544,128]{1,0:T(8,128)S(1)}, u32[]{:S(2)}, u32[]{:S(2)}) %collective-permute-start.14) | collective-permute-done | bytes 278560 | tf_op jit(solution)/shard_map/ppermute | solution.py:434
  112.2 7.7 %collective-permute-done.15 = f32[544,128]{1,0:T(8,128)S(1)} collective-permute-done((f32[544,128]{1,0:T(8,128)S(1)}, f32[544,128]{1,0:T(8,128)S(1)}, u32[]{:S(2)}, u32[]{:S(2)}) %collective-permute-start.15) | collective-permute-done | bytes 278560 | tf_op jit(solution)/shard_map/ppermute | solution.py:434
  120.0 1.9 %shard_map.78 = (f32[32,2,8,128]{3,2,1,0:T(8,128)}, f32[32,2,8,128]{3,2,1,0:T(8,128)}) custom-call(f32[32,2,8,128]{3,2,1,0:T(8,128)S(1)} %bitcast.100, f32[32,2,8,128]{3,2,1,0:T(8,128)S(1)} %bitcast.99, f32[34,2,8,128]{3,2,1,0:T(8,128)S(1)} %bitcast.97, f32[34,2,8,128]{3,2,1,0:T(8,128)S(1)} %bitcast.96, f32[34,2,8,128]{3,2,1,0:T(8,128)S(1)} %bitcast.103, ...), custom_call_target="tpu_custom_call" | custom-call | bytes 4194304 | tf_op jit(solution)/shard_map/pallas_call | solution.py:355
  (5 shorter events, 0.1 us)
Async XLA Ops:
  18.9 4.6 %collective-permute-start.9 = (f32[2,2,2,544,128]{4,3,2,1,0:T(8,128)}, f32[2,2,2,544,128]{4,3,2,1,0:T(8,128)S(1)}, u32[]{:S(2)}, u32[]{:S(2)}) collective-permute-start(f32[2,2,2,544,128]{4,3,2,1,0:T(8,128)} %get-tuple-element.25), channel_id=1, source_target_pairs={{0,8},{8,0},{16,24},{24,16},{32,40},{40,32},{48,56},{56,48},{64,72... | collective-permute-start | bytes 6684680 | tf_op jit(solution)/shard_map/ppermute | solution.py:385
  19.0 10.5 %collective-permute-start.3 = (f32[4,2,512,128]{3,2,1,0:T(8,128)}, f32[4,2,512,128]{3,2,1,0:T(8,128)S(1)}, u32[]{:S(2)}, u32[]{:S(2)}) collective-permute-start(f32[4,2,512,128]{3,2,1,0:T(8,128)} %get-tuple-element.19), channel_id=1, source_target_pairs={{0,8},{8,0},{16,24},{24,16},{32,40},{40,32},{48,56},{56,48},{64,72... | collective-permute-start | bytes 6291464 | tf_op jit(solution)/shard_map/ppermute | solution.py:385
  19.5 16.5 %collective-permute-start.8 = (f32[2,2,2,544,128]{4,3,2,1,0:T(8,128)}, f32[2,2,2,544,128]{4,3,2,1,0:T(8,128)}, u32[]{:S(2)}, u32[]{:S(2)}) collective-permute-start(f32[2,2,2,544,128]{4,3,2,1,0:T(8,128)} %get-tuple-element.23), channel_id=1, source_target_pairs={{0,8},{8,0},{16,24},{24,16},{32,40},{40,32},{48,56},{56,48},{64,72... | collective-permute-start | bytes 6684680 | tf_op jit(solution)/shard_map/ppermute | solution.py:385
  23.5 6.0 %copy-start.1 = (f32[4,2,512,128]{3,2,1,0:T(8,128)S(1)}, f32[4,2,512,128]{3,2,1,0:T(8,128)}, u32[]{:S(2)}) copy-start(f32[4,2,512,128]{3,2,1,0:T(8,128)} %get-tuple-element.18) | copy-start | bytes 6291460
  26.6 23.8 %collective-permute-start.11 = (f32[2,2,544,128]{3,2,1,0:T(8,128)}, f32[2,2,544,128]{3,2,1,0:T(8,128)}, u32[]{:S(2)}, u32[]{:S(2)}) collective-permute-start(f32[2,2,544,128]{3,2,1,0:T(8,128)} %get-tuple-element.33), channel_id=1, source_target_pairs={{0,16},{8,56},{16,32},{24,8},{32,48},{40,24},{48,0},{56,40},{64,80... | collective-permute-start | bytes 3342344 | tf_op jit(solution)/shard_map/ppermute | solution.py:389
  28.2 52.5 %collective-permute-start.2 = (f32[4,2,512,128]{3,2,1,0:T(8,128)}, f32[4,2,512,128]{3,2,1,0:T(8,128)}, u32[]{:S(2)}, u32[]{:S(2)}) collective-permute-start(f32[4,2,512,128]{3,2,1,0:T(8,128)} %get-tuple-element.17), channel_id=1, source_target_pairs={{0,8},{8,0},{16,24},{24,16},{32,40},{40,32},{48,56},{56,48},{64,72... | collective-permute-start | bytes 6291464 | tf_op jit(solution)/shard_map/ppermute | solution.py:385
  29.5 20.8 %copy-start = (f32[2,2,2,544,128]{4,3,2,1,0:T(8,128)S(1)}, f32[2,2,2,544,128]{4,3,2,1,0:T(8,128)}, u32[]{:S(2)}) copy-start(f32[2,2,2,544,128]{4,3,2,1,0:T(8,128)} %get-tuple-element.22) | copy-start | bytes 6684676
  31.0 49.6 %collective-permute-start.4 = (f32[4,2,512,128]{3,2,1,0:T(8,128)}, f32[4,2,512,128]{3,2,1,0:T(8,128)}, u32[]{:S(2)}, u32[]{:S(2)}) collective-permute-start(f32[4,2,512,128]{3,2,1,0:T(8,128)} %add.114), channel_id=1, source_target_pairs={{0,64},{8,72},{16,80},{24,88},{32,96},{40,104},{48,112},{56,120},{... | collective-permute-start | bytes 6291464 | tf_op jit(solution)/shard_map/ppermute | solution.py:397
  32.9 49.9 %collective-permute-start.10 = (f32[2,2,544,128]{3,2,1,0:T(8,128)S(1)}, f32[2,2,544,128]{3,2,1,0:T(8,128)}, u32[]{:S(2)}, u32[]{:S(2)}) collective-permute-start(f32[2,2,544,128]{3,2,1,0:T(8,128)S(1)} %get-tuple-element.32), channel_id=1, source_target_pairs={{0,48},{8,24},{16,0},{24,40},{32,16},{40,56},{48,32},{56,8},{64,11... | collective-permute-start | bytes 3342344 | tf_op jit(solution)/shard_map/ppermute | solution.py:393
  53.1 29.7 %collective-permute-start.12 = (f32[2,2,544,128]{3,2,1,0:T(8,128)}, f32[2,2,544,128]{3,2,1,0:T(8,128)}, u32[]{:S(2)}, u32[]{:S(2)}) collective-permute-start(f32[2,2,544,128]{3,2,1,0:T(8,128)} %fusion.2), channel_id=1, source_target_pairs={{0,16},{8,56},{16,32},{24,8},{32,48},{40,24},{48,0},{56,40},{64,80... | collective-permute-start | bytes 3342344 | tf_op jit(solution)/shard_map/ppermute | solution.py:389
  55.4 11.7 %collective-permute-start = (f32[544,128]{1,0:T(8,128)S(1)}, f32[544,128]{1,0:T(8,128)S(1)}, u32[]{:S(2)}, u32[]{:S(2)}) collective-permute-start(f32[544,128]{1,0:T(8,128)S(1)} %pad_maximum_fusion), channel_id=1, source_target_pairs={{0,1},{1,2},{2,3},{3,4},{4,5},{5,6},{6,7},{8,9},{9,10},{10,11},{11... | collective-permute-start | bytes 835592 | tf_op jit(solution)/shard_map/ppermute | solution.py:427
  67.1 13.6 %collective-permute-start.1 = (f32[544,128]{1,0:T(8,128)S(1)}, f32[544,128]{1,0:T(8,128)S(1)}, u32[]{:S(2)}, u32[]{:S(2)}) collective-permute-start(f32[544,128]{1,0:T(8,128)S(1)} %pad_maximum_fusion), channel_id=1, source_target_pairs={{1,0},{2,1},{3,2},{4,3},{5,4},{6,5},{7,6},{9,8},{10,9},{11,10},{12... | collective-permute-start | bytes 835592 | tf_op jit(solution)/shard_map/ppermute | solution.py:427
  82.7 13.3 %copy-start.2 = (f32[4,2,512,128]{3,2,1,0:T(8,128)S(1)}, f32[4,2,512,128]{3,2,1,0:T(8,128)}, u32[]{:S(2)}) copy-start(f32[4,2,512,128]{3,2,1,0:T(8,128)} %get-tuple-element.16) | copy-start | bytes 6291460
  82.7 13.3 %collective-permute-start.6 = (f32[2,512,128]{2,1,0:T(8,128)S(1)}, f32[2,512,128]{2,1,0:T(8,128)S(1)}, u32[]{:S(2)}, u32[]{:S(2)}) collective-permute-start(f32[2,512,128]{2,1,0:T(8,128)S(1)} %get-tuple-element.31), channel_id=1, source_target_pairs={{0,16},{8,56},{16,32},{24,8},{32,48},{40,24},{48,0},{56,40},{64,80... | collective-permute-start | bytes 1572872 | tf_op jit(solution)/shard_map/ppermute | solution.py:389
  84.4 15.3 %collective-permute-start.13 = (f32[2,544,128]{2,1,0:T(8,128)S(1)}, f32[2,544,128]{2,1,0:T(8,128)S(1)}, u32[]{:S(2)}, u32[]{:S(2)}) collective-permute-start(f32[2,544,128]{2,1,0:T(8,128)S(1)} %fusion.4), channel_id=1, source_target_pairs={{0,64},{8,72},{16,80},{24,88},{32,96},{40,104},{48,112},{56,120},{... | collective-permute-start | bytes 1671176 | tf_op jit(solution)/shard_map/ppermute | solution.py:397
  87.2 21.3 %collective-permute-start.5 = (f32[2,512,128]{2,1,0:T(8,128)S(1)}, f32[2,512,128]{2,1,0:T(8,128)S(1)}, u32[]{:S(2)}, u32[]{:S(2)}) collective-permute-start(f32[2,512,128]{2,1,0:T(8,128)S(1)} %get-tuple-element.30), channel_id=1, source_target_pairs={{0,48},{8,24},{16,0},{24,40},{32,16},{40,56},{48,32},{56,8},{64,11... | collective-permute-start | bytes 1572872 | tf_op jit(solution)/shard_map/ppermute | solution.py:393
  97.3 11.1 %collective-permute-start.7 = (f32[2,512,128]{2,1,0:T(8,128)S(1)}, f32[2,512,128]{2,1,0:T(8,128)S(1)}, u32[]{:S(2)}, u32[]{:S(2)}) collective-permute-start(f32[2,512,128]{2,1,0:T(8,128)S(1)} %bitcast_add_fusion), channel_id=1, source_target_pairs={{0,16},{8,56},{16,32},{24,8},{32,48},{40,24},{48,0},{56,40},{64,80... | collective-permute-start | bytes 1572872 | tf_op jit(solution)/shard_map/ppermute | solution.py:389
  101.3 10.9 %collective-permute-start.14 = (f32[544,128]{1,0:T(8,128)S(1)}, f32[544,128]{1,0:T(8,128)S(1)}, u32[]{:S(2)}, u32[]{:S(2)}) collective-permute-start(f32[544,128]{1,0:T(8,128)S(1)} %get-tuple-element.37), channel_id=1, source_target_pairs={{0,1},{1,2},{2,3},{3,4},{4,5},{5,6},{6,7},{8,9},{9,10},{10,11},{11... | collective-permute-start | bytes 835592 | tf_op jit(solution)/shard_map/ppermute | solution.py:434
  106.5 13.4 %collective-permute-start.15 = (f32[544,128]{1,0:T(8,128)S(1)}, f32[544,128]{1,0:T(8,128)S(1)}, u32[]{:S(2)}, u32[]{:S(2)}) collective-permute-start(f32[544,128]{1,0:T(8,128)S(1)} %get-tuple-element.36), channel_id=1, source_target_pairs={{1,0},{2,1},{3,2},{4,3},{5,4},{6,5},{7,6},{9,8},{10,9},{11,10},{12... | collective-permute-start | bytes 835592 | tf_op jit(solution)/shard_map/ppermute | solution.py:434

commit v8 on v7

--- a/solution.py
+++ b/solution.py
@@ -410,10 +410,12 @@
     outs = series(series_coeffs, u, k, p, cos, sin)
     far_other, far_same, near_other, near_same, ends_other, ends_same, rest_other, rest_same = outs
 
-    far_came, ends_came = to_sibling(far_other), to_sibling(ends_other)
+    ends_came, far_came = to_sibling(ends_other), to_sibling(far_other)
     rest_came, near_came = to_sibling(rest_other), to_sibling(near_other)
-    far_came = across(far_same + far_came)
     ends_two = forth(ends_same[0] + ends_came[0])
+    far_ends = far_same[2:] + far_came[2:]
+    far_ends, ends_came = after(far_ends, ends_came)
+    far_ends_came, far_rest_came = across(far_ends), across(far_same[:2] + far_came[:2])
     ends_back = back(ends_same[1] + ends_came[1])
 
     start = me * rows * 16
@@ -427,17 +429,19 @@
     k_low, k_high = lax.ppermute(k_here, "gz", UP), lax.ppermute(k_here, "gz", DOWN)
 
     ring = forth(rest_same[1] + rest_came[1] + ends_two)
-    (k_low, k_high, near_came), far_came = after((k_low, k_high, near_came), far_came)
-    edge_far = across(rest_same[0, 1] + rest_came[0, 1] + ends_back[1] + ring[1])
+    two, direct = (near_same[t] + near_came[t] + far_ends_came[t - 2] for t in (2, 3))
+    (two, direct, k_low, k_high), ring = after((two, direct, k_low, k_high), ring)
+    two, direct = forth(two), back(direct)
+    edge_far = rest_same[0, 1] + rest_came[0, 1] + ends_back[1] + ring[1]
+    edge_far, far_rest_came = after(edge_far, far_rest_came)
+    edge_far = across(edge_far)
+    last = near_same[1] + near_came[1] + far_rest_came[1] + two
+    last, edge_far = after(last, edge_far)
+    last = forth(last)
     edge = rest_same[0, 0] + rest_came[0, 0] + ends_back[0] + ring[0] + edge_far
     low, high = edge[0], edge[1]
     above, below = lax.ppermute(low, "gz", DOWN), lax.ppermute(high, "gz", UP)
-
-    def both(turn):
-        return near_same[turn] + near_came[turn] + far_came[turn]
-
-    two, direct = forth(both(2)), back(both(3))
-    result = both(0) + direct + forth(both(1) + two)
+    result = near_same[0] + near_came[0] + far_rest_came[0] + direct + last
     d, v = result[0], result[1]
 
     wide = (a.reshape(rows + 2, *CELL) for a in (low, high, below, above, k_here, k_low, k_high))

time: 122 us -> 114 us (0.934)
  waiting for transfers between devices: 53.8 us -> 49.5 us
  other arithmetic: 15.9 us -> 13 us
    ppermute x2 -> x3, waiting for transfers between devices: 2.29 us -> 7.95 us  [across(): return lax.ppermute(cells, 'tm', ACROSS)]
    ppermute x1, waiting for transfers between devices: 5.69 us -> 0.2 us  [local(): lax.ppermute(k_here, 'gz', UP)]
    ppermute x1, waiting for transfers between devices: 11.7 us -> 7.84 us  [local(): lax.ppermute(k_here, 'gz', DOWN)]
    add x1, other arithmetic: 3.08 us -> 0.22 us  [local(): ends_back = back(ends_same[1] + ends_came[1])]
    ppermute x2, starting transfers between devices: 6.14 us -> 3.76 us  [back(): return lax.ppermute(cells, 'tm', BACK)]
    ppermute x2, waiting for transfers between devices: 10.1 us -> 8.45 us  [local(): above, below = (lax.ppermute(low, 'gz', DOWN), lax.ppermute(high, 'gz', UP))]
    add x5, other arithmetic: 7.82 us -> 9.39 us  [the longest x1 3.2 us: local(): far_same[:2] + far_came[:2]]
    add x1, other arithmetic: 2.78 us -> 1.23 us  [local(): ring = forth(rest_same[1] + rest_came[1] + ends_two)]
  transfers between devices with their start and end apart: 16 -> 17, of which waited for: 9 -> 11; matrix products, arithmetic and copies ran while one was open for 14% -> 12% of each run, Pallas kernels for 0% -> 0%
where the time goes in v8:
time: 114 us
  waiting for transfers between devices  49.5 us (43%)
  starting transfers between devices  29.2 us (26%)
  Pallas kernels  20.1 us (18%)
  other arithmetic  13 us (11%)
    ppermute x4, waiting for transfers between devices, forth(): return lax.ppermute(cells, 'tm', FORTH)  21.3 us
    pallas_call x1, Pallas kernels, series(): pl.pallas_call(series_kernel, out_shape=(share,) * 4 + (edge,) * 4, in_sp...  18.3 us
    ppermute x2, waiting for transfers between devices, local(): above, below = (lax.ppermute(low, 'gz', DOWN), lax.ppermute(high, 'gz', UP))  8.45 us
    ppermute x3, waiting for transfers between devices, across(): return lax.ppermute(cells, 'tm', ACROSS)  7.95 us
    ppermute x1, waiting for transfers between devices, local(): lax.ppermute(k_here, 'gz', DOWN)  7.84 us
    ppermute x2, starting transfers between devices, local(): above, below = (lax.ppermute(low, 'gz', DOWN), lax.ppermute(high, 'gz', UP))  7.3 us
    ppermute x3, starting transfers between devices, across(): return lax.ppermute(cells, 'tm', ACROSS)  5.54 us
    ppermute x1, starting transfers between devices, local(): lax.ppermute(k_here, 'gz', UP)  5.41 us
  transfers between devices with their start and end apart: 17, of which 11 were waited for; matrix products, arithmetic and copies ran while one was open for 12% of the time, Pallas kernels for 0%

profile of v8, /device:TPU:6, one launch (start us, length us, event | category | flops | bytes accessed | tf_op | source)
XLA Modules:
  0.0 113.7 jit_solution(3371070234378971336)
XLA Ops:
  0.6 18.3 %shard_map.77 = (f32[4,2,512,128]{3,2,1,0:T(8,128)}, f32[4,2,512,128]{3,2,1,0:T(8,128)}, f32[4,2,512,128]{3,2,1,0:T(8,128)}, f32[4,2,512,128]{3,2,1,0:T(8,128)},...) custom-call(f32[1,4]{1,0:T(1,128)} %coeffs.1, ...), custom_call_target="tpu_custom_call" | custom-call | bytes 47185920 | tf_op jit(solution)/shard_map/pallas_call | solution.py:335
  18.9 0.1 collective-permute-start.2
  19.0 0.5 collective-permute-start.3
  19.5 0.1 collective-permute-start.1
  19.6 3.8 %collective-permute-done.2 = f32[4,2,512,128]{3,2,1,0:T(8,128)S(1)} collective-permute-done((f32[4,2,512,128]{3,2,1,0:T(8,128)}, f32[4,2,512,128]{3,2,1,0:T(8,128)S(1)}, u32[]{:S(2)}, u32[]{:S(2)}) %collective-permute-start.2) | collective-permute-done | bytes 2097184 | tf_op jit(solution)/shard_map/ppermute | solution.py:385
  23.4 3.2 %slice_add_fusion.2 = (f32[2,2,512,128]{3,2,1,0:T(8,128)}, f32[2,2,512,128]{3,2,1,0:T(8,128)}) fusion(f32[4,2,512,128]{3,2,1,0:T(8,128)S(1)} %collective-permute-done.2, f32[4,2,512,128]{3,2,1,0:T(8,128)} %get-tuple-element.28), kind=kLoop, calls=%fused_computation.6 | loop fusion | flops 524288 | bytes 6291456 | tf_op jit(solution)/shard_map/add | solution.py:418
  26.6 0.0 collective-permute-done.3
  26.6 0.0 copy-done.3
  26.6 0.2 add_bitcast_fusion
  26.8 1.6 %collective-permute-start.8 = (f32[2,2,544,128]{3,2,1,0:T(8,128)S(1)}, f32[2,2,544,128]{3,2,1,0:T(8,128)S(1)}, u32[]{:S(2)}, u32[]{:S(2)}) collective-permute-start(f32[2,2,544,128]{3,2,1,0:T(8,128)S(1)} %get-tuple-element.51), channel_id=1, source_target_pairs={{0,16},{8,56},{16,32},{24,8},{32,48},{40,24},{48,0},{56,40},{64,80... | collective-permute-start | bytes 3342344 | tf_op jit(solution)/shard_map/ppermute | solution.py:389
  28.4 1.2 %collective-permute-start = (f32[4,2,512,128]{3,2,1,0:T(8,128)}, f32[4,2,512,128]{3,2,1,0:T(8,128)}, u32[]{:S(2)}, u32[]{:S(2)}) collective-permute-start(f32[4,2,512,128]{3,2,1,0:T(8,128)} %get-tuple-element.24), channel_id=1, source_target_pairs={{0,8},{8,0},{16,24},{24,16},{32,40},{40,32},{48,56},{56,48},{64,72... | collective-permute-start | bytes 6291464 | tf_op jit(solution)/shard_map/ppermute | solution.py:385
  29.7 1.9 %collective-permute-start.5 = (f32[2,2,512,128]{3,2,1,0:T(8,128)}, f32[2,2,512,128]{3,2,1,0:T(8,128)}, u32[]{:S(2)}, u32[]{:S(2)}) collective-permute-start(f32[2,2,512,128]{3,2,1,0:T(8,128)} %get-tuple-element.32), channel_id=1, source_target_pairs={{0,64},{8,72},{16,80},{24,88},{32,96},{40,104},{48,112},{56,120},{... | collective-permute-start | bytes 3145736 | tf_op jit(solution)/shard_map/ppermute | solution.py:397
  31.6 0.0 collective-permute-done.1
  31.6 12.0 %collective-permute-done.8 = f32[2,2,544,128]{3,2,1,0:T(8,128)S(1)} collective-permute-done((f32[2,2,544,128]{3,2,1,0:T(8,128)S(1)}, f32[2,2,544,128]{3,2,1,0:T(8,128)S(1)}, u32[]{:S(2)}, u32[]{:S(2)}) %collective-permute-start.8) | collective-permute-done | bytes 1114144 | tf_op jit(solution)/shard_map/ppermute | solution.py:389
  43.6 1.2 %fusion.2 = f32[2,2,544,128]{3,2,1,0:T(8,128)} fusion(f32[2,2,544,128]{3,2,1,0:T(8,128)S(1)} %collective-permute-done.8, f32[2,2,2,544,128]{4,3,2,1,0:T(8,128)S(1)} %collective-permute-done.1, f32[2,2,2,544,128]{4,3,2,1,0:T(8,128)S(1)} %copy-done), kind=kLoop, calls=%fused_computation.4 | loop fusion | flops 557056 | bytes 4456448 | tf_op jit(solution)/shard_map/add | solution.py:431
  44.8 0.4 collective-permute-start.9
  45.2 2.9 %collective-permute-start.4 = (f32[2,2,544,128]{3,2,1,0:T(8,128)S(1)}, f32[2,2,544,128]{3,2,1,0:T(8,128)}, u32[]{:S(2)}, u32[]{:S(2)}) collective-permute-start(f32[2,2,544,128]{3,2,1,0:T(8,128)S(1)} %get-tuple-element.50), channel_id=1, source_target_pairs={{0,48},{8,24},{16,0},{24,40},{32,16},{40,56},{48,32},{56,8},{64,11... | collective-permute-start | bytes 3342344 | tf_op jit(solution)/shard_map/ppermute | solution.py:393
  48.0 1.9 %collective-permute-start.10 = (f32[2,2,512,128]{3,2,1,0:T(8,128)}, f32[2,2,512,128]{3,2,1,0:T(8,128)}, u32[]{:S(2)}, u32[]{:S(2)}) collective-permute-start(f32[2,2,512,128]{3,2,1,0:T(8,128)} %get-tuple-element.46), channel_id=1, source_target_pairs={{0,64},{8,72},{16,80},{24,88},{32,96},{40,104},{48,112},{56,120},{... | collective-permute-start | bytes 3145736 | tf_op jit(solution)/shard_map/ppermute | solution.py:397
  49.9 0.7 dynamic-slice_select_fusion.1
  50.7 1.0 constant_dynamic-slice_fusion
  51.7 0.0 collective-permute-done
  51.7 5.4 %collective-permute-start.6 = (f32[544,128]{1,0:T(8,128)S(1)}, f32[544,128]{1,0:T(8,128)S(1)}, u32[]{:S(2)}, u32[]{:S(2)}) collective-permute-start(f32[544,128]{1,0:T(8,128)S(1)} %pad_maximum_fusion), channel_id=1, source_target_pairs={{0,1},{1,2},{2,3},{3,4},{4,5},{5,6},{6,7},{8,9},{9,10},{10,11},{11... | collective-permute-start | bytes 835592 | tf_op jit(solution)/shard_map/ppermute | solution.py:429
  57.1 0.0 collective-permute-done.5
  57.1 1.9 %collective-permute-start.7 = (f32[544,128]{1,0:T(8,128)S(1)}, f32[544,128]{1,0:T(8,128)S(1)}, u32[]{:S(2)}, u32[]{:S(2)}) collective-permute-start(f32[544,128]{1,0:T(8,128)S(1)} %pad_maximum_fusion), channel_id=1, source_target_pairs={{1,0},{2,1},{3,2},{4,3},{5,4},{6,5},{7,6},{9,8},{10,9},{11,10},{12... | collective-permute-start | bytes 835592 | tf_op jit(solution)/shard_map/ppermute | solution.py:429
  59.0 2.1 %fusion.13 = (f32[2,512,128]{2,1,0:T(8,128)S(1)}, f32[2,512,128]{2,1,0:T(8,128)S(1)}) fusion(f32[2,2,512,128]{3,2,1,0:T(8,128)} %collective-permute-done.5, f32[4,2,512,128]{3,2,1,0:T(8,128)} %collective-permute-done, f32[4,2,512,128]{3,2,1,0:T(8,128)} %get-tuple-element.23), kind=kLoop, calls=%fused_computation.24 | loop fusion | flops 524288 | bytes 4194304 | tf_op jit(solution)/shard_map/add | solution.py:432
  61.2 0.2 collective-permute-done.6
  61.4 7.8 %collective-permute-done.7 = f32[544,128]{1,0:T(8,128)S(1)} collective-permute-done((f32[544,128]{1,0:T(8,128)S(1)}, f32[544,128]{1,0:T(8,128)S(1)}, u32[]{:S(2)}, u32[]{:S(2)}) %collective-permute-start.7) | collective-permute-done | bytes 278560 | tf_op jit(solution)/shard_map/ppermute | solution.py:429
  69.2 4.1 %collective-permute-done.9 = f32[2,2,544,128]{3,2,1,0:T(8,128)} collective-permute-done((f32[2,2,544,128]{3,2,1,0:T(8,128)}, f32[2,2,544,128]{3,2,1,0:T(8,128)}, u32[]{:S(2)}, u32[]{:S(2)}) %collective-permute-start.9) | collective-permute-done | bytes 1114144 | tf_op jit(solution)/shard_map/ppermute | solution.py:389
  73.4 0.0 collective-permute-start.12
  73.4 0.0 collective-permute-done.4
  73.4 1.3 %fusion.8 = f32[2,544,128]{2,1,0:T(8,128)S(1)} fusion(f32[2,2,544,128]{3,2,1,0:T(8,128)} %collective-permute-done.4, f32[2,2,2,544,128]{4,3,2,1,0:T(8,128)S(1)} %copy-done.2, f32[2,2,544,128]{3,2,1,0:T(8,128)} %collective-permute-done.9, f32[2,2,2,544,128]{4,3,2,1,0:T(8,128)S(1)} %copy-done), kind=kLoop, calls=%fused_computation.16 | loop fusion | flops 417792 | bytes 2785280 | tf_op jit(solution)/shard_map/add | solution.py:435
  74.7 3.0 %collective-permute-done.10 = f32[2,2,512,128]{3,2,1,0:T(8,128)} collective-permute-done((f32[2,2,512,128]{3,2,1,0:T(8,128)}, f32[2,2,512,128]{3,2,1,0:T(8,128)}, u32[]{:S(2)}, u32[]{:S(2)}) %collective-permute-start.10) | collective-permute-done | bytes 1048608 | tf_op jit(solution)/shard_map/ppermute | solution.py:397
  77.7 1.7 %collective-permute-start.13 = (f32[2,544,128]{2,1,0:T(8,128)S(1)}, f32[2,544,128]{2,1,0:T(8,128)S(1)}, u32[]{:S(2)}, u32[]{:S(2)}) collective-permute-start(f32[2,544,128]{2,1,0:T(8,128)S(1)} %fusion.8), channel_id=1, source_target_pairs={{0,64},{8,72},{16,80},{24,88},{32,96},{40,104},{48,112},{56,120},{... | collective-permute-start | bytes 1671176 | tf_op jit(solution)/shard_map/ppermute | solution.py:397
  79.5 0.9 collective-permute-start.11
  80.3 4.9 %collective-permute-done.12 = f32[2,512,128]{2,1,0:T(8,128)S(1)} collective-permute-done((f32[2,512,128]{2,1,0:T(8,128)S(1)}, f32[2,512,128]{2,1,0:T(8,128)S(1)}, u32[]{:S(2)}, u32[]{:S(2)}) %collective-permute-start.12) | collective-permute-done | bytes 524320 | tf_op jit(solution)/shard_map/ppermute | solution.py:389
  85.3 1.3 %fusion.12 = f32[2,512,128]{2,1,0:T(8,128)S(1)} fusion(f32[2,512,128]{2,1,0:T(8,128)S(1)} %collective-permute-done.12, f32[4,2,512,128]{3,2,1,0:T(8,128)} %collective-permute-done, f32[2,2,512,128]{3,2,1,0:T(8,128)} %collective-permute-done.10, f32[4,2,512,128]{3,2,1,0:T(8,128)S(1)} %copy-done.4), kind=kLoop, calls=%fused_computation.22 | loop fusion | flops 393216 | bytes 2621440 | tf_op jit(solution)/shard_map/add | solution.py:438
  86.6 5.0 %collective-permute-done.13 = f32[2,544,128]{2,1,0:T(8,128)S(1)} collective-permute-done((f32[2,544,128]{2,1,0:T(8,128)S(1)}, f32[2,544,128]{2,1,0:T(8,128)S(1)}, u32[]{:S(2)}, u32[]{:S(2)}) %collective-permute-start.13) | collective-permute-done | bytes 557088 | tf_op jit(solution)/shard_map/ppermute | solution.py:397
  91.6 1.4 %collective-permute-start.14 = (f32[2,512,128]{2,1,0:T(8,128)S(1)}, f32[2,512,128]{2,1,0:T(8,128)S(1)}, u32[]{:S(2)}, u32[]{:S(2)}) collective-permute-start(f32[2,512,128]{2,1,0:T(8,128)S(1)} %fusion.12), channel_id=1, source_target_pairs={{0,16},{8,56},{16,32},{24,8},{32,48},{40,24},{48,0},{56,40},{64,80... | collective-permute-start | bytes 1572872 | tf_op jit(solution)/shard_map/ppermute | solution.py:389
  92.9 1.4 %fusion.5 = f32[2,544,128]{2,1,0:T(8,128)S(1)} fusion(f32[2,544,128]{2,1,0:T(8,128)S(1)} %collective-permute-done.13, f32[2,2,544,128]{3,2,1,0:T(8,128)} %collective-permute-done.4, f32[2,2,2,544,128]{4,3,2,1,0:T(8,128)S(1)} %copy-done.2, f32[2,2,544,128]{3,2,1,0:T(8,128)} %collective-permute-done.9, f32[2,2,2,544,128]{4,3,2,1,0:T(8,128)S(1)} %copy-done), kind=kLoop, calls=%fused_computation.11 | loop fusion | flops 557056 | bytes 3342336 | tf_op jit(solution)/shard_map/add | solution.py:441
  94.3 0.1 slice_bitcast_fusion.3
  94.4 5.4 %collective-permute-start.15 = (f32[544,128]{1,0:T(8,128)S(1)}, f32[544,128]{1,0:T(8,128)S(1)}, u32[]{:S(2)}, u32[]{:S(2)}) collective-permute-start(f32[544,128]{1,0:T(8,128)S(1)} %get-tuple-element.53), channel_id=1, source_target_pairs={{0,1},{1,2},{2,3},{3,4},{4,5},{5,6},{6,7},{8,9},{9,10},{10,11},{11... | collective-permute-start | bytes 835592 | tf_op jit(solution)/shard_map/ppermute | solution.py:443
  99.8 1.9 %collective-permute-start.16 = (f32[544,128]{1,0:T(8,128)S(1)}, f32[544,128]{1,0:T(8,128)S(1)}, u32[]{:S(2)}, u32[]{:S(2)}) collective-permute-start(f32[544,128]{1,0:T(8,128)S(1)} %get-tuple-element.52), channel_id=1, source_target_pairs={{1,0},{2,1},{3,2},{4,3},{5,4},{6,5},{7,6},{9,8},{10,9},{11,10},{12... | collective-permute-start | bytes 835592 | tf_op jit(solution)/shard_map/ppermute | solution.py:443
  101.7 0.0 collective-permute-done.11
  101.7 0.2 collective-permute-done.14
  102.0 1.4 %fusion.18 = f32[2,512,128]{2,1,0:T(8,128)S(1)} fusion(f32[2,512,128]{2,1,0:T(8,128)S(1)} %collective-permute-done.14, f32[2,512,128]{2,1,0:T(8,128)S(1)} %collective-permute-done.11, f32[4,2,512,128]{3,2,1,0:T(8,128)} %collective-permute-done, f32[2,2,512,128]{3,2,1,0:T(8,128)} %collective-permute-done.10, f32[4,2,512,128]{3,2,1,0:T(8,128)S(1)} %copy-done.4), kind=kLoop, calls=%fused_computation.33 | loop fusion | flops 524288 | bytes 3145728 | tf_op jit(solution)/shard_map/add | solution.py:444
  103.4 0.4 collective-permute-done.15
  103.9 8.0 %collective-permute-done.16 = f32[544,128]{1,0:T(8,128)S(1)} collective-permute-done((f32[544,128]{1,0:T(8,128)S(1)}, f32[544,128]{1,0:T(8,128)S(1)}, u32[]{:S(2)}, u32[]{:S(2)}) %collective-permute-start.16) | collective-permute-done | bytes 278560 | tf_op jit(solution)/shard_map/ppermute | solution.py:443
  111.9 1.9 %shard_map.78 = (f32[32,2,8,128]{3,2,1,0:T(8,128)}, f32[32,2,8,128]{3,2,1,0:T(8,128)}) custom-call(f32[32,2,8,128]{3,2,1,0:T(8,128)S(1)} %bitcast.100, f32[32,2,8,128]{3,2,1,0:T(8,128)S(1)} %bitcast.99, f32[34,2,8,128]{3,2,1,0:T(8,128)S(1)} %bitcast.97, f32[34,2,8,128]{3,2,1,0:T(8,128)S(1)} %bitcast.96, f32[34,2,8,128]{3,2,1,0:T(8,128)S(1)} %bitcast.103, ...), custom_call_target="tpu_custom_call" | custom-call | bytes 4194304 | tf_op jit(solution)/shard_map/pallas_call | solution.py:355
  (11 shorter events, 0.1 us)
Async XLA Ops:
  18.9 4.5 %collective-permute-start.2 = (f32[4,2,512,128]{3,2,1,0:T(8,128)}, f32[4,2,512,128]{3,2,1,0:T(8,128)S(1)}, u32[]{:S(2)}, u32[]{:S(2)}) collective-permute-start(f32[4,2,512,128]{3,2,1,0:T(8,128)} %get-tuple-element.29), channel_id=1, source_target_pairs={{0,8},{8,0},{16,24},{24,16},{32,40},{40,32},{48,56},{56,48},{64,72... | collective-permute-start | bytes 6291464 | tf_op jit(solution)/shard_map/ppermute | solution.py:385
  19.0 7.6 %collective-permute-start.3 = (f32[2,2,2,544,128]{4,3,2,1,0:T(8,128)}, f32[2,2,2,544,128]{4,3,2,1,0:T(8,128)S(1)}, u32[]{:S(2)}, u32[]{:S(2)}) collective-permute-start(f32[2,2,2,544,128]{4,3,2,1,0:T(8,128)} %get-tuple-element.30), channel_id=1, source_target_pairs={{0,8},{8,0},{16,24},{24,16},{32,40},{40,32},{48,56},{56,48},{64,72... | collective-permute-start | bytes 6684680 | tf_op jit(solution)/shard_map/ppermute | solution.py:385
  19.5 12.1 %collective-permute-start.1 = (f32[2,2,2,544,128]{4,3,2,1,0:T(8,128)}, f32[2,2,2,544,128]{4,3,2,1,0:T(8,128)S(1)}, u32[]{:S(2)}, u32[]{:S(2)}) collective-permute-start(f32[2,2,2,544,128]{4,3,2,1,0:T(8,128)} %get-tuple-element.26), channel_id=1, source_target_pairs={{0,8},{8,0},{16,24},{24,16},{32,40},{40,32},{48,56},{56,48},{64,72... | collective-permute-start | bytes 6684680 | tf_op jit(solution)/shard_map/ppermute | solution.py:385
  23.3 3.2 %copy-start.3 = (f32[2,2,2,544,128]{4,3,2,1,0:T(8,128)S(1)}, f32[2,2,2,544,128]{4,3,2,1,0:T(8,128)}, u32[]{:S(2)}) copy-start(f32[2,2,2,544,128]{4,3,2,1,0:T(8,128)} %get-tuple-element.27) | copy-start | bytes 6684676
  26.6 17.0 %copy-start = (f32[2,2,2,544,128]{4,3,2,1,0:T(8,128)S(1)}, f32[2,2,2,544,128]{4,3,2,1,0:T(8,128)}, u32[]{:S(2)}) copy-start(f32[2,2,2,544,128]{4,3,2,1,0:T(8,128)} %get-tuple-element.25) | copy-start | bytes 6684676
  26.8 16.8 %collective-permute-start.8 = (f32[2,2,544,128]{3,2,1,0:T(8,128)S(1)}, f32[2,2,544,128]{3,2,1,0:T(8,128)S(1)}, u32[]{:S(2)}, u32[]{:S(2)}) collective-permute-start(f32[2,2,544,128]{3,2,1,0:T(8,128)S(1)} %get-tuple-element.51), channel_id=1, source_target_pairs={{0,16},{8,56},{16,32},{24,8},{32,48},{40,24},{48,0},{56,40},{64,80... | collective-permute-start | bytes 3342344 | tf_op jit(solution)/shard_map/ppermute | solution.py:389
  28.4 23.2 %collective-permute-start = (f32[4,2,512,128]{3,2,1,0:T(8,128)}, f32[4,2,512,128]{3,2,1,0:T(8,128)}, u32[]{:S(2)}, u32[]{:S(2)}) collective-permute-start(f32[4,2,512,128]{3,2,1,0:T(8,128)} %get-tuple-element.24), channel_id=1, source_target_pairs={{0,8},{8,0},{16,24},{24,16},{32,40},{40,32},{48,56},{56,48},{64,72... | collective-permute-start | bytes 6291464 | tf_op jit(solution)/shard_map/ppermute | solution.py:385
  29.7 27.4 %collective-permute-start.5 = (f32[2,2,512,128]{3,2,1,0:T(8,128)}, f32[2,2,512,128]{3,2,1,0:T(8,128)}, u32[]{:S(2)}, u32[]{:S(2)}) collective-permute-start(f32[2,2,512,128]{3,2,1,0:T(8,128)} %get-tuple-element.32), channel_id=1, source_target_pairs={{0,64},{8,72},{16,80},{24,88},{32,96},{40,104},{48,112},{56,120},{... | collective-permute-start | bytes 3145736 | tf_op jit(solution)/shard_map/ppermute | solution.py:397
  31.6 13.2 %copy-start.1 = (f32[2,2,2,544,128]{4,3,2,1,0:T(8,128)}, f32[2,2,2,544,128]{4,3,2,1,0:T(8,128)S(1)}, u32[]{:S(2)}) copy-start(f32[2,2,2,544,128]{4,3,2,1,0:T(8,128)S(1)} %collective-permute-done.1) | copy-start | bytes 6684676
  44.8 28.5 %collective-permute-start.9 = (f32[2,2,544,128]{3,2,1,0:T(8,128)}, f32[2,2,544,128]{3,2,1,0:T(8,128)}, u32[]{:S(2)}, u32[]{:S(2)}) collective-permute-start(f32[2,2,544,128]{3,2,1,0:T(8,128)} %fusion.2), channel_id=1, source_target_pairs={{0,16},{8,56},{16,32},{24,8},{32,48},{40,24},{48,0},{56,40},{64,80... | collective-permute-start | bytes 3342344 | tf_op jit(solution)/shard_map/ppermute | solution.py:389
  45.2 28.2 %collective-permute-start.4 = (f32[2,2,544,128]{3,2,1,0:T(8,128)S(1)}, f32[2,2,544,128]{3,2,1,0:T(8,128)}, u32[]{:S(2)}, u32[]{:S(2)}) collective-permute-start(f32[2,2,544,128]{3,2,1,0:T(8,128)S(1)} %get-tuple-element.50), channel_id=1, source_target_pairs={{0,48},{8,24},{16,0},{24,40},{32,16},{40,56},{48,32},{56,8},{64,11... | collective-permute-start | bytes 3342344 | tf_op jit(solution)/shard_map/ppermute | solution.py:393
  48.0 29.7 %collective-permute-start.10 = (f32[2,2,512,128]{3,2,1,0:T(8,128)}, f32[2,2,512,128]{3,2,1,0:T(8,128)}, u32[]{:S(2)}, u32[]{:S(2)}) collective-permute-start(f32[2,2,512,128]{3,2,1,0:T(8,128)} %get-tuple-element.46), channel_id=1, source_target_pairs={{0,64},{8,72},{16,80},{24,88},{32,96},{40,104},{48,112},{56,120},{... | collective-permute-start | bytes 3145736 | tf_op jit(solution)/shard_map/ppermute | solution.py:397
  51.7 9.7 %collective-permute-start.6 = (f32[544,128]{1,0:T(8,128)S(1)}, f32[544,128]{1,0:T(8,128)S(1)}, u32[]{:S(2)}, u32[]{:S(2)}) collective-permute-start(f32[544,128]{1,0:T(8,128)S(1)} %pad_maximum_fusion), channel_id=1, source_target_pairs={{0,1},{1,2},{2,3},{3,4},{4,5},{5,6},{6,7},{8,9},{9,10},{10,11},{11... | collective-permute-start | bytes 835592 | tf_op jit(solution)/shard_map/ppermute | solution.py:429
  57.1 12.1 %collective-permute-start.7 = (f32[544,128]{1,0:T(8,128)S(1)}, f32[544,128]{1,0:T(8,128)S(1)}, u32[]{:S(2)}, u32[]{:S(2)}) collective-permute-start(f32[544,128]{1,0:T(8,128)S(1)} %pad_maximum_fusion), channel_id=1, source_target_pairs={{1,0},{2,1},{3,2},{4,3},{5,4},{6,5},{7,6},{9,8},{10,9},{11,10},{12... | collective-permute-start | bytes 835592 | tf_op jit(solution)/shard_map/ppermute | solution.py:429
  59.0 14.3 %copy-start.2 = (f32[2,2,2,544,128]{4,3,2,1,0:T(8,128)S(1)}, f32[2,2,2,544,128]{4,3,2,1,0:T(8,128)}, u32[]{:S(2)}) copy-start(f32[2,2,2,544,128]{4,3,2,1,0:T(8,128)} %copy-done.1) | copy-start | bytes 6684676
  61.2 24.1 %copy-start.4 = (f32[4,2,512,128]{3,2,1,0:T(8,128)S(1)}, f32[4,2,512,128]{3,2,1,0:T(8,128)}, u32[]{:S(2)}) copy-start(f32[4,2,512,128]{3,2,1,0:T(8,128)} %get-tuple-element.23) | copy-start | bytes 6291460
  73.4 11.9 %collective-permute-start.12 = (f32[2,512,128]{2,1,0:T(8,128)S(1)}, f32[2,512,128]{2,1,0:T(8,128)S(1)}, u32[]{:S(2)}, u32[]{:S(2)}) collective-permute-start(f32[2,512,128]{2,1,0:T(8,128)S(1)} %get-tuple-element.36), channel_id=1, source_target_pairs={{0,16},{8,56},{16,32},{24,8},{32,48},{40,24},{48,0},{56,40},{64,80... | collective-permute-start | bytes 1572872 | tf_op jit(solution)/shard_map/ppermute | solution.py:389
  77.7 13.9 %collective-permute-start.13 = (f32[2,544,128]{2,1,0:T(8,128)S(1)}, f32[2,544,128]{2,1,0:T(8,128)S(1)}, u32[]{:S(2)}, u32[]{:S(2)}) collective-permute-start(f32[2,544,128]{2,1,0:T(8,128)S(1)} %fusion.8), channel_id=1, source_target_pairs={{0,64},{8,72},{16,80},{24,88},{32,96},{40,104},{48,112},{56,120},{... | collective-permute-start | bytes 1671176 | tf_op jit(solution)/shard_map/ppermute | solution.py:397
  79.5 22.3 %collective-permute-start.11 = (f32[2,512,128]{2,1,0:T(8,128)S(1)}, f32[2,512,128]{2,1,0:T(8,128)S(1)}, u32[]{:S(2)}, u32[]{:S(2)}) collective-permute-start(f32[2,512,128]{2,1,0:T(8,128)S(1)} %get-tuple-element.35), channel_id=1, source_target_pairs={{0,48},{8,24},{16,0},{24,40},{32,16},{40,56},{48,32},{56,8},{64,11... | collective-permute-start | bytes 1572872 | tf_op jit(solution)/shard_map/ppermute | solution.py:393
  91.6 10.4 %collective-permute-start.14 = (f32[2,512,128]{2,1,0:T(8,128)S(1)}, f32[2,512,128]{2,1,0:T(8,128)S(1)}, u32[]{:S(2)}, u32[]{:S(2)}) collective-permute-start(f32[2,512,128]{2,1,0:T(8,128)S(1)} %fusion.12), channel_id=1, source_target_pairs={{0,16},{8,56},{16,32},{24,8},{32,48},{40,24},{48,0},{56,40},{64,80... | collective-permute-start | bytes 1572872 | tf_op jit(solution)/shard_map/ppermute | solution.py:389
  94.4 9.4 %collective-permute-start.15 = (f32[544,128]{1,0:T(8,128)S(1)}, f32[544,128]{1,0:T(8,128)S(1)}, u32[]{:S(2)}, u32[]{:S(2)}) collective-permute-start(f32[544,128]{1,0:T(8,128)S(1)} %get-tuple-element.53), channel_id=1, source_target_pairs={{0,1},{1,2},{2,3},{3,4},{4,5},{5,6},{6,7},{8,9},{9,10},{10,11},{11... | collective-permute-start | bytes 835592 | tf_op jit(solution)/shard_map/ppermute | solution.py:443
  99.8 12.1 %collective-permute-start.16 = (f32[544,128]{1,0:T(8,128)S(1)}, f32[544,128]{1,0:T(8,128)S(1)}, u32[]{:S(2)}, u32[]{:S(2)}) collective-permute-start(f32[544,128]{1,0:T(8,128)S(1)} %get-tuple-element.52), channel_id=1, source_target_pairs={{1,0},{2,1},{3,2},{4,3},{5,4},{6,5},{7,6},{9,8},{10,9},{11,10},{12... | collective-permute-start | bytes 835592 | tf_op jit(solution)/shard_map/ppermute | solution.py:443

commit v9 on v8

--- a/solution.py
+++ b/solution.py
@@ -415,7 +415,7 @@
     ends_two = forth(ends_same[0] + ends_came[0])
     far_ends = far_same[2:] + far_came[2:]
     far_ends, ends_came = after(far_ends, ends_came)
-    far_ends_came, far_rest_came = across(far_ends), across(far_same[:2] + far_came[:2])
+    far_ends_came = across(far_ends)
     ends_back = back(ends_same[1] + ends_came[1])
 
     start = me * rows * 16
@@ -428,20 +428,23 @@
     )
     k_low, k_high = lax.ppermute(k_here, "gz", UP), lax.ppermute(k_here, "gz", DOWN)
 
+    (ends_two, ends_back), far_came = after((ends_two, ends_back), far_came)
     ring = forth(rest_same[1] + rest_came[1] + ends_two)
+    far_next_came = across(far_same[1] + far_came[1])
     two, direct = (near_same[t] + near_came[t] + far_ends_came[t - 2] for t in (2, 3))
     (two, direct, k_low, k_high), ring = after((two, direct, k_low, k_high), ring)
     two, direct = forth(two), back(direct)
     edge_far = rest_same[0, 1] + rest_came[0, 1] + ends_back[1] + ring[1]
-    edge_far, far_rest_came = after(edge_far, far_rest_came)
+    edge_far, (far_came, far_next_came) = after(edge_far, (far_came, far_next_came))
     edge_far = across(edge_far)
-    last = near_same[1] + near_came[1] + far_rest_came[1] + two
+    far_own_came = across(far_same[0] + far_came[0])
+    last = near_same[1] + near_came[1] + far_next_came + two
     last, edge_far = after(last, edge_far)
     last = forth(last)
     edge = rest_same[0, 0] + rest_came[0, 0] + ends_back[0] + ring[0] + edge_far
     low, high = edge[0], edge[1]
     above, below = lax.ppermute(low, "gz", DOWN), lax.ppermute(high, "gz", UP)
-    result = near_same[0] + near_came[0] + far_rest_came[0] + direct + last
+    result = near_same[0] + near_came[0] + far_own_came + direct + last
     d, v = result[0], result[1]
 
     wide = (a.reshape(rows + 2, *CELL) for a in (low, high, below, above, k_here, k_low, k_high))

time: 114 us -> 122 us (1.070)
  waiting for transfers between devices: 49.5 us -> 54.3 us
  other arithmetic: 13 us -> 14.8 us
    ppermute x4, waiting for transfers between devices: 21.3 us -> 24.8 us  [forth(): return lax.ppermute(cells, 'tm', FORTH)]
    add x3 -> x5, other arithmetic: 5.92 us -> 8.01 us  [the longest x1 3.12 us: local(): far_ends = far_same[2:] + far_came[2:]]
    ppermute x2, starting transfers between devices: 7.3 us -> 9.2 us  [local(): above, below = (lax.ppermute(low, 'gz', DOWN), lax.ppermute(high, 'gz', UP))]
    ppermute x4, starting transfers between devices: 1.91 us -> 0.68 us  [to_sibling(): return lax.ppermute(other, 'tm', SIBLING)]
    ppermute x3 -> x4, waiting for transfers between devices: 7.95 us -> 7.42 us  [across(): return lax.ppermute(cells, 'tm', ACROSS)]
    ppermute x3 -> x4, starting transfers between devices: 5.54 us -> 5.17 us  [across(): return lax.ppermute(cells, 'tm', ACROSS)]
  transfers between devices with their start and end apart: 17 -> 18, of which waited for: 11 -> 11; matrix products, arithmetic and copies ran while one was open for 12% -> 13% of each run, Pallas kernels for 0% -> 0%
where the time goes in v9:
time: 122 us; the launch traced here: 121 us
  waiting for transfers between devices  54.3 us (45%)
  starting transfers between devices  29.9 us (25%)
  Pallas kernels  20.1 us (16%)
  other arithmetic  14.8 us (12%)
  local copies, waits for them, and re-layouts  1.48 us (1%)
    ppermute x4, waiting for transfers between devices, forth(): return lax.ppermute(cells, 'tm', FORTH)  24.8 us
    pallas_call x1, Pallas kernels, series(): pl.pallas_call(series_kernel, out_shape=(share,) * 4 + (edge,) * 4, in_sp...  18.2 us
    ppermute x2, starting transfers between devices, local(): above, below = (lax.ppermute(low, 'gz', DOWN), lax.ppermute(high, 'gz', UP))  9.2 us
    ppermute x2, waiting for transfers between devices, local(): above, below = (lax.ppermute(low, 'gz', DOWN), lax.ppermute(high, 'gz', UP))  8.97 us
    ppermute x1, waiting for transfers between devices, local(): lax.ppermute(k_here, 'gz', DOWN)  8.31 us
    ppermute x4, waiting for transfers between devices, across(): return lax.ppermute(cells, 'tm', ACROSS)  7.42 us
    ppermute x1, starting transfers between devices, local(): lax.ppermute(k_here, 'gz', UP)  5.7 us
    ppermute x4, starting transfers between devices, across(): return lax.ppermute(cells, 'tm', ACROSS)  5.17 us
  transfers between devices with their start and end apart: 18, of which 11 were waited for; matrix products, arithmetic and copies ran while one was open for 13% of the time, Pallas kernels for 0%

profile of v9, /device:TPU:6, one launch (start us, length us, event | category | flops | bytes accessed | tf_op | source)
XLA Modules:
  0.0 121.4 jit_solution(9161548982926416208)
XLA Ops:
  0.6 18.2 %shard_map.77 = (f32[4,2,512,128]{3,2,1,0:T(8,128)}, f32[4,2,512,128]{3,2,1,0:T(8,128)}, f32[4,2,512,128]{3,2,1,0:T(8,128)}, f32[4,2,512,128]{3,2,1,0:T(8,128)},...) custom-call(f32[1,4]{1,0:T(1,128)} %coeffs.1, ...), custom_call_target="tpu_custom_call" | custom-call | bytes 47185920 | tf_op jit(solution)/shard_map/pallas_call | solution.py:335
  18.9 0.1 collective-permute-start.4
  19.0 0.5 collective-permute-start.2
  19.5 0.1 collective-permute-start.1
  19.6 3.8 %collective-permute-done.4 = f32[4,2,512,128]{3,2,1,0:T(8,128)S(1)} collective-permute-done((f32[4,2,512,128]{3,2,1,0:T(8,128)}, f32[4,2,512,128]{3,2,1,0:T(8,128)S(1)}, u32[]{:S(2)}, u32[]{:S(2)}) %collective-permute-start.4) | collective-permute-done | bytes 2097184 | tf_op jit(solution)/shard_map/ppermute | solution.py:385
  23.3 3.1 %slice_add_fusion.2 = f32[2,2,512,128]{3,2,1,0:T(8,128)} fusion(f32[4,2,512,128]{3,2,1,0:T(8,128)S(1)} %collective-permute-done.4, f32[4,2,512,128]{3,2,1,0:T(8,128)} %get-tuple-element.29), kind=kLoop, calls=%fused_computation.6 | loop fusion | flops 262144 | bytes 3145728 | tf_op jit(solution)/shard_map/add | solution.py:416
  26.5 0.1 collective-permute-done.2
  26.5 0.2 add_bitcast_fusion
  26.8 1.7 %collective-permute-start.3 = (f32[2,2,544,128]{3,2,1,0:T(8,128)S(1)}, f32[2,2,544,128]{3,2,1,0:T(8,128)S(1)}, u32[]{:S(2)}, u32[]{:S(2)}) collective-permute-start(f32[2,2,544,128]{3,2,1,0:T(8,128)S(1)} %get-tuple-element.57), channel_id=1, source_target_pairs={{0,16},{8,56},{16,32},{24,8},{32,48},{40,24},{48,0},{56,40},{64,80... | collective-permute-start | bytes 3342344 | tf_op jit(solution)/shard_map/ppermute | solution.py:389
  28.4 1.6 %collective-permute-start.5 = (f32[2,2,544,128]{3,2,1,0:T(8,128)S(1)}, f32[2,2,544,128]{3,2,1,0:T(8,128)S(1)}, u32[]{:S(2)}, u32[]{:S(2)}) collective-permute-start(f32[2,2,544,128]{3,2,1,0:T(8,128)S(1)} %get-tuple-element.56), channel_id=1, source_target_pairs={{0,48},{8,24},{16,0},{24,40},{32,16},{40,56},{48,32},{56,8},{64,11... | collective-permute-start | bytes 3342344 | tf_op jit(solution)/shard_map/ppermute | solution.py:393
  30.1 1.9 %collective-permute-start.6 = (f32[2,2,512,128]{3,2,1,0:T(8,128)}, f32[2,2,512,128]{3,2,1,0:T(8,128)}, u32[]{:S(2)}, u32[]{:S(2)}) collective-permute-start(f32[2,2,512,128]{3,2,1,0:T(8,128)} %slice_add_fusion.2), channel_id=1, source_target_pairs={{0,64},{8,72},{16,80},{24,88},{32,96},{40,104},{48,112},{56,120},{... | collective-permute-start | bytes 3145736 | tf_op jit(solution)/shard_map/ppermute | solution.py:397
  32.0 21.5 %collective-permute-done.3 = f32[2,2,544,128]{3,2,1,0:T(8,128)S(1)} collective-permute-done((f32[2,2,544,128]{3,2,1,0:T(8,128)S(1)}, f32[2,2,544,128]{3,2,1,0:T(8,128)S(1)}, u32[]{:S(2)}, u32[]{:S(2)}) %collective-permute-start.3) | collective-permute-done | bytes 1114144 | tf_op jit(solution)/shard_map/ppermute | solution.py:389
  53.5 0.4 collective-permute-done.5
  53.9 0.0 collective-permute-done.1
  53.9 1.4 %fusion.1 = f32[2,2,544,128]{3,2,1,0:T(8,128)} fusion(f32[2,2,544,128]{3,2,1,0:T(8,128)S(1)} %collective-permute-done.3, f32[2,2,2,544,128]{4,3,2,1,0:T(8,128)S(1)} %collective-permute-done.1, f32[2,2,2,544,128]{4,3,2,1,0:T(8,128)S(1)} %copy-done), kind=kLoop, calls=%fused_computation.2 | loop fusion | flops 557056 | bytes 4456448 | tf_op jit(solution)/shard_map/add | solution.py:432
  55.3 0.4 copy-done.1
  55.7 1.4 %collective-permute-start.9 = (f32[2,2,544,128]{3,2,1,0:T(8,128)}, f32[2,2,544,128]{3,2,1,0:T(8,128)}, u32[]{:S(2)}, u32[]{:S(2)}) collective-permute-start(f32[2,2,544,128]{3,2,1,0:T(8,128)} %fusion.1), channel_id=1, source_target_pairs={{0,16},{8,56},{16,32},{24,8},{32,48},{40,24},{48,0},{56,40},{64,80... | collective-permute-start | bytes 3342344 | tf_op jit(solution)/shard_map/ppermute | solution.py:389
  57.1 0.9 dynamic-slice_select_fusion.1
  58.0 1.0 constant_dynamic-slice_fusion
  59.0 5.7 %collective-permute-start.7 = (f32[544,128]{1,0:T(8,128)S(1)}, f32[544,128]{1,0:T(8,128)S(1)}, u32[]{:S(2)}, u32[]{:S(2)}) collective-permute-start(f32[544,128]{1,0:T(8,128)S(1)} %pad_maximum_fusion), channel_id=1, source_target_pairs={{0,1},{1,2},{2,3},{3,4},{4,5},{5,6},{6,7},{8,9},{9,10},{10,11},{11... | collective-permute-start | bytes 835592 | tf_op jit(solution)/shard_map/ppermute | solution.py:429
  64.7 1.9 %collective-permute-start.8 = (f32[544,128]{1,0:T(8,128)S(1)}, f32[544,128]{1,0:T(8,128)S(1)}, u32[]{:S(2)}, u32[]{:S(2)}) collective-permute-start(f32[544,128]{1,0:T(8,128)S(1)} %pad_maximum_fusion), channel_id=1, source_target_pairs={{1,0},{2,1},{3,2},{4,3},{5,4},{6,5},{7,6},{9,8},{10,9},{11,10},{12... | collective-permute-start | bytes 835592 | tf_op jit(solution)/shard_map/ppermute | solution.py:429
  66.7 1.3 %add_bitcast_fusion.2 = f32[2,512,128]{2,1,0:T(8,128)S(1)} fusion(f32[4,2,512,128]{3,2,1,0:T(8,128)} %copy-done.4, f32[4,2,512,128]{3,2,1,0:T(8,128)} %get-tuple-element.29), kind=kLoop, calls=%fused_computation.32 | loop fusion | flops 131072 | bytes 1572864 | tf_op jit(solution)/shard_map/add | solution.py:433
  67.9 1.1 collective-permute-start.10
  69.1 1.9 %fusion.13 = (f32[2,512,128]{2,1,0:T(8,128)S(1)}, f32[2,512,128]{2,1,0:T(8,128)S(1)}) fusion(f32[2,2,512,128]{3,2,1,0:T(8,128)} %collective-permute-done.6, f32[4,2,512,128]{3,2,1,0:T(8,128)} %collective-permute-done, f32[4,2,512,128]{3,2,1,0:T(8,128)S(1)} %copy-done.5), kind=kLoop, calls=%fused_computation.21 | loop fusion | flops 524288 | bytes 4194304 | tf_op jit(solution)/shard_map/add | solution.py:434
  71.0 0.6 collective-permute-done.7
  71.5 8.3 %collective-permute-done.8 = f32[544,128]{1,0:T(8,128)S(1)} collective-permute-done((f32[544,128]{1,0:T(8,128)S(1)}, f32[544,128]{1,0:T(8,128)S(1)}, u32[]{:S(2)}, u32[]{:S(2)}) %collective-permute-start.8) | collective-permute-done | bytes 278560 | tf_op jit(solution)/shard_map/ppermute | solution.py:429
  79.9 0.0 collective-permute-done.9
  79.9 0.4 collective-permute-start.13
  80.3 1.2 fusion.9
  81.5 1.3 %collective-permute-done.10 = f32[2,512,128]{2,1,0:T(8,128)S(1)} collective-permute-done((f32[2,512,128]{2,1,0:T(8,128)S(1)}, f32[2,512,128]{2,1,0:T(8,128)S(1)}, u32[]{:S(2)}, u32[]{:S(2)}) %collective-permute-start.10) | collective-permute-done | bytes 524320 | tf_op jit(solution)/shard_map/ppermute | solution.py:397
  82.8 1.0 collective-permute-start.14
  83.8 1.3 %add_bitcast_fusion.1 = f32[2,512,128]{2,1,0:T(8,128)S(1)} fusion(f32[4,2,512,128]{3,2,1,0:T(8,128)} %copy-done.4, f32[4,2,512,128]{3,2,1,0:T(8,128)} %get-tuple-element.29), kind=kLoop, calls=%fused_computation.31 | loop fusion | flops 131072 | bytes 1572864 | tf_op jit(solution)/shard_map/add | solution.py:440
  85.0 1.1 collective-permute-start.11
  86.1 1.6 %collective-permute-start.12 = (f32[2,512,128]{2,1,0:T(8,128)S(1)}, f32[2,512,128]{2,1,0:T(8,128)S(1)}, u32[]{:S(2)}, u32[]{:S(2)}) collective-permute-start(f32[2,512,128]{2,1,0:T(8,128)S(1)} %get-tuple-element.42), channel_id=1, source_target_pairs={{0,48},{8,24},{16,0},{24,40},{32,16},{40,56},{48,32},{56,8},{64,11... | collective-permute-start | bytes 1572872 | tf_op jit(solution)/shard_map/ppermute | solution.py:393
  87.7 3.2 %collective-permute-done.13 = f32[2,512,128]{2,1,0:T(8,128)S(1)} collective-permute-done((f32[2,512,128]{2,1,0:T(8,128)S(1)}, f32[2,512,128]{2,1,0:T(8,128)S(1)}, u32[]{:S(2)}, u32[]{:S(2)}) %collective-permute-start.13) | collective-permute-done | bytes 524320 | tf_op jit(solution)/shard_map/ppermute | solution.py:389
  91.0 1.2 fusion.12
  92.1 6.1 %collective-permute-done.14 = f32[2,544,128]{2,1,0:T(8,128)S(1)} collective-permute-done((f32[2,544,128]{2,1,0:T(8,128)S(1)}, f32[2,544,128]{2,1,0:T(8,128)S(1)}, u32[]{:S(2)}, u32[]{:S(2)}) %collective-permute-start.14) | collective-permute-done | bytes 557088 | tf_op jit(solution)/shard_map/ppermute | solution.py:397
  98.3 0.5 collective-permute-start.15
  98.8 1.2 %fusion.6 = f32[2,544,128]{2,1,0:T(8,128)S(1)} fusion(f32[2,544,128]{2,1,0:T(8,128)S(1)} %collective-permute-done.14, f32[2,2,2,544,128]{4,3,2,1,0:T(8,128)S(1)} %copy-done.2, f32[2,2,544,128]{3,2,1,0:T(8,128)} %collective-permute-done.9, f32[2,2,544,128]{3,2,1,0:T(8,128)S(1)} %collective-permute-done.5, f32[2,2,2,544,128]{4,3,2,1,0:T(8,128)S(1)} %copy-done), kind=kLoop, calls=%fused_computation.11 | loop fusion | flops 557056 | bytes 3342336 | tf_op jit(solution)/shard_map/add | solution.py:444
  100.0 0.1 slice_bitcast_fusion.1
  100.1 7.3 %collective-permute-start.16 = (f32[544,128]{1,0:T(8,128)S(1)}, f32[544,128]{1,0:T(8,128)S(1)}, u32[]{:S(2)}, u32[]{:S(2)}) collective-permute-start(f32[544,128]{1,0:T(8,128)S(1)} %get-tuple-element.59), channel_id=1, source_target_pairs={{0,1},{1,2},{2,3},{3,4},{4,5},{5,6},{6,7},{8,9},{9,10},{10,11},{11... | collective-permute-start | bytes 835592 | tf_op jit(solution)/shard_map/ppermute | solution.py:446
  107.4 1.9 %collective-permute-start.17 = (f32[544,128]{1,0:T(8,128)S(1)}, f32[544,128]{1,0:T(8,128)S(1)}, u32[]{:S(2)}, u32[]{:S(2)}) collective-permute-start(f32[544,128]{1,0:T(8,128)S(1)} %get-tuple-element.58), channel_id=1, source_target_pairs={{1,0},{2,1},{3,2},{4,3},{5,4},{6,5},{7,6},{9,8},{10,9},{11,10},{12... | collective-permute-start | bytes 835592 | tf_op jit(solution)/shard_map/ppermute | solution.py:446
  109.3 0.0 collective-permute-done.12
  109.3 0.0 collective-permute-done.15
  109.3 1.2 fusion.18
  110.5 0.9 collective-permute-done.16
  111.4 8.1 %collective-permute-done.17 = f32[544,128]{1,0:T(8,128)S(1)} collective-permute-done((f32[544,128]{1,0:T(8,128)S(1)}, f32[544,128]{1,0:T(8,128)S(1)}, u32[]{:S(2)}, u32[]{:S(2)}) %collective-permute-start.17) | collective-permute-done | bytes 278560 | tf_op jit(solution)/shard_map/ppermute | solution.py:446
  119.5 1.9 %shard_map.78 = (f32[32,2,8,128]{3,2,1,0:T(8,128)}, f32[32,2,8,128]{3,2,1,0:T(8,128)}) custom-call(f32[32,2,8,128]{3,2,1,0:T(8,128)S(1)} %bitcast.104, f32[32,2,8,128]{3,2,1,0:T(8,128)S(1)} %bitcast.103, f32[34,2,8,128]{3,2,1,0:T(8,128)S(1)} %bitcast.101, f32[34,2,8,128]{3,2,1,0:T(8,128)S(1)} %bitcast.100, f32[34,2,8,128]{3,2,1,0:T(8,128)S(1)} %bitcast.107, ...), custom_call_target="tpu_custom_call" | custom-call | bytes 4194304 | tf_op jit(solution)/shard_map/pallas_call | solution.py:355
  (17 shorter events, 0.1 us)
Async XLA Ops:
  18.9 7.7 %copy-start.3 = (f32[2,2,2,544,128]{4,3,2,1,0:T(8,128)S(1)}, f32[2,2,2,544,128]{4,3,2,1,0:T(8,128)}, u32[]{:S(2)}) copy-start(f32[2,2,2,544,128]{4,3,2,1,0:T(8,128)} %get-tuple-element.32) | copy-start | bytes 6684676
  18.9 4.5 %collective-permute-start.4 = (f32[4,2,512,128]{3,2,1,0:T(8,128)}, f32[4,2,512,128]{3,2,1,0:T(8,128)S(1)}, u32[]{:S(2)}, u32[]{:S(2)}) collective-permute-start(f32[4,2,512,128]{3,2,1,0:T(8,128)} %get-tuple-element.34), channel_id=1, source_target_pairs={{0,8},{8,0},{16,24},{24,16},{32,40},{40,32},{48,56},{56,48},{64,72... | collective-permute-start | bytes 6291464 | tf_op jit(solution)/shard_map/ppermute | solution.py:385
  19.0 7.5 %collective-permute-start.2 = (f32[2,2,2,544,128]{4,3,2,1,0:T(8,128)}, f32[2,2,2,544,128]{4,3,2,1,0:T(8,128)S(1)}, u32[]{:S(2)}, u32[]{:S(2)}) collective-permute-start(f32[2,2,2,544,128]{4,3,2,1,0:T(8,128)} %get-tuple-element.33), channel_id=1, source_target_pairs={{0,8},{8,0},{16,24},{24,16},{32,40},{40,32},{48,56},{56,48},{64,72... | collective-permute-start | bytes 6684680 | tf_op jit(solution)/shard_map/ppermute | solution.py:385
  19.5 34.5 %collective-permute-start.1 = (f32[2,2,2,544,128]{4,3,2,1,0:T(8,128)}, f32[2,2,2,544,128]{4,3,2,1,0:T(8,128)S(1)}, u32[]{:S(2)}, u32[]{:S(2)}) collective-permute-start(f32[2,2,2,544,128]{4,3,2,1,0:T(8,128)} %get-tuple-element.31), channel_id=1, source_target_pairs={{0,8},{8,0},{16,24},{24,16},{32,40},{40,32},{48,56},{56,48},{64,72... | collective-permute-start | bytes 6684680 | tf_op jit(solution)/shard_map/ppermute | solution.py:385
  23.3 3.2 %copy-start.4 = (f32[4,2,512,128]{3,2,1,0:T(8,128)}, f32[4,2,512,128]{3,2,1,0:T(8,128)S(1)}, u32[]{:S(2)}) copy-start(f32[4,2,512,128]{3,2,1,0:T(8,128)S(1)} %collective-permute-done.4) | copy-start | bytes 6291460
  26.5 27.4 %copy-start = (f32[2,2,2,544,128]{4,3,2,1,0:T(8,128)S(1)}, f32[2,2,2,544,128]{4,3,2,1,0:T(8,128)}, u32[]{:S(2)}) copy-start(f32[2,2,2,544,128]{4,3,2,1,0:T(8,128)} %get-tuple-element.30) | copy-start | bytes 6684676
  26.8 26.8 %collective-permute-start.3 = (f32[2,2,544,128]{3,2,1,0:T(8,128)S(1)}, f32[2,2,544,128]{3,2,1,0:T(8,128)S(1)}, u32[]{:S(2)}, u32[]{:S(2)}) collective-permute-start(f32[2,2,544,128]{3,2,1,0:T(8,128)S(1)} %get-tuple-element.57), channel_id=1, source_target_pairs={{0,16},{8,56},{16,32},{24,8},{32,48},{40,24},{48,0},{56,40},{64,80... | collective-permute-start | bytes 3342344 | tf_op jit(solution)/shard_map/ppermute | solution.py:389
  28.4 25.5 %collective-permute-start.5 = (f32[2,2,544,128]{3,2,1,0:T(8,128)S(1)}, f32[2,2,544,128]{3,2,1,0:T(8,128)S(1)}, u32[]{:S(2)}, u32[]{:S(2)}) collective-permute-start(f32[2,2,544,128]{3,2,1,0:T(8,128)S(1)} %get-tuple-element.56), channel_id=1, source_target_pairs={{0,48},{8,24},{16,0},{24,40},{32,16},{40,56},{48,32},{56,8},{64,11... | collective-permute-start | bytes 3342344 | tf_op jit(solution)/shard_map/ppermute | solution.py:393
  30.1 37.9 %collective-permute-start = (f32[4,2,512,128]{3,2,1,0:T(8,128)}, f32[4,2,512,128]{3,2,1,0:T(8,128)}, u32[]{:S(2)}, u32[]{:S(2)}) collective-permute-start(f32[4,2,512,128]{3,2,1,0:T(8,128)} %get-tuple-element.28), channel_id=1, source_target_pairs={{0,8},{8,0},{16,24},{24,16},{32,40},{40,32},{48,56},{56,48},{64,72... | collective-permute-start | bytes 6291464 | tf_op jit(solution)/shard_map/ppermute | solution.py:385
  30.1 39.0 %collective-permute-start.6 = (f32[2,2,512,128]{3,2,1,0:T(8,128)}, f32[2,2,512,128]{3,2,1,0:T(8,128)}, u32[]{:S(2)}, u32[]{:S(2)}) collective-permute-start(f32[2,2,512,128]{3,2,1,0:T(8,128)} %slice_add_fusion.2), channel_id=1, source_target_pairs={{0,64},{8,72},{16,80},{24,88},{32,96},{40,104},{48,112},{56,120},{... | collective-permute-start | bytes 3145736 | tf_op jit(solution)/shard_map/ppermute | solution.py:397
  53.9 1.8 %copy-start.1 = (f32[2,2,2,544,128]{4,3,2,1,0:T(8,128)}, f32[2,2,2,544,128]{4,3,2,1,0:T(8,128)S(1)}, u32[]{:S(2)}) copy-start(f32[2,2,2,544,128]{4,3,2,1,0:T(8,128)S(1)} %collective-permute-done.1) | copy-start | bytes 6684676
  55.7 24.1 %collective-permute-start.9 = (f32[2,2,544,128]{3,2,1,0:T(8,128)}, f32[2,2,544,128]{3,2,1,0:T(8,128)}, u32[]{:S(2)}, u32[]{:S(2)}) collective-permute-start(f32[2,2,544,128]{3,2,1,0:T(8,128)} %fusion.1), channel_id=1, source_target_pairs={{0,16},{8,56},{16,32},{24,8},{32,48},{40,24},{48,0},{56,40},{64,80... | collective-permute-start | bytes 3342344 | tf_op jit(solution)/shard_map/ppermute | solution.py:389
  57.1 11.9 %copy-start.5 = (f32[4,2,512,128]{3,2,1,0:T(8,128)S(1)}, f32[4,2,512,128]{3,2,1,0:T(8,128)}, u32[]{:S(2)}) copy-start(f32[4,2,512,128]{3,2,1,0:T(8,128)} %get-tuple-element.27) | copy-start | bytes 6291460
  59.0 12.5 %collective-permute-start.7 = (f32[544,128]{1,0:T(8,128)S(1)}, f32[544,128]{1,0:T(8,128)S(1)}, u32[]{:S(2)}, u32[]{:S(2)}) collective-permute-start(f32[544,128]{1,0:T(8,128)S(1)} %pad_maximum_fusion), channel_id=1, source_target_pairs={{0,1},{1,2},{2,3},{3,4},{4,5},{5,6},{6,7},{8,9},{9,10},{10,11},{11... | collective-permute-start | bytes 835592 | tf_op jit(solution)/shard_map/ppermute | solution.py:429
  64.7 15.1 %collective-permute-start.8 = (f32[544,128]{1,0:T(8,128)S(1)}, f32[544,128]{1,0:T(8,128)S(1)}, u32[]{:S(2)}, u32[]{:S(2)}) collective-permute-start(f32[544,128]{1,0:T(8,128)S(1)} %pad_maximum_fusion), channel_id=1, source_target_pairs={{1,0},{2,1},{3,2},{4,3},{5,4},{6,5},{7,6},{9,8},{10,9},{11,10},{12... | collective-permute-start | bytes 835592 | tf_op jit(solution)/shard_map/ppermute | solution.py:429
  67.9 14.9 %collective-permute-start.10 = (f32[2,512,128]{2,1,0:T(8,128)S(1)}, f32[2,512,128]{2,1,0:T(8,128)S(1)}, u32[]{:S(2)}, u32[]{:S(2)}) collective-permute-start(f32[2,512,128]{2,1,0:T(8,128)S(1)} %add_bitcast_fusion.2), channel_id=1, source_target_pairs={{0,64},{8,72},{16,80},{24,88},{32,96},{40,104},{48,112},{56,120},{... | collective-permute-start | bytes 1572872 | tf_op jit(solution)/shard_map/ppermute | solution.py:397
  69.1 11.2 %copy-start.2 = (f32[2,2,2,544,128]{4,3,2,1,0:T(8,128)S(1)}, f32[2,2,2,544,128]{4,3,2,1,0:T(8,128)}, u32[]{:S(2)}) copy-start(f32[2,2,2,544,128]{4,3,2,1,0:T(8,128)} %copy-done.1) | copy-start | bytes 6684676
  79.9 11.1 %collective-permute-start.13 = (f32[2,512,128]{2,1,0:T(8,128)S(1)}, f32[2,512,128]{2,1,0:T(8,128)S(1)}, u32[]{:S(2)}, u32[]{:S(2)}) collective-permute-start(f32[2,512,128]{2,1,0:T(8,128)S(1)} %get-tuple-element.44), channel_id=1, source_target_pairs={{0,16},{8,56},{16,32},{24,8},{32,48},{40,24},{48,0},{56,40},{64,80... | collective-permute-start | bytes 1572872 | tf_op jit(solution)/shard_map/ppermute | solution.py:389
  82.8 15.5 %collective-permute-start.14 = (f32[2,544,128]{2,1,0:T(8,128)S(1)}, f32[2,544,128]{2,1,0:T(8,128)S(1)}, u32[]{:S(2)}, u32[]{:S(2)}) collective-permute-start(f32[2,544,128]{2,1,0:T(8,128)S(1)} %fusion.9), channel_id=1, source_target_pairs={{0,64},{8,72},{16,80},{24,88},{32,96},{40,104},{48,112},{56,120},{... | collective-permute-start | bytes 1671176 | tf_op jit(solution)/shard_map/ppermute | solution.py:397
  85.0 24.3 %collective-permute-start.11 = (f32[2,512,128]{2,1,0:T(8,128)S(1)}, f32[2,512,128]{2,1,0:T(8,128)S(1)}, u32[]{:S(2)}, u32[]{:S(2)}) collective-permute-start(f32[2,512,128]{2,1,0:T(8,128)S(1)} %add_bitcast_fusion.1), channel_id=1, source_target_pairs={{0,64},{8,72},{16,80},{24,88},{32,96},{40,104},{48,112},{56,120},{... | collective-permute-start | bytes 1572872 | tf_op jit(solution)/shard_map/ppermute | solution.py:397
  86.1 23.2 %collective-permute-start.12 = (f32[2,512,128]{2,1,0:T(8,128)S(1)}, f32[2,512,128]{2,1,0:T(8,128)S(1)}, u32[]{:S(2)}, u32[]{:S(2)}) collective-permute-start(f32[2,512,128]{2,1,0:T(8,128)S(1)} %get-tuple-element.42), channel_id=1, source_target_pairs={{0,48},{8,24},{16,0},{24,40},{32,16},{40,56},{48,32},{56,8},{64,11... | collective-permute-start | bytes 1572872 | tf_op jit(solution)/shard_map/ppermute | solution.py:393
  98.3 11.0 %collective-permute-start.15 = (f32[2,512,128]{2,1,0:T(8,128)S(1)}, f32[2,512,128]{2,1,0:T(8,128)S(1)}, u32[]{:S(2)}, u32[]{:S(2)}) collective-permute-start(f32[2,512,128]{2,1,0:T(8,128)S(1)} %fusion.12), channel_id=1, source_target_pairs={{0,16},{8,56},{16,32},{24,8},{32,48},{40,24},{48,0},{56,40},{64,80... | collective-permute-start | bytes 1572872 | tf_op jit(solution)/shard_map/ppermute | solution.py:389
  100.1 11.4 %collective-permute-start.16 = (f32[544,128]{1,0:T(8,128)S(1)}, f32[544,128]{1,0:T(8,128)S(1)}, u32[]{:S(2)}, u32[]{:S(2)}) collective-permute-start(f32[544,128]{1,0:T(8,128)S(1)} %get-tuple-element.59), channel_id=1, source_target_pairs={{0,1},{1,2},{2,3},{3,4},{4,5},{5,6},{6,7},{8,9},{9,10},{10,11},{11... | collective-permute-start | bytes 835592 | tf_op jit(solution)/shard_map/ppermute | solution.py:446
  107.4 12.2 %collective-permute-start.17 = (f32[544,128]{1,0:T(8,128)S(1)}, f32[544,128]{1,0:T(8,128)S(1)}, u32[]{:S(2)}, u32[]{:S(2)}) collective-permute-start(f32[544,128]{1,0:T(8,128)S(1)} %get-tuple-element.58), channel_id=1, source_target_pairs={{1,0},{2,1},{3,2},{4,3},{5,4},{6,5},{7,6},{9,8},{10,9},{11,10},{12... | collective-permute-start | bytes 835592 | tf_op jit(solution)/shard_map/ppermute | solution.py:446

commit v10 on v9

--- a/solution.py
+++ b/solution.py
@@ -428,7 +428,7 @@
     )
     k_low, k_high = lax.ppermute(k_here, "gz", UP), lax.ppermute(k_here, "gz", DOWN)
 
-    (ends_two, ends_back), far_came = after((ends_two, ends_back), far_came)
+    ends_two, far_came = after(ends_two, far_came)
     ring = forth(rest_same[1] + rest_came[1] + ends_two)
     far_next_came = across(far_same[1] + far_came[1])
     two, direct = (near_same[t] + near_came[t] + far_ends_came[t - 2] for t in (2, 3))

time: 122 us -> 114 us (0.934)
  waiting for transfers between devices: 54.3 us -> 44.4 us
    ppermute x4, waiting for transfers between devices: 7.42 us -> 3.77 us  [across(): return lax.ppermute(cells, 'tm', ACROSS)]
    ppermute x4, waiting for transfers between devices: 24.8 us -> 21.5 us  [forth(): return lax.ppermute(cells, 'tm', FORTH)]
    ppermute x2, starting transfers between devices: 3.22 us -> 6.07 us  [back(): return lax.ppermute(cells, 'tm', BACK)]
    ppermute x4, starting transfers between devices: 4.04 us -> 2.07 us  [forth(): return lax.ppermute(cells, 'tm', FORTH)]
    ppermute x2, starting transfers between devices: 9.2 us -> 7.64 us  [local(): above, below = (lax.ppermute(low, 'gz', DOWN), lax.ppermute(high, 'gz', UP))]
    ppermute x4, starting transfers between devices: 0.68 us -> 1.92 us  [to_sibling(): return lax.ppermute(other, 'tm', SIBLING)]
  transfers between devices with their start and end apart: 18 -> 18, of which waited for: 11 -> 10; matrix products, arithmetic and copies ran while one was open for 13% -> 14% of each run, Pallas kernels for 0% -> 0%
where the time goes in v10:
time: 114 us; the launch traced here: 112 us
  waiting for transfers between devices  44.4 us (39%)
  starting transfers between devices  30.5 us (27%)
  Pallas kernels  20.1 us (18%)
  other arithmetic  15.2 us (13%)
  local copies, waits for them, and re-layouts  1.46 us (1%)
    ppermute x4, waiting for transfers between devices, forth(): return lax.ppermute(cells, 'tm', FORTH)  21.5 us
    pallas_call x1, Pallas kernels, series(): pl.pallas_call(series_kernel, out_shape=(share,) * 4 + (edge,) * 4, in_sp...  18.2 us
    ppermute x2, waiting for transfers between devices, local(): above, below = (lax.ppermute(low, 'gz', DOWN), lax.ppermute(high, 'gz', UP))  7.87 us
    ppermute x2, starting transfers between devices, local(): above, below = (lax.ppermute(low, 'gz', DOWN), lax.ppermute(high, 'gz', UP))  7.64 us
    ppermute x1, waiting for transfers between devices, local(): lax.ppermute(k_here, 'gz', DOWN)  7.39 us
    ppermute x2, starting transfers between devices, back(): return lax.ppermute(cells, 'tm', BACK)  6.07 us
    ppermute x1, starting transfers between devices, local(): lax.ppermute(k_here, 'gz', UP)  5.7 us
    ppermute x4, starting transfers between devices, across(): return lax.ppermute(cells, 'tm', ACROSS)  5.22 us
  transfers between devices with their start and end apart: 18, of which 10 were waited for; matrix products, arithmetic and copies ran while one was open for 14% of the time, Pallas kernels for 0%

profile of v10, /device:TPU:6, one launch (start us, length us, event | category | flops | bytes accessed | tf_op | source)
XLA Modules:
  0.0 112.5 jit_solution(15480328583021267403)
XLA Ops:
  0.6 18.2 %shard_map.77 = (f32[4,2,512,128]{3,2,1,0:T(8,128)}, f32[4,2,512,128]{3,2,1,0:T(8,128)}, f32[4,2,512,128]{3,2,1,0:T(8,128)}, f32[4,2,512,128]{3,2,1,0:T(8,128)},...) custom-call(f32[1,4]{1,0:T(1,128)} %coeffs.1, ...), custom_call_target="tpu_custom_call" | custom-call | bytes 47185920 | tf_op jit(solution)/shard_map/pallas_call | solution.py:335
  18.9 0.1 collective-permute-start.2
  19.0 0.5 collective-permute-start.3
  19.5 0.1 collective-permute-start.1
  19.6 3.8 %collective-permute-done.2 = f32[4,2,512,128]{3,2,1,0:T(8,128)S(1)} collective-permute-done((f32[4,2,512,128]{3,2,1,0:T(8,128)}, f32[4,2,512,128]{3,2,1,0:T(8,128)S(1)}, u32[]{:S(2)}, u32[]{:S(2)}) %collective-permute-start.2) | collective-permute-done | bytes 2097184 | tf_op jit(solution)/shard_map/ppermute | solution.py:385
  23.3 3.1 %slice_add_fusion.2 = f32[2,2,512,128]{3,2,1,0:T(8,128)} fusion(f32[4,2,512,128]{3,2,1,0:T(8,128)S(1)} %collective-permute-done.2, f32[4,2,512,128]{3,2,1,0:T(8,128)} %get-tuple-element.28), kind=kLoop, calls=%fused_computation.6 | loop fusion | flops 262144 | bytes 3145728 | tf_op jit(solution)/shard_map/add | solution.py:416
  26.5 0.1 collective-permute-done.3
  26.5 0.2 add_bitcast_fusion
  26.8 1.7 %collective-permute-start.8 = (f32[2,2,544,128]{3,2,1,0:T(8,128)S(1)}, f32[2,2,544,128]{3,2,1,0:T(8,128)S(1)}, u32[]{:S(2)}, u32[]{:S(2)}) collective-permute-start(f32[2,2,544,128]{3,2,1,0:T(8,128)S(1)} %get-tuple-element.55), channel_id=1, source_target_pairs={{0,16},{8,56},{16,32},{24,8},{32,48},{40,24},{48,0},{56,40},{64,80... | collective-permute-start | bytes 3342344 | tf_op jit(solution)/shard_map/ppermute | solution.py:389
  28.4 1.2 %collective-permute-start = (f32[4,2,512,128]{3,2,1,0:T(8,128)}, f32[4,2,512,128]{3,2,1,0:T(8,128)}, u32[]{:S(2)}, u32[]{:S(2)}) collective-permute-start(f32[4,2,512,128]{3,2,1,0:T(8,128)} %get-tuple-element.27), channel_id=1, source_target_pairs={{0,8},{8,0},{16,24},{24,16},{32,40},{40,32},{48,56},{56,48},{64,72... | collective-permute-start | bytes 6291464 | tf_op jit(solution)/shard_map/ppermute | solution.py:385
  29.7 1.9 %collective-permute-start.5 = (f32[2,2,512,128]{3,2,1,0:T(8,128)}, f32[2,2,512,128]{3,2,1,0:T(8,128)}, u32[]{:S(2)}, u32[]{:S(2)}) collective-permute-start(f32[2,2,512,128]{3,2,1,0:T(8,128)} %slice_add_fusion.2), channel_id=1, source_target_pairs={{0,64},{8,72},{16,80},{24,88},{32,96},{40,104},{48,112},{56,120},{... | collective-permute-start | bytes 3145736 | tf_op jit(solution)/shard_map/ppermute | solution.py:397
  31.6 11.9 %collective-permute-done.8 = f32[2,2,544,128]{3,2,1,0:T(8,128)S(1)} collective-permute-done((f32[2,2,544,128]{3,2,1,0:T(8,128)S(1)}, f32[2,2,544,128]{3,2,1,0:T(8,128)S(1)}, u32[]{:S(2)}, u32[]{:S(2)}) %collective-permute-start.8) | collective-permute-done | bytes 1114144 | tf_op jit(solution)/shard_map/ppermute | solution.py:389
  43.5 0.0 collective-permute-done.1
  43.5 1.4 %fusion.2 = f32[2,2,544,128]{3,2,1,0:T(8,128)} fusion(f32[2,2,544,128]{3,2,1,0:T(8,128)S(1)} %collective-permute-done.8, f32[2,2,2,544,128]{4,3,2,1,0:T(8,128)S(1)} %collective-permute-done.1, f32[2,2,2,544,128]{4,3,2,1,0:T(8,128)S(1)} %copy-done), kind=kLoop, calls=%fused_computation.4 | loop fusion | flops 557056 | bytes 4456448 | tf_op jit(solution)/shard_map/add | solution.py:432
  44.9 0.4 copy-done.1
  45.3 0.4 collective-permute-start.9
  45.7 2.8 %collective-permute-start.4 = (f32[2,2,544,128]{3,2,1,0:T(8,128)S(1)}, f32[2,2,544,128]{3,2,1,0:T(8,128)}, u32[]{:S(2)}, u32[]{:S(2)}) collective-permute-start(f32[2,2,544,128]{3,2,1,0:T(8,128)S(1)} %get-tuple-element.54), channel_id=1, source_target_pairs={{0,48},{8,24},{16,0},{24,40},{32,16},{40,56},{48,32},{56,8},{64,11... | collective-permute-start | bytes 3342344 | tf_op jit(solution)/shard_map/ppermute | solution.py:393
  48.5 0.9 dynamic-slice_select_fusion.1
  49.4 1.0 constant_dynamic-slice_fusion
  50.4 5.7 %collective-permute-start.6 = (f32[544,128]{1,0:T(8,128)S(1)}, f32[544,128]{1,0:T(8,128)S(1)}, u32[]{:S(2)}, u32[]{:S(2)}) collective-permute-start(f32[544,128]{1,0:T(8,128)S(1)} %pad_maximum_fusion), channel_id=1, source_target_pairs={{0,1},{1,2},{2,3},{3,4},{4,5},{5,6},{6,7},{8,9},{9,10},{10,11},{11... | collective-permute-start | bytes 835592 | tf_op jit(solution)/shard_map/ppermute | solution.py:429
  56.1 1.3 %add_bitcast_fusion.2 = f32[2,512,128]{2,1,0:T(8,128)S(1)} fusion(f32[4,2,512,128]{3,2,1,0:T(8,128)} %copy-done.4, f32[4,2,512,128]{3,2,1,0:T(8,128)} %get-tuple-element.28), kind=kLoop, calls=%fused_computation.34 | loop fusion | flops 131072 | bytes 1572864 | tf_op jit(solution)/shard_map/add | solution.py:433
  57.4 0.0 collective-permute-done
  57.4 1.9 %collective-permute-start.7 = (f32[544,128]{1,0:T(8,128)S(1)}, f32[544,128]{1,0:T(8,128)S(1)}, u32[]{:S(2)}, u32[]{:S(2)}) collective-permute-start(f32[544,128]{1,0:T(8,128)S(1)} %pad_maximum_fusion), channel_id=1, source_target_pairs={{1,0},{2,1},{3,2},{4,3},{5,4},{6,5},{7,6},{9,8},{10,9},{11,10},{12... | collective-permute-start | bytes 835592 | tf_op jit(solution)/shard_map/ppermute | solution.py:429
  59.3 0.0 collective-permute-done.5
  59.3 1.1 collective-permute-start.10
  60.5 1.9 %fusion.13 = (f32[2,512,128]{2,1,0:T(8,128)S(1)}, f32[2,512,128]{2,1,0:T(8,128)S(1)}) fusion(f32[2,2,512,128]{3,2,1,0:T(8,128)} %collective-permute-done.5, f32[4,2,512,128]{3,2,1,0:T(8,128)} %collective-permute-done, f32[4,2,512,128]{3,2,1,0:T(8,128)S(1)} %copy-done.5), kind=kLoop, calls=%fused_computation.23 | loop fusion | flops 524288 | bytes 4194304 | tf_op jit(solution)/shard_map/add | solution.py:434
  62.4 0.0 collective-permute-done.6
  62.4 7.4 %collective-permute-done.7 = f32[544,128]{1,0:T(8,128)S(1)} collective-permute-done((f32[544,128]{1,0:T(8,128)S(1)}, f32[544,128]{1,0:T(8,128)S(1)}, u32[]{:S(2)}, u32[]{:S(2)}) %collective-permute-start.7) | collective-permute-done | bytes 278560 | tf_op jit(solution)/shard_map/ppermute | solution.py:429
  69.8 4.1 %collective-permute-done.9 = f32[2,2,544,128]{3,2,1,0:T(8,128)} collective-permute-done((f32[2,2,544,128]{3,2,1,0:T(8,128)}, f32[2,2,544,128]{3,2,1,0:T(8,128)}, u32[]{:S(2)}, u32[]{:S(2)}) %collective-permute-start.9) | collective-permute-done | bytes 1114144 | tf_op jit(solution)/shard_map/ppermute | solution.py:389
  73.8 1.3 %fusion.8 = f32[2,544,128]{2,1,0:T(8,128)S(1)} fusion(f32[2,2,544,128]{3,2,1,0:T(8,128)} %collective-permute-done.4, f32[2,2,2,544,128]{4,3,2,1,0:T(8,128)S(1)} %copy-done.2, f32[2,2,544,128]{3,2,1,0:T(8,128)} %collective-permute-done.9, f32[2,2,2,544,128]{4,3,2,1,0:T(8,128)S(1)} %copy-done), kind=kLoop, calls=%fused_computation.15 | loop fusion | flops 417792 | bytes 2785280 | tf_op jit(solution)/shard_map/add | solution.py:437
  75.2 0.0 collective-permute-done.10
  75.2 2.0 %collective-permute-start.14 = (f32[2,544,128]{2,1,0:T(8,128)S(1)}, f32[2,544,128]{2,1,0:T(8,128)S(1)}, u32[]{:S(2)}, u32[]{:S(2)}) collective-permute-start(f32[2,544,128]{2,1,0:T(8,128)S(1)} %fusion.8), channel_id=1, source_target_pairs={{0,64},{8,72},{16,80},{24,88},{32,96},{40,104},{48,112},{56,120},{... | collective-permute-start | bytes 1671176 | tf_op jit(solution)/shard_map/ppermute | solution.py:397
  77.2 3.2 %collective-permute-start.12 = (f32[2,512,128]{2,1,0:T(8,128)S(1)}, f32[2,512,128]{2,1,0:T(8,128)S(1)}, u32[]{:S(2)}, u32[]{:S(2)}) collective-permute-start(f32[2,512,128]{2,1,0:T(8,128)S(1)} %get-tuple-element.40), channel_id=1, source_target_pairs={{0,48},{8,24},{16,0},{24,40},{32,16},{40,56},{48,32},{56,8},{64,11... | collective-permute-start | bytes 1572872 | tf_op jit(solution)/shard_map/ppermute | solution.py:393
  80.4 1.3 %add_bitcast_fusion.1 = f32[2,512,128]{2,1,0:T(8,128)S(1)} fusion(f32[4,2,512,128]{3,2,1,0:T(8,128)} %copy-done.4, f32[4,2,512,128]{3,2,1,0:T(8,128)} %get-tuple-element.28), kind=kLoop, calls=%fused_computation.33 | loop fusion | flops 131072 | bytes 1572864 | tf_op jit(solution)/shard_map/add | solution.py:440
  81.7 0.2 collective-permute-start.11
  81.9 5.5 %collective-permute-done.13 = f32[2,512,128]{2,1,0:T(8,128)S(1)} collective-permute-done((f32[2,512,128]{2,1,0:T(8,128)S(1)}, f32[2,512,128]{2,1,0:T(8,128)S(1)}, u32[]{:S(2)}, u32[]{:S(2)}) %collective-permute-start.13) | collective-permute-done | bytes 524320 | tf_op jit(solution)/shard_map/ppermute | solution.py:389
  87.4 1.2 %fusion.12 = f32[2,512,128]{2,1,0:T(8,128)S(1)} fusion(f32[2,512,128]{2,1,0:T(8,128)S(1)} %collective-permute-done.13, f32[2,512,128]{2,1,0:T(8,128)S(1)} %collective-permute-done.10, f32[4,2,512,128]{3,2,1,0:T(8,128)} %collective-permute-done, f32[4,2,512,128]{3,2,1,0:T(8,128)S(1)} %copy-done.5), kind=kLoop, calls=%fused_computation.21 | loop fusion | flops 393216 | bytes 2621440 | tf_op jit(solution)/shard_map/add | solution.py:441
  88.6 2.1 %collective-permute-done.14 = f32[2,544,128]{2,1,0:T(8,128)S(1)} collective-permute-done((f32[2,544,128]{2,1,0:T(8,128)S(1)}, f32[2,544,128]{2,1,0:T(8,128)S(1)}, u32[]{:S(2)}, u32[]{:S(2)}) %collective-permute-start.14) | collective-permute-done | bytes 557088 | tf_op jit(solution)/shard_map/ppermute | solution.py:397
  90.7 1.4 %fusion.5 = f32[2,544,128]{2,1,0:T(8,128)S(1)} fusion(f32[2,544,128]{2,1,0:T(8,128)S(1)} %collective-permute-done.14, f32[2,2,544,128]{3,2,1,0:T(8,128)} %collective-permute-done.4, f32[2,2,2,544,128]{4,3,2,1,0:T(8,128)S(1)} %copy-done.2, f32[2,2,544,128]{3,2,1,0:T(8,128)} %collective-permute-done.9, f32[2,2,2,544,128]{4,3,2,1,0:T(8,128)S(1)} %copy-done), kind=kLoop, calls=%fused_computation.10 | loop fusion | flops 557056 | bytes 3342336 | tf_op jit(solution)/shard_map/add | solution.py:444
  92.1 0.1 slice_bitcast_fusion.3
  92.2 5.7 %collective-permute-start.16 = (f32[544,128]{1,0:T(8,128)S(1)}, f32[544,128]{1,0:T(8,128)S(1)}, u32[]{:S(2)}, u32[]{:S(2)}) collective-permute-start(f32[544,128]{1,0:T(8,128)S(1)} %get-tuple-element.57), channel_id=1, source_target_pairs={{0,1},{1,2},{2,3},{3,4},{4,5},{5,6},{6,7},{8,9},{9,10},{10,11},{11... | collective-permute-start | bytes 835592 | tf_op jit(solution)/shard_map/ppermute | solution.py:446
  97.9 1.9 %collective-permute-start.17 = (f32[544,128]{1,0:T(8,128)S(1)}, f32[544,128]{1,0:T(8,128)S(1)}, u32[]{:S(2)}, u32[]{:S(2)}) collective-permute-start(f32[544,128]{1,0:T(8,128)S(1)} %get-tuple-element.56), channel_id=1, source_target_pairs={{1,0},{2,1},{3,2},{4,3},{5,4},{6,5},{7,6},{9,8},{10,9},{11,10},{12... | collective-permute-start | bytes 835592 | tf_op jit(solution)/shard_map/ppermute | solution.py:446
  99.8 0.0 collective-permute-done.12
  99.9 1.6 %collective-permute-done.11 = f32[2,512,128]{2,1,0:T(8,128)S(1)} collective-permute-done((f32[2,512,128]{2,1,0:T(8,128)S(1)}, f32[2,512,128]{2,1,0:T(8,128)S(1)}, u32[]{:S(2)}, u32[]{:S(2)}) %collective-permute-start.11) | collective-permute-done | bytes 524320 | tf_op jit(solution)/shard_map/ppermute | solution.py:397
  101.5 1.2 %fusion.18 = f32[2,512,128]{2,1,0:T(8,128)S(1)} fusion(f32[2,512,128]{2,1,0:T(8,128)S(1)} %collective-permute-done.15, f32[2,512,128]{2,1,0:T(8,128)S(1)} %collective-permute-done.12, f32[2,512,128]{2,1,0:T(8,128)S(1)} %collective-permute-done.11, f32[4,2,512,128]{3,2,1,0:T(8,128)} %collective-permute-done, f32[4,2,512,128]{3,2,1,0:T(8,128)S(1)} %copy-done.5), kind=kLoop, calls=%fused_computation.32 | loop fusion | flops 524288 | bytes 3145728 | tf_op jit(solution)/shard_map/add | solution.py:447
  102.7 0.1 collective-permute-done.16
  102.8 7.8 %collective-permute-done.17 = f32[544,128]{1,0:T(8,128)S(1)} collective-permute-done((f32[544,128]{1,0:T(8,128)S(1)}, f32[544,128]{1,0:T(8,128)S(1)}, u32[]{:S(2)}, u32[]{:S(2)}) %collective-permute-start.17) | collective-permute-done | bytes 278560 | tf_op jit(solution)/shard_map/ppermute | solution.py:446
  110.6 1.9 %shard_map.78 = (f32[32,2,8,128]{3,2,1,0:T(8,128)}, f32[32,2,8,128]{3,2,1,0:T(8,128)}) custom-call(f32[32,2,8,128]{3,2,1,0:T(8,128)S(1)} %bitcast.108, f32[32,2,8,128]{3,2,1,0:T(8,128)S(1)} %bitcast.107, f32[34,2,8,128]{3,2,1,0:T(8,128)S(1)} %bitcast.105, f32[34,2,8,128]{3,2,1,0:T(8,128)S(1)} %bitcast.104, f32[34,2,8,128]{3,2,1,0:T(8,128)S(1)} %bitcast.111, ...), custom_call_target="tpu_custom_call" | custom-call | bytes 4194304 | tf_op jit(solution)/shard_map/pallas_call | solution.py:355
  (17 shorter events, 0.1 us)
Async XLA Ops:
  18.9 7.7 %copy-start.3 = (f32[2,2,2,544,128]{4,3,2,1,0:T(8,128)S(1)}, f32[2,2,2,544,128]{4,3,2,1,0:T(8,128)}, u32[]{:S(2)}) copy-start(f32[2,2,2,544,128]{4,3,2,1,0:T(8,128)} %get-tuple-element.31) | copy-start | bytes 6684676
  18.9 4.5 %collective-permute-start.2 = (f32[4,2,512,128]{3,2,1,0:T(8,128)}, f32[4,2,512,128]{3,2,1,0:T(8,128)S(1)}, u32[]{:S(2)}, u32[]{:S(2)}) collective-permute-start(f32[4,2,512,128]{3,2,1,0:T(8,128)} %get-tuple-element.32), channel_id=1, source_target_pairs={{0,8},{8,0},{16,24},{24,16},{32,40},{40,32},{48,56},{56,48},{64,72... | collective-permute-start | bytes 6291464 | tf_op jit(solution)/shard_map/ppermute | solution.py:385
  19.0 7.5 %collective-permute-start.3 = (f32[2,2,2,544,128]{4,3,2,1,0:T(8,128)}, f32[2,2,2,544,128]{4,3,2,1,0:T(8,128)S(1)}, u32[]{:S(2)}, u32[]{:S(2)}) collective-permute-start(f32[2,2,2,544,128]{4,3,2,1,0:T(8,128)} %get-tuple-element.33), channel_id=1, source_target_pairs={{0,8},{8,0},{16,24},{24,16},{32,40},{40,32},{48,56},{56,48},{64,72... | collective-permute-start | bytes 6684680 | tf_op jit(solution)/shard_map/ppermute | solution.py:385
  19.5 24.1 %collective-permute-start.1 = (f32[2,2,2,544,128]{4,3,2,1,0:T(8,128)}, f32[2,2,2,544,128]{4,3,2,1,0:T(8,128)S(1)}, u32[]{:S(2)}, u32[]{:S(2)}) collective-permute-start(f32[2,2,2,544,128]{4,3,2,1,0:T(8,128)} %get-tuple-element.30), channel_id=1, source_target_pairs={{0,8},{8,0},{16,24},{24,16},{32,40},{40,32},{48,56},{56,48},{64,72... | collective-permute-start | bytes 6684680 | tf_op jit(solution)/shard_map/ppermute | solution.py:385
  23.3 3.2 %copy-start.4 = (f32[4,2,512,128]{3,2,1,0:T(8,128)}, f32[4,2,512,128]{3,2,1,0:T(8,128)S(1)}, u32[]{:S(2)}) copy-start(f32[4,2,512,128]{3,2,1,0:T(8,128)S(1)} %collective-permute-done.2) | copy-start | bytes 6291460
  26.5 17.0 %copy-start = (f32[2,2,2,544,128]{4,3,2,1,0:T(8,128)S(1)}, f32[2,2,2,544,128]{4,3,2,1,0:T(8,128)}, u32[]{:S(2)}) copy-start(f32[2,2,2,544,128]{4,3,2,1,0:T(8,128)} %get-tuple-element.29) | copy-start | bytes 6684676
  26.8 16.8 %collective-permute-start.8 = (f32[2,2,544,128]{3,2,1,0:T(8,128)S(1)}, f32[2,2,544,128]{3,2,1,0:T(8,128)S(1)}, u32[]{:S(2)}, u32[]{:S(2)}) collective-permute-start(f32[2,2,544,128]{3,2,1,0:T(8,128)S(1)} %get-tuple-element.55), channel_id=1, source_target_pairs={{0,16},{8,56},{16,32},{24,8},{32,48},{40,24},{48,0},{56,40},{64,80... | collective-permute-start | bytes 3342344 | tf_op jit(solution)/shard_map/ppermute | solution.py:389
  28.4 29.0 %collective-permute-start = (f32[4,2,512,128]{3,2,1,0:T(8,128)}, f32[4,2,512,128]{3,2,1,0:T(8,128)}, u32[]{:S(2)}, u32[]{:S(2)}) collective-permute-start(f32[4,2,512,128]{3,2,1,0:T(8,128)} %get-tuple-element.27), channel_id=1, source_target_pairs={{0,8},{8,0},{16,24},{24,16},{32,40},{40,32},{48,56},{56,48},{64,72... | collective-permute-start | bytes 6291464 | tf_op jit(solution)/shard_map/ppermute | solution.py:385
  29.7 29.7 %collective-permute-start.5 = (f32[2,2,512,128]{3,2,1,0:T(8,128)}, f32[2,2,512,128]{3,2,1,0:T(8,128)}, u32[]{:S(2)}, u32[]{:S(2)}) collective-permute-start(f32[2,2,512,128]{3,2,1,0:T(8,128)} %slice_add_fusion.2), channel_id=1, source_target_pairs={{0,64},{8,72},{16,80},{24,88},{32,96},{40,104},{48,112},{56,120},{... | collective-permute-start | bytes 3145736 | tf_op jit(solution)/shard_map/ppermute | solution.py:397
  43.5 1.8 %copy-start.1 = (f32[2,2,2,544,128]{4,3,2,1,0:T(8,128)}, f32[2,2,2,544,128]{4,3,2,1,0:T(8,128)S(1)}, u32[]{:S(2)}) copy-start(f32[2,2,2,544,128]{4,3,2,1,0:T(8,128)S(1)} %collective-permute-done.1) | copy-start | bytes 6684676
  45.3 28.5 %collective-permute-start.9 = (f32[2,2,544,128]{3,2,1,0:T(8,128)}, f32[2,2,544,128]{3,2,1,0:T(8,128)}, u32[]{:S(2)}, u32[]{:S(2)}) collective-permute-start(f32[2,2,544,128]{3,2,1,0:T(8,128)} %fusion.2), channel_id=1, source_target_pairs={{0,16},{8,56},{16,32},{24,8},{32,48},{40,24},{48,0},{56,40},{64,80... | collective-permute-start | bytes 3342344 | tf_op jit(solution)/shard_map/ppermute | solution.py:389
  45.7 28.1 %collective-permute-start.4 = (f32[2,2,544,128]{3,2,1,0:T(8,128)S(1)}, f32[2,2,544,128]{3,2,1,0:T(8,128)}, u32[]{:S(2)}, u32[]{:S(2)}) collective-permute-start(f32[2,2,544,128]{3,2,1,0:T(8,128)S(1)} %get-tuple-element.54), channel_id=1, source_target_pairs={{0,48},{8,24},{16,0},{24,40},{32,16},{40,56},{48,32},{56,8},{64,11... | collective-permute-start | bytes 3342344 | tf_op jit(solution)/shard_map/ppermute | solution.py:393
  48.5 11.9 %copy-start.5 = (f32[4,2,512,128]{3,2,1,0:T(8,128)S(1)}, f32[4,2,512,128]{3,2,1,0:T(8,128)}, u32[]{:S(2)}) copy-start(f32[4,2,512,128]{3,2,1,0:T(8,128)} %get-tuple-element.26) | copy-start | bytes 6291460
  50.4 11.9 %collective-permute-start.6 = (f32[544,128]{1,0:T(8,128)S(1)}, f32[544,128]{1,0:T(8,128)S(1)}, u32[]{:S(2)}, u32[]{:S(2)}) collective-permute-start(f32[544,128]{1,0:T(8,128)S(1)} %pad_maximum_fusion), channel_id=1, source_target_pairs={{0,1},{1,2},{2,3},{3,4},{4,5},{5,6},{6,7},{8,9},{9,10},{10,11},{11... | collective-permute-start | bytes 835592 | tf_op jit(solution)/shard_map/ppermute | solution.py:429
  57.4 12.4 %collective-permute-start.7 = (f32[544,128]{1,0:T(8,128)S(1)}, f32[544,128]{1,0:T(8,128)S(1)}, u32[]{:S(2)}, u32[]{:S(2)}) collective-permute-start(f32[544,128]{1,0:T(8,128)S(1)} %pad_maximum_fusion), channel_id=1, source_target_pairs={{1,0},{2,1},{3,2},{4,3},{5,4},{6,5},{7,6},{9,8},{10,9},{11,10},{12... | collective-permute-start | bytes 835592 | tf_op jit(solution)/shard_map/ppermute | solution.py:429
  59.3 15.8 %collective-permute-start.10 = (f32[2,512,128]{2,1,0:T(8,128)S(1)}, f32[2,512,128]{2,1,0:T(8,128)S(1)}, u32[]{:S(2)}, u32[]{:S(2)}) collective-permute-start(f32[2,512,128]{2,1,0:T(8,128)S(1)} %add_bitcast_fusion.2), channel_id=1, source_target_pairs={{0,64},{8,72},{16,80},{24,88},{32,96},{40,104},{48,112},{56,120},{... | collective-permute-start | bytes 1572872 | tf_op jit(solution)/shard_map/ppermute | solution.py:397
  60.5 13.4 %copy-start.2 = (f32[2,2,2,544,128]{4,3,2,1,0:T(8,128)S(1)}, f32[2,2,2,544,128]{4,3,2,1,0:T(8,128)}, u32[]{:S(2)}) copy-start(f32[2,2,2,544,128]{4,3,2,1,0:T(8,128)} %copy-done.1) | copy-start | bytes 6684676
  73.8 13.6 %collective-permute-start.13 = (f32[2,512,128]{2,1,0:T(8,128)S(1)}, f32[2,512,128]{2,1,0:T(8,128)S(1)}, u32[]{:S(2)}, u32[]{:S(2)}) collective-permute-start(f32[2,512,128]{2,1,0:T(8,128)S(1)} %get-tuple-element.42), channel_id=1, source_target_pairs={{0,16},{8,56},{16,32},{24,8},{32,48},{40,24},{48,0},{56,40},{64,80... | collective-permute-start | bytes 1572872 | tf_op jit(solution)/shard_map/ppermute | solution.py:389
  75.2 15.5 %collective-permute-start.14 = (f32[2,544,128]{2,1,0:T(8,128)S(1)}, f32[2,544,128]{2,1,0:T(8,128)S(1)}, u32[]{:S(2)}, u32[]{:S(2)}) collective-permute-start(f32[2,544,128]{2,1,0:T(8,128)S(1)} %fusion.8), channel_id=1, source_target_pairs={{0,64},{8,72},{16,80},{24,88},{32,96},{40,104},{48,112},{56,120},{... | collective-permute-start | bytes 1671176 | tf_op jit(solution)/shard_map/ppermute | solution.py:397
  77.2 22.6 %collective-permute-start.12 = (f32[2,512,128]{2,1,0:T(8,128)S(1)}, f32[2,512,128]{2,1,0:T(8,128)S(1)}, u32[]{:S(2)}, u32[]{:S(2)}) collective-permute-start(f32[2,512,128]{2,1,0:T(8,128)S(1)} %get-tuple-element.40), channel_id=1, source_target_pairs={{0,48},{8,24},{16,0},{24,40},{32,16},{40,56},{48,32},{56,8},{64,11... | collective-permute-start | bytes 1572872 | tf_op jit(solution)/shard_map/ppermute | solution.py:393
  81.7 19.8 %collective-permute-start.11 = (f32[2,512,128]{2,1,0:T(8,128)S(1)}, f32[2,512,128]{2,1,0:T(8,128)S(1)}, u32[]{:S(2)}, u32[]{:S(2)}) collective-permute-start(f32[2,512,128]{2,1,0:T(8,128)S(1)} %add_bitcast_fusion.1), channel_id=1, source_target_pairs={{0,64},{8,72},{16,80},{24,88},{32,96},{40,104},{48,112},{56,120},{... | collective-permute-start | bytes 1572872 | tf_op jit(solution)/shard_map/ppermute | solution.py:397
  90.7 10.8 %collective-permute-start.15 = (f32[2,512,128]{2,1,0:T(8,128)S(1)}, f32[2,512,128]{2,1,0:T(8,128)S(1)}, u32[]{:S(2)}, u32[]{:S(2)}) collective-permute-start(f32[2,512,128]{2,1,0:T(8,128)S(1)} %fusion.12), channel_id=1, source_target_pairs={{0,16},{8,56},{16,32},{24,8},{32,48},{40,24},{48,0},{56,40},{64,80... | collective-permute-start | bytes 1572872 | tf_op jit(solution)/shard_map/ppermute | solution.py:389
  92.2 10.6 %collective-permute-start.16 = (f32[544,128]{1,0:T(8,128)S(1)}, f32[544,128]{1,0:T(8,128)S(1)}, u32[]{:S(2)}, u32[]{:S(2)}) collective-permute-start(f32[544,128]{1,0:T(8,128)S(1)} %get-tuple-element.57), channel_id=1, source_target_pairs={{0,1},{1,2},{2,3},{3,4},{4,5},{5,6},{6,7},{8,9},{9,10},{10,11},{11... | collective-permute-start | bytes 835592 | tf_op jit(solution)/shard_map/ppermute | solution.py:446
  97.9 12.7 %collective-permute-start.17 = (f32[544,128]{1,0:T(8,128)S(1)}, f32[544,128]{1,0:T(8,128)S(1)}, u32[]{:S(2)}, u32[]{:S(2)}) collective-permute-start(f32[544,128]{1,0:T(8,128)S(1)} %get-tuple-element.56), channel_id=1, source_target_pairs={{1,0},{2,1},{3,2},{4,3},{5,4},{6,5},{7,6},{9,8},{10,9},{11,10},{12... | collective-permute-start | bytes 835592 | tf_op jit(solution)/shard_map/ppermute | solution.py:446

commit v11 on v8

--- a/solution.py
+++ b/solution.py
@@ -80,8 +80,9 @@
     return me // 8, lax.rem(me // 2, 4), lax.rem(me, 2)
 
 
-def series_kernel(coeffs, u, k, p, cos, sin, far_other, far_same, near_other, near_same, ends_other, ends_same, rest_other, rest_same,
-                  us, ks, ns, ds, vs, fx, fy, fw, fz, fm, es, in_sem, out_sem, edge_sem):
+def series_kernel(coeffs, u, k, p, cos, sin, *refs):
+    near, far_rest, far_ends, rest, two, three = (refs[2 * i : 2 * i + 2] for i in range(6))
+    us, ks, ns, ds, vs, fx, fy, fw, fz, fm, es, in_sem, out_sem, edge_sem = refs[12:]
     cells = u.shape[0] // 16
     rows = cells // CHIPS
     half_rows = rows // 2
@@ -218,31 +219,31 @@
     def place(c, core):
         return lax.rem((1 - 2 * core) * (lax.rem(c, 4) - my_y) + 8, 4), lax.rem(c // 4 + my_z, 2)
 
-    def stores(c, core, same, far):
+    def stores(c, core, same, kind):
         turn, _ = place(c, core)
         here = pl.ds((c * rows + core * half_rows) * 16, half_rows * 16)
-        to = ((far_other, far_same) if far else (near_other, near_same))[same]
-        return [pltpu.make_async_copy(a.at[here], to.at[turn, i], out_sem.at[i, core, c]) for i, a in enumerate((ds, vs))]
-
-    def edge_stores(c, core, same, is_end):
+        to = (near, far_rest, far_ends)[kind][same].at[turn - 2 if kind == 2 else turn]
+        return [pltpu.make_async_copy(a.at[here], to.at[i], out_sem.at[i, core, c]) for i, a in enumerate((ds, vs))]
+
+    def edge_stores(c, core, same, kind):
         turn, side = place(c, core)
         here = pl.ds((c * rows + core * half_rows) * 16, (half_rows + 2) * 16)
-        to = ((ends_other, ends_same) if is_end else (rest_other, rest_same))[same]
-        return [pltpu.make_async_copy(es.at[i, here], to.at[lax.rem(turn, 2), side, i], edge_sem.at[i, core, c]) for i in (0, 1)]
-
-    def send(copies, c, core, test):
+        to = (rest[same].at[turn, side], two[same].at[side], three[same].at[side])[kind]
+        return [pltpu.make_async_copy(es.at[i, here], to.at[i], edge_sem.at[i, core, c]) for i in (0, 1)]
+
+    def send(copies, c, core, kind_of):
         for same in (0, 1):
-            for kind in (0, 1):
-                @pl.when(((my_core == core) == (same == 1)) & (test(*place(c, core)) == (kind == 1)))
+            for kind in (0, 1, 2):
+                @pl.when(((my_core == core) == (same == 1)) & (kind_of(*place(c, core)) == kind))
                 def _():
                     for copy in copies(c, core, same, kind):
                         copy.start()
 
     def send_edges(c, core):
-        send(edge_stores, c, core, lambda turn, side: turn >= 2)
+        send(edge_stores, c, core, lambda turn, side: jnp.maximum(turn - 1, 0))
 
     def send_series(c, core):
-        send(stores, c, core, lambda turn, side: side == 1)
+        send(stores, c, core, lambda turn, side: side * (1 + turn // 2))
 
     def chunk(c, carry):
         @pl.when(c < CHIPS)
@@ -276,7 +277,7 @@
 
     def end(c, carry):
         for core in (0, 1):
-            for copy in stores(c, core, 1, 1) + edge_stores(c, core, 1, 1):
+            for copy in stores(c, core, 1, 0) + edge_stores(c, core, 1, 1):
                 copy.wait()
         return carry
 
@@ -328,15 +329,15 @@
 
 def series(coeffs, u, k, p, cos, sin):
     cells = u.shape[0] // 16
-    share = jax.ShapeDtypeStruct((4, 2, cells // COUNT * 16, 128), F32)
-    edge = jax.ShapeDtypeStruct((2, 2, 2, (cells // COUNT + 2) * 16, 128), F32)
+    share, edge = (2, cells // COUNT * 16, 128), (2, (cells // COUNT + 2) * 16, 128)
+    shapes = ((4, *share), (2, *share), (2, *share), (2, 2, *edge), (2, *edge), (2, *edge))
     wide = pltpu.VMEM(((cells + 2) * 16, 128), F32)
     exact = pltpu.VMEM((cells * 16, 128), F32)
     return pl.pallas_call(
         series_kernel,
-        out_shape=(share,) * 4 + (edge,) * 4,
+        out_shape=[jax.ShapeDtypeStruct(shape, F32) for shape in shapes for _ in range(2)],
         in_specs=[SMEM] + [ANYWHERE] * 5,
-        out_specs=(ANYWHERE,) * 8,
+        out_specs=[ANYWHERE] * 12,
         scratch_shapes=[wide, wide, wide, exact, exact, wide, wide, wide, wide, wide]
         + [
             pltpu.VMEM((2, (cells + 2) * 16, 128), F32),
@@ -408,15 +409,15 @@
     me = lax.axis_index("tm")
 
     outs = series(series_coeffs, u, k, p, cos, sin)
-    far_other, far_same, near_other, near_same, ends_other, ends_same, rest_other, rest_same = outs
-
-    ends_came, far_came = to_sibling(ends_other), to_sibling(far_other)
-    rest_came, near_came = to_sibling(rest_other), to_sibling(near_other)
-    ends_two = forth(ends_same[0] + ends_came[0])
-    far_ends = far_same[2:] + far_came[2:]
-    far_ends, ends_came = after(far_ends, ends_came)
-    far_ends_came, far_rest_came = across(far_ends), across(far_same[:2] + far_came[:2])
-    ends_back = back(ends_same[1] + ends_came[1])
+    near, far_rest, far_ends, rest, two, three = (outs[2 * i : 2 * i + 2] for i in range(6))
+
+    two_came, far_came, three_came = to_sibling(two[0]), to_sibling(far_ends[0]), to_sibling(three[0])
+    two_came, others = after(two_came, (rest[0], near[0], far_rest[0]))
+    rest_came, near_came, far_rest_came = (to_sibling(other) for other in others)
+    two, far_came = after(two[1] + two_came, far_came)
+    two = forth(two)
+    far_ends = across(far_ends[1] + far_came)
+    three = back(three[1] + three_came)
 
     start = me * rows * 16
     k_here = jnp.concatenate(
@@ -428,20 +429,23 @@
     )
     k_low, k_high = lax.ppermute(k_here, "gz", UP), lax.ppermute(k_here, "gz", DOWN)
 
-    ring = forth(rest_same[1] + rest_came[1] + ends_two)
-    two, direct = (near_same[t] + near_came[t] + far_ends_came[t - 2] for t in (2, 3))
-    (two, direct, k_low, k_high), ring = after((two, direct, k_low, k_high), ring)
-    two, direct = forth(two), back(direct)
-    edge_far = rest_same[0, 1] + rest_came[0, 1] + ends_back[1] + ring[1]
-    edge_far, far_rest_came = after(edge_far, far_rest_came)
+    ring = forth(rest[1][1] + rest_came[1] + two)
+    two, far_rest_came = after(two, far_rest_came)
+    far_next = across(far_rest[1][1] + far_rest_came[1])
+    relay, direct = (near[1][t] + near_came[t] + far_ends[t - 2] for t in (2, 3))
+    far_own = far_rest[1][0] + far_rest_came[0]
+    (relay, direct, far_own, k_low, k_high), ring = after((relay, direct, far_own, k_low, k_high), ring)
+    relay, direct, far_own = forth(relay), back(direct), across(far_own)
+    edge_far = rest[1][0, 1] + rest_came[0, 1] + three[1] + ring[1]
+    edge_far, far_next = after(edge_far, far_next)
     edge_far = across(edge_far)
-    last = near_same[1] + near_came[1] + far_rest_came[1] + two
+    last = near[1][1] + near_came[1] + far_next + relay
     last, edge_far = after(last, edge_far)
     last = forth(last)
-    edge = rest_same[0, 0] + rest_came[0, 0] + ends_back[0] + ring[0] + edge_far
+    edge = rest[1][0, 0] + rest_came[0, 0] + three[0] + ring[0] + edge_far
     low, high = edge[0], edge[1]
     above, below = lax.ppermute(low, "gz", DOWN), lax.ppermute(high, "gz", UP)
-    result = near_same[0] + near_came[0] + far_rest_came[0] + direct + last
+    result = near[1][0] + near_came[0] + far_own + direct + last
     d, v = result[0], result[1]
 
     wide = (a.reshape(rows + 2, *CELL) for a in (low, high, below, above, k_here, k_low, k_high))

time: 114 us -> 126 us (1.11)
  the two profiles are of different devices: /device:TPU:6 before, /device:TPU:126 now
where the time goes in v11:
time: 126 us
  waiting for transfers between devices  72.5 us (58%)
  Pallas kernels  20.4 us (16%)
  starting transfers between devices  16.5 us (13%)
  other arithmetic  13.8 us (11%)
  local copies, waits for them, and re-layouts  1.8 us (1%)
    ppermute x4, waiting for transfers between devices, across(): return lax.ppermute(cells, 'tm', ACROSS)  49.1 us
    pallas_call x1, Pallas kernels, series(): pl.pallas_call(series_kernel, out_shape=[jax.ShapeDtypeStruct(shape, F32)...  18.5 us
    ppermute x4, waiting for transfers between devices, forth(): return lax.ppermute(cells, 'tm', FORTH)  13.3 us
    ppermute x6, waiting for transfers between devices, to_sibling(): return lax.ppermute(other, 'tm', SIBLING)  7.14 us
    ppermute x2, starting transfers between devices, local(): above, below = (lax.ppermute(low, 'gz', DOWN), lax.ppermute(high, 'gz', UP))  5.86 us
    ppermute x1, waiting for transfers between devices, local(): lax.ppermute(k_here, 'gz', DOWN)  3.02 us
    ppermute x4, starting transfers between devices, across(): return lax.ppermute(cells, 'tm', ACROSS)  2.89 us
    ppermute x1, starting transfers between devices, local(): lax.ppermute(k_here, 'gz', DOWN)  2.74 us
  transfers between devices with their start and end apart: 20, of which 8 were waited for; matrix products, arithmetic and copies ran while one was open for 12% of the time, Pallas kernels for 0%

profile of v11, /device:TPU:126, one launch (start us, length us, event | category | flops | bytes accessed | tf_op | source)
XLA Modules:
  0.0 125.8 jit_solution(6416653344721438695)
XLA Ops:
  0.6 18.5 %shard_map.77 = (f32[4,2,512,128]{3,2,1,0:T(8,128)}, f32[4,2,512,128]{3,2,1,0:T(8,128)}, f32[2,2,512,128]{3,2,1,0:T(8,128)}, f32[2,2,512,128]{3,2,1,0:T(8,128)},...) custom-call(f32[1,4]{1,0:T(1,128)} %coeffs.1, ...), custom_call_target="tpu_custom_call" | custom-call | bytes 47185920 | tf_op jit(solution)/shard_map/pallas_call | solution.py:336
  19.1 0.1 collective-permute-start
  19.2 3.0 %collective-permute-done = f32[2,2,544,128]{3,2,1,0:T(8,128)S(1)} collective-permute-done((f32[2,2,544,128]{3,2,1,0:T(8,128)}, f32[2,2,544,128]{3,2,1,0:T(8,128)S(1)}, u32[]{:S(2)}, u32[]{:S(2)}) %collective-permute-start) | collective-permute-done | bytes 1114144 | tf_op jit(solution)/shard_map/ppermute | solution.py:386
  22.2 0.1 collective-permute-start.8
  22.3 0.4 collective-permute-start.2
  22.7 1.4 %add.118 = f32[2,2,544,128]{3,2,1,0:T(8,128)S(1)} add(f32[2,2,544,128]{3,2,1,0:T(8,128)} %get-tuple-element.40, f32[2,2,544,128]{3,2,1,0:T(8,128)S(1)} %collective-permute-done) | non-fusion elementwise | flops 278528 | bytes 3342336 | tf_op jit(solution)/shard_map/add | solution.py:417
  24.1 4.2 %collective-permute-done.2 = f32[2,2,512,128]{3,2,1,0:T(8,128)S(1)} collective-permute-done((f32[2,2,512,128]{3,2,1,0:T(8,128)}, f32[2,2,512,128]{3,2,1,0:T(8,128)S(1)}, u32[]{:S(2)}, u32[]{:S(2)}) %collective-permute-start.2) | collective-permute-done | bytes 1048608 | tf_op jit(solution)/shard_map/ppermute | solution.py:386
  28.2 0.2 collective-permute-start.4
  28.4 0.4 collective-permute-start.1
  28.9 0.1 collective-permute-start.12
  29.0 0.4 collective-permute-start.5
  29.4 1.1 add.119
  30.5 13.3 %collective-permute-done.4 = f32[2,2,544,128]{3,2,1,0:T(8,128)S(1)} collective-permute-done((f32[2,2,544,128]{3,2,1,0:T(8,128)S(1)}, f32[2,2,544,128]{3,2,1,0:T(8,128)S(1)}, u32[]{:S(2)}, u32[]{:S(2)}) %collective-permute-start.4) | collective-permute-done | bytes 1114144 | tf_op jit(solution)/shard_map/ppermute | solution.py:390
  43.7 0.4 collective-permute-start.3
  44.1 0.0 collective-permute-done.8
  44.2 1.2 fusion.1
  45.3 0.5 copy-done.1
  45.9 1.4 %collective-permute-start.9 = (f32[2,2,544,128]{3,2,1,0:T(8,128)}, f32[2,2,544,128]{3,2,1,0:T(8,128)S(1)}, u32[]{:S(2)}, u32[]{:S(2)}) collective-permute-start(f32[2,2,544,128]{3,2,1,0:T(8,128)} %fusion.1), channel_id=1, source_target_pairs={{0,16},{8,56},{16,32},{24,8},{32,48},{40,24},{48,0},{56,40},{64,80... | collective-permute-start | bytes 3342344 | tf_op jit(solution)/shard_map/ppermute | solution.py:390
  47.3 0.0 collective-permute-done.12
  47.3 1.1 add.139
  48.4 0.6 collective-permute-start.13
  49.0 0.7 dynamic-slice_select_fusion.1
  49.7 1.1 constant_dynamic-slice_fusion
  50.9 0.0 collective-permute-done.5
  50.9 1.3 %collective-permute-start.6 = (f32[544,128]{1,0:T(8,128)S(1)}, f32[544,128]{1,0:T(8,128)S(1)}, u32[]{:S(2)}, u32[]{:S(2)}) collective-permute-start(f32[544,128]{1,0:T(8,128)S(1)} %pad_maximum_fusion), channel_id=1, source_target_pairs={{0,1},{1,2},{2,3},{3,4},{4,5},{5,6},{6,7},{8,9},{9,10},{10,11},{11... | collective-permute-start | bytes 835592 | tf_op jit(solution)/shard_map/ppermute | solution.py:430
  52.2 1.6 %add_bitcast_fusion = (f32[2,512,128]{2,1,0:T(8,128)S(1)}, f32[2,512,128]{2,1,0:T(8,128)S(1)}) fusion(f32[2,2,512,128]{3,2,1,0:T(8,128)} %collective-permute-done.5, f32[2,2,512,128]{3,2,1,0:T(8,128)} %get-tuple-element.44), kind=kLoop, calls=%fused_computation.29 | loop fusion | flops 262144 | bytes 3145728 | tf_op jit(solution)/shard_map/add | solution.py:434
  53.8 15.5 %collective-permute-done.3 = f32[2,2,512,128]{3,2,1,0:T(8,128)} collective-permute-done((f32[2,2,512,128]{3,2,1,0:T(8,128)}, f32[2,2,512,128]{3,2,1,0:T(8,128)}, u32[]{:S(2)}, u32[]{:S(2)}) %collective-permute-start.3) | collective-permute-done | bytes 1048608 | tf_op jit(solution)/shard_map/ppermute | solution.py:398
  69.3 2.7 %collective-permute-start.7 = (f32[544,128]{1,0:T(8,128)S(1)}, f32[544,128]{1,0:T(8,128)S(1)}, u32[]{:S(2)}, u32[]{:S(2)}) collective-permute-start(f32[544,128]{1,0:T(8,128)S(1)} %pad_maximum_fusion), channel_id=1, source_target_pairs={{1,0},{2,1},{3,2},{4,3},{5,4},{6,5},{7,6},{9,8},{10,9},{11,10},{12... | collective-permute-start | bytes 835592 | tf_op jit(solution)/shard_map/ppermute | solution.py:430
  72.1 0.5 collective-permute-start.14
  72.6 1.9 %fusion.12 = (f32[2,512,128]{2,1,0:T(8,128)S(1)}, f32[2,512,128]{2,1,0:T(8,128)S(1)}) fusion(f32[2,2,512,128]{3,2,1,0:T(8,128)} %collective-permute-done.3, f32[4,2,512,128]{3,2,1,0:T(8,128)} %collective-permute-done.1, f32[4,2,512,128]{3,2,1,0:T(8,128)S(1)} %copy-done.3), kind=kLoop, calls=%fused_computation.19 | loop fusion | flops 524288 | bytes 4194304 | tf_op jit(solution)/shard_map/add | solution.py:435
  74.5 3.0 %collective-permute-done.7 = f32[544,128]{1,0:T(8,128)S(1)} collective-permute-done((f32[544,128]{1,0:T(8,128)S(1)}, f32[544,128]{1,0:T(8,128)S(1)}, u32[]{:S(2)}, u32[]{:S(2)}) %collective-permute-start.7) | collective-permute-done | bytes 278560 | tf_op jit(solution)/shard_map/ppermute | solution.py:430
  77.5 0.0 collective-permute-done.9
  77.5 0.0 collective-permute-start.15
  77.5 0.0 collective-permute-done.13
  77.5 1.2 fusion.7
  78.7 12.2 %collective-permute-done.14 = f32[2,512,128]{2,1,0:T(8,128)S(1)} collective-permute-done((f32[2,512,128]{2,1,0:T(8,128)S(1)}, f32[2,512,128]{2,1,0:T(8,128)S(1)}, u32[]{:S(2)}, u32[]{:S(2)}) %collective-permute-start.14) | collective-permute-done | bytes 524320 | tf_op jit(solution)/shard_map/ppermute | solution.py:398
  90.9 0.5 collective-permute-start.16
  91.4 1.5 %collective-permute-start.10 = (f32[2,512,128]{2,1,0:T(8,128)S(1)}, f32[2,512,128]{2,1,0:T(8,128)S(1)}, u32[]{:S(2)}, u32[]{:S(2)}) collective-permute-start(f32[2,512,128]{2,1,0:T(8,128)S(1)} %get-tuple-element.50), channel_id=1, source_target_pairs={{0,64},{8,72},{16,80},{24,88},{32,96},{40,104},{48,112},{56,120},{... | collective-permute-start | bytes 1572872 | tf_op jit(solution)/shard_map/ppermute | solution.py:398
  92.9 1.2 fusion.11
  94.1 12.3 %collective-permute-done.16 = f32[2,544,128]{2,1,0:T(8,128)S(1)} collective-permute-done((f32[2,544,128]{2,1,0:T(8,128)S(1)}, f32[2,544,128]{2,1,0:T(8,128)S(1)}, u32[]{:S(2)}, u32[]{:S(2)}) %collective-permute-start.16) | collective-permute-done | bytes 557088 | tf_op jit(solution)/shard_map/ppermute | solution.py:398
  106.4 0.0 collective-permute-start.17
  106.4 1.2 fusion.4
  107.6 0.1 slice_bitcast_fusion.3
  107.7 1.3 %collective-permute-start.18 = (f32[544,128]{1,0:T(8,128)S(1)}, f32[544,128]{1,0:T(8,128)S(1)}, u32[]{:S(2)}, u32[]{:S(2)}) collective-permute-start(f32[544,128]{1,0:T(8,128)S(1)} %get-tuple-element.71), channel_id=1, source_target_pairs={{0,1},{1,2},{2,3},{3,4},{4,5},{5,6},{6,7},{8,9},{9,10},{10,11},{11... | collective-permute-start | bytes 835592 | tf_op jit(solution)/shard_map/ppermute | solution.py:447
  109.0 4.6 %collective-permute-start.19 = (f32[544,128]{1,0:T(8,128)S(1)}, f32[544,128]{1,0:T(8,128)S(1)}, u32[]{:S(2)}, u32[]{:S(2)}) collective-permute-start(f32[544,128]{1,0:T(8,128)S(1)} %get-tuple-element.70), channel_id=1, source_target_pairs={{1,0},{2,1},{3,2},{4,3},{5,4},{6,5},{7,6},{9,8},{10,9},{11,10},{12... | collective-permute-start | bytes 835592 | tf_op jit(solution)/shard_map/ppermute | solution.py:447
  113.6 9.1 %collective-permute-done.10 = f32[2,512,128]{2,1,0:T(8,128)S(1)} collective-permute-done((f32[2,512,128]{2,1,0:T(8,128)S(1)}, f32[2,512,128]{2,1,0:T(8,128)S(1)}, u32[]{:S(2)}, u32[]{:S(2)}) %collective-permute-start.10) | collective-permute-done | bytes 524320 | tf_op jit(solution)/shard_map/ppermute | solution.py:398
  122.7 1.2 fusion.17
  123.9 1.9 %shard_map.78 = (f32[32,2,8,128]{3,2,1,0:T(8,128)}, f32[32,2,8,128]{3,2,1,0:T(8,128)}) custom-call(f32[32,2,8,128]{3,2,1,0:T(8,128)S(1)} %bitcast.104, f32[32,2,8,128]{3,2,1,0:T(8,128)S(1)} %bitcast.103, f32[34,2,8,128]{3,2,1,0:T(8,128)S(1)} %bitcast.101, f32[34,2,8,128]{3,2,1,0:T(8,128)S(1)} %bitcast.100, f32[34,2,8,128]{3,2,1,0:T(8,128)S(1)} %bitcast.107, ...), custom_call_target="tpu_custom_call" | custom-call | bytes 4194304 | tf_op jit(solution)/shard_map/pallas_call | solution.py:356
  (23 shorter events, 0.1 us)
Async XLA Ops:
  19.1 9.7 %copy-start.6 = (f32[2,2,544,128]{3,2,1,0:T(8,128)S(1)}, f32[2,2,544,128]{3,2,1,0:T(8,128)}, u32[]{:S(2)}) copy-start(f32[2,2,544,128]{3,2,1,0:T(8,128)} %get-tuple-element.53) | copy-start | bytes 3342340
  19.1 10.2 %copy-start.5 = (f32[2,2,512,128]{3,2,1,0:T(8,128)S(1)}, f32[2,2,512,128]{3,2,1,0:T(8,128)}, u32[]{:S(2)}) copy-start(f32[2,2,512,128]{3,2,1,0:T(8,128)} %get-tuple-element.39) | copy-start | bytes 3145732
  19.1 3.0 %collective-permute-start = (f32[2,2,544,128]{3,2,1,0:T(8,128)}, f32[2,2,544,128]{3,2,1,0:T(8,128)S(1)}, u32[]{:S(2)}, u32[]{:S(2)}) collective-permute-start(f32[2,2,544,128]{3,2,1,0:T(8,128)} %get-tuple-element.34), channel_id=1, source_target_pairs={{0,8},{8,0},{16,24},{24,16},{32,40},{40,32},{48,56},{56,48},{64,72... | collective-permute-start | bytes 3342344 | tf_op jit(solution)/shard_map/ppermute | solution.py:386
  22.2 22.0 %collective-permute-start.8 = (f32[2,2,2,544,128]{4,3,2,1,0:T(8,128)}, f32[2,2,2,544,128]{4,3,2,1,0:T(8,128)S(1)}, u32[]{:S(2)}, u32[]{:S(2)}) collective-permute-start(f32[2,2,2,544,128]{4,3,2,1,0:T(8,128)} %get-tuple-element.49), channel_id=1, source_target_pairs={{0,8},{8,0},{16,24},{24,16},{32,40},{40,32},{48,56},{56,48},{64,72... | collective-permute-start | bytes 6684680 | tf_op jit(solution)/shard_map/ppermute | solution.py:386
  22.3 5.9 %collective-permute-start.2 = (f32[2,2,512,128]{3,2,1,0:T(8,128)}, f32[2,2,512,128]{3,2,1,0:T(8,128)S(1)}, u32[]{:S(2)}, u32[]{:S(2)}) collective-permute-start(f32[2,2,512,128]{3,2,1,0:T(8,128)} %get-tuple-element.42), channel_id=1, source_target_pairs={{0,8},{8,0},{16,24},{24,16},{32,40},{40,32},{48,56},{56,48},{64,72... | collective-permute-start | bytes 3145736 | tf_op jit(solution)/shard_map/ppermute | solution.py:386
  24.1 20.1 %copy-start = (f32[2,2,2,544,128]{4,3,2,1,0:T(8,128)S(1)}, f32[2,2,2,544,128]{4,3,2,1,0:T(8,128)}, u32[]{:S(2)}) copy-start(f32[2,2,2,544,128]{4,3,2,1,0:T(8,128)} %get-tuple-element.48) | copy-start | bytes 6684676
  28.2 15.5 %collective-permute-start.4 = (f32[2,2,544,128]{3,2,1,0:T(8,128)S(1)}, f32[2,2,544,128]{3,2,1,0:T(8,128)S(1)}, u32[]{:S(2)}, u32[]{:S(2)}) collective-permute-start(f32[2,2,544,128]{3,2,1,0:T(8,128)S(1)} %add.118), channel_id=1, source_target_pairs={{0,16},{8,56},{16,32},{24,8},{32,48},{40,24},{48,0},{56,40},{64,80... | collective-permute-start | bytes 3342344 | tf_op jit(solution)/shard_map/ppermute | solution.py:390
  28.4 43.6 %collective-permute-start.1 = (f32[4,2,512,128]{3,2,1,0:T(8,128)}, f32[4,2,512,128]{3,2,1,0:T(8,128)}, u32[]{:S(2)}, u32[]{:S(2)}) collective-permute-start(f32[4,2,512,128]{3,2,1,0:T(8,128)} %get-tuple-element.38), channel_id=1, source_target_pairs={{0,8},{8,0},{16,24},{24,16},{32,40},{40,32},{48,56},{56,48},{64,72... | collective-permute-start | bytes 6291464 | tf_op jit(solution)/shard_map/ppermute | solution.py:386
  28.9 18.5 %collective-permute-start.12 = (f32[2,2,544,128]{3,2,1,0:T(8,128)S(1)}, f32[2,2,544,128]{3,2,1,0:T(8,128)S(1)}, u32[]{:S(2)}, u32[]{:S(2)}) collective-permute-start(f32[2,2,544,128]{3,2,1,0:T(8,128)S(1)} %copy-done.6), channel_id=1, source_target_pairs={{0,8},{8,0},{16,24},{24,16},{32,40},{40,32},{48,56},{56,48},{64,72... | collective-permute-start | bytes 3342344 | tf_op jit(solution)/shard_map/ppermute | solution.py:386
  29.0 21.9 %collective-permute-start.5 = (f32[2,2,512,128]{3,2,1,0:T(8,128)}, f32[2,2,512,128]{3,2,1,0:T(8,128)}, u32[]{:S(2)}, u32[]{:S(2)}) collective-permute-start(f32[2,2,512,128]{3,2,1,0:T(8,128)} %get-tuple-element.46), channel_id=1, source_target_pairs={{0,8},{8,0},{16,24},{24,16},{32,40},{40,32},{48,56},{56,48},{64,72... | collective-permute-start | bytes 3145736 | tf_op jit(solution)/shard_map/ppermute | solution.py:386
  43.7 25.6 %collective-permute-start.3 = (f32[2,2,512,128]{3,2,1,0:T(8,128)}, f32[2,2,512,128]{3,2,1,0:T(8,128)}, u32[]{:S(2)}, u32[]{:S(2)}) collective-permute-start(f32[2,2,512,128]{3,2,1,0:T(8,128)} %add.119), channel_id=1, source_target_pairs={{0,64},{8,72},{16,80},{24,88},{32,96},{40,104},{48,112},{56,120},{... | collective-permute-start | bytes 3145736 | tf_op jit(solution)/shard_map/ppermute | solution.py:398
  44.1 1.7 %copy-start.1 = (f32[2,2,2,544,128]{4,3,2,1,0:T(8,128)}, f32[2,2,2,544,128]{4,3,2,1,0:T(8,128)S(1)}, u32[]{:S(2)}) copy-start(f32[2,2,2,544,128]{4,3,2,1,0:T(8,128)S(1)} %collective-permute-done.8) | copy-start | bytes 6684676
  44.1 3.2 %copy-start.4 = (f32[2,2,544,128]{3,2,1,0:T(8,128)S(1)}, f32[2,2,544,128]{3,2,1,0:T(8,128)}, u32[]{:S(2)}) copy-start(f32[2,2,544,128]{3,2,1,0:T(8,128)} %get-tuple-element.52) | copy-start | bytes 3342340
  45.9 31.6 %collective-permute-start.9 = (f32[2,2,544,128]{3,2,1,0:T(8,128)}, f32[2,2,544,128]{3,2,1,0:T(8,128)S(1)}, u32[]{:S(2)}, u32[]{:S(2)}) collective-permute-start(f32[2,2,544,128]{3,2,1,0:T(8,128)} %fusion.1), channel_id=1, source_target_pairs={{0,16},{8,56},{16,32},{24,8},{32,48},{40,24},{48,0},{56,40},{64,80... | collective-permute-start | bytes 3342344 | tf_op jit(solution)/shard_map/ppermute | solution.py:390
  48.4 29.1 %collective-permute-start.13 = (f32[2,2,544,128]{3,2,1,0:T(8,128)}, f32[2,2,544,128]{3,2,1,0:T(8,128)}, u32[]{:S(2)}, u32[]{:S(2)}) collective-permute-start(f32[2,2,544,128]{3,2,1,0:T(8,128)} %add.139), channel_id=1, source_target_pairs={{0,48},{8,24},{16,0},{24,40},{32,16},{40,56},{48,32},{56,8},{64,11... | collective-permute-start | bytes 3342344 | tf_op jit(solution)/shard_map/ppermute | solution.py:394
  49.7 22.8 %copy-start.3 = (f32[4,2,512,128]{3,2,1,0:T(8,128)S(1)}, f32[4,2,512,128]{3,2,1,0:T(8,128)}, u32[]{:S(2)}) copy-start(f32[4,2,512,128]{3,2,1,0:T(8,128)} %get-tuple-element.33) | copy-start | bytes 6291460
  50.9 23.6 %collective-permute-start.6 = (f32[544,128]{1,0:T(8,128)S(1)}, f32[544,128]{1,0:T(8,128)S(1)}, u32[]{:S(2)}, u32[]{:S(2)}) collective-permute-start(f32[544,128]{1,0:T(8,128)S(1)} %pad_maximum_fusion), channel_id=1, source_target_pairs={{0,1},{1,2},{2,3},{3,4},{4,5},{5,6},{6,7},{8,9},{9,10},{10,11},{11... | collective-permute-start | bytes 835592 | tf_op jit(solution)/shard_map/ppermute | solution.py:430
  69.3 8.2 %collective-permute-start.7 = (f32[544,128]{1,0:T(8,128)S(1)}, f32[544,128]{1,0:T(8,128)S(1)}, u32[]{:S(2)}, u32[]{:S(2)}) collective-permute-start(f32[544,128]{1,0:T(8,128)S(1)} %pad_maximum_fusion), channel_id=1, source_target_pairs={{1,0},{2,1},{3,2},{4,3},{5,4},{6,5},{7,6},{9,8},{10,9},{11,10},{12... | collective-permute-start | bytes 835592 | tf_op jit(solution)/shard_map/ppermute | solution.py:430
  72.1 18.8 %collective-permute-start.14 = (f32[2,512,128]{2,1,0:T(8,128)S(1)}, f32[2,512,128]{2,1,0:T(8,128)S(1)}, u32[]{:S(2)}, u32[]{:S(2)}) collective-permute-start(f32[2,512,128]{2,1,0:T(8,128)S(1)} %get-tuple-element.68), channel_id=1, source_target_pairs={{0,64},{8,72},{16,80},{24,88},{32,96},{40,104},{48,112},{56,120},{... | collective-permute-start | bytes 1572872 | tf_op jit(solution)/shard_map/ppermute | solution.py:398
  72.6 4.9 %copy-start.2 = (f32[2,2,2,544,128]{4,3,2,1,0:T(8,128)S(1)}, f32[2,2,2,544,128]{4,3,2,1,0:T(8,128)}, u32[]{:S(2)}) copy-start(f32[2,2,2,544,128]{4,3,2,1,0:T(8,128)} %copy-done.1) | copy-start | bytes 6684676
  77.5 15.4 %collective-permute-start.15 = (f32[2,512,128]{2,1,0:T(8,128)S(1)}, f32[2,512,128]{2,1,0:T(8,128)S(1)}, u32[]{:S(2)}, u32[]{:S(2)}) collective-permute-start(f32[2,512,128]{2,1,0:T(8,128)S(1)} %get-tuple-element.56), channel_id=1, source_target_pairs={{0,16},{8,56},{16,32},{24,8},{32,48},{40,24},{48,0},{56,40},{64,80... | collective-permute-start | bytes 1572872 | tf_op jit(solution)/shard_map/ppermute | solution.py:390
  90.9 15.5 %collective-permute-start.16 = (f32[2,544,128]{2,1,0:T(8,128)S(1)}, f32[2,544,128]{2,1,0:T(8,128)S(1)}, u32[]{:S(2)}, u32[]{:S(2)}) collective-permute-start(f32[2,544,128]{2,1,0:T(8,128)S(1)} %fusion.7), channel_id=1, source_target_pairs={{0,64},{8,72},{16,80},{24,88},{32,96},{40,104},{48,112},{56,120},{... | collective-permute-start | bytes 1671176 | tf_op jit(solution)/shard_map/ppermute | solution.py:398
  91.4 31.2 %collective-permute-start.10 = (f32[2,512,128]{2,1,0:T(8,128)S(1)}, f32[2,512,128]{2,1,0:T(8,128)S(1)}, u32[]{:S(2)}, u32[]{:S(2)}) collective-permute-start(f32[2,512,128]{2,1,0:T(8,128)S(1)} %get-tuple-element.50), channel_id=1, source_target_pairs={{0,64},{8,72},{16,80},{24,88},{32,96},{40,104},{48,112},{56,120},{... | collective-permute-start | bytes 1572872 | tf_op jit(solution)/shard_map/ppermute | solution.py:398
  92.9 29.7 %collective-permute-start.11 = (f32[2,512,128]{2,1,0:T(8,128)S(1)}, f32[2,512,128]{2,1,0:T(8,128)S(1)}, u32[]{:S(2)}, u32[]{:S(2)}) collective-permute-start(f32[2,512,128]{2,1,0:T(8,128)S(1)} %get-tuple-element.51), channel_id=1, source_target_pairs={{0,48},{8,24},{16,0},{24,40},{32,16},{40,56},{48,32},{56,8},{64,11... | collective-permute-start | bytes 1572872 | tf_op jit(solution)/shard_map/ppermute | solution.py:394
  106.4 16.3 %collective-permute-start.17 = (f32[2,512,128]{2,1,0:T(8,128)S(1)}, f32[2,512,128]{2,1,0:T(8,128)S(1)}, u32[]{:S(2)}, u32[]{:S(2)}) collective-permute-start(f32[2,512,128]{2,1,0:T(8,128)S(1)} %fusion.11), channel_id=1, source_target_pairs={{0,16},{8,56},{16,32},{24,8},{32,48},{40,24},{48,0},{56,40},{64,80... | collective-permute-start | bytes 1572872 | tf_op jit(solution)/shard_map/ppermute | solution.py:390
  107.7 16.2 %collective-permute-start.18 = (f32[544,128]{1,0:T(8,128)S(1)}, f32[544,128]{1,0:T(8,128)S(1)}, u32[]{:S(2)}, u32[]{:S(2)}) collective-permute-start(f32[544,128]{1,0:T(8,128)S(1)} %get-tuple-element.71), channel_id=1, source_target_pairs={{0,1},{1,2},{2,3},{3,4},{4,5},{5,6},{6,7},{8,9},{9,10},{10,11},{11... | collective-permute-start | bytes 835592 | tf_op jit(solution)/shard_map/ppermute | solution.py:447
  109.0 14.9 %collective-permute-start.19 = (f32[544,128]{1,0:T(8,128)S(1)}, f32[544,128]{1,0:T(8,128)S(1)}, u32[]{:S(2)}, u32[]{:S(2)}) collective-permute-start(f32[544,128]{1,0:T(8,128)S(1)} %get-tuple-element.70), channel_id=1, source_target_pairs={{1,0},{2,1},{3,2},{4,3},{5,4},{6,5},{7,6},{9,8},{10,9},{11,10},{12... | collective-permute-start | bytes 835592 | tf_op jit(solution)/shard_map/ppermute | solution.py:447

commit v12 on v10

--- a/solution.py
+++ b/solution.py
@@ -411,13 +411,13 @@
     far_other, far_same, near_other, near_same, ends_other, ends_same, rest_other, rest_same = outs
 
     ends_came, far_came = to_sibling(ends_other), to_sibling(far_other)
-    rest_came, near_came = to_sibling(rest_other), to_sibling(near_other)
+    rest_came = to_sibling(rest_other)
     ends_two = forth(ends_same[0] + ends_came[0])
-    far_ends = far_same[2:] + far_came[2:]
-    far_ends, ends_came = after(far_ends, ends_came)
-    far_ends_came = across(far_ends)
+    far_two, ends_came = after(far_same[2] + far_came[2], ends_came)
+    far_two_came = across(far_two)
     ends_back = back(ends_same[1] + ends_came[1])
 
+    rest_came, k = after(rest_came, k)
     start = me * rows * 16
     k_here = jnp.concatenate(
         [
@@ -428,11 +428,14 @@
     )
     k_low, k_high = lax.ppermute(k_here, "gz", UP), lax.ppermute(k_here, "gz", DOWN)
 
-    ends_two, far_came = after(ends_two, far_came)
+    (far_two_came, k_low, k_high), ends_two = after((far_two_came, k_low, k_high), ends_two)
+    ends_two, (far_came, near_other) = after(ends_two, (far_came, near_other))
+    near_came = to_sibling(near_other)
     ring = forth(rest_same[1] + rest_came[1] + ends_two)
+    far_back_came = across(far_same[3] + far_came[3])
     far_next_came = across(far_same[1] + far_came[1])
-    two, direct = (near_same[t] + near_came[t] + far_ends_came[t - 2] for t in (2, 3))
-    (two, direct, k_low, k_high), ring = after((two, direct, k_low, k_high), ring)
+    two, direct = near_same[2] + near_came[2] + far_two_came, near_same[3] + near_came[3] + far_back_came
+    (two, direct), ring = after((two, direct), ring)
     two, direct = forth(two), back(direct)
     edge_far = rest_same[0, 1] + rest_came[0, 1] + ends_back[1] + ring[1]
     edge_far, (far_came, far_next_came) = after(edge_far, (far_came, far_next_came))

time: 114 us -> 124 us (1.088)
  the two profiles are of different devices: /device:TPU:6 before, /device:TPU:80 now
where the time goes in v12:
time: 124 us; the launch traced here: 123 us
  waiting for transfers between devices  61.8 us (50%)
  starting transfers between devices  28 us (23%)
  Pallas kernels  20.1 us (16%)
  other arithmetic  11.2 us (9%)
    pallas_call x1, Pallas kernels, series(): pl.pallas_call(series_kernel, out_shape=(share,) * 4 + (edge,) * 4, in_sp...  18.2 us
    ppermute x5, waiting for transfers between devices, across(): return lax.ppermute(cells, 'tm', ACROSS)  18.1 us
    ppermute x4, waiting for transfers between devices, forth(): return lax.ppermute(cells, 'tm', FORTH)  17.3 us
    ppermute x4, starting transfers between devices, forth(): return lax.ppermute(cells, 'tm', FORTH)  9.13 us
    ppermute x2, waiting for transfers between devices, local(): above, below = (lax.ppermute(low, 'gz', DOWN), lax.ppermute(high, 'gz', UP))  7.92 us
    ppermute x4, waiting for transfers between devices, to_sibling(): return lax.ppermute(other, 'tm', SIBLING)  7.89 us
    ppermute x1, waiting for transfers between devices, local(): lax.ppermute(k_here, 'gz', UP)  7.39 us
    ppermute x5, starting transfers between devices, across(): return lax.ppermute(cells, 'tm', ACROSS)  5.89 us
  transfers between devices with their start and end apart: 19, of which 10 were waited for; matrix products, arithmetic and copies ran while one was open for 10% of the time, Pallas kernels for 0%

profile of v12, /device:TPU:80, one launch (start us, length us, event | category | flops | bytes accessed | tf_op | source)
XLA Modules:
  0.0 123.1 jit_solution(7580675169693587844)
XLA Ops:
  0.6 18.2 %shard_map.77 = (f32[4,2,512,128]{3,2,1,0:T(8,128)}, f32[4,2,512,128]{3,2,1,0:T(8,128)}, f32[4,2,512,128]{3,2,1,0:T(8,128)}, f32[4,2,512,128]{3,2,1,0:T(8,128)},...) custom-call(f32[1,4]{1,0:T(1,128)} %coeffs.1, ...), custom_call_target="tpu_custom_call" | custom-call | bytes 47185920 | tf_op jit(solution)/shard_map/pallas_call | solution.py:335
  18.9 0.1 collective-permute-start
  19.0 0.5 collective-permute-start.1
  19.5 0.1 collective-permute-start.3
  19.6 3.8 %collective-permute-done = f32[4,2,512,128]{3,2,1,0:T(8,128)S(1)} collective-permute-done((f32[4,2,512,128]{3,2,1,0:T(8,128)}, f32[4,2,512,128]{3,2,1,0:T(8,128)S(1)}, u32[]{:S(2)}, u32[]{:S(2)}) %collective-permute-start) | collective-permute-done | bytes 2097184 | tf_op jit(solution)/shard_map/ppermute | solution.py:385
  23.3 2.2 %fusion.17 = f32[2,512,128]{2,1,0:T(8,128)} fusion(f32[4,2,512,128]{3,2,1,0:T(8,128)S(1)} %collective-permute-done, f32[4,2,512,128]{3,2,1,0:T(8,128)} %get-tuple-element.32), kind=kLoop, calls=%fused_computation.27 | loop fusion | flops 131072 | bytes 1572864 | tf_op jit(solution)/shard_map/add | solution.py:416
  25.6 4.1 %collective-permute-done.1 = f32[2,2,2,544,128]{4,3,2,1,0:T(8,128)S(1)} collective-permute-done((f32[2,2,2,544,128]{4,3,2,1,0:T(8,128)}, f32[2,2,2,544,128]{4,3,2,1,0:T(8,128)S(1)}, u32[]{:S(2)}, u32[]{:S(2)}) %collective-permute-start.1) | collective-permute-done | bytes 2228256 | tf_op jit(solution)/shard_map/ppermute | solution.py:385
  29.7 3.4 %add_bitcast_fusion = (f32[2,2,544,128]{3,2,1,0:T(8,128)}, f32[2,2,544,128]{3,2,1,0:T(8,128)}) fusion(f32[2,2,2,544,128]{4,3,2,1,0:T(8,128)S(1)} %collective-permute-done.1, f32[2,2,2,544,128]{4,3,2,1,0:T(8,128)} %get-tuple-element.38), kind=kLoop, calls=%fused_computation.3 | loop fusion | flops 557056 | bytes 6684672 | tf_op jit(solution)/shard_map/add | solution.py:418
  33.1 1.3 %collective-permute-start.6 = (f32[2,2,544,128]{3,2,1,0:T(8,128)}, f32[2,2,544,128]{3,2,1,0:T(8,128)}, u32[]{:S(2)}, u32[]{:S(2)}) collective-permute-start(f32[2,2,544,128]{3,2,1,0:T(8,128)} %get-tuple-element.67), channel_id=1, source_target_pairs={{0,16},{8,56},{16,32},{24,8},{32,48},{40,24},{48,0},{56,40},{64,80... | collective-permute-start | bytes 3342344 | tf_op jit(solution)/shard_map/ppermute | solution.py:389
  34.4 1.6 %collective-permute-start.2 = (f32[2,512,128]{2,1,0:T(8,128)}, f32[2,512,128]{2,1,0:T(8,128)S(1)}, u32[]{:S(2)}, u32[]{:S(2)}) collective-permute-start(f32[2,512,128]{2,1,0:T(8,128)} %fusion.17), channel_id=1, source_target_pairs={{0,64},{8,72},{16,80},{24,88},{32,96},{40,104},{48,112},{56,120},{... | collective-permute-start | bytes 1572872 | tf_op jit(solution)/shard_map/ppermute | solution.py:397
  36.0 0.0 collective-permute-done.3
  36.0 0.7 dynamic-slice_select_fusion.1
  36.8 1.1 constant_dynamic-slice_fusion
  37.9 4.1 %collective-permute-start.5 = (f32[544,128]{1,0:T(8,128)S(1)}, f32[544,128]{1,0:T(8,128)S(1)}, u32[]{:S(2)}, u32[]{:S(2)}) collective-permute-start(f32[544,128]{1,0:T(8,128)S(1)} %pad_maximum_fusion), channel_id=1, source_target_pairs={{1,0},{2,1},{3,2},{4,3},{5,4},{6,5},{7,6},{9,8},{10,9},{11,10},{12... | collective-permute-start | bytes 835592 | tf_op jit(solution)/shard_map/ppermute | solution.py:429
  41.9 1.9 %collective-permute-start.4 = (f32[544,128]{1,0:T(8,128)S(1)}, f32[544,128]{1,0:T(8,128)S(1)}, u32[]{:S(2)}, u32[]{:S(2)}) collective-permute-start(f32[544,128]{1,0:T(8,128)S(1)} %pad_maximum_fusion), channel_id=1, source_target_pairs={{0,1},{1,2},{2,3},{3,4},{4,5},{5,6},{6,7},{8,9},{9,10},{10,11},{11... | collective-permute-start | bytes 835592 | tf_op jit(solution)/shard_map/ppermute | solution.py:429
  43.9 3.3 %collective-permute-done.5 = f32[544,128]{1,0:T(8,128)S(1)} collective-permute-done((f32[544,128]{1,0:T(8,128)S(1)}, f32[544,128]{1,0:T(8,128)S(1)}, u32[]{:S(2)}, u32[]{:S(2)}) %collective-permute-start.5) | collective-permute-done | bytes 278560 | tf_op jit(solution)/shard_map/ppermute | solution.py:429
  47.1 7.4 %collective-permute-done.4 = f32[544,128]{1,0:T(8,128)S(1)} collective-permute-done((f32[544,128]{1,0:T(8,128)S(1)}, f32[544,128]{1,0:T(8,128)S(1)}, u32[]{:S(2)}, u32[]{:S(2)}) %collective-permute-start.4) | collective-permute-done | bytes 278560 | tf_op jit(solution)/shard_map/ppermute | solution.py:429
  54.5 0.0 collective-permute-done.2
  54.5 0.0 collective-permute-done.6
  54.5 0.0 collective-permute-start.7
  54.5 1.9 %bitcast_add_fusion = f32[2,2,544,128]{3,2,1,0:T(8,128)S(1)} fusion(f32[2,2,544,128]{3,2,1,0:T(8,128)} %collective-permute-done.6, f32[2,2,2,544,128]{4,3,2,1,0:T(8,128)} %collective-permute-done.3, f32[2,2,2,544,128]{4,3,2,1,0:T(8,128)S(1)} %copy-done), kind=kLoop, calls=%fused_computation.2 | loop fusion | flops 557056 | bytes 4456448 | tf_op jit(solution)/shard_map/add | solution.py:434
  56.4 1.6 %collective-permute-start.10 = (f32[2,2,544,128]{3,2,1,0:T(8,128)S(1)}, f32[2,2,544,128]{3,2,1,0:T(8,128)S(1)}, u32[]{:S(2)}, u32[]{:S(2)}) collective-permute-start(f32[2,2,544,128]{3,2,1,0:T(8,128)S(1)} %bitcast_add_fusion), channel_id=1, source_target_pairs={{0,16},{8,56},{16,32},{24,8},{32,48},{40,24},{48,0},{56,40},{64,80... | collective-permute-start | bytes 3342344 | tf_op jit(solution)/shard_map/ppermute | solution.py:389
  58.1 0.5 collective-permute-start.8
  58.5 0.1 add_bitcast_fusion.2
  58.7 1.0 collective-permute-start.9
  59.6 1.1 collective-permute-start.11
  60.8 12.8 %collective-permute-done.9 = f32[2,512,128]{2,1,0:T(8,128)S(1)} collective-permute-done((f32[2,512,128]{2,1,0:T(8,128)S(1)}, f32[2,512,128]{2,1,0:T(8,128)S(1)}, u32[]{:S(2)}, u32[]{:S(2)}) %collective-permute-start.9) | collective-permute-done | bytes 524320 | tf_op jit(solution)/shard_map/ppermute | solution.py:397
  73.5 0.0 collective-permute-done.7
  73.5 0.2 fusion.10
  73.7 9.3 %collective-permute-done.10 = f32[2,2,544,128]{3,2,1,0:T(8,128)S(1)} collective-permute-done((f32[2,2,544,128]{3,2,1,0:T(8,128)S(1)}, f32[2,2,544,128]{3,2,1,0:T(8,128)S(1)}, u32[]{:S(2)}, u32[]{:S(2)}) %collective-permute-start.10) | collective-permute-done | bytes 1114144 | tf_op jit(solution)/shard_map/ppermute | solution.py:389
  83.0 2.5 %collective-permute-start.14 = (f32[2,512,128]{2,1,0:T(8,128)S(1)}, f32[2,512,128]{2,1,0:T(8,128)S(1)}, u32[]{:S(2)}, u32[]{:S(2)}) collective-permute-start(f32[2,512,128]{2,1,0:T(8,128)S(1)} %get-tuple-element.52), channel_id=1, source_target_pairs={{0,16},{8,56},{16,32},{24,8},{32,48},{40,24},{48,0},{56,40},{64,80... | collective-permute-start | bytes 1572872 | tf_op jit(solution)/shard_map/ppermute | solution.py:389
  85.5 0.0 collective-permute-done.8
  85.5 1.2 fusion.5
  86.7 0.9 collective-permute-start.15
  87.6 0.1 add_bitcast_fusion.1
  87.7 1.3 %collective-permute-start.12 = (f32[2,512,128]{2,1,0:T(8,128)S(1)}, f32[2,512,128]{2,1,0:T(8,128)S(1)}, u32[]{:S(2)}, u32[]{:S(2)}) collective-permute-start(f32[2,512,128]{2,1,0:T(8,128)S(1)} %add_bitcast_fusion.1), channel_id=1, source_target_pairs={{0,64},{8,72},{16,80},{24,88},{32,96},{40,104},{48,112},{56,120},{... | collective-permute-start | bytes 1572872 | tf_op jit(solution)/shard_map/ppermute | solution.py:397
  89.0 8.0 %collective-permute-done.14 = f32[2,512,128]{2,1,0:T(8,128)S(1)} collective-permute-done((f32[2,512,128]{2,1,0:T(8,128)S(1)}, f32[2,512,128]{2,1,0:T(8,128)S(1)}, u32[]{:S(2)}, u32[]{:S(2)}) %collective-permute-start.14) | collective-permute-done | bytes 524320 | tf_op jit(solution)/shard_map/ppermute | solution.py:389
  96.9 0.1 fusion.8
  97.0 5.3 %collective-permute-done.15 = f32[2,544,128]{2,1,0:T(8,128)S(1)} collective-permute-done((f32[2,544,128]{2,1,0:T(8,128)S(1)}, f32[2,544,128]{2,1,0:T(8,128)S(1)}, u32[]{:S(2)}, u32[]{:S(2)}) %collective-permute-start.15) | collective-permute-done | bytes 557088 | tf_op jit(solution)/shard_map/ppermute | solution.py:397
  102.4 3.7 %collective-permute-start.16 = (f32[2,512,128]{2,1,0:T(8,128)S(1)}, f32[2,512,128]{2,1,0:T(8,128)S(1)}, u32[]{:S(2)}, u32[]{:S(2)}) collective-permute-start(f32[2,512,128]{2,1,0:T(8,128)S(1)} %fusion.8), channel_id=1, source_target_pairs={{0,16},{8,56},{16,32},{24,8},{32,48},{40,24},{48,0},{56,40},{64,80... | collective-permute-start | bytes 1572872 | tf_op jit(solution)/shard_map/ppermute | solution.py:389
  106.0 1.2 fusion.3
  107.2 0.1 slice_bitcast_fusion.3
  107.3 1.9 %collective-permute-start.18 = (f32[544,128]{1,0:T(8,128)S(1)}, f32[544,128]{1,0:T(8,128)S(1)}, u32[]{:S(2)}, u32[]{:S(2)}) collective-permute-start(f32[544,128]{1,0:T(8,128)S(1)} %get-tuple-element.68), channel_id=1, source_target_pairs={{1,0},{2,1},{3,2},{4,3},{5,4},{6,5},{7,6},{9,8},{10,9},{11,10},{12... | collective-permute-start | bytes 835592 | tf_op jit(solution)/shard_map/ppermute | solution.py:449
  109.2 3.9 %collective-permute-start.17 = (f32[544,128]{1,0:T(8,128)S(1)}, f32[544,128]{1,0:T(8,128)S(1)}, u32[]{:S(2)}, u32[]{:S(2)}) collective-permute-start(f32[544,128]{1,0:T(8,128)S(1)} %get-tuple-element.69), channel_id=1, source_target_pairs={{0,1},{1,2},{2,3},{3,4},{4,5},{5,6},{6,7},{8,9},{9,10},{10,11},{11... | collective-permute-start | bytes 835592 | tf_op jit(solution)/shard_map/ppermute | solution.py:449
  113.2 0.1 fusion.16
  113.4 2.4 %collective-permute-done.18 = f32[544,128]{1,0:T(8,128)S(1)} collective-permute-done((f32[544,128]{1,0:T(8,128)S(1)}, f32[544,128]{1,0:T(8,128)S(1)}, u32[]{:S(2)}, u32[]{:S(2)}) %collective-permute-start.18) | collective-permute-done | bytes 278560 | tf_op jit(solution)/shard_map/ppermute | solution.py:449
  115.7 5.5 %collective-permute-done.17 = f32[544,128]{1,0:T(8,128)S(1)} collective-permute-done((f32[544,128]{1,0:T(8,128)S(1)}, f32[544,128]{1,0:T(8,128)S(1)}, u32[]{:S(2)}, u32[]{:S(2)}) %collective-permute-start.17) | collective-permute-done | bytes 278560 | tf_op jit(solution)/shard_map/ppermute | solution.py:449
  121.3 1.8 %shard_map.78 = (f32[32,2,8,128]{3,2,1,0:T(8,128)}, f32[32,2,8,128]{3,2,1,0:T(8,128)}) custom-call(f32[32,2,8,128]{3,2,1,0:T(8,128)S(1)} %bitcast.110, f32[32,2,8,128]{3,2,1,0:T(8,128)S(1)} %bitcast.109, f32[34,2,8,128]{3,2,1,0:T(8,128)S(1)} %bitcast.107, f32[34,2,8,128]{3,2,1,0:T(8,128)S(1)} %bitcast.106, f32[34,2,8,128]{3,2,1,0:T(8,128)S(1)} %bitcast.114, ...), custom_call_target="tpu_custom_call" | custom-call | bytes 4194304 | tf_op jit(solution)/shard_map/pallas_call | solution.py:355
  (19 shorter events, 0.1 us)
Async XLA Ops:
  18.9 4.5 %collective-permute-start = (f32[4,2,512,128]{3,2,1,0:T(8,128)}, f32[4,2,512,128]{3,2,1,0:T(8,128)S(1)}, u32[]{:S(2)}, u32[]{:S(2)}) collective-permute-start(f32[4,2,512,128]{3,2,1,0:T(8,128)} %get-tuple-element.33), channel_id=1, source_target_pairs={{0,8},{8,0},{16,24},{24,16},{32,40},{40,32},{48,56},{56,48},{64,72... | collective-permute-start | bytes 6291464 | tf_op jit(solution)/shard_map/ppermute | solution.py:385
  19.0 10.7 %collective-permute-start.1 = (f32[2,2,2,544,128]{4,3,2,1,0:T(8,128)}, f32[2,2,2,544,128]{4,3,2,1,0:T(8,128)S(1)}, u32[]{:S(2)}, u32[]{:S(2)}) collective-permute-start(f32[2,2,2,544,128]{4,3,2,1,0:T(8,128)} %get-tuple-element.34), channel_id=1, source_target_pairs={{0,8},{8,0},{16,24},{24,16},{32,40},{40,32},{48,56},{56,48},{64,72... | collective-permute-start | bytes 6684680 | tf_op jit(solution)/shard_map/ppermute | solution.py:385
  19.5 16.6 %collective-permute-start.3 = (f32[2,2,2,544,128]{4,3,2,1,0:T(8,128)}, f32[2,2,2,544,128]{4,3,2,1,0:T(8,128)}, u32[]{:S(2)}, u32[]{:S(2)}) collective-permute-start(f32[2,2,2,544,128]{4,3,2,1,0:T(8,128)} %get-tuple-element.36), channel_id=1, source_target_pairs={{0,8},{8,0},{16,24},{24,16},{32,40},{40,32},{48,56},{56,48},{64,72... | collective-permute-start | bytes 6684680 | tf_op jit(solution)/shard_map/ppermute | solution.py:385
  23.3 6.4 %copy-start.2 = (f32[4,2,512,128]{3,2,1,0:T(8,128)}, f32[4,2,512,128]{3,2,1,0:T(8,128)S(1)}, u32[]{:S(2)}) copy-start(f32[4,2,512,128]{3,2,1,0:T(8,128)S(1)} %collective-permute-done) | copy-start | bytes 6291460
  29.7 24.8 %copy-start = (f32[2,2,2,544,128]{4,3,2,1,0:T(8,128)S(1)}, f32[2,2,2,544,128]{4,3,2,1,0:T(8,128)}, u32[]{:S(2)}) copy-start(f32[2,2,2,544,128]{4,3,2,1,0:T(8,128)} %get-tuple-element.42) | copy-start | bytes 6684676
  33.1 21.4 %collective-permute-start.6 = (f32[2,2,544,128]{3,2,1,0:T(8,128)}, f32[2,2,544,128]{3,2,1,0:T(8,128)}, u32[]{:S(2)}, u32[]{:S(2)}) collective-permute-start(f32[2,2,544,128]{3,2,1,0:T(8,128)} %get-tuple-element.67), channel_id=1, source_target_pairs={{0,16},{8,56},{16,32},{24,8},{32,48},{40,24},{48,0},{56,40},{64,80... | collective-permute-start | bytes 3342344 | tf_op jit(solution)/shard_map/ppermute | solution.py:389
  34.4 20.1 %collective-permute-start.2 = (f32[2,512,128]{2,1,0:T(8,128)}, f32[2,512,128]{2,1,0:T(8,128)S(1)}, u32[]{:S(2)}, u32[]{:S(2)}) collective-permute-start(f32[2,512,128]{2,1,0:T(8,128)} %fusion.17), channel_id=1, source_target_pairs={{0,64},{8,72},{16,80},{24,88},{32,96},{40,104},{48,112},{56,120},{... | collective-permute-start | bytes 1572872 | tf_op jit(solution)/shard_map/ppermute | solution.py:397
  36.8 21.3 %copy-start.5 = (f32[2,2,544,128]{3,2,1,0:T(8,128)S(1)}, f32[2,2,544,128]{3,2,1,0:T(8,128)}, u32[]{:S(2)}) copy-start(f32[2,2,544,128]{3,2,1,0:T(8,128)} %get-tuple-element.66) | copy-start | bytes 3342340
  37.9 9.2 %collective-permute-start.5 = (f32[544,128]{1,0:T(8,128)S(1)}, f32[544,128]{1,0:T(8,128)S(1)}, u32[]{:S(2)}, u32[]{:S(2)}) collective-permute-start(f32[544,128]{1,0:T(8,128)S(1)} %pad_maximum_fusion), channel_id=1, source_target_pairs={{1,0},{2,1},{3,2},{4,3},{5,4},{6,5},{7,6},{9,8},{10,9},{11,10},{12... | collective-permute-start | bytes 835592 | tf_op jit(solution)/shard_map/ppermute | solution.py:429
  41.9 12.6 %collective-permute-start.4 = (f32[544,128]{1,0:T(8,128)S(1)}, f32[544,128]{1,0:T(8,128)S(1)}, u32[]{:S(2)}, u32[]{:S(2)}) collective-permute-start(f32[544,128]{1,0:T(8,128)S(1)} %pad_maximum_fusion), channel_id=1, source_target_pairs={{0,1},{1,2},{2,3},{3,4},{4,5},{5,6},{6,7},{8,9},{9,10},{10,11},{11... | collective-permute-start | bytes 835592 | tf_op jit(solution)/shard_map/ppermute | solution.py:429
  54.5 19.0 %collective-permute-start.7 = (f32[4,2,512,128]{3,2,1,0:T(8,128)}, f32[4,2,512,128]{3,2,1,0:T(8,128)S(1)}, u32[]{:S(2)}, u32[]{:S(2)}) collective-permute-start(f32[4,2,512,128]{3,2,1,0:T(8,128)} %get-tuple-element.41), channel_id=1, source_target_pairs={{0,8},{8,0},{16,24},{24,16},{32,40},{40,32},{48,56},{56,48},{64,72... | collective-permute-start | bytes 6291464 | tf_op jit(solution)/shard_map/ppermute | solution.py:385
  54.5 4.0 %copy-start.1 = (f32[4,2,512,128]{3,2,1,0:T(8,128)S(1)}, f32[4,2,512,128]{3,2,1,0:T(8,128)}, u32[]{:S(2)}) copy-start(f32[4,2,512,128]{3,2,1,0:T(8,128)} %get-tuple-element.32) | copy-start | bytes 6291460
  54.5 4.0 %copy-start.3 = (f32[4,2,512,128]{3,2,1,0:T(8,128)S(1)}, f32[4,2,512,128]{3,2,1,0:T(8,128)}, u32[]{:S(2)}) copy-start(f32[4,2,512,128]{3,2,1,0:T(8,128)} %copy-done.2) | copy-start | bytes 6291460
  56.4 17.1 %copy-start.4 = (f32[4,2,512,128]{3,2,1,0:T(8,128)S(1)}, f32[4,2,512,128]{3,2,1,0:T(8,128)}, u32[]{:S(2)}) copy-start(f32[4,2,512,128]{3,2,1,0:T(8,128)} %get-tuple-element.31) | copy-start | bytes 6291460
  56.4 26.5 %collective-permute-start.10 = (f32[2,2,544,128]{3,2,1,0:T(8,128)S(1)}, f32[2,2,544,128]{3,2,1,0:T(8,128)S(1)}, u32[]{:S(2)}, u32[]{:S(2)}) collective-permute-start(f32[2,2,544,128]{3,2,1,0:T(8,128)S(1)} %bitcast_add_fusion), channel_id=1, source_target_pairs={{0,16},{8,56},{16,32},{24,8},{32,48},{40,24},{48,0},{56,40},{64,80... | collective-permute-start | bytes 3342344 | tf_op jit(solution)/shard_map/ppermute | solution.py:389
  58.1 27.5 %collective-permute-start.8 = (f32[2,2,544,128]{3,2,1,0:T(8,128)S(1)}, f32[2,2,544,128]{3,2,1,0:T(8,128)S(1)}, u32[]{:S(2)}, u32[]{:S(2)}) collective-permute-start(f32[2,2,544,128]{3,2,1,0:T(8,128)S(1)} %copy-done.5), channel_id=1, source_target_pairs={{0,48},{8,24},{16,0},{24,40},{32,16},{40,56},{48,32},{56,8},{64,11... | collective-permute-start | bytes 3342344 | tf_op jit(solution)/shard_map/ppermute | solution.py:393
  58.7 14.9 %collective-permute-start.9 = (f32[2,512,128]{2,1,0:T(8,128)S(1)}, f32[2,512,128]{2,1,0:T(8,128)S(1)}, u32[]{:S(2)}, u32[]{:S(2)}) collective-permute-start(f32[2,512,128]{2,1,0:T(8,128)S(1)} %get-tuple-element.61), channel_id=1, source_target_pairs={{0,64},{8,72},{16,80},{24,88},{32,96},{40,104},{48,112},{56,120},{... | collective-permute-start | bytes 1572872 | tf_op jit(solution)/shard_map/ppermute | solution.py:397
  59.6 27.1 %collective-permute-start.11 = (f32[2,512,128]{2,1,0:T(8,128)S(1)}, f32[2,512,128]{2,1,0:T(8,128)S(1)}, u32[]{:S(2)}, u32[]{:S(2)}) collective-permute-start(f32[2,512,128]{2,1,0:T(8,128)S(1)} %get-tuple-element.60), channel_id=1, source_target_pairs={{0,64},{8,72},{16,80},{24,88},{32,96},{40,104},{48,112},{56,120},{... | collective-permute-start | bytes 1572872 | tf_op jit(solution)/shard_map/ppermute | solution.py:397
  83.0 13.9 %collective-permute-start.14 = (f32[2,512,128]{2,1,0:T(8,128)S(1)}, f32[2,512,128]{2,1,0:T(8,128)S(1)}, u32[]{:S(2)}, u32[]{:S(2)}) collective-permute-start(f32[2,512,128]{2,1,0:T(8,128)S(1)} %get-tuple-element.52), channel_id=1, source_target_pairs={{0,16},{8,56},{16,32},{24,8},{32,48},{40,24},{48,0},{56,40},{64,80... | collective-permute-start | bytes 1572872 | tf_op jit(solution)/shard_map/ppermute | solution.py:389
  86.7 15.6 %collective-permute-start.15 = (f32[2,544,128]{2,1,0:T(8,128)S(1)}, f32[2,544,128]{2,1,0:T(8,128)S(1)}, u32[]{:S(2)}, u32[]{:S(2)}) collective-permute-start(f32[2,544,128]{2,1,0:T(8,128)S(1)} %fusion.5), channel_id=1, source_target_pairs={{0,64},{8,72},{16,80},{24,88},{32,96},{40,104},{48,112},{56,120},{... | collective-permute-start | bytes 1671176 | tf_op jit(solution)/shard_map/ppermute | solution.py:397
  87.6 25.5 %collective-permute-start.13 = (f32[2,512,128]{2,1,0:T(8,128)S(1)}, f32[2,512,128]{2,1,0:T(8,128)S(1)}, u32[]{:S(2)}, u32[]{:S(2)}) collective-permute-start(f32[2,512,128]{2,1,0:T(8,128)S(1)} %get-tuple-element.50), channel_id=1, source_target_pairs={{0,48},{8,24},{16,0},{24,40},{32,16},{40,56},{48,32},{56,8},{64,11... | collective-permute-start | bytes 1572872 | tf_op jit(solution)/shard_map/ppermute | solution.py:393
  87.7 25.5 %collective-permute-start.12 = (f32[2,512,128]{2,1,0:T(8,128)S(1)}, f32[2,512,128]{2,1,0:T(8,128)S(1)}, u32[]{:S(2)}, u32[]{:S(2)}) collective-permute-start(f32[2,512,128]{2,1,0:T(8,128)S(1)} %add_bitcast_fusion.1), channel_id=1, source_target_pairs={{0,64},{8,72},{16,80},{24,88},{32,96},{40,104},{48,112},{56,120},{... | collective-permute-start | bytes 1572872 | tf_op jit(solution)/shard_map/ppermute | solution.py:397
  102.4 10.8 %collective-permute-start.16 = (f32[2,512,128]{2,1,0:T(8,128)S(1)}, f32[2,512,128]{2,1,0:T(8,128)S(1)}, u32[]{:S(2)}, u32[]{:S(2)}) collective-permute-start(f32[2,512,128]{2,1,0:T(8,128)S(1)} %fusion.8), channel_id=1, source_target_pairs={{0,16},{8,56},{16,32},{24,8},{32,48},{40,24},{48,0},{56,40},{64,80... | collective-permute-start | bytes 1572872 | tf_op jit(solution)/shard_map/ppermute | solution.py:389
  107.3 8.4 %collective-permute-start.18 = (f32[544,128]{1,0:T(8,128)S(1)}, f32[544,128]{1,0:T(8,128)S(1)}, u32[]{:S(2)}, u32[]{:S(2)}) collective-permute-start(f32[544,128]{1,0:T(8,128)S(1)} %get-tuple-element.68), channel_id=1, source_target_pairs={{1,0},{2,1},{3,2},{4,3},{5,4},{6,5},{7,6},{9,8},{10,9},{11,10},{12... | collective-permute-start | bytes 835592 | tf_op jit(solution)/shard_map/ppermute | solution.py:449
  109.2 12.1 %collective-permute-start.17 = (f32[544,128]{1,0:T(8,128)S(1)}, f32[544,128]{1,0:T(8,128)S(1)}, u32[]{:S(2)}, u32[]{:S(2)}) collective-permute-start(f32[544,128]{1,0:T(8,128)S(1)} %get-tuple-element.69), channel_id=1, source_target_pairs={{0,1},{1,2},{2,3},{3,4},{4,5},{5,6},{6,7},{8,9},{9,10},{10,11},{11... | collective-permute-start | bytes 835592 | tf_op jit(solution)/shard_map/ppermute | solution.py:449

commit v13 on v8

--- a/solution.py
+++ b/solution.py
@@ -398,7 +398,7 @@
 
 
 def after(first, then):
-    return lax.optimization_barrier((first, then))
+    return lax.optimization_barrier((first, then))[1]
 
 
 def local(prev_term, last_term, cos_sum, sin_sum, speed_sq, series_coeffs):
@@ -414,7 +414,7 @@
     rest_came, near_came = to_sibling(rest_other), to_sibling(near_other)
     ends_two = forth(ends_same[0] + ends_came[0])
     far_ends = far_same[2:] + far_came[2:]
-    far_ends, ends_came = after(far_ends, ends_came)
+    ends_came = after(far_ends, ends_came)
     far_ends_came, far_rest_came = across(far_ends), across(far_same[:2] + far_came[:2])
     ends_back = back(ends_same[1] + ends_came[1])
 
@@ -430,13 +430,13 @@
 
     ring = forth(rest_same[1] + rest_came[1] + ends_two)
     two, direct = (near_same[t] + near_came[t] + far_ends_came[t - 2] for t in (2, 3))
-    (two, direct, k_low, k_high), ring = after((two, direct, k_low, k_high), ring)
+    ring = after((two, direct, k_low, k_high), ring)
     two, direct = forth(two), back(direct)
     edge_far = rest_same[0, 1] + rest_came[0, 1] + ends_back[1] + ring[1]
-    edge_far, far_rest_came = after(edge_far, far_rest_came)
+    far_rest_came = after(edge_far, far_rest_came)
     edge_far = across(edge_far)
     last = near_same[1] + near_came[1] + far_rest_came[1] + two
-    last, edge_far = after(last, edge_far)
+    edge_far = after(last, edge_far)
     last = forth(last)
     edge = rest_same[0, 0] + rest_came[0, 0] + ends_back[0] + ring[0] + edge_far
     low, high = edge[0], edge[1]

time: 114 us -> 113 us (level)
  waiting for transfers between devices: 49.5 us -> 47.2 us
  starting transfers between devices: 29.2 us -> 31.1 us
    ppermute x4, waiting for transfers between devices: 21.3 us -> 16 us  [forth(): return lax.ppermute(cells, 'tm', FORTH)]
    ppermute x2, starting transfers between devices: 3.76 us -> 6.4 us  [back(): return lax.ppermute(cells, 'tm', BACK)]
    ppermute x2, waiting for transfers between devices: 8.45 us -> 10.6 us  [local(): above, below = (lax.ppermute(low, 'gz', DOWN), lax.ppermute(high, 'gz', UP))]
    ppermute x4, starting transfers between devices: 3.37 us -> 2.09 us  [forth(): return lax.ppermute(cells, 'tm', FORTH)]
  transfers between devices with their start and end apart: 17 -> 17, of which waited for: 11 -> 8; matrix products, arithmetic and copies ran while one was open for 12% -> 12% of each run, Pallas kernels for 0% -> 0%
where the time goes in v13:
time: 113 us
  waiting for transfers between devices  47.2 us (42%)
  starting transfers between devices  31.1 us (28%)
  Pallas kernels  20.1 us (18%)
  other arithmetic  12.6 us (11%)
    pallas_call x1, Pallas kernels, series(): pl.pallas_call(series_kernel, out_shape=(share,) * 4 + (edge,) * 4, in_sp...  18.3 us
    ppermute x4, waiting for transfers between devices, forth(): return lax.ppermute(cells, 'tm', FORTH)  16 us
    ppermute x2, waiting for transfers between devices, local(): above, below = (lax.ppermute(low, 'gz', DOWN), lax.ppermute(high, 'gz', UP))  10.6 us
    ppermute x3, waiting for transfers between devices, across(): return lax.ppermute(cells, 'tm', ACROSS)  8.77 us
    ppermute x1, waiting for transfers between devices, local(): lax.ppermute(k_here, 'gz', DOWN)  7.83 us
    ppermute x2, starting transfers between devices, local(): above, below = (lax.ppermute(low, 'gz', DOWN), lax.ppermute(high, 'gz', UP))  7.55 us
    ppermute x2, starting transfers between devices, back(): return lax.ppermute(cells, 'tm', BACK)  6.4 us
    ppermute x3, starting transfers between devices, across(): return lax.ppermute(cells, 'tm', ACROSS)  5.81 us
  transfers between devices with their start and end apart: 17, of which 8 were waited for; matrix products, arithmetic and copies ran while one was open for 12% of the time, Pallas kernels for 0%

profile of v13, /device:TPU:6, one launch (start us, length us, event | category | flops | bytes accessed | tf_op | source)
XLA Modules:
  0.0 113.0 jit_solution(571334514167583745)
XLA Ops:
  0.6 18.3 %shard_map.77 = (f32[4,2,512,128]{3,2,1,0:T(8,128)}, f32[4,2,512,128]{3,2,1,0:T(8,128)}, f32[4,2,512,128]{3,2,1,0:T(8,128)}, f32[4,2,512,128]{3,2,1,0:T(8,128)},...) custom-call(f32[1,4]{1,0:T(1,128)} %coeffs.1, ...), custom_call_target="tpu_custom_call" | custom-call | bytes 47185920 | tf_op jit(solution)/shard_map/pallas_call | solution.py:335
  18.9 0.1 collective-permute-start.2
  19.0 0.5 collective-permute-start.3
  19.5 0.1 collective-permute-start.1
  19.6 3.8 %collective-permute-done.2 = f32[4,2,512,128]{3,2,1,0:T(8,128)S(1)} collective-permute-done((f32[4,2,512,128]{3,2,1,0:T(8,128)}, f32[4,2,512,128]{3,2,1,0:T(8,128)S(1)}, u32[]{:S(2)}, u32[]{:S(2)}) %collective-permute-start.2) | collective-permute-done | bytes 2097184 | tf_op jit(solution)/shard_map/ppermute | solution.py:385
  23.4 3.2 %slice_add_fusion.2 = (f32[2,2,512,128]{3,2,1,0:T(8,128)}, f32[2,2,512,128]{3,2,1,0:T(8,128)}) fusion(f32[4,2,512,128]{3,2,1,0:T(8,128)S(1)} %collective-permute-done.2, f32[4,2,512,128]{3,2,1,0:T(8,128)} %get-tuple-element.21), kind=kLoop, calls=%fused_computation.6 | loop fusion | flops 524288 | bytes 6291456 | tf_op jit(solution)/shard_map/add | solution.py:418
  26.6 0.0 collective-permute-done.3
  26.6 0.0 copy-done.3
  26.6 0.2 fusion
  26.8 1.6 %collective-permute-start.8 = (f32[2,2,544,128]{3,2,1,0:T(8,128)S(1)}, f32[2,2,544,128]{3,2,1,0:T(8,128)S(1)}, u32[]{:S(2)}, u32[]{:S(2)}) collective-permute-start(f32[2,2,544,128]{3,2,1,0:T(8,128)S(1)} %get-tuple-element.36), channel_id=1, source_target_pairs={{0,16},{8,56},{16,32},{24,8},{32,48},{40,24},{48,0},{56,40},{64,80... | collective-permute-start | bytes 3342344 | tf_op jit(solution)/shard_map/ppermute | solution.py:389
  28.4 1.2 %collective-permute-start = (f32[4,2,512,128]{3,2,1,0:T(8,128)}, f32[4,2,512,128]{3,2,1,0:T(8,128)}, u32[]{:S(2)}, u32[]{:S(2)}) collective-permute-start(f32[4,2,512,128]{3,2,1,0:T(8,128)} %get-tuple-element.17), channel_id=1, source_target_pairs={{0,8},{8,0},{16,24},{24,16},{32,40},{40,32},{48,56},{56,48},{64,72... | collective-permute-start | bytes 6291464 | tf_op jit(solution)/shard_map/ppermute | solution.py:385
  29.7 1.9 %collective-permute-start.5 = (f32[2,2,512,128]{3,2,1,0:T(8,128)}, f32[2,2,512,128]{3,2,1,0:T(8,128)}, u32[]{:S(2)}, u32[]{:S(2)}) collective-permute-start(f32[2,2,512,128]{3,2,1,0:T(8,128)} %get-tuple-element.33), channel_id=1, source_target_pairs={{0,64},{8,72},{16,80},{24,88},{32,96},{40,104},{48,112},{56,120},{... | collective-permute-start | bytes 3145736 | tf_op jit(solution)/shard_map/ppermute | solution.py:397
  31.6 0.0 collective-permute-done.1
  31.6 12.0 %collective-permute-done.8 = f32[2,2,544,128]{3,2,1,0:T(8,128)S(1)} collective-permute-done((f32[2,2,544,128]{3,2,1,0:T(8,128)S(1)}, f32[2,2,544,128]{3,2,1,0:T(8,128)S(1)}, u32[]{:S(2)}, u32[]{:S(2)}) %collective-permute-start.8) | collective-permute-done | bytes 1114144 | tf_op jit(solution)/shard_map/ppermute | solution.py:389
  43.6 1.2 %fusion.2 = f32[2,2,544,128]{3,2,1,0:T(8,128)} fusion(f32[2,2,544,128]{3,2,1,0:T(8,128)S(1)} %collective-permute-done.8, f32[2,2,2,544,128]{4,3,2,1,0:T(8,128)S(1)} %collective-permute-done.1, f32[2,2,2,544,128]{4,3,2,1,0:T(8,128)S(1)} %copy-done), kind=kLoop, calls=%fused_computation.4 | loop fusion | flops 557056 | bytes 4456448 | tf_op jit(solution)/shard_map/add | solution.py:431
  44.8 0.4 collective-permute-start.9
  45.2 2.9 %collective-permute-start.4 = (f32[2,2,544,128]{3,2,1,0:T(8,128)S(1)}, f32[2,2,544,128]{3,2,1,0:T(8,128)}, u32[]{:S(2)}, u32[]{:S(2)}) collective-permute-start(f32[2,2,544,128]{3,2,1,0:T(8,128)S(1)} %get-tuple-element.37), channel_id=1, source_target_pairs={{0,48},{8,24},{16,0},{24,40},{32,16},{40,56},{48,32},{56,8},{64,11... | collective-permute-start | bytes 3342344 | tf_op jit(solution)/shard_map/ppermute | solution.py:393
  48.0 1.0 constant_dynamic-slice_fusion
  49.0 2.0 %collective-permute-start.10 = (f32[2,2,512,128]{3,2,1,0:T(8,128)}, f32[2,2,512,128]{3,2,1,0:T(8,128)S(1)}, u32[]{:S(2)}, u32[]{:S(2)}) collective-permute-start(f32[2,2,512,128]{3,2,1,0:T(8,128)} %get-tuple-element.32), channel_id=1, source_target_pairs={{0,64},{8,72},{16,80},{24,88},{32,96},{40,104},{48,112},{56,120},{... | collective-permute-start | bytes 3145736 | tf_op jit(solution)/shard_map/ppermute | solution.py:397
  51.0 0.7 dynamic-slice_select_fusion.1
  51.7 0.0 collective-permute-done
  51.7 5.4 %collective-permute-start.6 = (f32[544,128]{1,0:T(8,128)S(1)}, f32[544,128]{1,0:T(8,128)S(1)}, u32[]{:S(2)}, u32[]{:S(2)}) collective-permute-start(f32[544,128]{1,0:T(8,128)S(1)} %pad_maximum_fusion), channel_id=1, source_target_pairs={{0,1},{1,2},{2,3},{3,4},{4,5},{5,6},{6,7},{8,9},{9,10},{10,11},{11... | collective-permute-start | bytes 835592 | tf_op jit(solution)/shard_map/ppermute | solution.py:429
  57.2 0.0 collective-permute-done.5
  57.2 1.9 %collective-permute-start.7 = (f32[544,128]{1,0:T(8,128)S(1)}, f32[544,128]{1,0:T(8,128)S(1)}, u32[]{:S(2)}, u32[]{:S(2)}) collective-permute-start(f32[544,128]{1,0:T(8,128)S(1)} %pad_maximum_fusion), channel_id=1, source_target_pairs={{1,0},{2,1},{3,2},{4,3},{5,4},{6,5},{7,6},{9,8},{10,9},{11,10},{12... | collective-permute-start | bytes 835592 | tf_op jit(solution)/shard_map/ppermute | solution.py:429
  59.1 2.1 %fusion.13 = (f32[2,512,128]{2,1,0:T(8,128)S(1)}, f32[2,512,128]{2,1,0:T(8,128)S(1)}) fusion(f32[2,2,512,128]{3,2,1,0:T(8,128)} %collective-permute-done.5, f32[4,2,512,128]{3,2,1,0:T(8,128)} %collective-permute-done, f32[4,2,512,128]{3,2,1,0:T(8,128)} %get-tuple-element.16), kind=kLoop, calls=%fused_computation.24 | loop fusion | flops 524288 | bytes 4194304 | tf_op jit(solution)/shard_map/add | solution.py:432
  61.2 0.2 collective-permute-done.6
  61.4 0.0 collective-permute-start.12
  61.5 7.8 %collective-permute-done.7 = f32[544,128]{1,0:T(8,128)S(1)} collective-permute-done((f32[544,128]{1,0:T(8,128)S(1)}, f32[544,128]{1,0:T(8,128)S(1)}, u32[]{:S(2)}, u32[]{:S(2)}) %collective-permute-start.7) | collective-permute-done | bytes 278560 | tf_op jit(solution)/shard_map/ppermute | solution.py:429
  69.3 4.1 %collective-permute-done.9 = f32[2,2,544,128]{3,2,1,0:T(8,128)} collective-permute-done((f32[2,2,544,128]{3,2,1,0:T(8,128)}, f32[2,2,544,128]{3,2,1,0:T(8,128)}, u32[]{:S(2)}, u32[]{:S(2)}) %collective-permute-start.9) | collective-permute-done | bytes 1114144 | tf_op jit(solution)/shard_map/ppermute | solution.py:389
  73.4 0.0 collective-permute-done.4
  73.4 1.3 %fusion.8 = f32[2,544,128]{2,1,0:T(8,128)S(1)} fusion(f32[2,2,544,128]{3,2,1,0:T(8,128)} %collective-permute-done.4, f32[2,2,2,544,128]{4,3,2,1,0:T(8,128)S(1)} %copy-done.2, f32[2,2,544,128]{3,2,1,0:T(8,128)} %collective-permute-done.9, f32[2,2,2,544,128]{4,3,2,1,0:T(8,128)S(1)} %copy-done), kind=kLoop, calls=%fused_computation.16 | loop fusion | flops 417792 | bytes 2785280 | tf_op jit(solution)/shard_map/add | solution.py:435
  74.7 1.9 %collective-permute-start.14 = (f32[2,544,128]{2,1,0:T(8,128)S(1)}, f32[2,544,128]{2,1,0:T(8,128)S(1)}, u32[]{:S(2)}, u32[]{:S(2)}) collective-permute-start(f32[2,544,128]{2,1,0:T(8,128)S(1)} %fusion.8), channel_id=1, source_target_pairs={{0,64},{8,72},{16,80},{24,88},{32,96},{40,104},{48,112},{56,120},{... | collective-permute-start | bytes 1671176 | tf_op jit(solution)/shard_map/ppermute | solution.py:397
  76.6 3.5 %collective-permute-start.11 = (f32[2,512,128]{2,1,0:T(8,128)S(1)}, f32[2,512,128]{2,1,0:T(8,128)S(1)}, u32[]{:S(2)}, u32[]{:S(2)}) collective-permute-start(f32[2,512,128]{2,1,0:T(8,128)S(1)} %get-tuple-element.30), channel_id=1, source_target_pairs={{0,48},{8,24},{16,0},{24,40},{32,16},{40,56},{48,32},{56,8},{64,11... | collective-permute-start | bytes 1572872 | tf_op jit(solution)/shard_map/ppermute | solution.py:393
  80.2 0.0 collective-permute-done.10
  80.2 0.0 collective-permute-done.12
  80.2 1.2 %fusion.12 = f32[2,512,128]{2,1,0:T(8,128)S(1)} fusion(f32[2,512,128]{2,1,0:T(8,128)S(1)} %collective-permute-done.12, f32[4,2,512,128]{3,2,1,0:T(8,128)} %collective-permute-done, f32[2,2,512,128]{3,2,1,0:T(8,128)S(1)} %collective-permute-done.10, f32[4,2,512,128]{3,2,1,0:T(8,128)S(1)} %copy-done.4), kind=kLoop, calls=%fused_computation.22 | loop fusion | flops 393216 | bytes 2621440 | tf_op jit(solution)/shard_map/add | solution.py:438
  81.4 0.1 collective-permute-start.13
  81.5 8.8 %collective-permute-done.14 = f32[2,544,128]{2,1,0:T(8,128)S(1)} collective-permute-done((f32[2,544,128]{2,1,0:T(8,128)S(1)}, f32[2,544,128]{2,1,0:T(8,128)S(1)}, u32[]{:S(2)}, u32[]{:S(2)}) %collective-permute-start.14) | collective-permute-done | bytes 557088 | tf_op jit(solution)/shard_map/ppermute | solution.py:397
  90.2 1.4 %fusion.5 = f32[2,544,128]{2,1,0:T(8,128)S(1)} fusion(f32[2,544,128]{2,1,0:T(8,128)S(1)} %collective-permute-done.14, f32[2,2,544,128]{3,2,1,0:T(8,128)} %collective-permute-done.4, f32[2,2,2,544,128]{4,3,2,1,0:T(8,128)S(1)} %copy-done.2, f32[2,2,544,128]{3,2,1,0:T(8,128)} %collective-permute-done.9, f32[2,2,2,544,128]{4,3,2,1,0:T(8,128)S(1)} %copy-done), kind=kLoop, calls=%fused_computation.11 | loop fusion | flops 557056 | bytes 3342336 | tf_op jit(solution)/shard_map/add | solution.py:441
  91.6 0.1 slice_bitcast_fusion.3
  91.7 5.6 %collective-permute-start.15 = (f32[544,128]{1,0:T(8,128)S(1)}, f32[544,128]{1,0:T(8,128)S(1)}, u32[]{:S(2)}, u32[]{:S(2)}) collective-permute-start(f32[544,128]{1,0:T(8,128)S(1)} %get-tuple-element.39), channel_id=1, source_target_pairs={{0,1},{1,2},{2,3},{3,4},{4,5},{5,6},{6,7},{8,9},{9,10},{10,11},{11... | collective-permute-start | bytes 835592 | tf_op jit(solution)/shard_map/ppermute | solution.py:443
  97.3 1.9 %collective-permute-start.16 = (f32[544,128]{1,0:T(8,128)S(1)}, f32[544,128]{1,0:T(8,128)S(1)}, u32[]{:S(2)}, u32[]{:S(2)}) collective-permute-start(f32[544,128]{1,0:T(8,128)S(1)} %get-tuple-element.38), channel_id=1, source_target_pairs={{1,0},{2,1},{3,2},{4,3},{5,4},{6,5},{7,6},{9,8},{10,9},{11,10},{12... | collective-permute-start | bytes 835592 | tf_op jit(solution)/shard_map/ppermute | solution.py:443
  99.3 0.0 collective-permute-done.11
  99.3 0.0 collective-permute-done.13
  99.3 1.2 %fusion.18 = f32[2,512,128]{2,1,0:T(8,128)S(1)} fusion(f32[2,512,128]{2,1,0:T(8,128)S(1)} %collective-permute-done.13, f32[2,512,128]{2,1,0:T(8,128)S(1)} %collective-permute-done.11, f32[4,2,512,128]{3,2,1,0:T(8,128)} %collective-permute-done, f32[2,2,512,128]{3,2,1,0:T(8,128)S(1)} %collective-permute-done.10, f32[4,2,512,128]{3,2,1,0:T(8,128)S(1)} %copy-done.4), kind=kLoop, calls=%fused_computation.33 | loop fusion | flops 524288 | bytes 3145728 | tf_op jit(solution)/shard_map/add | solution.py:444
  100.5 2.9 %collective-permute-done.15 = f32[544,128]{1,0:T(8,128)S(1)} collective-permute-done((f32[544,128]{1,0:T(8,128)S(1)}, f32[544,128]{1,0:T(8,128)S(1)}, u32[]{:S(2)}, u32[]{:S(2)}) %collective-permute-start.15) | collective-permute-done | bytes 278560 | tf_op jit(solution)/shard_map/ppermute | solution.py:443
  103.4 7.7 %collective-permute-done.16 = f32[544,128]{1,0:T(8,128)S(1)} collective-permute-done((f32[544,128]{1,0:T(8,128)S(1)}, f32[544,128]{1,0:T(8,128)S(1)}, u32[]{:S(2)}, u32[]{:S(2)}) %collective-permute-start.16) | collective-permute-done | bytes 278560 | tf_op jit(solution)/shard_map/ppermute | solution.py:443
  111.1 1.9 %shard_map.78 = (f32[32,2,8,128]{3,2,1,0:T(8,128)}, f32[32,2,8,128]{3,2,1,0:T(8,128)}) custom-call(f32[32,2,8,128]{3,2,1,0:T(8,128)S(1)} %bitcast.100, f32[32,2,8,128]{3,2,1,0:T(8,128)S(1)} %bitcast.99, f32[34,2,8,128]{3,2,1,0:T(8,128)S(1)} %bitcast.97, f32[34,2,8,128]{3,2,1,0:T(8,128)S(1)} %bitcast.96, f32[34,2,8,128]{3,2,1,0:T(8,128)S(1)} %bitcast.103, ...), custom_call_target="tpu_custom_call" | custom-call | bytes 4194304 | tf_op jit(solution)/shard_map/pallas_call | solution.py:355
  (11 shorter events, 0.1 us)
Async XLA Ops:
  18.9 4.5 %collective-permute-start.2 = (f32[4,2,512,128]{3,2,1,0:T(8,128)}, f32[4,2,512,128]{3,2,1,0:T(8,128)S(1)}, u32[]{:S(2)}, u32[]{:S(2)}) collective-permute-start(f32[4,2,512,128]{3,2,1,0:T(8,128)} %get-tuple-element.22), channel_id=1, source_target_pairs={{0,8},{8,0},{16,24},{24,16},{32,40},{40,32},{48,56},{56,48},{64,72... | collective-permute-start | bytes 6291464 | tf_op jit(solution)/shard_map/ppermute | solution.py:385
  19.0 7.6 %collective-permute-start.3 = (f32[2,2,2,544,128]{4,3,2,1,0:T(8,128)}, f32[2,2,2,544,128]{4,3,2,1,0:T(8,128)S(1)}, u32[]{:S(2)}, u32[]{:S(2)}) collective-permute-start(f32[2,2,2,544,128]{4,3,2,1,0:T(8,128)} %get-tuple-element.23), channel_id=1, source_target_pairs={{0,8},{8,0},{16,24},{24,16},{32,40},{40,32},{48,56},{56,48},{64,72... | collective-permute-start | bytes 6684680 | tf_op jit(solution)/shard_map/ppermute | solution.py:385
  19.5 12.1 %collective-permute-start.1 = (f32[2,2,2,544,128]{4,3,2,1,0:T(8,128)}, f32[2,2,2,544,128]{4,3,2,1,0:T(8,128)S(1)}, u32[]{:S(2)}, u32[]{:S(2)}) collective-permute-start(f32[2,2,2,544,128]{4,3,2,1,0:T(8,128)} %get-tuple-element.19), channel_id=1, source_target_pairs={{0,8},{8,0},{16,24},{24,16},{32,40},{40,32},{48,56},{56,48},{64,72... | collective-permute-start | bytes 6684680 | tf_op jit(solution)/shard_map/ppermute | solution.py:385
  23.3 3.2 %copy-start.3 = (f32[2,2,2,544,128]{4,3,2,1,0:T(8,128)S(1)}, f32[2,2,2,544,128]{4,3,2,1,0:T(8,128)}, u32[]{:S(2)}) copy-start(f32[2,2,2,544,128]{4,3,2,1,0:T(8,128)} %get-tuple-element.20) | copy-start | bytes 6684676
  26.6 17.0 %copy-start = (f32[2,2,2,544,128]{4,3,2,1,0:T(8,128)S(1)}, f32[2,2,2,544,128]{4,3,2,1,0:T(8,128)}, u32[]{:S(2)}) copy-start(f32[2,2,2,544,128]{4,3,2,1,0:T(8,128)} %get-tuple-element.18) | copy-start | bytes 6684676
  26.8 16.8 %collective-permute-start.8 = (f32[2,2,544,128]{3,2,1,0:T(8,128)S(1)}, f32[2,2,544,128]{3,2,1,0:T(8,128)S(1)}, u32[]{:S(2)}, u32[]{:S(2)}) collective-permute-start(f32[2,2,544,128]{3,2,1,0:T(8,128)S(1)} %get-tuple-element.36), channel_id=1, source_target_pairs={{0,16},{8,56},{16,32},{24,8},{32,48},{40,24},{48,0},{56,40},{64,80... | collective-permute-start | bytes 3342344 | tf_op jit(solution)/shard_map/ppermute | solution.py:389
  28.4 23.3 %collective-permute-start = (f32[4,2,512,128]{3,2,1,0:T(8,128)}, f32[4,2,512,128]{3,2,1,0:T(8,128)}, u32[]{:S(2)}, u32[]{:S(2)}) collective-permute-start(f32[4,2,512,128]{3,2,1,0:T(8,128)} %get-tuple-element.17), channel_id=1, source_target_pairs={{0,8},{8,0},{16,24},{24,16},{32,40},{40,32},{48,56},{56,48},{64,72... | collective-permute-start | bytes 6291464 | tf_op jit(solution)/shard_map/ppermute | solution.py:385
  29.7 27.5 %collective-permute-start.5 = (f32[2,2,512,128]{3,2,1,0:T(8,128)}, f32[2,2,512,128]{3,2,1,0:T(8,128)}, u32[]{:S(2)}, u32[]{:S(2)}) collective-permute-start(f32[2,2,512,128]{3,2,1,0:T(8,128)} %get-tuple-element.33), channel_id=1, source_target_pairs={{0,64},{8,72},{16,80},{24,88},{32,96},{40,104},{48,112},{56,120},{... | collective-permute-start | bytes 3145736 | tf_op jit(solution)/shard_map/ppermute | solution.py:397
  31.6 13.2 %copy-start.1 = (f32[2,2,2,544,128]{4,3,2,1,0:T(8,128)}, f32[2,2,2,544,128]{4,3,2,1,0:T(8,128)S(1)}, u32[]{:S(2)}) copy-start(f32[2,2,2,544,128]{4,3,2,1,0:T(8,128)S(1)} %collective-permute-done.1) | copy-start | bytes 6684676
  44.8 28.5 %collective-permute-start.9 = (f32[2,2,544,128]{3,2,1,0:T(8,128)}, f32[2,2,544,128]{3,2,1,0:T(8,128)}, u32[]{:S(2)}, u32[]{:S(2)}) collective-permute-start(f32[2,2,544,128]{3,2,1,0:T(8,128)} %fusion.2), channel_id=1, source_target_pairs={{0,16},{8,56},{16,32},{24,8},{32,48},{40,24},{48,0},{56,40},{64,80... | collective-permute-start | bytes 3342344 | tf_op jit(solution)/shard_map/ppermute | solution.py:389
  45.2 28.2 %collective-permute-start.4 = (f32[2,2,544,128]{3,2,1,0:T(8,128)S(1)}, f32[2,2,544,128]{3,2,1,0:T(8,128)}, u32[]{:S(2)}, u32[]{:S(2)}) collective-permute-start(f32[2,2,544,128]{3,2,1,0:T(8,128)S(1)} %get-tuple-element.37), channel_id=1, source_target_pairs={{0,48},{8,24},{16,0},{24,40},{32,16},{40,56},{48,32},{56,8},{64,11... | collective-permute-start | bytes 3342344 | tf_op jit(solution)/shard_map/ppermute | solution.py:393
  49.0 31.2 %collective-permute-start.10 = (f32[2,2,512,128]{3,2,1,0:T(8,128)}, f32[2,2,512,128]{3,2,1,0:T(8,128)S(1)}, u32[]{:S(2)}, u32[]{:S(2)}) collective-permute-start(f32[2,2,512,128]{3,2,1,0:T(8,128)} %get-tuple-element.32), channel_id=1, source_target_pairs={{0,64},{8,72},{16,80},{24,88},{32,96},{40,104},{48,112},{56,120},{... | collective-permute-start | bytes 3145736 | tf_op jit(solution)/shard_map/ppermute | solution.py:397
  51.7 9.7 %collective-permute-start.6 = (f32[544,128]{1,0:T(8,128)S(1)}, f32[544,128]{1,0:T(8,128)S(1)}, u32[]{:S(2)}, u32[]{:S(2)}) collective-permute-start(f32[544,128]{1,0:T(8,128)S(1)} %pad_maximum_fusion), channel_id=1, source_target_pairs={{0,1},{1,2},{2,3},{3,4},{4,5},{5,6},{6,7},{8,9},{9,10},{10,11},{11... | collective-permute-start | bytes 835592 | tf_op jit(solution)/shard_map/ppermute | solution.py:429
  57.2 12.1 %collective-permute-start.7 = (f32[544,128]{1,0:T(8,128)S(1)}, f32[544,128]{1,0:T(8,128)S(1)}, u32[]{:S(2)}, u32[]{:S(2)}) collective-permute-start(f32[544,128]{1,0:T(8,128)S(1)} %pad_maximum_fusion), channel_id=1, source_target_pairs={{1,0},{2,1},{3,2},{4,3},{5,4},{6,5},{7,6},{9,8},{10,9},{11,10},{12... | collective-permute-start | bytes 835592 | tf_op jit(solution)/shard_map/ppermute | solution.py:429
  59.1 14.3 %copy-start.2 = (f32[2,2,2,544,128]{4,3,2,1,0:T(8,128)S(1)}, f32[2,2,2,544,128]{4,3,2,1,0:T(8,128)}, u32[]{:S(2)}) copy-start(f32[2,2,2,544,128]{4,3,2,1,0:T(8,128)} %copy-done.1) | copy-start | bytes 6684676
  61.2 18.9 %copy-start.4 = (f32[4,2,512,128]{3,2,1,0:T(8,128)S(1)}, f32[4,2,512,128]{3,2,1,0:T(8,128)}, u32[]{:S(2)}) copy-start(f32[4,2,512,128]{3,2,1,0:T(8,128)} %get-tuple-element.16) | copy-start | bytes 6291460
  61.4 18.7 %collective-permute-start.12 = (f32[2,512,128]{2,1,0:T(8,128)S(1)}, f32[2,512,128]{2,1,0:T(8,128)S(1)}, u32[]{:S(2)}, u32[]{:S(2)}) collective-permute-start(f32[2,512,128]{2,1,0:T(8,128)S(1)} %get-tuple-element.31), channel_id=1, source_target_pairs={{0,16},{8,56},{16,32},{24,8},{32,48},{40,24},{48,0},{56,40},{64,80... | collective-permute-start | bytes 1572872 | tf_op jit(solution)/shard_map/ppermute | solution.py:389
  74.7 15.5 %collective-permute-start.14 = (f32[2,544,128]{2,1,0:T(8,128)S(1)}, f32[2,544,128]{2,1,0:T(8,128)S(1)}, u32[]{:S(2)}, u32[]{:S(2)}) collective-permute-start(f32[2,544,128]{2,1,0:T(8,128)S(1)} %fusion.8), channel_id=1, source_target_pairs={{0,64},{8,72},{16,80},{24,88},{32,96},{40,104},{48,112},{56,120},{... | collective-permute-start | bytes 1671176 | tf_op jit(solution)/shard_map/ppermute | solution.py:397
  76.6 22.6 %collective-permute-start.11 = (f32[2,512,128]{2,1,0:T(8,128)S(1)}, f32[2,512,128]{2,1,0:T(8,128)S(1)}, u32[]{:S(2)}, u32[]{:S(2)}) collective-permute-start(f32[2,512,128]{2,1,0:T(8,128)S(1)} %get-tuple-element.30), channel_id=1, source_target_pairs={{0,48},{8,24},{16,0},{24,40},{32,16},{40,56},{48,32},{56,8},{64,11... | collective-permute-start | bytes 1572872 | tf_op jit(solution)/shard_map/ppermute | solution.py:393
  81.4 17.9 %collective-permute-start.13 = (f32[2,512,128]{2,1,0:T(8,128)S(1)}, f32[2,512,128]{2,1,0:T(8,128)S(1)}, u32[]{:S(2)}, u32[]{:S(2)}) collective-permute-start(f32[2,512,128]{2,1,0:T(8,128)S(1)} %fusion.12), channel_id=1, source_target_pairs={{0,16},{8,56},{16,32},{24,8},{32,48},{40,24},{48,0},{56,40},{64,80... | collective-permute-start | bytes 1572872 | tf_op jit(solution)/shard_map/ppermute | solution.py:389
  91.7 11.7 %collective-permute-start.15 = (f32[544,128]{1,0:T(8,128)S(1)}, f32[544,128]{1,0:T(8,128)S(1)}, u32[]{:S(2)}, u32[]{:S(2)}) collective-permute-start(f32[544,128]{1,0:T(8,128)S(1)} %get-tuple-element.39), channel_id=1, source_target_pairs={{0,1},{1,2},{2,3},{3,4},{4,5},{5,6},{6,7},{8,9},{9,10},{10,11},{11... | collective-permute-start | bytes 835592 | tf_op jit(solution)/shard_map/ppermute | solution.py:443
  97.3 13.8 %collective-permute-start.16 = (f32[544,128]{1,0:T(8,128)S(1)}, f32[544,128]{1,0:T(8,128)S(1)}, u32[]{:S(2)}, u32[]{:S(2)}) collective-permute-start(f32[544,128]{1,0:T(8,128)S(1)} %get-tuple-element.38), channel_id=1, source_target_pairs={{1,0},{2,1},{3,2},{4,3},{5,4},{6,5},{7,6},{9,8},{10,9},{11,10},{12... | collective-permute-start | bytes 835592 | tf_op jit(solution)/shard_map/ppermute | solution.py:443

commit v14 on v13

--- a/solution.py
+++ b/solution.py
@@ -433,13 +433,13 @@
     ring = after((two, direct, k_low, k_high), ring)
     two, direct = forth(two), back(direct)
     edge_far = rest_same[0, 1] + rest_came[0, 1] + ends_back[1] + ring[1]
+    edge = rest_same[0, 0] + rest_came[0, 0] + ends_back[0] + ring[0]
     far_rest_came = after(edge_far, far_rest_came)
-    edge_far = across(edge_far)
+    edge_came = across(edge_far)
     last = near_same[1] + near_came[1] + far_rest_came[1] + two
-    edge_far = after(last, edge_far)
+    edge_came = after((last, edge), edge_came)
     last = forth(last)
-    edge = rest_same[0, 0] + rest_came[0, 0] + ends_back[0] + ring[0] + edge_far
-    low, high = edge[0], edge[1]
+    low, high = edge[0] + edge_came[0], edge[1] + edge_came[1]
     above, below = lax.ppermute(low, "gz", DOWN), lax.ppermute(high, "gz", UP)
     result = near_same[0] + near_came[0] + far_rest_came[0] + direct + last
     d, v = result[0], result[1]

time: 113 us -> 116 us (1.027)
  waiting for transfers between devices: 47.2 us -> 50.1 us
  starting transfers between devices: 31.1 us -> 29.1 us
    ppermute x4, waiting for transfers between devices: 16 us -> 20.5 us  [forth(): return lax.ppermute(cells, 'tm', FORTH)]
    ppermute x3, waiting for transfers between devices: 8.77 us -> 4.95 us  [across(): return lax.ppermute(cells, 'tm', ACROSS)]
    ppermute x4, waiting for transfers between devices: 3.77 us -> 6.16 us  [to_sibling(): return lax.ppermute(other, 'tm', SIBLING)]
  transfers between devices with their start and end apart: 17 -> 17, of which waited for: 8 -> 9; matrix products, arithmetic and copies ran while one was open for 12% -> 13% of each run, Pallas kernels for 0% -> 0%
where the time goes in v14:
time: 116 us; the launch traced here: 115 us
  waiting for transfers between devices  50.1 us (43%)
  starting transfers between devices  29.1 us (25%)
  Pallas kernels  20.2 us (17%)
  other arithmetic  13.3 us (11%)
  local copies, waits for them, and re-layouts  1.72 us (1%)
    ppermute x4, waiting for transfers between devices, forth(): return lax.ppermute(cells, 'tm', FORTH)  20.5 us
    pallas_call x1, Pallas kernels, series(): pl.pallas_call(series_kernel, out_shape=(share,) * 4 + (edge,) * 4, in_sp...  18.3 us
    ppermute x2, waiting for transfers between devices, local(): above, below = (lax.ppermute(low, 'gz', DOWN), lax.ppermute(high, 'gz', UP))  10.5 us
    ppermute x1, waiting for transfers between devices, local(): lax.ppermute(k_here, 'gz', DOWN)  7.87 us
    ppermute x2, starting transfers between devices, local(): above, below = (lax.ppermute(low, 'gz', DOWN), lax.ppermute(high, 'gz', UP))  7.46 us
    ppermute x4, waiting for transfers between devices, to_sibling(): return lax.ppermute(other, 'tm', SIBLING)  6.16 us
    ppermute x2, starting transfers between devices, back(): return lax.ppermute(cells, 'tm', BACK)  5.77 us
    ppermute x3, starting transfers between devices, across(): return lax.ppermute(cells, 'tm', ACROSS)  5.44 us
  transfers between devices with their start and end apart: 17, of which 9 were waited for; matrix products, arithmetic and copies ran while one was open for 13% of the time, Pallas kernels for 0%

profile of v14, /device:TPU:6, one launch (start us, length us, event | category | flops | bytes accessed | tf_op | source)
XLA Modules:
  0.0 115.2 jit_solution(7046215558077998152)
XLA Ops:
  0.6 18.3 %shard_map.77 = (f32[4,2,512,128]{3,2,1,0:T(8,128)}, f32[4,2,512,128]{3,2,1,0:T(8,128)}, f32[4,2,512,128]{3,2,1,0:T(8,128)}, f32[4,2,512,128]{3,2,1,0:T(8,128)},...) custom-call(f32[1,4]{1,0:T(1,128)} %coeffs.1, ...), custom_call_target="tpu_custom_call" | custom-call | bytes 47185920 | tf_op jit(solution)/shard_map/pallas_call | solution.py:335
  18.9 0.1 collective-permute-start.2
  19.0 0.5 collective-permute-start.3
  19.5 0.1 collective-permute-start.1
  19.6 0.4 collective-permute-start
  20.0 3.3 %collective-permute-done.2 = f32[4,2,512,128]{3,2,1,0:T(8,128)S(1)} collective-permute-done((f32[4,2,512,128]{3,2,1,0:T(8,128)}, f32[4,2,512,128]{3,2,1,0:T(8,128)S(1)}, u32[]{:S(2)}, u32[]{:S(2)}) %collective-permute-start.2) | collective-permute-done | bytes 2097184 | tf_op jit(solution)/shard_map/ppermute | solution.py:385
  23.3 3.4 %slice_add_fusion.2 = (f32[2,2,512,128]{3,2,1,0:T(8,128)}, f32[2,2,512,128]{3,2,1,0:T(8,128)}) fusion(f32[4,2,512,128]{3,2,1,0:T(8,128)S(1)} %collective-permute-done.2, f32[4,2,512,128]{3,2,1,0:T(8,128)} %get-tuple-element.21), kind=kLoop, calls=%fused_computation.6 | loop fusion | flops 524288 | bytes 6291456 | tf_op jit(solution)/shard_map/add | solution.py:418
  26.7 2.8 %collective-permute-done.3 = f32[2,2,2,544,128]{4,3,2,1,0:T(8,128)S(1)} collective-permute-done((f32[2,2,2,544,128]{4,3,2,1,0:T(8,128)}, f32[2,2,2,544,128]{4,3,2,1,0:T(8,128)S(1)}, u32[]{:S(2)}, u32[]{:S(2)}) %collective-permute-start.3) | collective-permute-done | bytes 2228256 | tf_op jit(solution)/shard_map/ppermute | solution.py:385
  29.5 0.2 fusion
  29.8 1.6 %collective-permute-start.8 = (f32[2,2,544,128]{3,2,1,0:T(8,128)S(1)}, f32[2,2,544,128]{3,2,1,0:T(8,128)S(1)}, u32[]{:S(2)}, u32[]{:S(2)}) collective-permute-start(f32[2,2,544,128]{3,2,1,0:T(8,128)S(1)} %get-tuple-element.38), channel_id=1, source_target_pairs={{0,16},{8,56},{16,32},{24,8},{32,48},{40,24},{48,0},{56,40},{64,80... | collective-permute-start | bytes 3342344 | tf_op jit(solution)/shard_map/ppermute | solution.py:389
  31.4 1.9 %collective-permute-start.5 = (f32[2,2,512,128]{3,2,1,0:T(8,128)}, f32[2,2,512,128]{3,2,1,0:T(8,128)}, u32[]{:S(2)}, u32[]{:S(2)}) collective-permute-start(f32[2,2,512,128]{3,2,1,0:T(8,128)} %get-tuple-element.35), channel_id=1, source_target_pairs={{0,64},{8,72},{16,80},{24,88},{32,96},{40,104},{48,112},{56,120},{... | collective-permute-start | bytes 3145736 | tf_op jit(solution)/shard_map/ppermute | solution.py:397
  33.3 0.0 collective-permute-done.1
  33.3 13.2 %collective-permute-done.8 = f32[2,2,544,128]{3,2,1,0:T(8,128)S(1)} collective-permute-done((f32[2,2,544,128]{3,2,1,0:T(8,128)S(1)}, f32[2,2,544,128]{3,2,1,0:T(8,128)S(1)}, u32[]{:S(2)}, u32[]{:S(2)}) %collective-permute-start.8) | collective-permute-done | bytes 1114144 | tf_op jit(solution)/shard_map/ppermute | solution.py:389
  46.5 1.3 %fusion.2 = f32[2,2,544,128]{3,2,1,0:T(8,128)} fusion(f32[2,2,544,128]{3,2,1,0:T(8,128)S(1)} %collective-permute-done.8, f32[2,2,2,544,128]{4,3,2,1,0:T(8,128)S(1)} %collective-permute-done.1, f32[2,2,2,544,128]{4,3,2,1,0:T(8,128)S(1)} %copy-done), kind=kLoop, calls=%fused_computation.4 | loop fusion | flops 557056 | bytes 4456448 | tf_op jit(solution)/shard_map/add | solution.py:431
  47.8 0.3 collective-permute-start.9
  48.2 2.9 %collective-permute-start.4 = (f32[2,2,544,128]{3,2,1,0:T(8,128)S(1)}, f32[2,2,544,128]{3,2,1,0:T(8,128)}, u32[]{:S(2)}, u32[]{:S(2)}) collective-permute-start(f32[2,2,544,128]{3,2,1,0:T(8,128)S(1)} %get-tuple-element.39), channel_id=1, source_target_pairs={{0,48},{8,24},{16,0},{24,40},{32,16},{40,56},{48,32},{56,8},{64,11... | collective-permute-start | bytes 3342344 | tf_op jit(solution)/shard_map/ppermute | solution.py:393
  51.0 1.9 %collective-permute-start.10 = (f32[2,2,512,128]{3,2,1,0:T(8,128)}, f32[2,2,512,128]{3,2,1,0:T(8,128)}, u32[]{:S(2)}, u32[]{:S(2)}) collective-permute-start(f32[2,2,512,128]{3,2,1,0:T(8,128)} %get-tuple-element.34), channel_id=1, source_target_pairs={{0,64},{8,72},{16,80},{24,88},{32,96},{40,104},{48,112},{56,120},{... | collective-permute-start | bytes 3145736 | tf_op jit(solution)/shard_map/ppermute | solution.py:397
  53.0 1.7 %constant_dynamic-slice_fusion = f32[512,128]{1,0:T(8,128)} fusion(f32[8192,128]{1,0:T(8,128)} %bitcast.104, s32[]{:T(128)S(6)} %select_n.23), kind=kLoop, calls=%fused_computation.38 | loop fusion | bytes 524292 | tf_op jit(solution)/shard_map/dynamic_slice | solution.py:425
  54.7 0.7 dynamic-slice_select_fusion.1
  55.4 1.0 pad_maximum_fusion
  56.4 0.0 collective-permute-done
  56.4 5.4 %collective-permute-start.6 = (f32[544,128]{1,0:T(8,128)S(1)}, f32[544,128]{1,0:T(8,128)S(1)}, u32[]{:S(2)}, u32[]{:S(2)}) collective-permute-start(f32[544,128]{1,0:T(8,128)S(1)} %pad_maximum_fusion), channel_id=1, source_target_pairs={{0,1},{1,2},{2,3},{3,4},{4,5},{5,6},{6,7},{8,9},{9,10},{10,11},{11... | collective-permute-start | bytes 835592 | tf_op jit(solution)/shard_map/ppermute | solution.py:429
  61.8 0.0 collective-permute-done.5
  61.8 1.9 %collective-permute-start.7 = (f32[544,128]{1,0:T(8,128)S(1)}, f32[544,128]{1,0:T(8,128)S(1)}, u32[]{:S(2)}, u32[]{:S(2)}) collective-permute-start(f32[544,128]{1,0:T(8,128)S(1)} %pad_maximum_fusion), channel_id=1, source_target_pairs={{1,0},{2,1},{3,2},{4,3},{5,4},{6,5},{7,6},{9,8},{10,9},{11,10},{12... | collective-permute-start | bytes 835592 | tf_op jit(solution)/shard_map/ppermute | solution.py:429
  63.7 0.0 copy-start.2
  63.7 2.1 %fusion.12 = (f32[2,512,128]{2,1,0:T(8,128)S(1)}, f32[2,512,128]{2,1,0:T(8,128)S(1)}) fusion(f32[2,2,512,128]{3,2,1,0:T(8,128)} %collective-permute-done.5, f32[4,2,512,128]{3,2,1,0:T(8,128)} %collective-permute-done, f32[4,2,512,128]{3,2,1,0:T(8,128)} %get-tuple-element.16), kind=kLoop, calls=%fused_computation.23 | loop fusion | flops 524288 | bytes 4194304 | tf_op jit(solution)/shard_map/add | solution.py:432
  65.9 0.2 collective-permute-done.6
  66.0 0.0 collective-permute-start.12
  66.0 7.9 %collective-permute-done.7 = f32[544,128]{1,0:T(8,128)S(1)} collective-permute-done((f32[544,128]{1,0:T(8,128)S(1)}, f32[544,128]{1,0:T(8,128)S(1)}, u32[]{:S(2)}, u32[]{:S(2)}) %collective-permute-start.7) | collective-permute-done | bytes 278560 | tf_op jit(solution)/shard_map/ppermute | solution.py:429
  73.9 2.9 %collective-permute-start.11 = (f32[2,512,128]{2,1,0:T(8,128)S(1)}, f32[2,512,128]{2,1,0:T(8,128)S(1)}, u32[]{:S(2)}, u32[]{:S(2)}) collective-permute-start(f32[2,512,128]{2,1,0:T(8,128)S(1)} %get-tuple-element.32), channel_id=1, source_target_pairs={{0,48},{8,24},{16,0},{24,40},{32,16},{40,56},{48,32},{56,8},{64,11... | collective-permute-start | bytes 1572872 | tf_op jit(solution)/shard_map/ppermute | solution.py:393
  76.8 0.0 collective-permute-done.9
  76.8 0.0 collective-permute-done.4
  76.8 1.8 %fusion.4 = (f32[2,544,128]{2,1,0:T(8,128)S(1)}, f32[2,544,128]{2,1,0:T(8,128)S(1)}) fusion(f32[2,2,544,128]{3,2,1,0:T(8,128)} %collective-permute-done.4, f32[2,2,2,544,128]{4,3,2,1,0:T(8,128)S(1)} %copy-done.2, f32[2,2,544,128]{3,2,1,0:T(8,128)} %collective-permute-done.9, f32[2,2,2,544,128]{4,3,2,1,0:T(8,128)S(1)} %copy-done), kind=kLoop, calls=%fused_computation.10 | loop fusion | flops 835584 | bytes 5570560 | tf_op jit(solution)/shard_map/add | solution.py:436
  78.6 1.6 %collective-permute-start.14 = (f32[2,544,128]{2,1,0:T(8,128)S(1)}, f32[2,544,128]{2,1,0:T(8,128)S(1)}, u32[]{:S(2)}, u32[]{:S(2)}) collective-permute-start(f32[2,544,128]{2,1,0:T(8,128)S(1)} %get-tuple-element.31), channel_id=1, source_target_pairs={{0,64},{8,72},{16,80},{24,88},{32,96},{40,104},{48,112},{56,120},{... | collective-permute-start | bytes 1671176 | tf_op jit(solution)/shard_map/ppermute | solution.py:397
  80.2 0.0 collective-permute-done.10
  80.2 7.2 %collective-permute-done.12 = f32[2,512,128]{2,1,0:T(8,128)S(1)} collective-permute-done((f32[2,512,128]{2,1,0:T(8,128)S(1)}, f32[2,512,128]{2,1,0:T(8,128)S(1)}, u32[]{:S(2)}, u32[]{:S(2)}) %collective-permute-start.12) | collective-permute-done | bytes 524320 | tf_op jit(solution)/shard_map/ppermute | solution.py:389
  87.5 1.3 %fusion.11 = f32[2,512,128]{2,1,0:T(8,128)S(1)} fusion(f32[2,512,128]{2,1,0:T(8,128)S(1)} %collective-permute-done.12, f32[4,2,512,128]{3,2,1,0:T(8,128)} %collective-permute-done, f32[2,2,512,128]{3,2,1,0:T(8,128)} %collective-permute-done.10, f32[4,2,512,128]{3,2,1,0:T(8,128)S(1)} %copy-done.4), kind=kLoop, calls=%fused_computation.21 | loop fusion | flops 393216 | bytes 2621440 | tf_op jit(solution)/shard_map/add | solution.py:439
  88.8 0.1 collective-permute-start.13
  88.9 4.9 %collective-permute-done.14 = f32[2,544,128]{2,1,0:T(8,128)S(1)} collective-permute-done((f32[2,544,128]{2,1,0:T(8,128)S(1)}, f32[2,544,128]{2,1,0:T(8,128)S(1)}, u32[]{:S(2)}, u32[]{:S(2)}) %collective-permute-start.14) | collective-permute-done | bytes 557088 | tf_op jit(solution)/shard_map/ppermute | solution.py:397
  93.8 0.1 slice_add_fusion.12
  93.9 5.5 %collective-permute-start.15 = (f32[544,128]{1,0:T(8,128)S(1)}, f32[544,128]{1,0:T(8,128)S(1)}, u32[]{:S(2)}, u32[]{:S(2)}) collective-permute-start(f32[544,128]{1,0:T(8,128)S(1)} %bitcast.92), channel_id=1, source_target_pairs={{0,1},{1,2},{2,3},{3,4},{4,5},{5,6},{6,7},{8,9},{9,10},{10,11},{11... | collective-permute-start | bytes 835592 | tf_op jit(solution)/shard_map/ppermute | solution.py:443
  99.4 1.9 %collective-permute-start.16 = (f32[544,128]{1,0:T(8,128)S(1)}, f32[544,128]{1,0:T(8,128)S(1)}, u32[]{:S(2)}, u32[]{:S(2)}) collective-permute-start(f32[544,128]{1,0:T(8,128)S(1)} %bitcast.94), channel_id=1, source_target_pairs={{1,0},{2,1},{3,2},{4,3},{5,4},{6,5},{7,6},{9,8},{10,9},{11,10},{12... | collective-permute-start | bytes 835592 | tf_op jit(solution)/shard_map/ppermute | solution.py:443
  101.4 0.0 collective-permute-done.11
  101.4 0.0 collective-permute-done.13
  101.4 1.4 %fusion.17 = f32[2,512,128]{2,1,0:T(8,128)S(1)} fusion(f32[2,512,128]{2,1,0:T(8,128)S(1)} %collective-permute-done.13, f32[2,512,128]{2,1,0:T(8,128)S(1)} %collective-permute-done.11, f32[4,2,512,128]{3,2,1,0:T(8,128)} %collective-permute-done, f32[2,2,512,128]{3,2,1,0:T(8,128)} %collective-permute-done.10, f32[4,2,512,128]{3,2,1,0:T(8,128)S(1)} %copy-done.4), kind=kLoop, calls=%fused_computation.32 | loop fusion | flops 524288 | bytes 3145728 | tf_op jit(solution)/shard_map/add | solution.py:444
  102.8 2.7 %collective-permute-done.15 = f32[544,128]{1,0:T(8,128)S(1)} collective-permute-done((f32[544,128]{1,0:T(8,128)S(1)}, f32[544,128]{1,0:T(8,128)S(1)}, u32[]{:S(2)}, u32[]{:S(2)}) %collective-permute-start.15) | collective-permute-done | bytes 278560 | tf_op jit(solution)/shard_map/ppermute | solution.py:443
  105.5 7.7 %collective-permute-done.16 = f32[544,128]{1,0:T(8,128)S(1)} collective-permute-done((f32[544,128]{1,0:T(8,128)S(1)}, f32[544,128]{1,0:T(8,128)S(1)}, u32[]{:S(2)}, u32[]{:S(2)}) %collective-permute-start.16) | collective-permute-done | bytes 278560 | tf_op jit(solution)/shard_map/ppermute | solution.py:443
  113.3 1.9 %shard_map.78 = (f32[32,2,8,128]{3,2,1,0:T(8,128)}, f32[32,2,8,128]{3,2,1,0:T(8,128)}) custom-call(f32[32,2,8,128]{3,2,1,0:T(8,128)S(1)} %bitcast.98, f32[32,2,8,128]{3,2,1,0:T(8,128)S(1)} %bitcast.97, f32[34,2,8,128]{3,2,1,0:T(8,128)S(1)} %bitcast.95, f32[34,2,8,128]{3,2,1,0:T(8,128)S(1)} %bitcast.93, f32[34,2,8,128]{3,2,1,0:T(8,128)S(1)} %bitcast.101, ...), custom_call_target="tpu_custom_call" | custom-call | bytes 4194304 | tf_op jit(solution)/shard_map/pallas_call | solution.py:355
  (10 shorter events, 0.1 us)
Async XLA Ops:
  18.9 4.5 %collective-permute-start.2 = (f32[4,2,512,128]{3,2,1,0:T(8,128)}, f32[4,2,512,128]{3,2,1,0:T(8,128)S(1)}, u32[]{:S(2)}, u32[]{:S(2)}) collective-permute-start(f32[4,2,512,128]{3,2,1,0:T(8,128)} %get-tuple-element.22), channel_id=1, source_target_pairs={{0,8},{8,0},{16,24},{24,16},{32,40},{40,32},{48,56},{56,48},{64,72... | collective-permute-start | bytes 6291464 | tf_op jit(solution)/shard_map/ppermute | solution.py:385
  19.0 10.5 %collective-permute-start.3 = (f32[2,2,2,544,128]{4,3,2,1,0:T(8,128)}, f32[2,2,2,544,128]{4,3,2,1,0:T(8,128)S(1)}, u32[]{:S(2)}, u32[]{:S(2)}) collective-permute-start(f32[2,2,2,544,128]{4,3,2,1,0:T(8,128)} %get-tuple-element.23), channel_id=1, source_target_pairs={{0,8},{8,0},{16,24},{24,16},{32,40},{40,32},{48,56},{56,48},{64,72... | collective-permute-start | bytes 6684680 | tf_op jit(solution)/shard_map/ppermute | solution.py:385
  19.5 13.8 %collective-permute-start.1 = (f32[2,2,2,544,128]{4,3,2,1,0:T(8,128)}, f32[2,2,2,544,128]{4,3,2,1,0:T(8,128)S(1)}, u32[]{:S(2)}, u32[]{:S(2)}) collective-permute-start(f32[2,2,2,544,128]{4,3,2,1,0:T(8,128)} %get-tuple-element.19), channel_id=1, source_target_pairs={{0,8},{8,0},{16,24},{24,16},{32,40},{40,32},{48,56},{56,48},{64,72... | collective-permute-start | bytes 6684680 | tf_op jit(solution)/shard_map/ppermute | solution.py:385
  19.6 36.8 %collective-permute-start = (f32[4,2,512,128]{3,2,1,0:T(8,128)}, f32[4,2,512,128]{3,2,1,0:T(8,128)}, u32[]{:S(2)}, u32[]{:S(2)}) collective-permute-start(f32[4,2,512,128]{3,2,1,0:T(8,128)} %get-tuple-element.17), channel_id=1, source_target_pairs={{0,8},{8,0},{16,24},{24,16},{32,40},{40,32},{48,56},{56,48},{64,72... | collective-permute-start | bytes 6291464 | tf_op jit(solution)/shard_map/ppermute | solution.py:385
  23.3 6.2 %copy-start.3 = (f32[2,2,2,544,128]{4,3,2,1,0:T(8,128)S(1)}, f32[2,2,2,544,128]{4,3,2,1,0:T(8,128)}, u32[]{:S(2)}) copy-start(f32[2,2,2,544,128]{4,3,2,1,0:T(8,128)} %get-tuple-element.20) | copy-start | bytes 6684676
  29.5 17.0 %copy-start = (f32[2,2,2,544,128]{4,3,2,1,0:T(8,128)S(1)}, f32[2,2,2,544,128]{4,3,2,1,0:T(8,128)}, u32[]{:S(2)}) copy-start(f32[2,2,2,544,128]{4,3,2,1,0:T(8,128)} %get-tuple-element.18) | copy-start | bytes 6684676
  29.8 16.8 %collective-permute-start.8 = (f32[2,2,544,128]{3,2,1,0:T(8,128)S(1)}, f32[2,2,544,128]{3,2,1,0:T(8,128)S(1)}, u32[]{:S(2)}, u32[]{:S(2)}) collective-permute-start(f32[2,2,544,128]{3,2,1,0:T(8,128)S(1)} %get-tuple-element.38), channel_id=1, source_target_pairs={{0,16},{8,56},{16,32},{24,8},{32,48},{40,24},{48,0},{56,40},{64,80... | collective-permute-start | bytes 3342344 | tf_op jit(solution)/shard_map/ppermute | solution.py:389
  31.4 30.4 %collective-permute-start.5 = (f32[2,2,512,128]{3,2,1,0:T(8,128)}, f32[2,2,512,128]{3,2,1,0:T(8,128)}, u32[]{:S(2)}, u32[]{:S(2)}) collective-permute-start(f32[2,2,512,128]{3,2,1,0:T(8,128)} %get-tuple-element.35), channel_id=1, source_target_pairs={{0,64},{8,72},{16,80},{24,88},{32,96},{40,104},{48,112},{56,120},{... | collective-permute-start | bytes 3145736 | tf_op jit(solution)/shard_map/ppermute | solution.py:397
  33.3 14.5 %copy-start.1 = (f32[2,2,2,544,128]{4,3,2,1,0:T(8,128)}, f32[2,2,2,544,128]{4,3,2,1,0:T(8,128)S(1)}, u32[]{:S(2)}) copy-start(f32[2,2,2,544,128]{4,3,2,1,0:T(8,128)S(1)} %collective-permute-done.1) | copy-start | bytes 6684676
  47.8 29.0 %collective-permute-start.9 = (f32[2,2,544,128]{3,2,1,0:T(8,128)}, f32[2,2,544,128]{3,2,1,0:T(8,128)}, u32[]{:S(2)}, u32[]{:S(2)}) collective-permute-start(f32[2,2,544,128]{3,2,1,0:T(8,128)} %fusion.2), channel_id=1, source_target_pairs={{0,16},{8,56},{16,32},{24,8},{32,48},{40,24},{48,0},{56,40},{64,80... | collective-permute-start | bytes 3342344 | tf_op jit(solution)/shard_map/ppermute | solution.py:389
  48.2 28.6 %collective-permute-start.4 = (f32[2,2,544,128]{3,2,1,0:T(8,128)S(1)}, f32[2,2,544,128]{3,2,1,0:T(8,128)}, u32[]{:S(2)}, u32[]{:S(2)}) collective-permute-start(f32[2,2,544,128]{3,2,1,0:T(8,128)S(1)} %get-tuple-element.39), channel_id=1, source_target_pairs={{0,48},{8,24},{16,0},{24,40},{32,16},{40,56},{48,32},{56,8},{64,11... | collective-permute-start | bytes 3342344 | tf_op jit(solution)/shard_map/ppermute | solution.py:393
  51.0 29.2 %collective-permute-start.10 = (f32[2,2,512,128]{3,2,1,0:T(8,128)}, f32[2,2,512,128]{3,2,1,0:T(8,128)}, u32[]{:S(2)}, u32[]{:S(2)}) collective-permute-start(f32[2,2,512,128]{3,2,1,0:T(8,128)} %get-tuple-element.34), channel_id=1, source_target_pairs={{0,64},{8,72},{16,80},{24,88},{32,96},{40,104},{48,112},{56,120},{... | collective-permute-start | bytes 3145736 | tf_op jit(solution)/shard_map/ppermute | solution.py:397
  56.4 9.7 %collective-permute-start.6 = (f32[544,128]{1,0:T(8,128)S(1)}, f32[544,128]{1,0:T(8,128)S(1)}, u32[]{:S(2)}, u32[]{:S(2)}) collective-permute-start(f32[544,128]{1,0:T(8,128)S(1)} %pad_maximum_fusion), channel_id=1, source_target_pairs={{0,1},{1,2},{2,3},{3,4},{4,5},{5,6},{6,7},{8,9},{9,10},{10,11},{11... | collective-permute-start | bytes 835592 | tf_op jit(solution)/shard_map/ppermute | solution.py:429
  61.8 12.1 %collective-permute-start.7 = (f32[544,128]{1,0:T(8,128)S(1)}, f32[544,128]{1,0:T(8,128)S(1)}, u32[]{:S(2)}, u32[]{:S(2)}) collective-permute-start(f32[544,128]{1,0:T(8,128)S(1)} %pad_maximum_fusion), channel_id=1, source_target_pairs={{1,0},{2,1},{3,2},{4,3},{5,4},{6,5},{7,6},{9,8},{10,9},{11,10},{12... | collective-permute-start | bytes 835592 | tf_op jit(solution)/shard_map/ppermute | solution.py:429
  63.7 13.1 %copy-start.2 = (f32[2,2,2,544,128]{4,3,2,1,0:T(8,128)S(1)}, f32[2,2,2,544,128]{4,3,2,1,0:T(8,128)}, u32[]{:S(2)}) copy-start(f32[2,2,2,544,128]{4,3,2,1,0:T(8,128)} %copy-done.1) | copy-start | bytes 6684676
  66.0 21.4 %collective-permute-start.12 = (f32[2,512,128]{2,1,0:T(8,128)S(1)}, f32[2,512,128]{2,1,0:T(8,128)S(1)}, u32[]{:S(2)}, u32[]{:S(2)}) collective-permute-start(f32[2,512,128]{2,1,0:T(8,128)S(1)} %get-tuple-element.33), channel_id=1, source_target_pairs={{0,16},{8,56},{16,32},{24,8},{32,48},{40,24},{48,0},{56,40},{64,80... | collective-permute-start | bytes 1572872 | tf_op jit(solution)/shard_map/ppermute | solution.py:389
  73.9 13.6 %copy-start.4 = (f32[4,2,512,128]{3,2,1,0:T(8,128)S(1)}, f32[4,2,512,128]{3,2,1,0:T(8,128)}, u32[]{:S(2)}) copy-start(f32[4,2,512,128]{3,2,1,0:T(8,128)} %get-tuple-element.16) | copy-start | bytes 6291460
  73.9 27.5 %collective-permute-start.11 = (f32[2,512,128]{2,1,0:T(8,128)S(1)}, f32[2,512,128]{2,1,0:T(8,128)S(1)}, u32[]{:S(2)}, u32[]{:S(2)}) collective-permute-start(f32[2,512,128]{2,1,0:T(8,128)S(1)} %get-tuple-element.32), channel_id=1, source_target_pairs={{0,48},{8,24},{16,0},{24,40},{32,16},{40,56},{48,32},{56,8},{64,11... | collective-permute-start | bytes 1572872 | tf_op jit(solution)/shard_map/ppermute | solution.py:393
  78.6 15.2 %collective-permute-start.14 = (f32[2,544,128]{2,1,0:T(8,128)S(1)}, f32[2,544,128]{2,1,0:T(8,128)S(1)}, u32[]{:S(2)}, u32[]{:S(2)}) collective-permute-start(f32[2,544,128]{2,1,0:T(8,128)S(1)} %get-tuple-element.31), channel_id=1, source_target_pairs={{0,64},{8,72},{16,80},{24,88},{32,96},{40,104},{48,112},{56,120},{... | collective-permute-start | bytes 1671176 | tf_op jit(solution)/shard_map/ppermute | solution.py:397
  88.8 12.6 %collective-permute-start.13 = (f32[2,512,128]{2,1,0:T(8,128)S(1)}, f32[2,512,128]{2,1,0:T(8,128)S(1)}, u32[]{:S(2)}, u32[]{:S(2)}) collective-permute-start(f32[2,512,128]{2,1,0:T(8,128)S(1)} %fusion.11), channel_id=1, source_target_pairs={{0,16},{8,56},{16,32},{24,8},{32,48},{40,24},{48,0},{56,40},{64,80... | collective-permute-start | bytes 1572872 | tf_op jit(solution)/shard_map/ppermute | solution.py:389
  93.9 11.6 %collective-permute-start.15 = (f32[544,128]{1,0:T(8,128)S(1)}, f32[544,128]{1,0:T(8,128)S(1)}, u32[]{:S(2)}, u32[]{:S(2)}) collective-permute-start(f32[544,128]{1,0:T(8,128)S(1)} %bitcast.92), channel_id=1, source_target_pairs={{0,1},{1,2},{2,3},{3,4},{4,5},{5,6},{6,7},{8,9},{9,10},{10,11},{11... | collective-permute-start | bytes 835592 | tf_op jit(solution)/shard_map/ppermute | solution.py:443
  99.4 13.8 %collective-permute-start.16 = (f32[544,128]{1,0:T(8,128)S(1)}, f32[544,128]{1,0:T(8,128)S(1)}, u32[]{:S(2)}, u32[]{:S(2)}) collective-permute-start(f32[544,128]{1,0:T(8,128)S(1)} %bitcast.94), channel_id=1, source_target_pairs={{1,0},{2,1},{3,2},{4,3},{5,4},{6,5},{7,6},{9,8},{10,9},{11,10},{12... | collective-permute-start | bytes 835592 | tf_op jit(solution)/shard_map/ppermute | solution.py:443

commit v15 on v14

--- a/solution.py
+++ b/solution.py
@@ -411,8 +411,10 @@
     far_other, far_same, near_other, near_same, ends_other, ends_same, rest_other, rest_same = outs
 
     ends_came, far_came = to_sibling(ends_other), to_sibling(far_other)
-    rest_came, near_came = to_sibling(rest_other), to_sibling(near_other)
-    ends_two = forth(ends_same[0] + ends_came[0])
+    rest_came = to_sibling(rest_other)
+    ends_two = ends_same[0] + ends_came[0]
+    near_came = to_sibling(after(ends_two, near_other))
+    ends_two = forth(ends_two)
     far_ends = far_same[2:] + far_came[2:]
     ends_came = after(far_ends, ends_came)
     far_ends_came, far_rest_came = across(far_ends), across(far_same[:2] + far_came[:2])

time: 116 us -> 112 us (0.966)
  starting transfers between devices: 29.1 us -> 26.8 us
  waiting for transfers between devices: 50.1 us -> 48.9 us
    ppermute x4, waiting for transfers between devices: 20.5 us -> 14.6 us  [forth(): return lax.ppermute(cells, 'tm', FORTH)]
    ppermute x3, waiting for transfers between devices: 4.95 us -> 9.46 us  [across(): return lax.ppermute(cells, 'tm', ACROSS)]
    ppermute x1, waiting for transfers between devices: 0.17 us -> 2.98 us  [local(): lax.ppermute(k_here, 'gz', UP)]
    ppermute x4, waiting for transfers between devices: 6.16 us -> 3.77 us  [to_sibling(): return lax.ppermute(other, 'tm', SIBLING)]
    ppermute x2, starting transfers between devices: 5.77 us -> 3.39 us  [back(): return lax.ppermute(cells, 'tm', BACK)]
    ppermute x4, starting transfers between devices: 2.05 us -> 3.5 us  [forth(): return lax.ppermute(cells, 'tm', FORTH)]
where the time goes in v15:
time: 112 us
  waiting for transfers between devices  48.9 us (44%)
  starting transfers between devices  26.8 us (24%)
  Pallas kernels  20.2 us (18%)
  other arithmetic  13.3 us (12%)
  local copies, waits for them, and re-layouts  1.72 us (2%)
    pallas_call x1, Pallas kernels, series(): pl.pallas_call(series_kernel, out_shape=(share,) * 4 + (edge,) * 4, in_sp...  18.2 us
    ppermute x4, waiting for transfers between devices, forth(): return lax.ppermute(cells, 'tm', FORTH)  14.6 us
    ppermute x2, waiting for transfers between devices, local(): above, below = (lax.ppermute(low, 'gz', DOWN), lax.ppermute(high, 'gz', UP))  10.2 us
    ppermute x3, waiting for transfers between devices, across(): return lax.ppermute(cells, 'tm', ACROSS)  9.46 us
    ppermute x1, waiting for transfers between devices, local(): lax.ppermute(k_here, 'gz', DOWN)  7.82 us
    ppermute x2, starting transfers between devices, local(): above, below = (lax.ppermute(low, 'gz', DOWN), lax.ppermute(high, 'gz', UP))  6.3 us
    ppermute x1, starting transfers between devices, local(): lax.ppermute(k_here, 'gz', UP)  5.88 us
    ppermute x3, starting transfers between devices, across(): return lax.ppermute(cells, 'tm', ACROSS)  4.9 us
  transfers between devices with their start and end apart: 17, of which 9 were waited for; matrix products, arithmetic and copies ran while one was open for 13% of the time, Pallas kernels for 0%

profile of v15, /device:TPU:6, one launch (start us, length us, event | category | flops | bytes accessed | tf_op | source)
XLA Modules:
  0.0 111.6 jit_solution(14222516171027421860)
XLA Ops:
  0.6 18.2 %shard_map.77 = (f32[4,2,512,128]{3,2,1,0:T(8,128)}, f32[4,2,512,128]{3,2,1,0:T(8,128)}, f32[4,2,512,128]{3,2,1,0:T(8,128)}, f32[4,2,512,128]{3,2,1,0:T(8,128)},...) custom-call(f32[1,4]{1,0:T(1,128)} %coeffs.1, ...), custom_call_target="tpu_custom_call" | custom-call | bytes 47185920 | tf_op jit(solution)/shard_map/pallas_call | solution.py:335
  18.9 0.1 collective-permute-start.3
  19.0 0.5 collective-permute-start
  19.5 0.1 collective-permute-start.2
  19.6 3.8 %collective-permute-done.3 = f32[4,2,512,128]{3,2,1,0:T(8,128)S(1)} collective-permute-done((f32[4,2,512,128]{3,2,1,0:T(8,128)}, f32[4,2,512,128]{3,2,1,0:T(8,128)S(1)}, u32[]{:S(2)}, u32[]{:S(2)}) %collective-permute-start.3) | collective-permute-done | bytes 2097184 | tf_op jit(solution)/shard_map/ppermute | solution.py:385
  23.3 3.3 %slice_add_fusion.2 = (f32[2,2,512,128]{3,2,1,0:T(8,128)}, f32[2,2,512,128]{3,2,1,0:T(8,128)}) fusion(f32[4,2,512,128]{3,2,1,0:T(8,128)S(1)} %collective-permute-done.3, f32[4,2,512,128]{3,2,1,0:T(8,128)} %get-tuple-element.24), kind=kLoop, calls=%fused_computation.6 | loop fusion | flops 524288 | bytes 6291456 | tf_op jit(solution)/shard_map/add | solution.py:420
  26.7 0.0 collective-permute-done
  26.7 0.2 add_bitcast_fusion
  26.9 0.2 collective-permute-start.1
  27.1 1.6 %collective-permute-start.8 = (f32[2,2,544,128]{3,2,1,0:T(8,128)S(1)}, f32[2,2,544,128]{3,2,1,0:T(8,128)S(1)}, u32[]{:S(2)}, u32[]{:S(2)}) collective-permute-start(f32[2,2,544,128]{3,2,1,0:T(8,128)S(1)} %get-tuple-element.41), channel_id=1, source_target_pairs={{0,16},{8,56},{16,32},{24,8},{32,48},{40,24},{48,0},{56,40},{64,80... | collective-permute-start | bytes 3342344 | tf_op jit(solution)/shard_map/ppermute | solution.py:389
  28.7 1.9 %collective-permute-start.5 = (f32[2,2,512,128]{3,2,1,0:T(8,128)}, f32[2,2,512,128]{3,2,1,0:T(8,128)}, u32[]{:S(2)}, u32[]{:S(2)}) collective-permute-start(f32[2,2,512,128]{3,2,1,0:T(8,128)} %get-tuple-element.37), channel_id=1, source_target_pairs={{0,64},{8,72},{16,80},{24,88},{32,96},{40,104},{48,112},{56,120},{... | collective-permute-start | bytes 3145736 | tf_op jit(solution)/shard_map/ppermute | solution.py:397
  30.6 0.0 collective-permute-done.2
  30.6 13.2 %collective-permute-done.8 = f32[2,2,544,128]{3,2,1,0:T(8,128)S(1)} collective-permute-done((f32[2,2,544,128]{3,2,1,0:T(8,128)S(1)}, f32[2,2,544,128]{3,2,1,0:T(8,128)S(1)}, u32[]{:S(2)}, u32[]{:S(2)}) %collective-permute-start.8) | collective-permute-done | bytes 1114144 | tf_op jit(solution)/shard_map/ppermute | solution.py:389
  43.8 1.2 %fusion.1 = f32[2,2,544,128]{3,2,1,0:T(8,128)} fusion(f32[2,2,544,128]{3,2,1,0:T(8,128)S(1)} %collective-permute-done.8, f32[2,2,2,544,128]{4,3,2,1,0:T(8,128)S(1)} %collective-permute-done.2, f32[2,2,2,544,128]{4,3,2,1,0:T(8,128)S(1)} %copy-done), kind=kLoop, calls=%fused_computation.2 | loop fusion | flops 557056 | bytes 4456448 | tf_op jit(solution)/shard_map/add | solution.py:433
  45.1 0.0 copy-done.1
  45.1 0.4 collective-permute-start.9
  45.5 2.8 %collective-permute-start.4 = (f32[2,2,544,128]{3,2,1,0:T(8,128)S(1)}, f32[2,2,544,128]{3,2,1,0:T(8,128)}, u32[]{:S(2)}, u32[]{:S(2)}) collective-permute-start(f32[2,2,544,128]{3,2,1,0:T(8,128)S(1)} %get-tuple-element.40), channel_id=1, source_target_pairs={{0,48},{8,24},{16,0},{24,40},{32,16},{40,56},{48,32},{56,8},{64,11... | collective-permute-start | bytes 3342344 | tf_op jit(solution)/shard_map/ppermute | solution.py:393
  48.3 1.9 %collective-permute-start.10 = (f32[2,2,512,128]{3,2,1,0:T(8,128)}, f32[2,2,512,128]{3,2,1,0:T(8,128)}, u32[]{:S(2)}, u32[]{:S(2)}) collective-permute-start(f32[2,2,512,128]{3,2,1,0:T(8,128)} %get-tuple-element.36), channel_id=1, source_target_pairs={{0,64},{8,72},{16,80},{24,88},{32,96},{40,104},{48,112},{56,120},{... | collective-permute-start | bytes 3145736 | tf_op jit(solution)/shard_map/ppermute | solution.py:397
  50.2 1.7 %constant_dynamic-slice_fusion = f32[512,128]{1,0:T(8,128)} fusion(f32[8192,128]{1,0:T(8,128)} %bitcast.104, s32[]{:T(128)S(6)} %select_n.23), kind=kLoop, calls=%fused_computation.38 | loop fusion | bytes 524292 | tf_op jit(solution)/shard_map/dynamic_slice | solution.py:427
  51.9 0.7 dynamic-slice_select_fusion.1
  52.6 1.0 pad_maximum_fusion
  53.6 0.9 collective-permute-done.5
  54.5 5.9 %collective-permute-start.6 = (f32[544,128]{1,0:T(8,128)S(1)}, f32[544,128]{1,0:T(8,128)S(1)}, u32[]{:S(2)}, u32[]{:S(2)}) collective-permute-start(f32[544,128]{1,0:T(8,128)S(1)} %pad_maximum_fusion), channel_id=1, source_target_pairs={{0,1},{1,2},{2,3},{3,4},{4,5},{5,6},{6,7},{8,9},{9,10},{10,11},{11... | collective-permute-start | bytes 835592 | tf_op jit(solution)/shard_map/ppermute | solution.py:431
  60.4 0.0 collective-permute-done.1
  60.4 1.9 %collective-permute-start.7 = (f32[544,128]{1,0:T(8,128)S(1)}, f32[544,128]{1,0:T(8,128)S(1)}, u32[]{:S(2)}, u32[]{:S(2)}) collective-permute-start(f32[544,128]{1,0:T(8,128)S(1)} %pad_maximum_fusion), channel_id=1, source_target_pairs={{1,0},{2,1},{3,2},{4,3},{5,4},{6,5},{7,6},{9,8},{10,9},{11,10},{12... | collective-permute-start | bytes 835592 | tf_op jit(solution)/shard_map/ppermute | solution.py:431
  62.3 2.1 %fusion.12 = (f32[2,512,128]{2,1,0:T(8,128)S(1)}, f32[2,512,128]{2,1,0:T(8,128)S(1)}) fusion(f32[2,2,512,128]{3,2,1,0:T(8,128)} %collective-permute-done.5, f32[4,2,512,128]{3,2,1,0:T(8,128)} %collective-permute-done.1, f32[4,2,512,128]{3,2,1,0:T(8,128)} %get-tuple-element.17), kind=kLoop, calls=%fused_computation.23 | loop fusion | flops 524288 | bytes 4194304 | tf_op jit(solution)/shard_map/add | solution.py:434
  64.4 3.0 %collective-permute-done.6 = f32[544,128]{1,0:T(8,128)S(1)} collective-permute-done((f32[544,128]{1,0:T(8,128)S(1)}, f32[544,128]{1,0:T(8,128)S(1)}, u32[]{:S(2)}, u32[]{:S(2)}) %collective-permute-start.6) | collective-permute-done | bytes 278560 | tf_op jit(solution)/shard_map/ppermute | solution.py:431
  67.4 0.0 collective-permute-start.12
  67.4 7.8 %collective-permute-done.7 = f32[544,128]{1,0:T(8,128)S(1)} collective-permute-done((f32[544,128]{1,0:T(8,128)S(1)}, f32[544,128]{1,0:T(8,128)S(1)}, u32[]{:S(2)}, u32[]{:S(2)}) %collective-permute-start.7) | collective-permute-done | bytes 278560 | tf_op jit(solution)/shard_map/ppermute | solution.py:431
  75.2 0.5 collective-permute-start.11
  75.8 0.0 collective-permute-done.9
  75.8 0.0 collective-permute-done.4
  75.8 1.9 %fusion.4 = (f32[2,544,128]{2,1,0:T(8,128)S(1)}, f32[2,544,128]{2,1,0:T(8,128)S(1)}) fusion(f32[2,2,544,128]{3,2,1,0:T(8,128)} %collective-permute-done.4, f32[2,2,2,544,128]{4,3,2,1,0:T(8,128)S(1)} %copy-done.2, f32[2,2,544,128]{3,2,1,0:T(8,128)} %collective-permute-done.9, f32[2,2,2,544,128]{4,3,2,1,0:T(8,128)S(1)} %copy-done), kind=kLoop, calls=%fused_computation.10 | loop fusion | flops 835584 | bytes 5570560 | tf_op jit(solution)/shard_map/add | solution.py:438
  77.7 1.1 collective-permute-start.14
  78.8 0.0 collective-permute-done.10
  78.8 1.4 %collective-permute-done.12 = f32[2,512,128]{2,1,0:T(8,128)S(1)} collective-permute-done((f32[2,512,128]{2,1,0:T(8,128)S(1)}, f32[2,512,128]{2,1,0:T(8,128)S(1)}, u32[]{:S(2)}, u32[]{:S(2)}) %collective-permute-start.12) | collective-permute-done | bytes 524320 | tf_op jit(solution)/shard_map/ppermute | solution.py:389
  80.2 1.3 %fusion.11 = f32[2,512,128]{2,1,0:T(8,128)S(1)} fusion(f32[2,512,128]{2,1,0:T(8,128)S(1)} %collective-permute-done.12, f32[4,2,512,128]{3,2,1,0:T(8,128)} %collective-permute-done.1, f32[2,2,512,128]{3,2,1,0:T(8,128)} %collective-permute-done.10, f32[4,2,512,128]{3,2,1,0:T(8,128)S(1)} %copy-done.4), kind=kLoop, calls=%fused_computation.21 | loop fusion | flops 393216 | bytes 2621440 | tf_op jit(solution)/shard_map/add | solution.py:441
  81.6 1.5 %collective-permute-start.13 = (f32[2,512,128]{2,1,0:T(8,128)S(1)}, f32[2,512,128]{2,1,0:T(8,128)S(1)}, u32[]{:S(2)}, u32[]{:S(2)}) collective-permute-start(f32[2,512,128]{2,1,0:T(8,128)S(1)} %fusion.11), channel_id=1, source_target_pairs={{0,16},{8,56},{16,32},{24,8},{32,48},{40,24},{48,0},{56,40},{64,80... | collective-permute-start | bytes 1572872 | tf_op jit(solution)/shard_map/ppermute | solution.py:389
  83.1 8.6 %collective-permute-done.14 = f32[2,544,128]{2,1,0:T(8,128)S(1)} collective-permute-done((f32[2,544,128]{2,1,0:T(8,128)S(1)}, f32[2,544,128]{2,1,0:T(8,128)S(1)}, u32[]{:S(2)}, u32[]{:S(2)}) %collective-permute-start.14) | collective-permute-done | bytes 557088 | tf_op jit(solution)/shard_map/ppermute | solution.py:397
  91.6 0.1 slice_add_fusion.12
  91.7 4.4 %collective-permute-start.15 = (f32[544,128]{1,0:T(8,128)S(1)}, f32[544,128]{1,0:T(8,128)S(1)}, u32[]{:S(2)}, u32[]{:S(2)}) collective-permute-start(f32[544,128]{1,0:T(8,128)S(1)} %bitcast.92), channel_id=1, source_target_pairs={{0,1},{1,2},{2,3},{3,4},{4,5},{5,6},{6,7},{8,9},{9,10},{10,11},{11... | collective-permute-start | bytes 835592 | tf_op jit(solution)/shard_map/ppermute | solution.py:445
  96.1 1.9 %collective-permute-start.16 = (f32[544,128]{1,0:T(8,128)S(1)}, f32[544,128]{1,0:T(8,128)S(1)}, u32[]{:S(2)}, u32[]{:S(2)}) collective-permute-start(f32[544,128]{1,0:T(8,128)S(1)} %bitcast.94), channel_id=1, source_target_pairs={{1,0},{2,1},{3,2},{4,3},{5,4},{6,5},{7,6},{9,8},{10,9},{11,10},{12... | collective-permute-start | bytes 835592 | tf_op jit(solution)/shard_map/ppermute | solution.py:445
  98.0 0.0 collective-permute-done.11
  98.0 0.0 collective-permute-done.13
  98.0 1.4 %fusion.17 = f32[2,512,128]{2,1,0:T(8,128)S(1)} fusion(f32[2,512,128]{2,1,0:T(8,128)S(1)} %collective-permute-done.13, f32[2,512,128]{2,1,0:T(8,128)S(1)} %collective-permute-done.11, f32[4,2,512,128]{3,2,1,0:T(8,128)} %collective-permute-done.1, f32[2,2,512,128]{3,2,1,0:T(8,128)} %collective-permute-done.10, f32[4,2,512,128]{3,2,1,0:T(8,128)S(1)} %copy-done.4), kind=kLoop, calls=%fused_computation.32 | loop fusion | flops 524288 | bytes 3145728 | tf_op jit(solution)/shard_map/add | solution.py:446
  99.4 2.5 %collective-permute-done.15 = f32[544,128]{1,0:T(8,128)S(1)} collective-permute-done((f32[544,128]{1,0:T(8,128)S(1)}, f32[544,128]{1,0:T(8,128)S(1)}, u32[]{:S(2)}, u32[]{:S(2)}) %collective-permute-start.15) | collective-permute-done | bytes 278560 | tf_op jit(solution)/shard_map/ppermute | solution.py:445
  101.9 7.7 %collective-permute-done.16 = f32[544,128]{1,0:T(8,128)S(1)} collective-permute-done((f32[544,128]{1,0:T(8,128)S(1)}, f32[544,128]{1,0:T(8,128)S(1)}, u32[]{:S(2)}, u32[]{:S(2)}) %collective-permute-start.16) | collective-permute-done | bytes 278560 | tf_op jit(solution)/shard_map/ppermute | solution.py:445
  109.6 1.9 %shard_map.78 = (f32[32,2,8,128]{3,2,1,0:T(8,128)}, f32[32,2,8,128]{3,2,1,0:T(8,128)}) custom-call(f32[32,2,8,128]{3,2,1,0:T(8,128)S(1)} %bitcast.98, f32[32,2,8,128]{3,2,1,0:T(8,128)S(1)} %bitcast.97, f32[34,2,8,128]{3,2,1,0:T(8,128)S(1)} %bitcast.95, f32[34,2,8,128]{3,2,1,0:T(8,128)S(1)} %bitcast.93, f32[34,2,8,128]{3,2,1,0:T(8,128)S(1)} %bitcast.101, ...), custom_call_target="tpu_custom_call" | custom-call | bytes 4194304 | tf_op jit(solution)/shard_map/pallas_call | solution.py:355
  (10 shorter events, 0.1 us)
Async XLA Ops:
  18.9 4.5 %collective-permute-start.3 = (f32[4,2,512,128]{3,2,1,0:T(8,128)}, f32[4,2,512,128]{3,2,1,0:T(8,128)S(1)}, u32[]{:S(2)}, u32[]{:S(2)}) collective-permute-start(f32[4,2,512,128]{3,2,1,0:T(8,128)} %get-tuple-element.25), channel_id=1, source_target_pairs={{0,8},{8,0},{16,24},{24,16},{32,40},{40,32},{48,56},{56,48},{64,72... | collective-permute-start | bytes 6291464 | tf_op jit(solution)/shard_map/ppermute | solution.py:385
  19.0 7.7 %collective-permute-start = (f32[2,2,2,544,128]{4,3,2,1,0:T(8,128)}, f32[2,2,2,544,128]{4,3,2,1,0:T(8,128)S(1)}, u32[]{:S(2)}, u32[]{:S(2)}) collective-permute-start(f32[2,2,2,544,128]{4,3,2,1,0:T(8,128)} %get-tuple-element.19), channel_id=1, source_target_pairs={{0,8},{8,0},{16,24},{24,16},{32,40},{40,32},{48,56},{56,48},{64,72... | collective-permute-start | bytes 6684680 | tf_op jit(solution)/shard_map/ppermute | solution.py:385
  19.5 11.2 %collective-permute-start.2 = (f32[2,2,2,544,128]{4,3,2,1,0:T(8,128)}, f32[2,2,2,544,128]{4,3,2,1,0:T(8,128)S(1)}, u32[]{:S(2)}, u32[]{:S(2)}) collective-permute-start(f32[2,2,2,544,128]{4,3,2,1,0:T(8,128)} %get-tuple-element.23), channel_id=1, source_target_pairs={{0,8},{8,0},{16,24},{24,16},{32,40},{40,32},{48,56},{56,48},{64,72... | collective-permute-start | bytes 6684680 | tf_op jit(solution)/shard_map/ppermute | solution.py:385
  23.3 3.3 %copy-start.3 = (f32[2,2,2,544,128]{4,3,2,1,0:T(8,128)S(1)}, f32[2,2,2,544,128]{4,3,2,1,0:T(8,128)}, u32[]{:S(2)}) copy-start(f32[2,2,2,544,128]{4,3,2,1,0:T(8,128)} %get-tuple-element.18) | copy-start | bytes 6684676
  26.7 17.2 %copy-start = (f32[2,2,2,544,128]{4,3,2,1,0:T(8,128)S(1)}, f32[2,2,2,544,128]{4,3,2,1,0:T(8,128)}, u32[]{:S(2)}) copy-start(f32[2,2,2,544,128]{4,3,2,1,0:T(8,128)} %get-tuple-element.22) | copy-start | bytes 6684676
  26.9 33.4 %collective-permute-start.1 = (f32[4,2,512,128]{3,2,1,0:T(8,128)}, f32[4,2,512,128]{3,2,1,0:T(8,128)}, u32[]{:S(2)}, u32[]{:S(2)}) collective-permute-start(f32[4,2,512,128]{3,2,1,0:T(8,128)} %get-tuple-element.21), channel_id=1, source_target_pairs={{0,8},{8,0},{16,24},{24,16},{32,40},{40,32},{48,56},{56,48},{64,72... | collective-permute-start | bytes 6291464 | tf_op jit(solution)/shard_map/ppermute | solution.py:385
  27.1 16.7 %collective-permute-start.8 = (f32[2,2,544,128]{3,2,1,0:T(8,128)S(1)}, f32[2,2,544,128]{3,2,1,0:T(8,128)S(1)}, u32[]{:S(2)}, u32[]{:S(2)}) collective-permute-start(f32[2,2,544,128]{3,2,1,0:T(8,128)S(1)} %get-tuple-element.41), channel_id=1, source_target_pairs={{0,16},{8,56},{16,32},{24,8},{32,48},{40,24},{48,0},{56,40},{64,80... | collective-permute-start | bytes 3342344 | tf_op jit(solution)/shard_map/ppermute | solution.py:389
  28.7 25.7 %collective-permute-start.5 = (f32[2,2,512,128]{3,2,1,0:T(8,128)}, f32[2,2,512,128]{3,2,1,0:T(8,128)}, u32[]{:S(2)}, u32[]{:S(2)}) collective-permute-start(f32[2,2,512,128]{3,2,1,0:T(8,128)} %get-tuple-element.37), channel_id=1, source_target_pairs={{0,64},{8,72},{16,80},{24,88},{32,96},{40,104},{48,112},{56,120},{... | collective-permute-start | bytes 3145736 | tf_op jit(solution)/shard_map/ppermute | solution.py:397
  30.6 14.4 %copy-start.1 = (f32[2,2,2,544,128]{4,3,2,1,0:T(8,128)}, f32[2,2,2,544,128]{4,3,2,1,0:T(8,128)S(1)}, u32[]{:S(2)}) copy-start(f32[2,2,2,544,128]{4,3,2,1,0:T(8,128)S(1)} %collective-permute-done.2) | copy-start | bytes 6684676
  45.1 30.7 %collective-permute-start.9 = (f32[2,2,544,128]{3,2,1,0:T(8,128)}, f32[2,2,544,128]{3,2,1,0:T(8,128)}, u32[]{:S(2)}, u32[]{:S(2)}) collective-permute-start(f32[2,2,544,128]{3,2,1,0:T(8,128)} %fusion.1), channel_id=1, source_target_pairs={{0,16},{8,56},{16,32},{24,8},{32,48},{40,24},{48,0},{56,40},{64,80... | collective-permute-start | bytes 3342344 | tf_op jit(solution)/shard_map/ppermute | solution.py:389
  45.5 30.3 %collective-permute-start.4 = (f32[2,2,544,128]{3,2,1,0:T(8,128)S(1)}, f32[2,2,544,128]{3,2,1,0:T(8,128)}, u32[]{:S(2)}, u32[]{:S(2)}) collective-permute-start(f32[2,2,544,128]{3,2,1,0:T(8,128)S(1)} %get-tuple-element.40), channel_id=1, source_target_pairs={{0,48},{8,24},{16,0},{24,40},{32,16},{40,56},{48,32},{56,8},{64,11... | collective-permute-start | bytes 3342344 | tf_op jit(solution)/shard_map/ppermute | solution.py:393
  48.3 30.5 %collective-permute-start.10 = (f32[2,2,512,128]{3,2,1,0:T(8,128)}, f32[2,2,512,128]{3,2,1,0:T(8,128)}, u32[]{:S(2)}, u32[]{:S(2)}) collective-permute-start(f32[2,2,512,128]{3,2,1,0:T(8,128)} %get-tuple-element.36), channel_id=1, source_target_pairs={{0,64},{8,72},{16,80},{24,88},{32,96},{40,104},{48,112},{56,120},{... | collective-permute-start | bytes 3145736 | tf_op jit(solution)/shard_map/ppermute | solution.py:397
  54.5 12.9 %collective-permute-start.6 = (f32[544,128]{1,0:T(8,128)S(1)}, f32[544,128]{1,0:T(8,128)S(1)}, u32[]{:S(2)}, u32[]{:S(2)}) collective-permute-start(f32[544,128]{1,0:T(8,128)S(1)} %pad_maximum_fusion), channel_id=1, source_target_pairs={{0,1},{1,2},{2,3},{3,4},{4,5},{5,6},{6,7},{8,9},{9,10},{10,11},{11... | collective-permute-start | bytes 835592 | tf_op jit(solution)/shard_map/ppermute | solution.py:431
  60.4 14.9 %collective-permute-start.7 = (f32[544,128]{1,0:T(8,128)S(1)}, f32[544,128]{1,0:T(8,128)S(1)}, u32[]{:S(2)}, u32[]{:S(2)}) collective-permute-start(f32[544,128]{1,0:T(8,128)S(1)} %pad_maximum_fusion), channel_id=1, source_target_pairs={{1,0},{2,1},{3,2},{4,3},{5,4},{6,5},{7,6},{9,8},{10,9},{11,10},{12... | collective-permute-start | bytes 835592 | tf_op jit(solution)/shard_map/ppermute | solution.py:431
  62.3 13.5 %copy-start.2 = (f32[2,2,2,544,128]{4,3,2,1,0:T(8,128)S(1)}, f32[2,2,2,544,128]{4,3,2,1,0:T(8,128)}, u32[]{:S(2)}) copy-start(f32[2,2,2,544,128]{4,3,2,1,0:T(8,128)} %copy-done.1) | copy-start | bytes 6684676
  67.4 12.8 %collective-permute-start.12 = (f32[2,512,128]{2,1,0:T(8,128)S(1)}, f32[2,512,128]{2,1,0:T(8,128)S(1)}, u32[]{:S(2)}, u32[]{:S(2)}) collective-permute-start(f32[2,512,128]{2,1,0:T(8,128)S(1)} %get-tuple-element.35), channel_id=1, source_target_pairs={{0,16},{8,56},{16,32},{24,8},{32,48},{40,24},{48,0},{56,40},{64,80... | collective-permute-start | bytes 1572872 | tf_op jit(solution)/shard_map/ppermute | solution.py:389
  75.2 5.0 %copy-start.4 = (f32[4,2,512,128]{3,2,1,0:T(8,128)S(1)}, f32[4,2,512,128]{3,2,1,0:T(8,128)}, u32[]{:S(2)}) copy-start(f32[4,2,512,128]{3,2,1,0:T(8,128)} %get-tuple-element.17) | copy-start | bytes 6291460
  75.2 22.8 %collective-permute-start.11 = (f32[2,512,128]{2,1,0:T(8,128)S(1)}, f32[2,512,128]{2,1,0:T(8,128)S(1)}, u32[]{:S(2)}, u32[]{:S(2)}) collective-permute-start(f32[2,512,128]{2,1,0:T(8,128)S(1)} %get-tuple-element.34), channel_id=1, source_target_pairs={{0,48},{8,24},{16,0},{24,40},{32,16},{40,56},{48,32},{56,8},{64,11... | collective-permute-start | bytes 1572872 | tf_op jit(solution)/shard_map/ppermute | solution.py:393
  77.7 13.9 %collective-permute-start.14 = (f32[2,544,128]{2,1,0:T(8,128)S(1)}, f32[2,544,128]{2,1,0:T(8,128)S(1)}, u32[]{:S(2)}, u32[]{:S(2)}) collective-permute-start(f32[2,544,128]{2,1,0:T(8,128)S(1)} %get-tuple-element.33), channel_id=1, source_target_pairs={{0,64},{8,72},{16,80},{24,88},{32,96},{40,104},{48,112},{56,120},{... | collective-permute-start | bytes 1671176 | tf_op jit(solution)/shard_map/ppermute | solution.py:397
  81.6 16.5 %collective-permute-start.13 = (f32[2,512,128]{2,1,0:T(8,128)S(1)}, f32[2,512,128]{2,1,0:T(8,128)S(1)}, u32[]{:S(2)}, u32[]{:S(2)}) collective-permute-start(f32[2,512,128]{2,1,0:T(8,128)S(1)} %fusion.11), channel_id=1, source_target_pairs={{0,16},{8,56},{16,32},{24,8},{32,48},{40,24},{48,0},{56,40},{64,80... | collective-permute-start | bytes 1572872 | tf_op jit(solution)/shard_map/ppermute | solution.py:389
  91.7 10.2 %collective-permute-start.15 = (f32[544,128]{1,0:T(8,128)S(1)}, f32[544,128]{1,0:T(8,128)S(1)}, u32[]{:S(2)}, u32[]{:S(2)}) collective-permute-start(f32[544,128]{1,0:T(8,128)S(1)} %bitcast.92), channel_id=1, source_target_pairs={{0,1},{1,2},{2,3},{3,4},{4,5},{5,6},{6,7},{8,9},{9,10},{10,11},{11... | collective-permute-start | bytes 835592 | tf_op jit(solution)/shard_map/ppermute | solution.py:445
  96.1 13.5 %collective-permute-start.16 = (f32[544,128]{1,0:T(8,128)S(1)}, f32[544,128]{1,0:T(8,128)S(1)}, u32[]{:S(2)}, u32[]{:S(2)}) collective-permute-start(f32[544,128]{1,0:T(8,128)S(1)} %bitcast.94), channel_id=1, source_target_pairs={{1,0},{2,1},{3,2},{4,3},{5,4},{6,5},{7,6},{9,8},{10,9},{11,10},{12... | collective-permute-start | bytes 835592 | tf_op jit(solution)/shard_map/ppermute | solution.py:445

commit v16 on v15

--- a/solution.py
+++ b/solution.py
@@ -430,12 +430,14 @@
     )
     k_low, k_high = lax.ppermute(k_here, "gz", UP), lax.ppermute(k_here, "gz", DOWN)
 
-    ring = forth(rest_same[1] + rest_came[1] + ends_two)
+    rest = rest_same + rest_came
+    ends_two, rest = lax.optimization_barrier((ends_two, rest))
+    ring = forth(rest[1] + ends_two)
     two, direct = (near_same[t] + near_came[t] + far_ends_came[t - 2] for t in (2, 3))
     ring = after((two, direct, k_low, k_high), ring)
     two, direct = forth(two), back(direct)
-    edge_far = rest_same[0, 1] + rest_came[0, 1] + ends_back[1] + ring[1]
-    edge = rest_same[0, 0] + rest_came[0, 0] + ends_back[0] + ring[0]
+    edge_far = rest[0, 1] + ends_back[1] + ring[1]
+    edge = rest[0, 0] + ends_back[0] + ring[0]
     far_rest_came = after(edge_far, far_rest_came)
     edge_came = across(edge_far)
     last = near_same[1] + near_came[1] + far_rest_came[1] + two

time: 112 us -> 112 us (level)
    add x2 -> x3, other arithmetic: 3.13 us -> 3.3 us  [the longest x1 1.84 us: local(): edge = rest[0, 0] + ends_back[0] + ring[0]]
where the time goes in v16:
time: 112 us; the launch traced here: 111 us
  waiting for transfers between devices  48.9 us (44%)
  starting transfers between devices  26.5 us (24%)
  Pallas kernels  20.2 us (18%)
  other arithmetic  13.3 us (12%)
  local copies, waits for them, and re-layouts  1.72 us (2%)
    pallas_call x1, Pallas kernels, series(): pl.pallas_call(series_kernel, out_shape=(share,) * 4 + (edge,) * 4, in_sp...  18.3 us
    ppermute x4, waiting for transfers between devices, forth(): return lax.ppermute(cells, 'tm', FORTH)  14.6 us
    ppermute x2, waiting for transfers between devices, local(): above, below = (lax.ppermute(low, 'gz', DOWN), lax.ppermute(high, 'gz', UP))  10.1 us
    ppermute x3, waiting for transfers between devices, across(): return lax.ppermute(cells, 'tm', ACROSS)  9.41 us
    ppermute x1, waiting for transfers between devices, local(): lax.ppermute(k_here, 'gz', DOWN)  7.95 us
    ppermute x2, starting transfers between devices, local(): above, below = (lax.ppermute(low, 'gz', DOWN), lax.ppermute(high, 'gz', UP))  6.25 us
    ppermute x1, starting transfers between devices, local(): lax.ppermute(k_here, 'gz', UP)  5.85 us
    ppermute x3, starting transfers between devices, across(): return lax.ppermute(cells, 'tm', ACROSS)  4.8 us
  transfers between devices with their start and end apart: 17, of which 9 were waited for; matrix products, arithmetic and copies ran while one was open for 13% of the time, Pallas kernels for 0%

profile of v16, /device:TPU:6, one launch (start us, length us, event | category | flops | bytes accessed | tf_op | source)
XLA Modules:
  0.0 111.4 jit_solution(2607861891604300559)
XLA Ops:
  0.6 18.3 %shard_map.77 = (f32[4,2,512,128]{3,2,1,0:T(8,128)}, f32[4,2,512,128]{3,2,1,0:T(8,128)}, f32[4,2,512,128]{3,2,1,0:T(8,128)}, f32[4,2,512,128]{3,2,1,0:T(8,128)},...) custom-call(f32[1,4]{1,0:T(1,128)} %coeffs.1, ...), custom_call_target="tpu_custom_call" | custom-call | bytes 47185920 | tf_op jit(solution)/shard_map/pallas_call | solution.py:335
  18.9 0.1 collective-permute-start.4
  19.0 0.5 collective-permute-start
  19.5 0.1 collective-permute-start.3
  19.6 3.8 %collective-permute-done.4 = f32[4,2,512,128]{3,2,1,0:T(8,128)S(1)} collective-permute-done((f32[4,2,512,128]{3,2,1,0:T(8,128)}, f32[4,2,512,128]{3,2,1,0:T(8,128)S(1)}, u32[]{:S(2)}, u32[]{:S(2)}) %collective-permute-start.4) | collective-permute-done | bytes 2097184 | tf_op jit(solution)/shard_map/ppermute | solution.py:385
  23.4 3.3 %slice_add_fusion.1 = (f32[2,2,512,128]{3,2,1,0:T(8,128)}, f32[2,2,512,128]{3,2,1,0:T(8,128)}) fusion(f32[4,2,512,128]{3,2,1,0:T(8,128)S(1)} %collective-permute-done.4, f32[4,2,512,128]{3,2,1,0:T(8,128)} %get-tuple-element.27), kind=kLoop, calls=%fused_computation.4 | loop fusion | flops 524288 | bytes 6291456 | tf_op jit(solution)/shard_map/add | solution.py:420
  26.7 0.0 collective-permute-done
  26.7 0.2 add_bitcast_fusion
  26.9 0.2 collective-permute-start.1
  27.1 1.6 %collective-permute-start.2 = (f32[2,2,544,128]{3,2,1,0:T(8,128)S(1)}, f32[2,2,544,128]{3,2,1,0:T(8,128)S(1)}, u32[]{:S(2)}, u32[]{:S(2)}) collective-permute-start(f32[2,2,544,128]{3,2,1,0:T(8,128)S(1)} %get-tuple-element.45), channel_id=1, source_target_pairs={{0,16},{8,56},{16,32},{24,8},{32,48},{40,24},{48,0},{56,40},{64,80... | collective-permute-start | bytes 3342344 | tf_op jit(solution)/shard_map/ppermute | solution.py:389
  28.7 1.9 %collective-permute-start.6 = (f32[2,2,512,128]{3,2,1,0:T(8,128)}, f32[2,2,512,128]{3,2,1,0:T(8,128)}, u32[]{:S(2)}, u32[]{:S(2)}) collective-permute-start(f32[2,2,512,128]{3,2,1,0:T(8,128)} %get-tuple-element.41), channel_id=1, source_target_pairs={{0,64},{8,72},{16,80},{24,88},{32,96},{40,104},{48,112},{56,120},{... | collective-permute-start | bytes 3145736 | tf_op jit(solution)/shard_map/ppermute | solution.py:397
  30.6 0.0 collective-permute-done.3
  30.6 0.2 add.119
  30.8 13.0 %collective-permute-done.2 = f32[2,2,544,128]{3,2,1,0:T(8,128)S(1)} collective-permute-done((f32[2,2,544,128]{3,2,1,0:T(8,128)S(1)}, f32[2,2,544,128]{3,2,1,0:T(8,128)S(1)}, u32[]{:S(2)}, u32[]{:S(2)}) %collective-permute-start.2) | collective-permute-done | bytes 1114144 | tf_op jit(solution)/shard_map/ppermute | solution.py:389
  43.9 1.2 %bitcast_add_fusion = f32[2,2,544,128]{3,2,1,0:T(8,128)} fusion(f32[2,2,544,128]{3,2,1,0:T(8,128)S(1)} %collective-permute-done.2, f32[2,2,2,544,128]{4,3,2,1,0:T(8,128)S(1)} %add.119), kind=kLoop, calls=%fused_computation.2 | loop fusion | flops 278528 | bytes 3342336 | tf_op jit(solution)/shard_map/add | solution.py:435
  45.1 0.4 collective-permute-start.9
  45.4 2.9 %collective-permute-start.5 = (f32[2,2,544,128]{3,2,1,0:T(8,128)S(1)}, f32[2,2,544,128]{3,2,1,0:T(8,128)}, u32[]{:S(2)}, u32[]{:S(2)}) collective-permute-start(f32[2,2,544,128]{3,2,1,0:T(8,128)S(1)} %get-tuple-element.44), channel_id=1, source_target_pairs={{0,48},{8,24},{16,0},{24,40},{32,16},{40,56},{48,32},{56,8},{64,11... | collective-permute-start | bytes 3342344 | tf_op jit(solution)/shard_map/ppermute | solution.py:393
  48.3 1.9 %collective-permute-start.10 = (f32[2,2,512,128]{3,2,1,0:T(8,128)}, f32[2,2,512,128]{3,2,1,0:T(8,128)}, u32[]{:S(2)}, u32[]{:S(2)}) collective-permute-start(f32[2,2,512,128]{3,2,1,0:T(8,128)} %get-tuple-element.40), channel_id=1, source_target_pairs={{0,64},{8,72},{16,80},{24,88},{32,96},{40,104},{48,112},{56,120},{... | collective-permute-start | bytes 3145736 | tf_op jit(solution)/shard_map/ppermute | solution.py:397
  50.2 1.7 %constant_dynamic-slice_fusion = f32[512,128]{1,0:T(8,128)} fusion(f32[8192,128]{1,0:T(8,128)} %bitcast.98, s32[]{:T(128)S(6)} %select_n.23), kind=kLoop, calls=%fused_computation.32 | loop fusion | bytes 524292 | tf_op jit(solution)/shard_map/dynamic_slice | solution.py:427
  51.9 0.7 dynamic-slice_select_fusion.1
  52.6 1.0 pad_maximum_fusion
  53.6 0.9 collective-permute-done.6
  54.4 5.9 %collective-permute-start.7 = (f32[544,128]{1,0:T(8,128)S(1)}, f32[544,128]{1,0:T(8,128)S(1)}, u32[]{:S(2)}, u32[]{:S(2)}) collective-permute-start(f32[544,128]{1,0:T(8,128)S(1)} %pad_maximum_fusion), channel_id=1, source_target_pairs={{0,1},{1,2},{2,3},{3,4},{4,5},{5,6},{6,7},{8,9},{9,10},{10,11},{11... | collective-permute-start | bytes 835592 | tf_op jit(solution)/shard_map/ppermute | solution.py:431
  60.3 0.0 collective-permute-done.1
  60.3 1.9 %collective-permute-start.8 = (f32[544,128]{1,0:T(8,128)S(1)}, f32[544,128]{1,0:T(8,128)S(1)}, u32[]{:S(2)}, u32[]{:S(2)}) collective-permute-start(f32[544,128]{1,0:T(8,128)S(1)} %pad_maximum_fusion), channel_id=1, source_target_pairs={{1,0},{2,1},{3,2},{4,3},{5,4},{6,5},{7,6},{9,8},{10,9},{11,10},{12... | collective-permute-start | bytes 835592 | tf_op jit(solution)/shard_map/ppermute | solution.py:431
  62.2 2.0 %fusion.8 = (f32[2,512,128]{2,1,0:T(8,128)S(1)}, f32[2,512,128]{2,1,0:T(8,128)S(1)}) fusion(f32[2,2,512,128]{3,2,1,0:T(8,128)} %collective-permute-done.6, f32[4,2,512,128]{3,2,1,0:T(8,128)} %collective-permute-done.1, f32[4,2,512,128]{3,2,1,0:T(8,128)} %get-tuple-element.19), kind=kLoop, calls=%fused_computation.17 | loop fusion | flops 524288 | bytes 4194304 | tf_op jit(solution)/shard_map/add | solution.py:436
  64.2 3.1 %collective-permute-done.7 = f32[544,128]{1,0:T(8,128)S(1)} collective-permute-done((f32[544,128]{1,0:T(8,128)S(1)}, f32[544,128]{1,0:T(8,128)S(1)}, u32[]{:S(2)}, u32[]{:S(2)}) %collective-permute-start.7) | collective-permute-done | bytes 278560 | tf_op jit(solution)/shard_map/ppermute | solution.py:431
  67.3 0.0 collective-permute-start.12
  67.3 8.0 %collective-permute-done.8 = f32[544,128]{1,0:T(8,128)S(1)} collective-permute-done((f32[544,128]{1,0:T(8,128)S(1)}, f32[544,128]{1,0:T(8,128)S(1)}, u32[]{:S(2)}, u32[]{:S(2)}) %collective-permute-start.8) | collective-permute-done | bytes 278560 | tf_op jit(solution)/shard_map/ppermute | solution.py:431
  75.2 0.5 collective-permute-start.11
  75.7 0.0 collective-permute-done.9
  75.7 0.0 collective-permute-done.5
  75.7 1.8 %fusion.2 = (f32[2,544,128]{2,1,0:T(8,128)S(1)}, f32[2,544,128]{2,1,0:T(8,128)S(1)}) fusion(f32[2,2,544,128]{3,2,1,0:T(8,128)} %collective-permute-done.5, f32[2,2,544,128]{3,2,1,0:T(8,128)} %collective-permute-done.9, f32[2,2,2,544,128]{4,3,2,1,0:T(8,128)S(1)} %add.119), kind=kLoop, calls=%fused_computation.8 | loop fusion | flops 557056 | bytes 4456448 | tf_op jit(solution)/shard_map/add | solution.py:440
  77.6 1.1 collective-permute-start.14
  78.6 0.0 collective-permute-done.10
  78.7 1.5 %collective-permute-done.12 = f32[2,512,128]{2,1,0:T(8,128)S(1)} collective-permute-done((f32[2,512,128]{2,1,0:T(8,128)S(1)}, f32[2,512,128]{2,1,0:T(8,128)S(1)}, u32[]{:S(2)}, u32[]{:S(2)}) %collective-permute-start.12) | collective-permute-done | bytes 524320 | tf_op jit(solution)/shard_map/ppermute | solution.py:389
  80.2 1.3 %fusion.7 = f32[2,512,128]{2,1,0:T(8,128)S(1)} fusion(f32[2,512,128]{2,1,0:T(8,128)S(1)} %collective-permute-done.12, f32[4,2,512,128]{3,2,1,0:T(8,128)} %collective-permute-done.1, f32[2,2,512,128]{3,2,1,0:T(8,128)} %collective-permute-done.10, f32[4,2,512,128]{3,2,1,0:T(8,128)S(1)} %copy-done.2), kind=kLoop, calls=%fused_computation.15 | loop fusion | flops 393216 | bytes 2621440 | tf_op jit(solution)/shard_map/add | solution.py:443
  81.5 1.5 %collective-permute-start.13 = (f32[2,512,128]{2,1,0:T(8,128)S(1)}, f32[2,512,128]{2,1,0:T(8,128)S(1)}, u32[]{:S(2)}, u32[]{:S(2)}) collective-permute-start(f32[2,512,128]{2,1,0:T(8,128)S(1)} %fusion.7), channel_id=1, source_target_pairs={{0,16},{8,56},{16,32},{24,8},{32,48},{40,24},{48,0},{56,40},{64,80... | collective-permute-start | bytes 1572872 | tf_op jit(solution)/shard_map/ppermute | solution.py:389
  83.0 8.5 %collective-permute-done.14 = f32[2,544,128]{2,1,0:T(8,128)S(1)} collective-permute-done((f32[2,544,128]{2,1,0:T(8,128)S(1)}, f32[2,544,128]{2,1,0:T(8,128)S(1)}, u32[]{:S(2)}, u32[]{:S(2)}) %collective-permute-start.14) | collective-permute-done | bytes 557088 | tf_op jit(solution)/shard_map/ppermute | solution.py:397
  91.6 0.1 slice_add_fusion.9
  91.7 4.3 %collective-permute-start.15 = (f32[544,128]{1,0:T(8,128)S(1)}, f32[544,128]{1,0:T(8,128)S(1)}, u32[]{:S(2)}, u32[]{:S(2)}) collective-permute-start(f32[544,128]{1,0:T(8,128)S(1)} %bitcast.86), channel_id=1, source_target_pairs={{0,1},{1,2},{2,3},{3,4},{4,5},{5,6},{6,7},{8,9},{9,10},{10,11},{11... | collective-permute-start | bytes 835592 | tf_op jit(solution)/shard_map/ppermute | solution.py:447
  96.0 1.9 %collective-permute-start.16 = (f32[544,128]{1,0:T(8,128)S(1)}, f32[544,128]{1,0:T(8,128)S(1)}, u32[]{:S(2)}, u32[]{:S(2)}) collective-permute-start(f32[544,128]{1,0:T(8,128)S(1)} %bitcast.88), channel_id=1, source_target_pairs={{1,0},{2,1},{3,2},{4,3},{5,4},{6,5},{7,6},{9,8},{10,9},{11,10},{12... | collective-permute-start | bytes 835592 | tf_op jit(solution)/shard_map/ppermute | solution.py:447
  97.9 0.0 collective-permute-done.11
  97.9 0.0 collective-permute-done.13
  97.9 1.4 %fusion.13 = f32[2,512,128]{2,1,0:T(8,128)S(1)} fusion(f32[2,512,128]{2,1,0:T(8,128)S(1)} %collective-permute-done.13, f32[2,512,128]{2,1,0:T(8,128)S(1)} %collective-permute-done.11, f32[4,2,512,128]{3,2,1,0:T(8,128)} %collective-permute-done.1, f32[2,2,512,128]{3,2,1,0:T(8,128)} %collective-permute-done.10, f32[4,2,512,128]{3,2,1,0:T(8,128)S(1)} %copy-done.2), kind=kLoop, calls=%fused_computation.26 | loop fusion | flops 524288 | bytes 3145728 | tf_op jit(solution)/shard_map/add | solution.py:448
  99.4 2.4 %collective-permute-done.15 = f32[544,128]{1,0:T(8,128)S(1)} collective-permute-done((f32[544,128]{1,0:T(8,128)S(1)}, f32[544,128]{1,0:T(8,128)S(1)}, u32[]{:S(2)}, u32[]{:S(2)}) %collective-permute-start.15) | collective-permute-done | bytes 278560 | tf_op jit(solution)/shard_map/ppermute | solution.py:447
  101.8 7.7 %collective-permute-done.16 = f32[544,128]{1,0:T(8,128)S(1)} collective-permute-done((f32[544,128]{1,0:T(8,128)S(1)}, f32[544,128]{1,0:T(8,128)S(1)}, u32[]{:S(2)}, u32[]{:S(2)}) %collective-permute-start.16) | collective-permute-done | bytes 278560 | tf_op jit(solution)/shard_map/ppermute | solution.py:447
  109.5 1.9 %shard_map.78 = (f32[32,2,8,128]{3,2,1,0:T(8,128)}, f32[32,2,8,128]{3,2,1,0:T(8,128)}) custom-call(f32[32,2,8,128]{3,2,1,0:T(8,128)S(1)} %bitcast.92, f32[32,2,8,128]{3,2,1,0:T(8,128)S(1)} %bitcast.91, f32[34,2,8,128]{3,2,1,0:T(8,128)S(1)} %bitcast.89, f32[34,2,8,128]{3,2,1,0:T(8,128)S(1)} %bitcast.87, f32[34,2,8,128]{3,2,1,0:T(8,128)S(1)} %bitcast.95, ...), custom_call_target="tpu_custom_call" | custom-call | bytes 4194304 | tf_op jit(solution)/shard_map/pallas_call | solution.py:355
  (7 shorter events, 0.0 us)
Async XLA Ops:
  18.9 4.5 %collective-permute-start.4 = (f32[4,2,512,128]{3,2,1,0:T(8,128)}, f32[4,2,512,128]{3,2,1,0:T(8,128)S(1)}, u32[]{:S(2)}, u32[]{:S(2)}) collective-permute-start(f32[4,2,512,128]{3,2,1,0:T(8,128)} %get-tuple-element.28), channel_id=1, source_target_pairs={{0,8},{8,0},{16,24},{24,16},{32,40},{40,32},{48,56},{56,48},{64,72... | collective-permute-start | bytes 6291464 | tf_op jit(solution)/shard_map/ppermute | solution.py:385
  19.0 7.7 %collective-permute-start = (f32[2,2,2,544,128]{4,3,2,1,0:T(8,128)}, f32[2,2,2,544,128]{4,3,2,1,0:T(8,128)S(1)}, u32[]{:S(2)}, u32[]{:S(2)}) collective-permute-start(f32[2,2,2,544,128]{4,3,2,1,0:T(8,128)} %get-tuple-element.21), channel_id=1, source_target_pairs={{0,8},{8,0},{16,24},{24,16},{32,40},{40,32},{48,56},{56,48},{64,72... | collective-permute-start | bytes 6684680 | tf_op jit(solution)/shard_map/ppermute | solution.py:385
  19.5 11.1 %collective-permute-start.3 = (f32[2,2,2,544,128]{4,3,2,1,0:T(8,128)}, f32[2,2,2,544,128]{4,3,2,1,0:T(8,128)S(1)}, u32[]{:S(2)}, u32[]{:S(2)}) collective-permute-start(f32[2,2,2,544,128]{4,3,2,1,0:T(8,128)} %get-tuple-element.25), channel_id=1, source_target_pairs={{0,8},{8,0},{16,24},{24,16},{32,40},{40,32},{48,56},{56,48},{64,72... | collective-permute-start | bytes 6684680 | tf_op jit(solution)/shard_map/ppermute | solution.py:385
  23.4 3.3 %copy-start.1 = (f32[2,2,2,544,128]{4,3,2,1,0:T(8,128)S(1)}, f32[2,2,2,544,128]{4,3,2,1,0:T(8,128)}, u32[]{:S(2)}) copy-start(f32[2,2,2,544,128]{4,3,2,1,0:T(8,128)} %get-tuple-element.20) | copy-start | bytes 6684676
  26.7 3.9 %copy-start = (f32[2,2,2,544,128]{4,3,2,1,0:T(8,128)S(1)}, f32[2,2,2,544,128]{4,3,2,1,0:T(8,128)}, u32[]{:S(2)}) copy-start(f32[2,2,2,544,128]{4,3,2,1,0:T(8,128)} %get-tuple-element.24) | copy-start | bytes 6684676
  26.9 33.4 %collective-permute-start.1 = (f32[4,2,512,128]{3,2,1,0:T(8,128)}, f32[4,2,512,128]{3,2,1,0:T(8,128)}, u32[]{:S(2)}, u32[]{:S(2)}) collective-permute-start(f32[4,2,512,128]{3,2,1,0:T(8,128)} %get-tuple-element.23), channel_id=1, source_target_pairs={{0,8},{8,0},{16,24},{24,16},{32,40},{40,32},{48,56},{56,48},{64,72... | collective-permute-start | bytes 6291464 | tf_op jit(solution)/shard_map/ppermute | solution.py:385
  27.1 16.7 %collective-permute-start.2 = (f32[2,2,544,128]{3,2,1,0:T(8,128)S(1)}, f32[2,2,544,128]{3,2,1,0:T(8,128)S(1)}, u32[]{:S(2)}, u32[]{:S(2)}) collective-permute-start(f32[2,2,544,128]{3,2,1,0:T(8,128)S(1)} %get-tuple-element.45), channel_id=1, source_target_pairs={{0,16},{8,56},{16,32},{24,8},{32,48},{40,24},{48,0},{56,40},{64,80... | collective-permute-start | bytes 3342344 | tf_op jit(solution)/shard_map/ppermute | solution.py:389
  28.7 25.7 %collective-permute-start.6 = (f32[2,2,512,128]{3,2,1,0:T(8,128)}, f32[2,2,512,128]{3,2,1,0:T(8,128)}, u32[]{:S(2)}, u32[]{:S(2)}) collective-permute-start(f32[2,2,512,128]{3,2,1,0:T(8,128)} %get-tuple-element.41), channel_id=1, source_target_pairs={{0,64},{8,72},{16,80},{24,88},{32,96},{40,104},{48,112},{56,120},{... | collective-permute-start | bytes 3145736 | tf_op jit(solution)/shard_map/ppermute | solution.py:397
  45.1 30.6 %collective-permute-start.9 = (f32[2,2,544,128]{3,2,1,0:T(8,128)}, f32[2,2,544,128]{3,2,1,0:T(8,128)}, u32[]{:S(2)}, u32[]{:S(2)}) collective-permute-start(f32[2,2,544,128]{3,2,1,0:T(8,128)} %bitcast_add_fusion), channel_id=1, source_target_pairs={{0,16},{8,56},{16,32},{24,8},{32,48},{40,24},{48,0},{56,40},{64,80... | collective-permute-start | bytes 3342344 | tf_op jit(solution)/shard_map/ppermute | solution.py:389
  45.4 30.3 %collective-permute-start.5 = (f32[2,2,544,128]{3,2,1,0:T(8,128)S(1)}, f32[2,2,544,128]{3,2,1,0:T(8,128)}, u32[]{:S(2)}, u32[]{:S(2)}) collective-permute-start(f32[2,2,544,128]{3,2,1,0:T(8,128)S(1)} %get-tuple-element.44), channel_id=1, source_target_pairs={{0,48},{8,24},{16,0},{24,40},{32,16},{40,56},{48,32},{56,8},{64,11... | collective-permute-start | bytes 3342344 | tf_op jit(solution)/shard_map/ppermute | solution.py:393
  48.3 30.3 %collective-permute-start.10 = (f32[2,2,512,128]{3,2,1,0:T(8,128)}, f32[2,2,512,128]{3,2,1,0:T(8,128)}, u32[]{:S(2)}, u32[]{:S(2)}) collective-permute-start(f32[2,2,512,128]{3,2,1,0:T(8,128)} %get-tuple-element.40), channel_id=1, source_target_pairs={{0,64},{8,72},{16,80},{24,88},{32,96},{40,104},{48,112},{56,120},{... | collective-permute-start | bytes 3145736 | tf_op jit(solution)/shard_map/ppermute | solution.py:397
  54.4 12.9 %collective-permute-start.7 = (f32[544,128]{1,0:T(8,128)S(1)}, f32[544,128]{1,0:T(8,128)S(1)}, u32[]{:S(2)}, u32[]{:S(2)}) collective-permute-start(f32[544,128]{1,0:T(8,128)S(1)} %pad_maximum_fusion), channel_id=1, source_target_pairs={{0,1},{1,2},{2,3},{3,4},{4,5},{5,6},{6,7},{8,9},{9,10},{10,11},{11... | collective-permute-start | bytes 835592 | tf_op jit(solution)/shard_map/ppermute | solution.py:431
  60.3 14.9 %collective-permute-start.8 = (f32[544,128]{1,0:T(8,128)S(1)}, f32[544,128]{1,0:T(8,128)S(1)}, u32[]{:S(2)}, u32[]{:S(2)}) collective-permute-start(f32[544,128]{1,0:T(8,128)S(1)} %pad_maximum_fusion), channel_id=1, source_target_pairs={{1,0},{2,1},{3,2},{4,3},{5,4},{6,5},{7,6},{9,8},{10,9},{11,10},{12... | collective-permute-start | bytes 835592 | tf_op jit(solution)/shard_map/ppermute | solution.py:431
  67.3 12.9 %collective-permute-start.12 = (f32[2,512,128]{2,1,0:T(8,128)S(1)}, f32[2,512,128]{2,1,0:T(8,128)S(1)}, u32[]{:S(2)}, u32[]{:S(2)}) collective-permute-start(f32[2,512,128]{2,1,0:T(8,128)S(1)} %get-tuple-element.37), channel_id=1, source_target_pairs={{0,16},{8,56},{16,32},{24,8},{32,48},{40,24},{48,0},{56,40},{64,80... | collective-permute-start | bytes 1572872 | tf_op jit(solution)/shard_map/ppermute | solution.py:389
  75.2 4.9 %copy-start.2 = (f32[4,2,512,128]{3,2,1,0:T(8,128)S(1)}, f32[4,2,512,128]{3,2,1,0:T(8,128)}, u32[]{:S(2)}) copy-start(f32[4,2,512,128]{3,2,1,0:T(8,128)} %get-tuple-element.19) | copy-start | bytes 6291460
  75.2 22.7 %collective-permute-start.11 = (f32[2,512,128]{2,1,0:T(8,128)S(1)}, f32[2,512,128]{2,1,0:T(8,128)S(1)}, u32[]{:S(2)}, u32[]{:S(2)}) collective-permute-start(f32[2,512,128]{2,1,0:T(8,128)S(1)} %get-tuple-element.36), channel_id=1, source_target_pairs={{0,48},{8,24},{16,0},{24,40},{32,16},{40,56},{48,32},{56,8},{64,11... | collective-permute-start | bytes 1572872 | tf_op jit(solution)/shard_map/ppermute | solution.py:393
  77.6 14.0 %collective-permute-start.14 = (f32[2,544,128]{2,1,0:T(8,128)S(1)}, f32[2,544,128]{2,1,0:T(8,128)S(1)}, u32[]{:S(2)}, u32[]{:S(2)}) collective-permute-start(f32[2,544,128]{2,1,0:T(8,128)S(1)} %get-tuple-element.39), channel_id=1, source_target_pairs={{0,64},{8,72},{16,80},{24,88},{32,96},{40,104},{48,112},{56,120},{... | collective-permute-start | bytes 1671176 | tf_op jit(solution)/shard_map/ppermute | solution.py:397
  81.5 16.4 %collective-permute-start.13 = (f32[2,512,128]{2,1,0:T(8,128)S(1)}, f32[2,512,128]{2,1,0:T(8,128)S(1)}, u32[]{:S(2)}, u32[]{:S(2)}) collective-permute-start(f32[2,512,128]{2,1,0:T(8,128)S(1)} %fusion.7), channel_id=1, source_target_pairs={{0,16},{8,56},{16,32},{24,8},{32,48},{40,24},{48,0},{56,40},{64,80... | collective-permute-start | bytes 1572872 | tf_op jit(solution)/shard_map/ppermute | solution.py:389
  91.7 10.1 %collective-permute-start.15 = (f32[544,128]{1,0:T(8,128)S(1)}, f32[544,128]{1,0:T(8,128)S(1)}, u32[]{:S(2)}, u32[]{:S(2)}) collective-permute-start(f32[544,128]{1,0:T(8,128)S(1)} %bitcast.86), channel_id=1, source_target_pairs={{0,1},{1,2},{2,3},{3,4},{4,5},{5,6},{6,7},{8,9},{9,10},{10,11},{11... | collective-permute-start | bytes 835592 | tf_op jit(solution)/shard_map/ppermute | solution.py:447
  96.0 13.5 %collective-permute-start.16 = (f32[544,128]{1,0:T(8,128)S(1)}, f32[544,128]{1,0:T(8,128)S(1)}, u32[]{:S(2)}, u32[]{:S(2)}) collective-permute-start(f32[544,128]{1,0:T(8,128)S(1)} %bitcast.88), channel_id=1, source_target_pairs={{1,0},{2,1},{3,2},{4,3},{5,4},{6,5},{7,6},{9,8},{10,9},{11,10},{12... | collective-permute-start | bytes 835592 | tf_op jit(solution)/shard_map/ppermute | solution.py:447
